TPU v7x, 32 devices: a whole 2x2x4 slice. The times are simulated.
32 devices in a mesh: dp: 16 (over z, y, x), fsdp: 2 (over core).
Axes of the slice: x: 2, y: 2, z: 4, core: 2. Of those that a mesh axis runs over, the one named last changes fastest.
Arguments:
- tokens: bfloat16 [64, 1024, 768], P(('dp', 'fsdp')), may hold values from -6 to 6
- cotangent: bfloat16 [64, 1024, 768], P(('dp', 'fsdp')), may hold values from -6 to 6
- segments: int32 [64, 1024], P(('dp', 'fsdp')), may hold values from 0 to 3, never falling along the last dimension, each value on 1 to 800 neighbouring positions
- in_gain: bfloat16 [768], P(('dp', 'fsdp')), may hold values from 0.099609375 to 1.8984375
- weight_in: bfloat16 [768, 3352], P(('dp', 'fsdp')), as said below
- conv_weight: bfloat16 [4, 1792], P(None, ('dp', 'fsdp')), may hold values from -3 to 3
- conv_bias: bfloat16 [1792], P(('dp', 'fsdp')), may hold values from -3 to 3
- step_bias: float32 [24], P('fsdp'), may hold values from -9 to -5
- decay_log: float32 [24], P('fsdp'), may hold values from 0 to 2.75
- skip_gain: float32 [24], P('fsdp'), may hold values from 0.5 to 1.5
- gate_gain: bfloat16 [1536], P(('dp', 'fsdp')), may hold values from 0.099609375 to 1.8984375
- weight_out: bfloat16 [1536, 768], P(('dp', 'fsdp')), may hold values from -0.15625 to 0.15625
Outputs:
- layer_out: bfloat16 [64, 1024, 768], P(('dp', 'fsdp'))
- grad_tokens: bfloat16 [64, 1024, 768], P(('dp', 'fsdp'))
- grad_in_gain: float32 [768], P(('dp', 'fsdp'))
- grad_weight_in: float32 [768, 3352], P(('dp', 'fsdp'))
- grad_conv_weight: float32 [4, 1792], P(None, ('dp', 'fsdp'))
- grad_conv_bias: float32 [1792], P(('dp', 'fsdp'))
- grad_step_bias: float32 [24], P('fsdp')
- grad_decay_log: float32 [24], P('fsdp')
- grad_skip_gain: float32 [24], P('fsdp')
- grad_gate_gain: float32 [1536], P(('dp', 'fsdp'))
- grad_weight_out: float32 [1536, 768], P(('dp', 'fsdp'))
Inputs may be any that keep to these rules, and one draw needn't show every extreme that they name: `segments`: in each sequence the document numbers never fall; each document holds 1 to 800 tokens, and one holds exactly 800. `weight_in`: A matrix of independent entries of mean zero.
All inputs are finite; a program needn't handle non-finite values.
Results may differ from a plain program's by a relative error of at most 0.014.
Values may be sent and summed in bfloat16 or wider, within the bound.
No kernel may reach another device: no remote copies, remote signals or barrier semaphores. Data moves between devices by JAX's collectives and lax.ppermute only.
A program may use at most 320 MiB of HBM per device.

v0:
```python
import jax
import jax.numpy as jnp
from jax import lax
from jax.sharding import PartitionSpec as P

SPAN = 256


epsilon = 1e-05


def root_norm(rows, gain):
    return rows * lax.rsqrt(jnp.mean(rows * rows, axis=-1, keepdims=True) + epsilon) * gain


def contract_rows(left, right):
    return lax.dot_general(
        left, right, (((0,), (0,)), ((), ())), preferred_element_type=jnp.float32
    )


def contract_cols(left, right):
    return lax.dot_general(
        left, right, (((1,), (1,)), ((), ())), preferred_element_type=jnp.float32
    )


def causal_conv(signal, docs, taps_weight, taps_bias):
    seqs, length, chans = signal.shape
    taps = taps_weight.shape[0]
    padded = jnp.pad(signal, ((0, 0), (taps - 1, 0), (0, 0)))
    doc_pad = jnp.pad(docs, ((0, 0), (taps - 1, 0)), constant_values=-1)
    total = jnp.zeros(signal.shape, jnp.float32) + taps_bias
    for offset in range(taps):
        window = padded[:, offset : offset + length]
        same = (doc_pad[:, offset : offset + length] == docs).astype(jnp.float32)[..., None]
        total = total + taps_weight[offset] * window * same
    return jax.nn.silu(total)


def span_update(state, pieces, rate, direct):
    block_x, block_step, block_b, block_c, block_doc, prev_doc = pieces
    width = block_x.shape[1]
    logs = jnp.cumsum(block_step * rate, axis=1)
    causal = jnp.arange(width)[:, None] >= jnp.arange(width)[None, :]
    joined = jnp.logical_and(causal[None], block_doc[:, :, None] == block_doc[:, None, :])[:, None]
    by_head = jnp.transpose(logs, (0, 2, 1))
    spread = by_head[:, :, :, None] - by_head[:, :, None, :]
    decay = jnp.exp(jnp.where(joined, spread, 0.0)) * joined.astype(jnp.float32)
    scores = jnp.einsum("sin,sjn->sij", block_c, block_b, preferred_element_type=jnp.float32)
    scaled = block_x * block_step[..., None]
    inside = jnp.einsum(
        "shij,sjhp->sihp", decay * scores[:, None], scaled, preferred_element_type=jnp.float32
    )
    carried = (block_doc == prev_doc[:, None]).astype(jnp.float32)
    reach = jnp.exp(logs) * carried[:, :, None]
    outside = (
        jnp.einsum("sin,shpn->sihp", block_c, state, preferred_element_type=jnp.float32)
        * reach[..., None]
    )
    ending = (block_doc == block_doc[:, -1:]).astype(jnp.float32)
    tail = jnp.exp(logs[:, -1:, :] - logs) * ending[:, :, None]
    fresh = jnp.einsum(
        "sjn,sjhp->shpn", block_b, scaled * tail[..., None], preferred_element_type=jnp.float32
    )
    keeping = jnp.exp(logs[:, -1, :]) * carried[:, -1:]
    state = state * keeping[:, :, None, None] + fresh
    return (state, inside + outside + block_x * direct[None, None, :, None])


def state_space(values, step, rate, inputs_b, outputs_c, docs, direct):
    seqs, length, heads, size = values.shape
    count = length // SPAN

    def split(arr):
        return jnp.swapaxes(arr.reshape((seqs, count, SPAN) + arr.shape[2:]), 0, 1)

    ends = docs.reshape(seqs, count, SPAN)[:, :, -1]
    prevs = jnp.concatenate([jnp.full((seqs, 1), -1, jnp.int32), ends[:, :-1]], axis=1).T
    start = jnp.zeros((seqs, heads, size, inputs_b.shape[-1]), jnp.float32)
    update = jax.checkpoint(lambda state, pieces: span_update(state, pieces, rate, direct))
    _, outs = lax.scan(
        update,
        start,
        (split(values), split(step), split(inputs_b), split(outputs_c), split(docs), prevs),
    )
    return jnp.swapaxes(outs, 0, 1).reshape(seqs, length, heads, size)


def mixer(projected, taps_weight, taps_bias, bias_step, log_decay, direct, gain, docs):
    seqs, length, _ = projected.shape
    inner = gain.shape[0]
    chans = taps_bias.shape[0]
    heads = bias_step.shape[0]
    states = (chans - inner) // 2
    gate = projected[..., :inner]
    conv_in = projected[..., inner : inner + chans]
    step_raw = projected[..., inner + chans :]
    conv_out = causal_conv(conv_in, docs, taps_weight, taps_bias)
    values = conv_out[..., :inner].reshape(seqs, length, heads, inner // heads)
    inputs_b = conv_out[..., inner : inner + states]
    outputs_c = conv_out[..., inner + states :]
    step = jax.nn.softplus(step_raw + bias_step)
    rate = -jnp.exp(log_decay)
    scanned = state_space(values, step, rate, inputs_b, outputs_c, docs, direct).reshape(
        seqs, length, inner
    )
    gated = scanned * jax.nn.silu(gate)
    return gated * lax.rsqrt(jnp.mean(gated * gated, axis=-1, keepdims=True) + epsilon) * gain


def local(
    tokens,
    cotangent,
    segments,
    in_gain,
    weight_in,
    conv_weight,
    conv_bias,
    step_bias,
    decay_log,
    skip_gain,
    gate_gain,
    weight_out,
):
    shards = (in_gain, weight_in, conv_weight, conv_bias, gate_gain, weight_out)
    gathered = (
        lax.all_gather(shards[0], ("dp", "fsdp"), axis=0, tiled=True),
        lax.all_gather(shards[1], ("dp", "fsdp"), axis=0, tiled=True),
        lax.all_gather(shards[2], ("dp", "fsdp"), axis=1, tiled=True),
        lax.all_gather(shards[3], ("dp", "fsdp"), axis=0, tiled=True),
        lax.all_gather(shards[4], ("dp", "fsdp"), axis=0, tiled=True),
        lax.all_gather(shards[5], ("dp", "fsdp"), axis=0, tiled=True),
    )
    head_terms = (
        lax.all_gather(step_bias, "fsdp", axis=0, tiled=True),
        lax.all_gather(decay_log, "fsdp", axis=0, tiled=True),
        lax.all_gather(skip_gain, "fsdp", axis=0, tiled=True),
    )
    seqs, length, width = tokens.shape
    rows = tokens.astype(jnp.float32).reshape(seqs * length, width)
    normed, norm_back = jax.vjp(root_norm, rows, gathered[0].astype(jnp.float32))
    normed_low = normed.astype(jnp.bfloat16)
    projected = jnp.dot(normed_low, gathered[1], preferred_element_type=jnp.float32)

    def mix_rows(proj_rows, taps_weight, taps_bias, bias_step, log_decay, direct, gain_gate):
        shaped = proj_rows.reshape(seqs, length, -1)
        return mixer(
            shaped, taps_weight, taps_bias, bias_step, log_decay, direct, gain_gate, segments
        ).reshape(seqs * length, -1)

    mixed, mix_back = jax.vjp(
        mix_rows,
        projected,
        gathered[2].astype(jnp.float32),
        gathered[3].astype(jnp.float32),
        head_terms[0],
        head_terms[1],
        head_terms[2],
        gathered[4].astype(jnp.float32),
    )
    mixed_low = mixed.astype(jnp.bfloat16)
    branch_out = jnp.dot(mixed_low, gathered[5], preferred_element_type=jnp.float32)
    layer_out = (rows + branch_out).astype(jnp.bfloat16).reshape(tokens.shape)
    weights = (
        lax.all_gather(shards[0], ("dp", "fsdp"), axis=0, tiled=True),
        lax.all_gather(shards[1], ("dp", "fsdp"), axis=0, tiled=True),
        lax.all_gather(shards[2], ("dp", "fsdp"), axis=1, tiled=True),
        lax.all_gather(shards[3], ("dp", "fsdp"), axis=0, tiled=True),
        lax.all_gather(shards[4], ("dp", "fsdp"), axis=0, tiled=True),
        lax.all_gather(shards[5], ("dp", "fsdp"), axis=0, tiled=True),
    )
    upstream = cotangent.reshape(seqs * length, width)
    grad_weight_out = contract_rows(mixed_low, upstream)
    grad_mixed = contract_cols(upstream, weights[5])
    grad_proj, grad_taps, grad_tap_bias, grad_bias_step, grad_log_decay, grad_direct, grad_gate = (
        mix_back(grad_mixed)
    )
    grad_proj_low = grad_proj.astype(jnp.bfloat16)
    grad_normed = contract_cols(grad_proj_low, weights[1])
    grad_weight_in = contract_rows(normed_low, grad_proj_low)
    grad_rows, grad_gain = norm_back(grad_normed)
    grad_tokens = (
        (upstream.astype(jnp.float32) + grad_rows).astype(jnp.bfloat16).reshape(tokens.shape)
    )
    summed = (
        lax.psum_scatter(grad_gain, ("dp", "fsdp"), scatter_dimension=0, tiled=True),
        lax.psum_scatter(grad_weight_in, ("dp", "fsdp"), scatter_dimension=0, tiled=True),
        lax.psum_scatter(grad_taps, ("dp", "fsdp"), scatter_dimension=1, tiled=True),
        lax.psum_scatter(grad_tap_bias, ("dp", "fsdp"), scatter_dimension=0, tiled=True),
        lax.psum_scatter(grad_gate, ("dp", "fsdp"), scatter_dimension=0, tiled=True),
        lax.psum_scatter(grad_weight_out, ("dp", "fsdp"), scatter_dimension=0, tiled=True),
    )
    head_sums = lax.psum((grad_bias_step, grad_log_decay, grad_direct), ("dp", "fsdp"))
    share = step_bias.shape[0]
    start_at = lax.axis_index("fsdp") * share
    owned = [lax.dynamic_slice_in_dim(term, start_at, share) for term in head_sums]
    return (
        layer_out,
        grad_tokens,
        summed[0],
        summed[1],
        summed[2],
        summed[3],
        owned[0],
        owned[1],
        owned[2],
        summed[4],
        summed[5],
    )


def solution(mesh):
    return jax.shard_map(
        local,
        mesh=mesh,
        in_specs=(
            P(("dp", "fsdp"), None, None),
            P(("dp", "fsdp"), None, None),
            P(("dp", "fsdp"), None),
            P(("dp", "fsdp")),
            P(("dp", "fsdp"), None),
            P(None, ("dp", "fsdp")),
            P(("dp", "fsdp")),
            P("fsdp"),
            P("fsdp"),
            P("fsdp"),
            P(("dp", "fsdp")),
            P(("dp", "fsdp"), None),
        ),
        out_specs=(
            P(("dp", "fsdp"), None, None),
            P(("dp", "fsdp"), None, None),
            P(("dp", "fsdp")),
            P(("dp", "fsdp"), None),
            P(None, ("dp", "fsdp")),
            P(("dp", "fsdp")),
            P("fsdp"),
            P("fsdp"),
            P("fsdp"),
            P(("dp", "fsdp")),
            P(("dp", "fsdp"), None),
        ),
        check_vma=False,
    )
```

profile of v0, /device:TPU:0, one launch (start us, length us, event | category | flops | bytes accessed | tf_op | source)
XLA Modules:
  0.0 1131.1 jit_solution(6356287721902963230)
XLA Ops:
  13.3 42.3 %all-reduce.32 = (bf16[768]{0:T(1024)(128)(2,1)S(1)}, bf16[1792]{0:T(1024)(128)(2,1)S(1)}, bf16[1536]{0:T(1024)(128)(2,1)S(1)}) all-reduce(bf16[768]{0:T(1024)(128)(2,1)S(1)} %dynamic-update-slice, bf16[1792]{0:T(1024)(128)(2,1)S(1)} %dynamic-update-slice.3, ...), channel_id=1, replica_groups=mesh['dp'=16,'fsdp'=2] {'dp','fsdp'}, use_global_device_ids=true, to_apply=%add.19 | all-reduce | flops 4096 | bytes 16384
  58.8 40.7 %all-gather = bf16[32,56,4]{1,2,0:T(4,128)(2,1)S(1)} all-gather(bf16[1,56,4]{1,2,0:T(4,128)(2,1)} %bitcast.492), channel_id=1, replica_groups=mesh['dp'=16,'fsdp'=2] {'dp','fsdp'}, dimensions={0}, use_global_device_ids=true | all-gather | bytes 14784 | tf_op jit(solution)/shard_map/all_gather | solution.py:130
  109.4 19.2 %fusion.125 = f32[2,1024,3352]{1,2,0:T(8,128)} fusion(bf16[768,3352]{1,0:T(8,128)(2,1)} %all-gather.4.cloned.1.call-done, bf16[2,1024,768]{2,1,0:T(8,128)(2,1)} %param.16, f32[768]{0:T(1024)S(1)} %convert_element_type.123, f32[2,1024]{1,0:T(2,128)S(1)} %get-tuple-element.948), kind=kOutput, calls=%fused_computation.216 | convolution fusion | flops 10550771712 | bytes 35765248 | tf_op jit(solution)/shard_map/dot_general | solution.py:144
  128.6 13.6 %slice.200 = f32[2,1024,1792]{1,2,0:T(8,128)} slice(f32[2,1024,3352]{1,2,0:T(8,128)} %fusion.125), slice={[0:2], [0:1024], [1536:3328]} | slice | bytes 29360128 | tf_op jit(solution)/shard_map/jvp()/slice | solution.py:97
  142.3 30.7 %fusion.111 = (f32[2,1024,1792]{1,2,0:T(8,128)}, f32[2,1024,1792]{1,2,0:T(8,128)}) fusion(f32[2,1024,1792]{1,2,0:T(8,128)} %slice.200, f32[1792]{0:T(1024)S(1)} %get-tuple-element.832, f32[2,1024]{1,0:T(2,128)S(1)} %get-tuple-element.950, f32[1792]{0:T(1024)S(1)} %get-tuple-element.833, f32[2,1024]{1,0:T(2,128)S(1)} %get-tuple-element.951, ...), kind=kLoop, calls=%fused_computation.182 | loop fusion | flops 55050240 | bytes 44100608 | tf_op jit(solution)/shard_map/jvp(jit(silu))/mul | solution.py:38
  174.7 11.9 %slice.204 = f32[2,1024,1536]{1,2,0:T(8,128)} slice(f32[2,1024,1792]{1,2,0:T(8,128)} %get-tuple-element.917), slice={[0:2], [0:1024], [0:1536]} | slice | bytes 25165824 | tf_op jit(solution)/shard_map/jvp()/slice | solution.py:100
  189.6 15.4 %reshape.576 = f32[2,4,256,24,64]{2,1,4,3,0:T(4,128)} reshape(f32[2,1024,1536]{1,2,0:T(8,128)} %slice.204) | data formatting | bytes 25165824 | tf_op jit(solution)/shard_map/jvp()/reshape;jvp()/reshape | solution.py:76
  205.1 11.6 %copy.323 = f32[2,4,256,24,64]{2,4,3,0,1:T(8,128)} copy(f32[2,4,256,24,64]{2,1,4,3,0:T(4,128)} %reshape.576) | data formatting | bytes 25165824 | tf_op jit(solution)/shard_map/jvp()/reshape;jvp()/reshape | solution.py:76
  217.8 6.2 broadcast.366.clone
  223.9 79.9 %while.43 = (s32[]{:T(128)}, f32[2,24,64,128]{3,2,1,0:T(8,128)S(1)}, f32[4,2,256,24,64]{2,4,3,1,0:T(8,128)}, f32[4,2,24,64,128]{4,3,2,1,0:T(8,128)}, f32[4,2,256...) while((s32[]{:T(128)}, ...), condition=%wide.region_4.5_spmd.clone, body=%wide.region_1.4_spmd.clone.sunk | while | flops 861010112 | bytes 30712980 | solution.py:82
  227.7 6.2 fusion.226
  234.4 5.2 bitcast_dynamic-update-slice_fusion.6
  247.6 6.2 fusion.226
  254.3 5.2 bitcast_dynamic-update-slice_fusion.6
  267.5 6.2 fusion.226
  274.2 5.4 bitcast_dynamic-update-slice_fusion.6
  287.6 6.2 fusion.226
  294.3 5.2 bitcast_dynamic-update-slice_fusion.6
  303.8 16.5 %copy.267 = f32[2,4,256,24,64]{2,1,4,3,0:T(4,128)} copy(f32[2,4,256,24,64]{2,4,3,0,1:T(8,128)} %bitcast.473) | data formatting | bytes 25165824 | tf_op jit(solution)/shard_map/jvp()/transpose | solution.py:87
  320.4 15.7 %reshape.579 = f32[2,1024,1536]{1,2,0:T(8,128)} reshape(f32[2,4,256,24,64]{2,1,4,3,0:T(4,128)} %copy.267) | data formatting | bytes 25165824 | tf_op jit(solution)/shard_map/jvp()/reshape;jvp()/reshape | solution.py:105
  336.0 16.0 %multiply_reduce_fusion.12 = (f32[2,1024]{1,0:T(2,128)S(1)}, f32[2,1024,1536]{1,2,0:T(8,128)}) fusion(f32[2,1024,1536]{1,2,0:T(8,128)} %reshape.579, f32[2,1024,3352]{1,2,0:T(8,128)} %fusion.125), kind=kLoop, calls=%fused_computation.194 | loop fusion | flops 22018048 | bytes 37756928 | tf_op jit(solution)/shard_map/jvp()/reduce_sum | solution.py:109
  352.1 13.3 %multiply_reduce_fusion.10 = (f32[1536]{0:T(1024)}, f32[2,1024]{1,0:T(2,128)S(1)}, f32[2,1024,1536]{1,2,0:T(8,128)}) fusion(f32[2,1024,1536]{1,2,0:T(8,128)} %get-tuple-element.916, f32[2,1024]{1,0:T(2,128)S(1)} %fusion.140, f32[1536]{0:T(1024)S(1)} %copy-done.37, bf16[2,1024,768]{2,1,0:T(8,128)(2,1)S(1)} %copy-done.18, ...), kind=kOutput, calls=%fused_computation.191 | convolution fusion | flops 4850708992 | bytes 30699520 | tf_op jit(solution)/shard_map/dot_general | solution.py:23
  365.4 30.0 %fusion.124 = (f32[2,1024,1536]{1,2,0:T(8,128)}, f32[2,1024,1536]{1,2,0:T(8,128)}, bf16[2,1024,1536]{1,2,0:T(8,128)(2,1)}) fusion(f32[2,1024,1536]{1,2,0:T(8,128)} %get-tuple-element.916, f32[2,1024]{1,0:T(2,128)S(1)} %multiply_multiply_fusion.3, f32[2,1024,1536]{1,2,0:T(8,128)} %get-tuple-element.954, f32[1536]{0:T(1024)S(1)} %copy-done.37, ...), kind=kLoop, calls=%fused_computation.215 | loop fusion | flops 62914560 | bytes 81811456 | tf_op jit(solution)/shard_map/transpose(jvp())/mul | solution.py:108
  395.4 15.5 %reshape.581 = f32[2,4,256,24,64]{2,1,4,3,0:T(4,128)} reshape(f32[2,1024,1536]{1,2,0:T(8,128)} %get-tuple-element.938) | data formatting | bytes 25165824 | tf_op jit(solution)/shard_map/transpose(jvp())/reshape;transpose(jvp())/reshape | solution.py:87
  410.9 11.5 %copy.322 = f32[2,4,256,24,64]{2,4,3,0,1:T(8,128)} copy(f32[2,4,256,24,64]{2,1,4,3,0:T(4,128)} %reshape.581) | data formatting | bytes 25165824 | tf_op jit(solution)/shard_map/transpose(jvp())/reshape;transpose(jvp())/reshape | solution.py:87
  422.4 6.1 broadcast.366
  431.4 393.0 %while.44 = (s32[]{:T(128)}, f32[24]{0:T(128)}, f32[24]{0:T(128)}, f32[2,24,64,128]{3,2,1,0:T(8,128)}, f32[4,2,256,24,64]{2,4,3,1,0:T(8,128)}, /*index=5*/f32[4,...) while((s32[]{:T(128)}, f32[24]{0:T(128)}, f32[24]{0:T(128)}, ...), condition=%wide.region_22.23_spmd.clone, body=%wide.region_7.22_spmd.clone.sunk | while | flops 1980537088 | bytes 115322104 | solution.py:82
  431.6 5.1 dynamic-slice_bitcast_fusion.17
  457.4 3.7 fusion.248
  464.3 9.6 multiply_reduce_fusion.18
  483.9 10.2 fusion.247
  509.4 6.3 reduce-window.74
  518.2 4.3 bitcast_dynamic-update-slice_fusion.8
  528.2 5.1 dynamic-slice_bitcast_fusion.17
  562.3 9.6 multiply_reduce_fusion.18
  581.9 10.2 fusion.247
  607.4 6.3 reduce-window.74
  616.2 4.4 bitcast_dynamic-update-slice_fusion.8
  627.0 5.1 dynamic-slice_bitcast_fusion.17
  661.1 9.6 multiply_reduce_fusion.18
  680.7 10.2 fusion.247
  706.2 6.3 reduce-window.74
  714.9 4.3 bitcast_dynamic-update-slice_fusion.8
  725.7 5.1 dynamic-slice_bitcast_fusion.17
  752.9 3.7 fusion.248
  759.7 9.6 multiply_reduce_fusion.18
  779.4 10.2 fusion.247
  804.8 6.3 reduce-window.74
  813.6 4.4 bitcast_dynamic-update-slice_fusion.8
  824.4 16.8 %copy.275 = f32[2,4,256,24,64]{2,1,4,3,0:T(4,128)} copy(f32[2,4,256,24,64]{2,4,3,0,1:T(8,128)} %bitcast.472) | data formatting | bytes 25165824 | tf_op jit(solution)/shard_map/transpose(jvp())/transpose | solution.py:76
  841.2 15.8 %reshape.585 = f32[2,1024,1536]{1,2,0:T(8,128)} reshape(f32[2,4,256,24,64]{2,1,4,3,0:T(4,128)} %copy.275) | data formatting | bytes 25165824 | tf_op jit(solution)/shard_map/transpose(jvp())/reshape;transpose(jvp())/reshape | solution.py:100
  861.3 9.6 convolution_bitcast_fusion.1
  871.0 30.6 %multiply_reduce_fusion.8 = (f32[1792]{0:T(1024)S(1)}, f32[1792]{0:T(1024)S(1)}, f32[1792]{0:T(1024)S(1)}, f32[1792]{0:T(1024)S(1)}, f32[1792]{0:T(1024)S(1)}, /*index=5*/f32[2,1024,1792]{1,2,0:T(8,128)S(1)}) fusion(f32[2,1024,1792]{1,2,0:T(8,128)} %slice.200, f32[2,1024]{1,0:T(2,128)S(1)} %copy-done.24, f32[2,1024]{1,0:T(2,128)S(1)} %copy-done.26, ...), kind=kLoop, calls=%fused_computation.179 | loop fusion | flops 84401408 | bytes 73460736 | tf_op jit(solution)/shard_map/transpose(jvp())/reduce_sum | solution.py:37
  901.6 20.1 %broadcast_multiply_fusion.2 = (f32[2,1024,1792]{1,2,0:T(8,128)}, f32[2,1024,1792]{1,2,0:T(8,128)}, f32[2,1024,1792]{1,2,0:T(8,128)}, f32[2,1024,1792]{1,2,0:T(8,128)}) fusion(f32[2,1024,1792]{1,2,0:T(8,128)S(1)} %get-tuple-element.914, f32[1792]{0:T(1024)S(1)} %copy-done.31, f32[2,1024]{1,0:T(2,128)S(1)} %copy-done.22, f32[1792]{0:T(1024)S(1)} %copy-done.29, ...), kind=kLoop, calls=%fused_computation.199 | loop fusion | flops 25690112 | bytes 73453568 | tf_op jit(solution)/shard_map/transpose(jvp())/mul | solution.py:37
  921.7 27.1 %pad_add_fusion = f32[2,1024,1792]{1,2,0:T(8,128)} fusion(f32[2,1024,1792]{1,2,0:T(8,128)} %get-tuple-element.941, f32[2,1024,1792]{1,2,0:T(8,128)} %get-tuple-element.942, f32[2,1024,1792]{1,2,0:T(8,128)} %get-tuple-element.943, f32[2,1024,1792]{1,2,0:T(8,128)} %get-tuple-element.940), kind=kLoop, calls=%fused_computation.174 | loop fusion | flops 11010048 | bytes 73400320 | tf_op jit(solution)/shard_map/transpose(jvp())/add_any | solution.py:35
  948.8 16.0 %add_convert_fusion = bf16[2,1024,3352]{1,2,0:T(8,128)(2,1)} fusion(f32[2,1024,1536]{1,2,0:T(8,128)} %get-tuple-element.939, f32[2,1024,1792]{1,2,0:T(8,128)} %pad_add_fusion, f32[2,1024,24]{1,2,0:T(8,128)S(1)} %get-tuple-element.913), kind=kLoop, calls=%fused_computation.165 | loop fusion | flops 20594688 | bytes 41189376 | tf_op jit(solution)/shard_map/convert_element_type | solution.py:179
  964.8 18.4 %convolution_bitcast_fusion = f32[768,3352]{1,0:T(8,128)} fusion(bf16[2,1024,3352]{1,2,0:T(8,128)(2,1)} %add_convert_fusion, bf16[2,1024,768]{2,1,0:T(8,128)(2,1)S(1)} %copy-done.11, f32[768]{0:T(1024)S(1)} %copy-done.40, f32[2,1024]{1,0:T(2,128)S(1)} %copy-done.43), kind=kOutput, calls=%fused_computation.198 | convolution fusion | flops 10550771712 | bytes 27184128 | tf_op jit(solution)/shard_map/dot_general | solution.py:17
  983.3 18.1 %copy.276 = bf16[2,1024,3352]{2,1,0:T(8,128)(2,1)} copy(bf16[2,1024,3352]{1,2,0:T(8,128)(2,1)} %add_convert_fusion) | data formatting | bytes 27459584 | tf_op jit(solution)/shard_map/convert_element_type | solution.py:179
  1001.4 8.8 copy.268
  1010.3 19.5 %fusion.123 = (f32[768]{0:T(1024)S(1)}, f32[2048]{0:T(1024)S(1)}, f32[2048,768]{1,0:T(8,128)}) fusion(bf16[2,1024,768]{2,1,0:T(8,128)(2,1)S(1)} %copy-done.11, f32[2048]{0:T(1024)S(1)} %bitcast_rsqrt_fusion, f32[768]{0:T(1024)S(1)} %copy-done.40, bf16[2048,3352]{1,0:T(8,128)(2,1)} %bitcast.475, bf16[768,3352]{1,0:T(8,128)(2,1)} %all-gather.4.cloned.1.call-done), kind=kOutput, calls=%fused_computation.214 | convolution fusion | flops 10555487232 | bytes 28338176 | tf_op jit(solution)/shard_map/dot_general | solution.py:23
  1029.9 41.6 %all-reduce.30 = (f32[768]{0:T(1024)S(1)}, f32[4,1792]{1,0:T(4,128)S(1)}, f32[1792]{0:T(1024)S(1)}, f32[24]{0:T(128)S(1)}, f32[24]{0:T(128)S(1)}, /*index=5*/f32[24]{0:T(128)S(1)}, f32[1536]{0:T(1024)S(1)}) all-reduce(f32[768]{0:T(1024)S(1)} %get-tuple-element.829, ...), channel_id=2, replica_groups=mesh['dp'=16,'fsdp'=2] {'dp','fsdp'}, use_global_device_ids=true, to_apply=%region_25.26.clone | all-reduce | flops 11336 | bytes 90688
  1075.7 5.8 fusion.116
  1081.5 9.8 fusion.120
  1091.4 32.9 %reduce-scatter.8.cloned.1.call-done = f32[24,3352]{1,0:T(8,128)} async-done(((f32[768,3352]{1,0:T(8,128)}), f32[24,3352]{1,0:T(8,128)}) %reduce-scatter.8.cloned.1.call-update) | async-done | bytes 321808
  (545 shorter events, 312.1 us)
Async XLA Ops:
  7.2 102.2 %all-gather.4.cloned.1.call-start = ((), (), s32[]{:S(2)}) async-start(), calls=%async_computation.2 | async-start | bytes 5474304 | tf_op jit(solution)/shard_map/all_gather | solution.py:129
  7.9 344.1 %all-gather.6.cloned.1.call-start = ((), (), s32[]{:S(2)}) async-start(), calls=%async_computation.3 | async-start | bytes 2433024 | tf_op jit(solution)/shard_map/all_gather | solution.py:133
  8.7 1082.7 %reduce-scatter.6.cloned.1.call-start = ((), (), s32[]{:S(2)}) async-start(), calls=%async_computation.4 | async-start | bytes 4866048 | tf_op jit(solution)/shard_map/reduce_scatter | solution.py:192
  9.7 132.6 %copy-start.21 = (f32[2,1024]{1,0:T(2,128)}, f32[2,1024]{1,0:T(2,128)S(1)}, u32[]{:S(2)}) copy-start(f32[2,1024]{1,0:T(2,128)S(1)} %get-tuple-element.949) | copy-start | bytes 24580
  9.7 132.6 %copy-start.23 = (f32[2,1024]{1,0:T(2,128)}, f32[2,1024]{1,0:T(2,128)S(1)}, u32[]{:S(2)}) copy-start(f32[2,1024]{1,0:T(2,128)S(1)} %get-tuple-element.950) | copy-start | bytes 24580
  9.7 132.6 %copy-start.25 = (f32[2,1024]{1,0:T(2,128)}, f32[2,1024]{1,0:T(2,128)S(1)}, u32[]{:S(2)}) copy-start(f32[2,1024]{1,0:T(2,128)S(1)} %get-tuple-element.951) | copy-start | bytes 24580
  10.6 118.0 %copy-start.12 = (s32[2,1024]{0,1:T(8,128)}, s32[2,1024]{0,1:T(8,128)S(1)}, u32[]{:S(2)}) copy-start(s32[2,1024]{0,1:T(8,128)S(1)} %copy.259) | copy-start | bytes 24580
  55.6 73.1 %copy-start.39 = (f32[768]{0:T(1024)}, f32[768]{0:T(1024)S(1)}, u32[]{:S(2)}) copy-start(f32[768]{0:T(1024)S(1)} %convert_element_type.123) | copy-start | bytes 9220
  58.7 69.9 %copy-start.42 = (f32[2,1024]{1,0:T(2,128)}, f32[2,1024]{1,0:T(2,128)S(1)}, u32[]{:S(2)}) copy-start(f32[2,1024]{1,0:T(2,128)S(1)} %get-tuple-element.948) | copy-start | bytes 24580
  99.6 42.6 %copy-start.28 = (f32[1792]{0:T(1024)}, f32[1792]{0:T(1024)S(1)}, u32[]{:S(2)}) copy-start(f32[1792]{0:T(1024)S(1)} %get-tuple-element.831) | copy-start | bytes 21508
  99.6 42.6 %copy-start.30 = (f32[1792]{0:T(1024)}, f32[1792]{0:T(1024)S(1)}, u32[]{:S(2)}) copy-start(f32[1792]{0:T(1024)S(1)} %get-tuple-element.832) | copy-start | bytes 21508
  99.7 42.6 %copy-start.32 = (f32[1792]{0:T(1024)}, f32[1792]{0:T(1024)S(1)}, u32[]{:S(2)}) copy-start(f32[1792]{0:T(1024)S(1)} %get-tuple-element.833) | copy-start | bytes 21508
  99.7 42.6 %copy-start.34 = (f32[1792]{0:T(1024)}, f32[1792]{0:T(1024)S(1)}, u32[]{:S(2)}) copy-start(f32[1792]{0:T(1024)S(1)} %get-tuple-element.834) | copy-start | bytes 21508
  107.3 109.4 %copy-start.45 = (f32[24]{0:T(128)}, f32[24]{0:T(128)S(1)}, u32[]{:S(2)}) copy-start(f32[24]{0:T(128)S(1)} %get-tuple-element.902) | copy-start | bytes 292
  303.8 16.6 %copy-start.19 = (f32[4,2,256,24]{2,3,1,0:T(8,128)}, f32[4,2,256,24]{2,3,1,0:T(8,128)S(1)}, u32[]{:S(2)}) copy-start(f32[4,2,256,24]{2,3,1,0:T(8,128)S(1)} %get-tuple-element.1338) | copy-start | bytes 589828
  336.0 16.0 %copy-start.18 = (bf16[2,1024,768]{2,1,0:T(8,128)(2,1)S(1)}, bf16[2,1024,768]{2,1,0:T(8,128)(2,1)}, u32[]{:S(2)}) copy-start(bf16[2,1024,768]{2,1,0:T(8,128)(2,1)} %param.17) | copy-start | bytes 9437188
  336.0 16.0 %copy-start.37 = (f32[1536]{0:T(1024)S(1)}, f32[1536]{0:T(1024)}, u32[]{:S(2)}) copy-start(f32[1536]{0:T(1024)} %convert_element_type.130) | copy-start | bytes 18436
  448.2 25.7 %copy-start.36 = (f32[2]{0:T(128)}, f32[2]{0:T(128)S(1)}, u32[]{:S(2)}) copy-start(f32[2]{0:T(128)S(1)} %slice_bitcast_fusion.6) | copy-start | bytes 28 | tf_op jit(solution)/shard_map/transpose(jvp())/while
  483.9 10.3 copy-start.3
  483.9 11.2 copy-start.1
  483.9 11.2 copy-start.2
  483.9 11.1 copy-start.5
  483.9 11.1 copy-start.13
  539.6 10.5 copy-start.4
  546.2 25.7 %copy-start.36 = (f32[2]{0:T(128)}, f32[2]{0:T(128)S(1)}, u32[]{:S(2)}) copy-start(f32[2]{0:T(128)S(1)} %slice_bitcast_fusion.6) | copy-start | bytes 28 | tf_op jit(solution)/shard_map/transpose(jvp())/while
  581.9 10.3 copy-start.3
  581.9 11.2 copy-start.1
  581.9 11.2 copy-start.2
  581.9 11.2 copy-start.5
  581.9 11.2 copy-start.13
  614.6 9.8 copy-start.6
  614.6 9.8 copy-start.9
  638.3 10.5 copy-start.4
  645.0 25.7 %copy-start.36 = (f32[2]{0:T(128)}, f32[2]{0:T(128)S(1)}, u32[]{:S(2)}) copy-start(f32[2]{0:T(128)S(1)} %slice_bitcast_fusion.6) | copy-start | bytes 28 | tf_op jit(solution)/shard_map/transpose(jvp())/while
  680.6 10.3 copy-start.3
  680.6 11.2 copy-start.1
  680.6 11.2 copy-start.2
  680.7 11.2 copy-start.5
  680.7 11.1 copy-start.13
  737.0 10.5 copy-start.4
  743.7 25.7 %copy-start.36 = (f32[2]{0:T(128)}, f32[2]{0:T(128)S(1)}, u32[]{:S(2)}) copy-start(f32[2]{0:T(128)S(1)} %slice_bitcast_fusion.6) | copy-start | bytes 28 | tf_op jit(solution)/shard_map/transpose(jvp())/while
  779.3 10.3 copy-start.3
  779.3 11.2 copy-start.1
  779.3 11.2 copy-start.2
  779.3 11.2 copy-start.5
  779.3 11.1 copy-start.13
  812.0 9.8 copy-start.6
  812.0 9.8 copy-start.9
  841.2 15.8 %copy-start.15 = (f32[4,2,256,128]{3,2,1,0:T(8,128)S(1)}, f32[4,2,256,128]{3,2,1,0:T(8,128)}, u32[]{:S(2)}) copy-start(f32[4,2,256,128]{3,2,1,0:T(8,128)} %get-tuple-element.492) | copy-start | bytes 3145732
  841.2 17.7 %copy-start.14 = (f32[4,2,256,128]{3,2,1,0:T(8,128)S(1)}, f32[4,2,256,128]{3,2,1,0:T(8,128)}, u32[]{:S(2)}) copy-start(f32[4,2,256,128]{3,2,1,0:T(8,128)} %get-tuple-element.493) | copy-start | bytes 3145732
  841.2 18.7 %copy-start.20 = (f32[4,2,256,24]{2,3,1,0:T(8,128)S(1)}, f32[4,2,256,24]{2,3,1,0:T(8,128)}, u32[]{:S(2)}) copy-start(f32[4,2,256,24]{2,3,1,0:T(8,128)} %get-tuple-element.491) | copy-start | bytes 589828
  841.2 18.7 %copy-start.46 = (f32[24]{0:T(128)S(1)}, f32[24]{0:T(128)}, u32[]{:S(2)}) copy-start(f32[24]{0:T(128)} %copy-done.45) | copy-start | bytes 292
  870.8 253.5 %reduce-scatter.8.cloned.1.call-start = ((), (), s32[]{:S(2)}) async-start(), calls=%async_computation.5 | async-start | bytes 10948608
  870.9 30.6 %copy-start.29 = (f32[1792]{0:T(1024)S(1)}, f32[1792]{0:T(1024)}, u32[]{:S(2)}) copy-start(f32[1792]{0:T(1024)} %copy-done.28) | copy-start | bytes 21508
  870.9 30.6 %copy-start.31 = (f32[1792]{0:T(1024)S(1)}, f32[1792]{0:T(1024)}, u32[]{:S(2)}) copy-start(f32[1792]{0:T(1024)} %copy-done.30) | copy-start | bytes 21508
  871.0 30.6 %copy-start.33 = (f32[1792]{0:T(1024)S(1)}, f32[1792]{0:T(1024)}, u32[]{:S(2)}) copy-start(f32[1792]{0:T(1024)} %copy-done.32) | copy-start | bytes 21508
  871.0 30.6 %copy-start.35 = (f32[1792]{0:T(1024)S(1)}, f32[1792]{0:T(1024)}, u32[]{:S(2)}) copy-start(f32[1792]{0:T(1024)} %copy-done.34) | copy-start | bytes 21508
  948.8 16.0 %copy-start.11 = (bf16[2,1024,768]{2,1,0:T(8,128)(2,1)S(1)}, bf16[2,1024,768]{2,1,0:T(8,128)(2,1)}, u32[]{:S(2)}) copy-start(bf16[2,1024,768]{2,1,0:T(8,128)(2,1)} %param.16) | copy-start | bytes 9437188
  948.8 16.0 %copy-start.40 = (f32[768]{0:T(1024)S(1)}, f32[768]{0:T(1024)}, u32[]{:S(2)}) copy-start(f32[768]{0:T(1024)} %copy-done.39) | copy-start | bytes 9220
  948.8 16.0 %copy-start.43 = (f32[2,1024]{1,0:T(2,128)S(1)}, f32[2,1024]{1,0:T(2,128)}, u32[]{:S(2)}) copy-start(f32[2,1024]{1,0:T(2,128)} %copy-done.42) | copy-start | bytes 24580
  964.8 18.5 %copy-start.27 = (f32[1,8,2,128]{3,2,1,0:T(2,128)S(1)}, f32[1,8,2,128]{3,2,1,0:T(2,128)}, u32[]{:S(2)}) copy-start(f32[1,8,2,128]{3,2,1,0:T(2,128)} %get-tuple-element.947) | copy-start | bytes 24580
  1010.3 19.6 %copy-start.38 = (f32[24]{0:T(128)S(1)}, f32[24]{0:T(128)}, u32[]{:S(2)}) copy-start(f32[24]{0:T(128)} %get-tuple-element.496) | copy-start | bytes 292
  1010.3 19.6 %copy-start.44 = (f32[1536]{0:T(1024)S(1)}, f32[1536]{0:T(1024)}, u32[]{:S(2)}) copy-start(f32[1536]{0:T(1024)} %get-tuple-element.825) | copy-start | bytes 18436
  1071.5 10.0 copy-start.47
  (32 other events, 224.4 us)
Sparse Core Ops, SparseCore 0:
  10.9 68.3 all-gather.3
  82.2 56.1 all-gather.5
  871.0 103.0 reduce-scatter.5
  983.4 140.8 reduce-scatter.7
where the time goes:
time: 1140 us; the launch traced here: 1130 us
  local copies, waits for them, and re-layouts  331 us (29%)
  other arithmetic  328 us (29%)
  matrix products  293 us (26%)
  blocking collectives  128 us (11%)
  waiting for transfers between devices  34.4 us (3%)
  between operations  15.3 us (1%)
    dot_general x12, matrix products, span_update(): jnp.einsum('shij,sjhp->sihp', decay * scores[:, None], scaled, preferred_...  104 us
    unnamed x3, blocking collectives  87.1 us
    dot_general x16, matrix products, span_update(): jnp.einsum('sin,shpn->sihp', block_c, state, preferred_element_type=jnp.f...  50.2 us
    squeeze x24, local copies, waits for them, and re-layouts, state_space(): lax.scan(update, start, (split(values), split(step), split(inputs_b), spl...  48 us
    another operation x36, other arithmetic  48 us
    all_gather x1, blocking collectives, local(): lax.all_gather(shards[2], ('dp', 'fsdp'), axis=1, tiled=True)  40.7 us
    unnamed x5, waiting for transfers between devices  34.4 us
    dot_general x2, matrix products, contract_cols(): lax.dot_general(left, right, (((1,), (1,)), ((), ())), preferred_element_...  32.8 us
  transfers between devices with their start and end apart: 4, of which 1 were waited for; matrix products, arithmetic and copies ran while one was open for 38% of the time, Pallas kernels for 0%

commit v1 on v0

v1 whole, which is shorter than its diff:
```python
import functools

import jax
import jax.numpy as jnp
import numpy as np
from jax import lax
from jax.experimental import pallas as pl
from jax.experimental.pallas import tpu as pltpu
from jax.sharding import PartitionSpec as P

EPS = 1e-05
LOG2E = 1.4426950408889634
NEG = -1e30
f32, bf16 = jnp.float32, jnp.bfloat16
Q = 128
VM = 60 * 1024 * 1024

D, DI, CONV, N, HD = 768, 1536, 1792, 128, 64


def dot(a, b):
    return lax.dot_general(a, b, (((1,), (0,)), ((), ())), preferred_element_type=f32)


def dot_nt(a, b):
    return lax.dot_general(a, b, (((1,), (1,)), ((), ())), preferred_element_type=f32)


def dot_tn(a, b):
    return lax.dot_general(a, b, (((0,), (0,)), ((), ())), preferred_element_type=f32)


def sigmoid(v):
    return 1.0 / (1.0 + jnp.exp(-v))


def cumsum_rows(v, reverse=False):
    rows = lax.broadcasted_iota(jnp.int32, v.shape, 0)
    count = v.shape[0]
    shift = 1
    while shift < count:
        if reverse:
            moved = pltpu.roll(v, count - shift, 0)
            v = v + jnp.where(rows < count - shift, moved, 0.0)
        else:
            moved = pltpu.roll(v, shift, 0)
            v = v + jnp.where(rows >= shift, moved, 0.0)
        shift *= 2
    return v


def step_terms(z):
    e = jnp.exp(-jnp.abs(z))
    soft = jnp.maximum(z, 0.0) + jnp.log1p(e)
    tiny = z < -15.0
    log_soft = jnp.where(tiny, z, jnp.log(jnp.where(tiny, 1.0, soft)))
    return soft, log_soft


def scan_factors(z, rate, doc, prev_doc):
    soft, log_soft = step_terms(z)
    a = cumsum_rows(soft * (rate * LOG2E))
    b = a - log_soft * LOG2E
    last = a[Q - 1 : Q, :]
    last_doc = doc[Q - 1 : Q, :]
    reach = jnp.where(doc == prev_doc, jnp.exp2(a), 0.0)
    tail = jnp.where(doc == last_doc, jnp.exp2(last - b), 0.0)
    keep = jnp.where(last_doc == prev_doc, jnp.exp2(last), 0.0)
    return soft, a, b, reach, tail, keep


def pair_of(cols, p, low):
    left = jnp.broadcast_to(cols[:, 2 * p : 2 * p + 1], low.shape)
    right = jnp.broadcast_to(cols[:, 2 * p + 1 : 2 * p + 2], low.shape)
    return jnp.where(low, left, right)


def forward_scan_kernel(heads, per_seq, tok, wc, gain, cw, cb, sb, rate, skip, docc, docr, m1, m2, m3,
                        cin_o, pre_o, nrm_o, scan_o, st_o, z_o, pbuf, vbuf, state, pdoc):
    i = pl.program_id(0)

    @pl.when(lax.rem(i, per_seq) == 0)
    def _():
        pbuf[0:8, :] = jnp.zeros((8, CONV), f32)
        state[...] = jnp.zeros_like(state)
        pdoc[...] = jnp.full(pdoc.shape, -1.0, f32)

    x = tok[...].astype(f32)
    r = lax.rsqrt(jnp.mean(x * x, axis=-1, keepdims=True) + EPS)
    nb = (x * r * gain[...]).astype(bf16)
    nrm_o[...] = nb
    proj = dot(nb, wc[...])
    z = proj[:, CONV:] + sb[...]
    z_o[...] = z
    pbuf[8 : 8 + Q, :] = proj[:, :CONV]
    masks = (m3[...].astype(f32), m2[...].astype(f32), m1[...].astype(f32))
    for t in range(CONV // 128):
        cols = slice(128 * t, 128 * t + 128)
        now = pbuf[8 : 8 + Q, cols]
        cin_o[:, cols] = now.astype(bf16)
        pre = cb[:, cols] + cw[3:4, cols] * now
        for k in range(3):
            pre = pre + cw[k : k + 1, cols] * (pbuf[5 + k : 5 + k + Q, cols] * masks[k])
        pre_o[:, cols] = pre.astype(bf16)
        vbuf[:, cols] = (pre * sigmoid(pre)).astype(bf16)
    pbuf[0:8, :] = pbuf[Q : Q + 8, :]

    doc = docc[...]
    prev = pdoc[0:1, :]
    soft, a, b, reach, tail, keep = scan_factors(z, rate[...], doc, prev)
    pdoc[...] = jnp.broadcast_to(doc[Q - 1 : Q, :], pdoc.shape)
    bt = b.T
    row = lax.broadcasted_iota(jnp.int32, (Q, Q), 0)
    lane = lax.broadcasted_iota(jnp.int32, (Q, Q), 1)
    joined = (row >= lane) & (doc == docr[0, 0:1, :])
    low = lane < HD
    low_row = low[0:1, :]
    bmat = vbuf[:, DI : DI + N]
    cmat = vbuf[:, DI + N :]
    bt_mat = bmat.astype(f32).T.astype(bf16)
    s = dot_nt(cmat, bmat)
    st_low = state[...].astype(bf16)
    st_o[0] = st_low
    cs = dot(cmat, st_low)
    zero = jnp.zeros((Q, Q), bf16)
    for p in range(heads // 2):
        cols = slice(128 * p, 128 * p + 128)
        parts = []
        for h in (2 * p, 2 * p + 1):
            spread = jnp.broadcast_to(a[:, h : h + 1], (Q, Q)) - bt[h : h + 1, :]
            parts.append((jnp.exp2(jnp.where(joined, spread, NEG)) * s).astype(bf16))
        xp = vbuf[:, cols]
        xbd = jnp.concatenate([jnp.where(low, xp, zero), jnp.where(low, zero, xp)], axis=0)
        y = dot(jnp.concatenate(parts, axis=1), xbd)
        xf = xp.astype(f32)
        y = y + cs[:, cols] * pair_of(reach, p, low) + xf * skip[:, cols]
        scan_o[:, cols] = y.astype(bf16)
        xw = (xf * pair_of(tail, p, low)).astype(bf16)
        state[:, cols] = state[:, cols] * pair_of(keep, p, low_row) + dot(bt_mat, xw)


def forward_scan(tok, wc, gain, cw, cb, sb, rate, skip, docc, docr, m1, m2, m3, heads, seqs):
    rows = tok.shape[0]
    n = rows // Q
    one = pl.Buffered(buffer_count=1)
    full = lambda arr: pl.BlockSpec(arr.shape, lambda i: (0,) * arr.ndim, pipeline_mode=one)
    blk = lambda w: pl.BlockSpec((Q, w), lambda i: (i, 0))
    return pl.pallas_call(
        functools.partial(forward_scan_kernel, heads, n // seqs),
        grid=(n,),
        in_specs=[blk(D), full(wc), full(gain), full(cw), full(cb), full(sb), full(rate), full(skip),
                  blk(128), pl.BlockSpec((1, 8, 128), lambda i: (i, 0, 0)), blk(128), blk(128), blk(128)],
        out_specs=[blk(CONV), blk(CONV), blk(D), blk(DI), pl.BlockSpec((1, N, DI), lambda i: (i, 0, 0)), blk(128)],
        out_shape=[jax.ShapeDtypeStruct((rows, CONV), bf16), jax.ShapeDtypeStruct((rows, CONV), bf16),
                   jax.ShapeDtypeStruct((rows, D), bf16), jax.ShapeDtypeStruct((rows, DI), bf16),
                   jax.ShapeDtypeStruct((n, N, DI), bf16), jax.ShapeDtypeStruct((rows, 128), f32)],
        scratch_shapes=[pltpu.VMEM((Q + 8, CONV), f32), pltpu.VMEM((Q, CONV), bf16),
                        pltpu.VMEM((N, DI), f32), pltpu.VMEM((8, 128), f32)],
        compiler_params=pltpu.CompilerParams(vmem_limit_bytes=VM),
        name="forward_scan",
    )(tok, wc, gain, cw, cb, sb, rate, skip, docc, docr, m1, m2, m3)


def gate_kernel(nrm, scan, cot, tok, wg_abs, wo, gg, order, out_o, dscan_o, gn_o, gwg_o, gwo_o, acc_g, acc_o, wg):
    i = pl.program_id(0)

    @pl.when(i == 0)
    def _():
        acc_g[...] = jnp.zeros_like(acc_g)
        acc_o[...] = jnp.zeros_like(acc_o)
        wg[...] = dot_tn(order[...], wg_abs[...]).astype(bf16)

    nb = nrm[...]
    up = cot[...]
    gate = dot(nb, wg[...])
    sig = sigmoid(gate)
    act = gate * sig
    sc = scan[...].astype(f32)
    gated = sc * act
    rr = lax.rsqrt(jnp.mean(gated * gated, axis=-1, keepdims=True) + EPS)
    unit = gated * rr
    mixed = (unit * gg[...]).astype(bf16)
    out_o[...] = (tok[...].astype(f32) + dot(mixed, wo[...])).astype(bf16)
    acc_o[...] += dot_tn(mixed, up)
    gm = dot_nt(up, wo[...])
    e = gm * gg[...]
    dgated = rr * (e - unit * jnp.mean(unit * e, axis=-1, keepdims=True))
    dscan_o[...] = (dgated * act).astype(bf16)
    dgate = (dgated * sc * (sig + act * (1.0 - sig))).astype(bf16)
    acc_g[...] += dot_tn(nb, dgate)
    gn_o[...] = dot_nt(dgate, wg[...])

    @pl.when(i == pl.num_programs(0) - 1)
    def _():
        gwg_o[...] = dot(order[...], acc_g[...].astype(bf16)).astype(bf16)
        gwo_o[...] = acc_o[...].astype(bf16)


def gate_pass(nrm, scan, cot, tok, wg, wo, gg, order, bm=256):
    rows = nrm.shape[0]
    one = pl.Buffered(buffer_count=1)
    full = lambda shape: pl.BlockSpec(shape, lambda i: (0,) * len(shape), pipeline_mode=one)
    blk = lambda w: pl.BlockSpec((bm, w), lambda i: (i, 0))
    return pl.pallas_call(
        gate_kernel,
        grid=(rows // bm,),
        in_specs=[blk(D), blk(DI), blk(D), blk(D), full(wg.shape), full(wo.shape), full(gg.shape), full(order.shape)],
        out_specs=[blk(D), blk(DI), blk(D), full((D, DI)), full((DI, D))],
        out_shape=[jax.ShapeDtypeStruct((rows, D), bf16), jax.ShapeDtypeStruct((rows, DI), bf16),
                   jax.ShapeDtypeStruct((rows, D), f32), jax.ShapeDtypeStruct((D, DI), bf16),
                   jax.ShapeDtypeStruct((DI, D), bf16)],
        scratch_shapes=[pltpu.VMEM((D, DI), f32), pltpu.VMEM((DI, D), f32), pltpu.VMEM((D, DI), bf16)],
        compiler_params=pltpu.CompilerParams(vmem_limit_bytes=VM),
        name="gate_pass",
    )(nrm, scan, cot, tok, wg, wo, gg, order)


def head_sums(v, onehot):
    hi = v.astype(bf16)
    lo = (v - hi.astype(f32)).astype(bf16)
    return dot(hi, onehot) + dot(lo, onehot)


def backward_scan_kernel(heads, per_seq, dscan, cin, pre_r, z_r, st, cw, rate, skip, docc, docr, pdocr, m1, m2, m3, onehot,
                         dproj_o, gcw_o, gcb_o, gsk_o, ghd_o,
                         vbuf, dbuf, dstate, p1buf, qbuf, xwbuf, rowbuf, lastbuf, mbuf):
    i = pl.program_id(0)

    @pl.when(i == 0)
    def _():
        gcw_o[...] = jnp.zeros_like(gcw_o)
        gcb_o[...] = jnp.zeros_like(gcb_o)
        gsk_o[...] = jnp.zeros_like(gsk_o)
        ghd_o[...] = jnp.zeros_like(ghd_o)
        rowbuf[...] = jnp.zeros_like(rowbuf)

    @pl.when(lax.rem(i, per_seq) == 0)
    def _():
        mbuf[:, Q : Q + 8, :] = jnp.zeros((3, 8, CONV), f32)
        dstate[...] = jnp.zeros_like(dstate)

    for t in range(CONV // 128):
        cols = slice(128 * t, 128 * t + 128)
        pre = pre_r[:, cols].astype(f32)
        vbuf[:, cols] = (pre * sigmoid(pre)).astype(bf16)

    z = z_r[...]
    doc = docc[...]
    prev = pdocr[0, 0:1, :]
    soft, a, b, reach, tail, keep = scan_factors(z, rate[...], doc, prev)
    at = a.T
    row = lax.broadcasted_iota(jnp.int32, (Q, Q), 0)
    lane = lax.broadcasted_iota(jnp.int32, (Q, Q), 1)
    joined = (lane >= row) & (doc == docr[0, 0:1, :])
    low = lane < HD
    low_row = low[0:1, :]
    bmat = vbuf[:, DI : DI + N]
    cmat = vbuf[:, DI + N :]
    ct_mat = cmat.astype(f32).T.astype(bf16)
    s = dot_nt(bmat, cmat)
    st_low = st[0]
    ds_low = dstate[...].astype(bf16)
    cs = dot(cmat, st_low)
    bd = dot(bmat, ds_low)
    zero = jnp.zeros((Q, Q), bf16)
    dst = jnp.zeros((Q, Q), f32)
    for p in range(heads // 2):
        cols = slice(128 * p, 128 * p + 128)
        xp = vbuf[:, cols]
        dy = dscan[:, cols]
        dybd = jnp.concatenate([jnp.where(low, dy, zero), jnp.where(low, zero, dy)], axis=0)
        dm = dot_nt(xp, dybd)
        parts = []
        for n, h in enumerate((2 * p, 2 * p + 1)):
            spread = at[h : h + 1, :] - jnp.broadcast_to(b[:, h : h + 1], (Q, Q))
            e = jnp.exp2(jnp.where(joined, spread, NEG))
            m = (e * s).astype(bf16)
            parts.append(m)
            dmh = dm[:, 128 * n : 128 * n + 128]
            dst = dst + dmh * e
            rowbuf[h : h + 1, :] = jnp.sum(dmh * m.astype(f32), axis=0, keepdims=True)
        dx = dot(jnp.concatenate(parts, axis=1), dybd)
        xf = xp.astype(f32)
        dyf = dy.astype(f32)
        tp = pair_of(tail, p, low)
        dx_fresh = bd[:, cols] * tp
        p1buf[:, cols] = xf * (dx + dx_fresh)
        dyr = (dyf * pair_of(reach, p, low)).astype(bf16)
        qbuf[:, cols] = dyr.astype(f32) * cs[:, cols]
        keep_p = pair_of(keep, p, low_row)
        ds = dstate[:, cols]
        lastbuf[0:1, cols] = jnp.sum(xf * dx_fresh, axis=0, keepdims=True) + keep_p * jnp.sum(
            ds * st_low[:, cols].astype(f32), axis=0, keepdims=True)
        gsk_o[:, cols] += jnp.sum((dyf * xf).reshape(-1, 8, 128), axis=0)
        dbuf[:, cols] = dx + dx_fresh + skip[:, cols] * dyf
        xwbuf[:, cols] = (xf * tp).astype(bf16)
        xwbuf[:, DI + 128 * p : DI + 128 * p + 128] = dyr
        dstate[:, cols] = ds * keep_p + dot(ct_mat, dyr)
    dst_low = dst.astype(bf16)
    dbuf[:, DI : DI + N] = dot(dst_low, cmat) + dot_nt(xwbuf[:, :DI], ds_low)
    dbuf[:, DI + N :] = dot_tn(dst_low, bmat) + dot_nt(xwbuf[:, DI:], st_low)
    hot = onehot[...]
    p1 = head_sums(p1buf[...], hot)
    last = head_sums(jnp.broadcast_to(lastbuf[0:1, :], (8, DI)), hot)[0:1, :]
    da = head_sums(qbuf[...], hot) - p1 + rowbuf[...].T
    g = cumsum_rows(da, reverse=True) + last
    sig = sigmoid(z)
    ratio = jnp.where(z < -15.0, 1.0, sig / jnp.where(z < -15.0, 1.0, soft))
    dz = g * rate[...] * sig + p1 * ratio
    dproj_o[:, CONV:] = dz.astype(bf16)
    ghd_o[0:8, :] += jnp.sum(dz.reshape(-1, 8, 128), axis=0)
    ghd_o[8:16, :] += jnp.sum((g * soft).reshape(-1, 8, 128), axis=0)

    masks = (m3[...].astype(f32), m2[...].astype(f32), m1[...].astype(f32))
    for t in range(CONV // 128):
        cols = slice(128 * t, 128 * t + 128)
        pre = pre_r[:, cols].astype(f32)
        sg = sigmoid(pre)
        dpre = dbuf[:, cols] * (sg * (1.0 + pre * (1.0 - sg)))
        cv = cin[:, cols].astype(f32)
        dcin = cw[3:4, cols] * dpre
        gcb_o[:, cols] += jnp.sum(dpre.reshape(-1, 8, 128), axis=0)
        gcw_o[24:32, cols] += jnp.sum((cv * dpre).reshape(-1, 8, 128), axis=0)
        for k in range(3):
            s_ = 3 - k
            mbuf[k, 0:Q, cols] = dpre * masks[k]
            moved = mbuf[k, s_ : s_ + Q, cols]
            dcin = dcin + cw[k : k + 1, cols] * moved
            gcw_o[8 * k : 8 * k + 8, cols] += jnp.sum((cv * moved).reshape(-1, 8, 128), axis=0)
        dproj_o[:, cols] = dcin.astype(bf16)
    mbuf[:, Q : Q + 8, :] = mbuf[:, 0:8, :]


def backward_scan(dscan, cin, pre, z, st, cw, rate, skip, docc, docr, pdocr, m1, m2, m3, onehot, heads, seqs):
    rows = dscan.shape[0]
    n = rows // Q
    one = pl.Buffered(buffer_count=1)
    full = lambda shape: pl.BlockSpec(shape, lambda i: (0,) * len(shape), pipeline_mode=one)
    blk = lambda w: pl.BlockSpec((Q, w), lambda i: (n - 1 - i, 0))
    blk3 = lambda s1, s2: pl.BlockSpec((1, s1, s2), lambda i: (n - 1 - i, 0, 0))
    return pl.pallas_call(
        functools.partial(backward_scan_kernel, heads, n // seqs),
        grid=(n,),
        in_specs=[blk(DI), blk(CONV), blk(CONV), blk(128), blk3(N, DI), full(cw.shape), full(rate.shape), full(skip.shape),
                  blk(128), blk3(8, 128), blk3(8, 128), blk(128), blk(128), blk(128), full(onehot.shape)],
        out_specs=[blk(CONV + 128), full((32, CONV)), full((8, CONV)), full((8, DI)), full((16, 128))],
        out_shape=[jax.ShapeDtypeStruct((rows, CONV + 128), bf16), jax.ShapeDtypeStruct((32, CONV), f32),
                   jax.ShapeDtypeStruct((8, CONV), f32), jax.ShapeDtypeStruct((8, DI), f32),
                   jax.ShapeDtypeStruct((16, 128), f32)],
        scratch_shapes=[pltpu.VMEM((Q, CONV), bf16), pltpu.VMEM((Q, CONV), f32), pltpu.VMEM((N, DI), f32),
                        pltpu.VMEM((Q, DI), f32), pltpu.VMEM((Q, DI), f32), pltpu.VMEM((Q, 2 * DI), bf16),
                        pltpu.VMEM((128, 128), f32), pltpu.VMEM((8, DI), f32), pltpu.VMEM((3, Q + 8, CONV), f32)],
        compiler_params=pltpu.CompilerParams(vmem_limit_bytes=VM),
        name="backward_scan",
    )(dscan, cin, pre, z, st, cw, rate, skip, docc, docr, pdocr, m1, m2, m3, onehot)


def norm_back_kernel(dproj, gn, tok, cot, wc, gain, order, out_o):
    grad = gn[...] + dot_nt(dproj[...], wc[...])
    x = tok[...].astype(f32)
    r = lax.rsqrt(jnp.mean(x * x, axis=-1, keepdims=True) + EPS)
    unit = x * r
    e = gain[...] * grad
    back = r * (e - unit * jnp.mean(unit * e, axis=-1, keepdims=True))
    res = (cot[...].astype(f32) + back).astype(bf16)
    out_o[...] = dot_nt(res, order[...]).astype(bf16)


def norm_back(dproj, gn, tok, cot, wc, gain, order, bm=512):
    rows = dproj.shape[0]
    one = pl.Buffered(buffer_count=1)
    full = lambda shape: pl.BlockSpec(shape, lambda i: (0,) * len(shape), pipeline_mode=one)
    blk = lambda w: pl.BlockSpec((bm, w), lambda i: (i, 0))
    return pl.pallas_call(
        norm_back_kernel,
        grid=(rows // bm,),
        in_specs=[blk(CONV + 128), blk(D), blk(D), blk(D), full(wc.shape), full(gain.shape), full(order.shape)],
        out_specs=blk(D),
        out_shape=jax.ShapeDtypeStruct((rows, D), bf16),
        compiler_params=pltpu.CompilerParams(vmem_limit_bytes=VM),
        name="norm_back",
    )(dproj, gn, tok, cot, wc, gain, order)


def stages_of(mesh):
    ndp, nf = mesh.shape["dp"], mesh.shape["fsdp"]
    out = []
    stride = 1
    while stride < nf:
        group = 2 if stride == 1 else min(4, nf // stride)
        out.append(("fsdp", stride, group, stride))
        stride *= group
    stride = 1
    while stride < ndp:
        group = min(4, ndp // stride)
        out.append(("dp", stride, group, stride * nf))
        stride *= group
    return out[::-1]


def swap(arr, axis, size, offset):
    return lax.ppermute(arr, axis, [(i, i ^ offset) for i in range(size)])


def gather_slots(shard, stages, sizes):
    block = shard
    for axis, stride, group, _ in stages:
        block = jnp.stack([block] + [swap(block, axis, sizes[axis], k * stride) for k in range(1, group)])
    return block


def scatter_slots(terms, stages, sizes):
    low, kept = terms, terms
    for axis, stride, group, _ in stages[::-1]:
        got = [swap(low[k], axis, sizes[axis], k * stride) for k in range(1, group)]
        kept = kept[0].astype(f32)
        for part in got:
            kept = kept + part.astype(f32)
        low = kept.astype(bf16)
    return kept


def three_parts(v):
    hi = lax.reduce_precision(v, 8, 7)
    mid = lax.reduce_precision(v - hi, 8, 7)
    return jnp.concatenate([hi.astype(bf16), mid.astype(bf16), (v - hi - mid).astype(bf16)])


def whole_parts(v):
    hi, mid, lo = jnp.split(v.astype(f32), 3, axis=-1)
    return (hi + mid + lo).reshape(-1)


def doc_terms(segments):
    seqs, length = segments.shape
    rows = seqs * length
    n = rows // Q
    seg = segments.astype(f32)
    pad = jnp.pad(seg, ((0, 0), (3, 0)), constant_values=-1.0)
    wide = lambda v: jnp.broadcast_to(v.reshape(rows, 1), (rows, 128))
    same = [wide((pad[:, 3 - s : 3 - s + length] == seg).astype(f32)) for s in (1, 2, 3)]
    docr = jnp.broadcast_to(seg.reshape(n, 1, Q), (n, 8, Q))
    ends = seg.reshape(seqs, length // Q, Q)[:, :, -1]
    prev = jnp.concatenate([jnp.full((seqs, 1), -1.0, f32), ends[:, :-1]], axis=1).reshape(n, 1, 1)
    return wide(seg), docr, jnp.broadcast_to(prev, (n, 8, 128)), same


def local(mesh, tokens, cotangent, segments, in_gain, weight_in, conv_weight, conv_bias, step_bias, decay_log, skip_gain,
          gate_gain, weight_out):
    sizes = {"dp": mesh.shape["dp"], "fsdp": mesh.shape["fsdp"]}
    nf = sizes["fsdp"]
    nd = sizes["dp"] * nf
    axes = ("dp", "fsdp")
    stages = stages_of(mesh)
    me = lax.axis_index("dp") * nf + lax.axis_index("fsdp")
    seqs, length, _ = tokens.shape
    rows = seqs * length
    ri, ro, cc, share = weight_in.shape[0], weight_out.shape[0], conv_bias.shape[0], step_bias.shape[0]
    heads = share * nf
    free = 128 - heads

    rel = np.zeros((1,), np.int32)
    for _, _, group, stride in stages:
        rel = (np.arange(group, dtype=np.int32)[:, None] * stride + rel[None, :]).reshape(-1)
    device = jnp.asarray(rel) ^ me
    feature = (device[:, None] * ri + jnp.arange(ri)[None, :]).reshape(-1)
    order = (jnp.arange(D)[:, None] == feature[None, :]).astype(bf16)
    slot_hot = (device[:, None] == jnp.arange(nd)[None, :]).astype(bf16)

    small = jnp.concatenate([in_gain, conv_weight.reshape(-1), conv_bias, gate_gain, three_parts(step_bias),
                             three_parts(decay_log), three_parts(skip_gain)])
    small = jnp.pad(small, (0, ri * free - small.shape[0])).reshape(ri, free)
    gathered = gather_slots(jnp.concatenate([weight_in[:, DI:], small], axis=1), stages, sizes)
    wc = gathered.reshape(D, CONV + 128)
    later = jnp.concatenate([weight_in[:, :DI], weight_out.reshape(2, ri, D).transpose(1, 0, 2).reshape(ri, DI)], axis=0)
    later = lax.all_gather(later, axes, axis=0)
    tok = tokens.reshape(rows, D)
    up = cotangent.reshape(rows, D)
    tok_s = jnp.dot(tok, order, preferred_element_type=bf16)
    up_s = jnp.dot(up, order, preferred_element_type=bf16)
    docc, docr, pdocr, same = doc_terms(segments)

    packed = gathered.reshape(nd, ri, CONV + 128)[:, :, CONV + heads :].reshape(nd, ri * free)
    gain = packed[:, :ri].reshape(1, D).astype(f32)
    packed = lax.dot_general(slot_hot, packed, (((0,), (0,)), ((), ())), preferred_element_type=f32)
    at = ri
    cw = packed[:, at : at + 4 * cc].reshape(nd, 4, cc).transpose(1, 0, 2).reshape(4, CONV)
    at += 4 * cc
    cb = packed[:, at : at + cc].reshape(1, CONV)
    at += cc
    gg = packed[:, at : at + ro].reshape(1, DI)
    at += ro
    per_head = []
    for _ in range(3):
        per_head.append(whole_parts(packed[:nf, at : at + 3 * share]))
        at += 3 * share
    lanes = lambda v: jnp.pad(v, (0, 128 - heads))[None]
    rate = lanes(-jnp.exp(per_head[1]))
    skip = jnp.repeat(per_head[2], HD)[None]
    cw = jnp.pad(cw, ((0, 4), (0, 0)))
    onehot = (jnp.arange(DI)[:, None] // HD == jnp.arange(128)[None, :]).astype(bf16)

    cin, pre, nrm, scan, st, z = forward_scan(
        tok_s, wc, gain, cw, cb, lanes(per_head[0]), rate, skip, docc, docr, *same, heads, seqs)

    wg = later[:, :ri].reshape(D, DI)
    wo = later[:, ri:].reshape(nd, ri, 2, D).transpose(0, 2, 1, 3).reshape(DI, D)
    out, dscan, gn, gwg, gwo = gate_pass(nrm, scan, up, tok, wg, wo, gg, order)
    early = jnp.concatenate([gwg.reshape(nd, ri, DI), gwo.reshape(nd, 2, ri, D).transpose(0, 2, 1, 3).reshape(nd, ri, DI)], axis=1)
    early = lax.psum_scatter(early, axes, scatter_dimension=0)

    dproj, gcw, gcb, gsk, ghd = backward_scan(
        dscan, cin, pre, z, st, cw, rate, skip, docc, docr, pdocr, *same, onehot, heads, seqs)
    gwc = lax.dot_general(nrm, dproj, (((0,), (0,)), ((), ())), preferred_element_type=f32).astype(bf16)

    taps = jnp.concatenate([gcw.reshape(4, 8, CONV).sum(1), gcb.sum(0)[None]], axis=0)
    taps = taps.reshape(5, nd, cc).transpose(1, 0, 2).reshape(nd, 5 * cc)
    head_terms = jnp.stack([ghd[:8].sum(0)[:heads], ghd[8:16].sum(0)[:heads] * rate[0, :heads],
                            gsk.sum(0).reshape(heads, HD).sum(1)])
    head_terms = jnp.tile(head_terms.reshape(3, nf, share).transpose(1, 0, 2).reshape(nf, 3 * share), (nd // nf, 1))
    terms = jnp.concatenate([taps, head_terms], axis=1)
    hi = lax.reduce_precision(terms, 8, 7)
    both = jnp.concatenate([hi, terms - hi], axis=1).astype(bf16)
    both = jnp.dot(slot_hot, both, preferred_element_type=f32).astype(bf16)
    width = 5 * cc + 3 * share
    both = jnp.pad(both, ((0, 0), (0, ri * free - 2 * width))).reshape(nd, ri, free)
    gwc = jnp.concatenate([gwc.reshape(nd, ri, CONV + 128)[:, :, : CONV + heads], both], axis=2)
    total = scatter_slots(gwc.reshape([g for _, _, g, _ in stages[::-1]] + [ri, CONV + 128]), stages, sizes)

    gtok = norm_back(dproj, gn, tok_s, up_s, wc, gain, order)

    early = early.astype(f32)
    g_in = jnp.concatenate([early[:ri], total[:, : CONV + heads]], axis=1)
    g_out = early[ri:].reshape(ri, 2, D).transpose(1, 0, 2).reshape(ro, D)
    packed = total[:, CONV + heads :].reshape(-1)
    packed = packed[:width] + packed[width : 2 * width]
    g_in_gain = jnp.sum(weight_in.astype(f32) * g_in, axis=1) / in_gain.astype(f32)
    g_gate_gain = jnp.sum(weight_out.astype(f32) * g_out, axis=1) / gate_gain.astype(f32)
    by_head = packed[5 * cc :].reshape(3, share)
    return (out.reshape(tokens.shape), gtok.reshape(tokens.shape), g_in_gain, g_in, packed[: 4 * cc].reshape(4, cc),
            packed[4 * cc : 5 * cc], by_head[0], by_head[1], by_head[2], g_gate_gain, g_out)


def solution(mesh):
    every = ("dp", "fsdp")
    return jax.shard_map(
        functools.partial(local, mesh),
        mesh=mesh,
        in_specs=(P(every, None, None), P(every, None, None), P(every, None), P(every), P(every, None), P(None, every),
                  P(every), P("fsdp"), P("fsdp"), P("fsdp"), P(every), P(every, None)),
        out_specs=(P(every, None, None), P(every, None, None), P(every), P(every, None), P(None, every), P(every),
                   P("fsdp"), P("fsdp"), P("fsdp"), P(every), P(every, None)),
        check_vma=False,
    )
```

time: 1140 us -> 361 us (0.32)
  other arithmetic: 328 us -> 17.4 us
  local copies, waits for them, and re-layouts: 331 us -> 44.6 us
  matrix products: 293 us -> 20.1 us
  Pallas kernels: 0 us -> 204 us
  blocking collectives: 128 us -> 0 us
  starting transfers between devices: 0.16 us -> 21.2 us
    dot_general x62 -> x5, matrix products: 293 us -> 20.1 us  [the longest x1 11.3 us: local(): lax.dot_general(nrm, dproj, (((0,), (0,)), ((), ())), preferred_element_t...]
    pallas_call x0 -> x4, Pallas kernels: none -> 204 us  [the longest x1 74.2 us: backward_scan(): pl.pallas_call(functools.partial(backward_scan_kernel, heads, n // seqs),...]
    mul x36 -> x1, other arithmetic: 109 us -> 0.01 us  [local(): ghd[8:16].sum(0)[:heads] * rate[0, :heads]]
    unnamed x3 -> x0, blocking collectives: 87.1 us -> none
    reshape x14 -> x20, local copies, waits for them, and re-layouts: 90.6 us -> 14.1 us  [the longest x1 4.96 us: local(): later[:, ri:].reshape(nd, ri, 2, D).transpose(0, 2, 1, 3).reshape(DI, D)]
    reduce_sum x12 -> x7, other arithmetic: 58 us -> 3.05 us  [the longest x1 1.06 us: local(): gcw.reshape(4, 8, CONV).sum(1)]
    another operation x40 -> x5, other arithmetic: 52.6 us -> 0.79 us  [the longest x4 0.7 us: gather_slots(): jnp.stack([block] + [swap(block, axis, sizes[axis], k * stride) for k in...]
    squeeze x24 -> x3, local copies, waits for them, and re-layouts: 48 us -> 0.19 us  [the longest x2 0.1 us: scatter_slots(): got = [swap(low[k], axis, sizes[axis], k * stride) for k in range(1, group)]]
  transfers between devices with their start and end apart: 4 -> 16, of which waited for: 1 -> 7; matrix products, arithmetic and copies ran while one was open for 38% -> 16% of each run, Pallas kernels for 0% -> 41%
where the time goes in v1:
time: 361 us; the launch traced here: 360 us
  Pallas kernels  204 us (57%)
  local copies, waits for them, and re-layouts  44.6 us (12%)
  waiting for transfers between devices  38.4 us (11%)
  starting transfers between devices  21.2 us (6%)
  matrix products  20.1 us (6%)
  other arithmetic  17.4 us (5%)
  between operations  14.5 us (4%)
    pallas_call x1, Pallas kernels, backward_scan(): pl.pallas_call(functools.partial(backward_scan_kernel, heads, n // seqs),...  74.2 us
    pallas_call x1, Pallas kernels, gate_pass(): pl.pallas_call(gate_kernel, grid=(rows // bm,), in_specs=[blk(D), blk(DI)...  54.8 us
    pallas_call x1, Pallas kernels, forward_scan(): pl.pallas_call(functools.partial(forward_scan_kernel, heads, n // seqs),...  53.3 us
    ppermute x14, waiting for transfers between devices, swap(): return lax.ppermute(arr, axis, [(i, i ^ offset) for i in range(size)])  38.3 us
    pallas_call x1, Pallas kernels, norm_back(): pl.pallas_call(norm_back_kernel, grid=(rows // bm,), in_specs=[blk(CONV +...  21.6 us
    ppermute x14, starting transfers between devices, swap(): return lax.ppermute(arr, axis, [(i, i ^ offset) for i in range(size)])  21.2 us
    dot_general x1, matrix products, local(): lax.dot_general(nrm, dproj, (((0,), (0,)), ((), ())), preferred_element_t...  11.3 us
    broadcast_in_dim x5, local copies, waits for them, and re-layouts, doc_terms(): wide = lambda v: jnp.broadcast_to(v.reshape(rows, 1), (rows, 128))  8.07 us
  transfers between devices with their start and end apart: 16, of which 7 were waited for; matrix products, arithmetic and copies ran while one was open for 16% of the time, Pallas kernels for 41%

profile of v1, /device:TPU:0, one launch (start us, length us, event | category | flops | bytes accessed | tf_op | source)
XLA Modules:
  0.0 360.2 jit_solution(16008048916509077831)
XLA Ops:
  7.2 0.9 copy.64
  8.1 0.9 slice.158
  9.0 0.7 pad_maximum_fusion.6
  9.7 0.9 slice.150
  10.7 0.8 reshape.251
  11.4 0.7 fusion.28
  12.1 0.7 fusion.26
  12.8 2.1 concatenate.37
  15.1 3.0 collective-permute-start
  18.1 2.6 collective-permute-start.1
  20.7 0.7 convert_bitcast_fusion
  21.5 0.7 broadcast_xor_fusion
  22.1 7.0 %collective-permute-done.1 = bf16[24,1920]{1,0:T(8,128)(2,1)S(1)} collective-permute-done((bf16[24,1920]{1,0:T(8,128)(2,1)S(1)}, bf16[24,1920]{1,0:T(8,128)(2,1)S(1)}, u32[]{:S(2)}, u32[]{:S(2)}) %collective-permute-start.1) | collective-permute-done | bytes 92192 | tf_op jit(solution)/shard_map/ppermute | solution.py:402
  29.2 1.6 collective-permute-start.3
  30.7 1.5 collective-permute-start.4
  32.9 0.6 broadcast_in_dim.73
  35.6 4.7 %collective-permute-done.3 = bf16[4,24,1920]{2,1,0:T(8,128)(2,1)S(1)} collective-permute-done((bf16[4,24,1920]{2,1,0:T(8,128)(2,1)S(1)}, bf16[4,24,1920]{2,1,0:T(8,128)(2,1)S(1)}, u32[]{:S(2)}, u32[]{:S(2)}) %collective-permute-start.3) | collective-permute-done | bytes 368672 | tf_op jit(solution)/shard_map/ppermute | solution.py:402
  40.3 6.2 %collective-permute-done.4 = bf16[4,24,1920]{2,1,0:T(8,128)(2,1)S(1)} collective-permute-done((bf16[4,24,1920]{2,1,0:T(8,128)(2,1)S(1)}, bf16[4,24,1920]{2,1,0:T(8,128)(2,1)S(1)}, u32[]{:S(2)}, u32[]{:S(2)}) %collective-permute-start.4) | collective-permute-done | bytes 368672 | tf_op jit(solution)/shard_map/ppermute | solution.py:402
  46.5 2.0 collective-permute-done.5
  48.8 0.6 copy_bitcast_fusion.2
  49.4 1.4 fusion.order
  50.9 1.0 fusion.4.onehot
  51.9 4.1 %convolution_bitcast_fusion.1.tok = bf16[2048,768]{1,0:T(8,128)(2,1)} fusion(bf16[2048,768]{1,0:T(8,128)(2,1)S(1)} %bitcast.135, s32[768]{0:T(1024)S(1)} %add.91), kind=kOutput, calls=%fused_computation.3 | convolution fusion | flops 2416508928 | bytes 6294528 | tf_op jit(solution)/shard_map/dot_general | solution.py:479
  57.0 0.9 slice.196
  58.1 0.6 copy.77
  58.7 0.9 reshape.257
  59.7 1.4 reshape.258.cb
  61.3 0.7 broadcast_in_dim_reshape.4.skip
  62.2 0.7 reshape.283.gain
  62.8 0.7 reshape.267.gg
  63.6 0.6 pad.25.cw
  64.8 2.1 broadcast_in_dim.80.m2
  66.8 2.0 broadcast_in_dim.83.m3
  68.9 2.0 broadcast_in_dim.77.m1
  70.9 0.6 broadcast_in_dim.74.docr
  71.5 1.4 broadcast_in_dim.72.docc
  72.9 53.3 %forward_scan.1 = (bf16[2048,1792]{1,0:T(8,128)(2,1)}, bf16[2048,1792]{1,0:T(8,128)(2,1)}, bf16[2048,768]{1,0:T(8,128)(2,1)}, bf16[2048,1536]{1,0:T(8,128)(2,1)}...) custom-call(bf16[2048,768]{1,0:T(8,128)(2,1)} %convolution_bitcast_fusion.1.tok, bf16[768,1920]{1,0:T(8,128)(2,1)} %bitcast.126, ...), custom_call_target="tpu_custom_call" | custom-call | tf_op jit(solution)/shard_map/forward_scan/pallas_call | solution.py:148
  126.2 4.9 %fusion.35 = (bf16[32,24,1536]{2,1,0:T(8,128)(2,1)}, bf16[32,24,1536]{2,1,0:T(8,128)(2,1)}) fusion(bf16[32,48,1536]{2,1,0:T(8,128)(2,1)} %bitcast.133), kind=kLoop, calls=%fused_computation.114 | loop fusion | bytes 9437184 | tf_op jit(solution)/shard_map/slice | solution.py:507
  131.1 5.0 %reshape.265 = bf16[32,24,2,768]{3,2,1,0:T(2,128)(2,1)S(1)} reshape(bf16[32,24,1536]{2,1,0:T(8,128)(2,1)} %get-tuple-element.49) | data formatting | bytes 4718592 | tf_op jit(solution)/shard_map/reshape | solution.py:507
  136.1 1.7 copy.54
  137.8 54.8 %gate_pass.1 = (bf16[2048,768]{1,0:T(8,128)(2,1)}, bf16[2048,1536]{1,0:T(8,128)(2,1)}, f32[2048,768]{1,0:T(8,128)}, bf16[768,1536]{1,0:T(8,128)(2,1)}, bf16[1536,768]{1,0:T(8,128)(2,1)}) custom-call(bf16[2048,768]{1,0:T(8,128)(2,1)} %get-tuple-element.27.nrm, bf16[2048,1536]{1,0:T(8,128)(2,1)} %get-tuple-element.28.scan, bf16[2048,768]{1,0:T(8,128)(2,1)} %bitcast.136, ...), custom_call_target="tpu_custom_call" | custom-call | tf_op jit(solution)/shard_map/gate_pass/pallas_call | solution.py:204
  192.7 2.0 copy.65
  195.0 2.7 pad_maximum_fusion
  197.7 0.6 copy-done.17
  198.4 0.7 broadcast_in_dim.85.pdocr
  199.1 74.2 %backward_scan.1 = (bf16[2048,1920]{1,0:T(8,128)(2,1)}, f32[32,1792]{1,0:T(8,128)}, f32[8,1792]{1,0:T(8,128)}, f32[8,1536]{1,0:T(8,128)}, f32[16,128]{1,0:T(8,128)}) custom-call(bf16[2048,1536]{1,0:T(8,128)(2,1)} %get-tuple-element.30.dscan, bf16[2048,1792]{1,0:T(8,128)(2,1)} %get-tuple-element.31.cin, bf16[2048,1792]{1,0:T(8,128)(2,1)} %get-tuple-element.32.pre_r, ...), custom_call_target="tpu_custom_call" | custom-call | tf_op jit(solution)/shard_map/backward_scan/pallas_call | solution.py:341
  273.3 1.1 bitcast_reduce_fusion
  274.5 0.8 reduce_sum.73
  275.6 11.3 %convolution_convert_fusion = bf16[768,1920]{1,0:T(8,128)(2,1)} fusion(bf16[2048,768]{1,0:T(8,128)(2,1)S(1)} %copy-done.3, bf16[2048,1920]{1,0:T(8,128)(2,1)} %get-tuple-element.35.dproj), kind=kOutput, calls=%fused_computation.1 | convolution fusion | flops 6041272320 | bytes 13959168 | tf_op jit(solution)/shard_map/dot_general | solution.py:514
  288.2 2.1 fusion.1
  290.8 2.9 collective-permute-done.7
  294.2 2.5 collective-permute-start.10
  296.9 1.4 collective-permute-start.9
  298.3 8.3 %collective-permute-done.10 = bf16[4,24,1920]{2,1,0:T(8,128)(2,1)S(1)} collective-permute-done((bf16[4,24,1920]{2,1,0:T(8,128)(2,1)S(1)}, bf16[4,24,1920]{2,1,0:T(8,128)(2,1)S(1)}, u32[]{:S(2)}, u32[]{:S(2)}) %collective-permute-start.10) | collective-permute-done | bytes 368672 | tf_op jit(solution)/shard_map/ppermute | solution.py:402
  306.6 7.3 %collective-permute-done.8 = bf16[4,24,1920]{2,1,0:T(8,128)(2,1)S(1)} collective-permute-done((bf16[4,24,1920]{2,1,0:T(8,128)(2,1)S(1)}, bf16[4,24,1920]{2,1,0:T(8,128)(2,1)S(1)}, u32[]{:S(2)}, u32[]{:S(2)}) %collective-permute-start.8) | collective-permute-done | bytes 368672 | tf_op jit(solution)/shard_map/ppermute | solution.py:402
  314.2 4.8 %collective-permute-start.11 = (bf16[24,1920]{1,0:T(8,128)(2,1)S(1)}, bf16[24,1920]{1,0:T(8,128)(2,1)S(1)}, u32[]{:S(2)}, u32[]{:S(2)}) collective-permute-start(bf16[24,1920]{1,0:T(8,128)(2,1)S(1)} %get-tuple-element.60), channel_id=1, source_target_pairs={{0,8},{2,10},{4,12},{6,14},{8,0},{10,2},{12,4},{14,6},{16,24},{18,... | collective-permute-start | bytes 276488 | tf_op jit(solution)/shard_map/ppermute | solution.py:402
  318.9 0.8 collective-permute-start.12
  319.7 1.7 collective-permute-start.13
  321.4 4.1 %convolution_bitcast_fusion.cot = bf16[2048,768]{1,0:T(8,128)(2,1)} fusion(bf16[2048,768]{1,0:T(8,128)(2,1)S(1)} %bitcast.137, s32[768]{0:T(1024)S(1)} %copy-done.12), kind=kOutput, calls=%fused_computation.2 | convolution fusion | flops 2416508928 | bytes 6294528 | tf_op jit(solution)/shard_map/dot_general | solution.py:480
  325.5 21.6 %norm_back.1 = bf16[2048,768]{1,0:T(8,128)(2,1)} custom-call(bf16[2048,1920]{1,0:T(8,128)(2,1)} %get-tuple-element.35.dproj, f32[2048,768]{1,0:T(8,128)} %get-tuple-element.36.gn, bf16[2048,768]{1,0:T(8,128)(2,1)} %convolution_bitcast_fusion.1.tok, bf16[2048,768]{1,0:T(8,128)(2,1)} %convolution_bitcast_fusion.cot, bf16[768,1920]{1,0:T(8,128)(2,1)} %bitcast.127, ...), custom_call_target="tpu_custom_call" | custom-call | tf_op jit(solution)/shard_map/norm_back/pallas_call | solution.py:374
  348.0 0.7 reshape.280
  349.2 0.9 convert_element_type.125
  350.2 0.9 multiply_reduce_fusion
  351.6 0.9 slice.217
  (129 shorter events, 12.0 us)
Async XLA Ops:
  7.2 119.0 %all-gather.3.cloned.1.call-start = ((), (), s32[]{:S(2)}) async-start(), calls=%async_computation.2 | async-start | bytes 4866048 | tf_op jit(solution)/shard_map/all_gather | solution.py:476
  9.7 339.5 %reduce-scatter.2.cloned.1.call-start = ((), (), s32[]{:S(2)}) async-start(), calls=%async_computation.1 | async-start | bytes 4866048 | tf_op jit(solution)/shard_map/reduce_scatter | solution.py:510
  15.1 7.1 %collective-permute-start = (bf16[24,1920]{1,0:T(8,128)(2,1)S(1)}, bf16[24,1920]{1,0:T(8,128)(2,1)S(1)}, u32[]{:S(2)}, u32[]{:S(2)}) collective-permute-start(bf16[24,1920]{1,0:T(8,128)(2,1)S(1)} %pad_maximum_fusion.7), channel_id=1, source_target_pairs={{0,8},{2,10},{4,12},{6,14},{8,0},{10,2},{12,4},{14,6},{16,24},{18,... | collective-permute-start | bytes 276488 | tf_op jit(solution)/shard_map/ppermute | solution.py:402
  18.1 11.0 %collective-permute-start.1 = (bf16[24,1920]{1,0:T(8,128)(2,1)S(1)}, bf16[24,1920]{1,0:T(8,128)(2,1)S(1)}, u32[]{:S(2)}, u32[]{:S(2)}) collective-permute-start(bf16[24,1920]{1,0:T(8,128)(2,1)S(1)} %pad_maximum_fusion.7), channel_id=1, source_target_pairs={{0,16},{2,18},{4,20},{6,22},{8,24},{10,26},{12,28},{14,30},{16,0},... | collective-permute-start | bytes 276488 | tf_op jit(solution)/shard_map/ppermute | solution.py:402
  20.7 8.4 %collective-permute-start.2 = (bf16[24,1920]{1,0:T(8,128)(2,1)S(1)}, bf16[24,1920]{1,0:T(8,128)(2,1)S(1)}, u32[]{:S(2)}, u32[]{:S(2)}) collective-permute-start(bf16[24,1920]{1,0:T(8,128)(2,1)S(1)} %pad_maximum_fusion.7), channel_id=1, source_target_pairs={{0,24},{2,26},{4,28},{6,30},{8,16},{10,18},{12,20},{14,22},{16,8},... | collective-permute-start | bytes 276488 | tf_op jit(solution)/shard_map/ppermute | solution.py:402
  22.1 34.5 %copy-start.14 = (s32[32]{0:T(128)}, s32[32]{0:T(128)S(1)}, u32[]{:S(2)}) copy-start(s32[32]{0:T(128)S(1)} %get-tuple-element.79) | copy-start | bytes 388
  29.2 11.2 %collective-permute-start.3 = (bf16[4,24,1920]{2,1,0:T(8,128)(2,1)S(1)}, bf16[4,24,1920]{2,1,0:T(8,128)(2,1)S(1)}, u32[]{:S(2)}, u32[]{:S(2)}) collective-permute-start(bf16[4,24,1920]{2,1,0:T(8,128)(2,1)S(1)} %get-tuple-element.64), channel_id=1, source_target_pairs={{0,2},{2,0},{4,6},{6,4},{8,10},{10,8},{12,14},{14,12},{16,18},{18,... | collective-permute-start | bytes 1105928 | tf_op jit(solution)/shard_map/ppermute | solution.py:402
  30.7 15.8 %collective-permute-start.4 = (bf16[4,24,1920]{2,1,0:T(8,128)(2,1)S(1)}, bf16[4,24,1920]{2,1,0:T(8,128)(2,1)S(1)}, u32[]{:S(2)}, u32[]{:S(2)}) collective-permute-start(bf16[4,24,1920]{2,1,0:T(8,128)(2,1)S(1)} %get-tuple-element.64), channel_id=1, source_target_pairs={{0,4},{2,6},{4,0},{6,2},{8,12},{10,14},{12,8},{14,10},{16,20},{18,... | collective-permute-start | bytes 1105928 | tf_op jit(solution)/shard_map/ppermute | solution.py:402
  32.3 16.2 %collective-permute-start.5 = (bf16[4,24,1920]{2,1,0:T(8,128)(2,1)S(1)}, bf16[4,24,1920]{2,1,0:T(8,128)(2,1)S(1)}, u32[]{:S(2)}, u32[]{:S(2)}) collective-permute-start(bf16[4,24,1920]{2,1,0:T(8,128)(2,1)S(1)} %get-tuple-element.64), channel_id=1, source_target_pairs={{0,6},{2,4},{4,2},{6,0},{8,14},{10,12},{12,10},{14,8},{16,22},{18,... | collective-permute-start | bytes 1105928 | tf_op jit(solution)/shard_map/ppermute | solution.py:402
  32.9 19.0 %copy-start.11 = (s32[768]{0:T(1024)}, s32[768]{0:T(1024)S(1)}, u32[]{:S(2)}) copy-start(s32[768]{0:T(1024)S(1)} %add.91) | copy-start | bytes 9220
  48.5 3.4 copy-start.1
  48.8 7.3 %collective-permute-start.6 = (bf16[4,4,24,1920]{3,2,1,0:T(8,128)(2,1)S(1)}, bf16[4,4,24,1920]{3,2,1,0:T(8,128)(2,1)S(1)}, u32[]{:S(2)}, u32[]{:S(2)}) collective-permute-start(bf16[4,4,24,1920]{3,2,1,0:T(8,128)(2,1)S(1)} %get-tuple-element.59), channel_id=1, source_target_pairs={{0,1},{1,0},{2,3},{3,2},{4,5},{5,4},{6,7},{7,6},{8,9},{9,8},{10,11... | collective-permute-start | bytes 4423688 | tf_op jit(solution)/shard_map/ppermute | solution.py:402
  56.3 16.6 %copy-start = (bf16[2,4,4,24,1920]{4,3,2,1,0:T(8,128)(2,1)}, bf16[2,4,4,24,1920]{4,3,2,1,0:T(8,128)(2,1)S(1)}, u32[]{:S(2)}) copy-start(bf16[2,4,4,24,1920]{4,3,2,1,0:T(8,128)(2,1)S(1)} %pad_maximum_fusion.1) | copy-start | bytes 8847364
  58.1 12.8 %copy-start.10 = (f32[16,128]{1,0:T(8,128)S(1)}, f32[16,128]{1,0:T(8,128)}, u32[]{:S(2)}) copy-start(f32[16,128]{1,0:T(8,128)} %broadcast_in_dim.73) | copy-start | bytes 24580
  58.1 13.4 %copy-start.9 = (f32[1,8,2,128]{3,1,2,0:T(8,128)S(1)}, f32[1,8,2,128]{3,1,2,0:T(8,128)}, u32[]{:S(2)}) copy-start(f32[1,8,2,128]{3,1,2,0:T(8,128)} %copy.80) | copy-start | bytes 24580
  63.5 9.3 %copy-start.16 = (f32[1,128]{1,0:T(1,128)}, f32[1,128]{1,0:T(1,128)S(1)}, u32[]{:S(2)}) copy-start(f32[1,128]{1,0:T(1,128)S(1)} %pad_bitcast_fusion.rate) | copy-start | bytes 1540
  192.7 2.4 copy-start.4
  197.7 0.7 copy-start.17
  199.1 76.5 %copy-start.3 = (bf16[2048,768]{1,0:T(8,128)(2,1)S(1)}, bf16[2048,768]{1,0:T(8,128)(2,1)}, u32[]{:S(2)}) copy-start(bf16[2048,768]{1,0:T(8,128)(2,1)} %get-tuple-element.27.nrm) | copy-start | bytes 9437188
  275.6 11.4 %copy-start.13 = (f32[16,128]{1,0:T(8,128)S(1)}, f32[16,128]{1,0:T(8,128)}, u32[]{:S(2)}) copy-start(f32[16,128]{1,0:T(8,128)} %get-tuple-element.41) | copy-start | bytes 24580
  275.6 11.5 %copy-start.8 = (f32[8,1536]{1,0:T(8,128)S(1)}, f32[8,1536]{1,0:T(8,128)}, u32[]{:S(2)}) copy-start(f32[8,1536]{1,0:T(8,128)} %get-tuple-element.42) | copy-start | bytes 147460
  275.6 12.0 %copy-start.15 = (s32[32]{0:T(128)S(1)}, s32[32]{0:T(128)}, u32[]{:S(2)}) copy-start(s32[32]{0:T(128)} %copy-done.14) | copy-start | bytes 388
  290.3 3.5 collective-permute-start.7
  294.1 27.3 %copy-start.2 = (bf16[2,1024,768]{2,1,0:T(8,128)(2,1)S(1)}, bf16[2,1024,768]{2,1,0:T(8,128)(2,1)}, u32[]{:S(2)}) copy-start(bf16[2,1024,768]{2,1,0:T(8,128)(2,1)} %param.14) | copy-start | bytes 9437188
  294.1 27.3 %copy-start.12 = (s32[768]{0:T(1024)S(1)}, s32[768]{0:T(1024)}, u32[]{:S(2)}) copy-start(s32[768]{0:T(1024)} %copy-done.11) | copy-start | bytes 9220
  294.2 12.4 %collective-permute-start.10 = (bf16[4,24,1920]{2,1,0:T(8,128)(2,1)S(1)}, bf16[4,24,1920]{2,1,0:T(8,128)(2,1)S(1)}, u32[]{:S(2)}, u32[]{:S(2)}) collective-permute-start(bf16[4,24,1920]{2,1,0:T(8,128)(2,1)S(1)} %get-tuple-element.56), channel_id=1, source_target_pairs={{0,6},{2,4},{4,2},{6,0},{8,14},{10,12},{12,10},{14,8},{16,22},{18,... | collective-permute-start | bytes 1105928 | tf_op jit(solution)/shard_map/ppermute | solution.py:402
  296.7 17.3 %collective-permute-start.8 = (bf16[4,24,1920]{2,1,0:T(8,128)(2,1)S(1)}, bf16[4,24,1920]{2,1,0:T(8,128)(2,1)S(1)}, u32[]{:S(2)}, u32[]{:S(2)}) collective-permute-start(bf16[4,24,1920]{2,1,0:T(8,128)(2,1)S(1)} %get-tuple-element.55), channel_id=1, source_target_pairs={{0,2},{2,0},{4,6},{6,4},{8,10},{10,8},{12,14},{14,12},{16,18},{18,... | collective-permute-start | bytes 1105928 | tf_op jit(solution)/shard_map/ppermute | solution.py:402
  296.9 17.0 %collective-permute-start.9 = (bf16[4,24,1920]{2,1,0:T(8,128)(2,1)S(1)}, bf16[4,24,1920]{2,1,0:T(8,128)(2,1)S(1)}, u32[]{:S(2)}, u32[]{:S(2)}) collective-permute-start(bf16[4,24,1920]{2,1,0:T(8,128)(2,1)S(1)} %get-tuple-element.57), channel_id=1, source_target_pairs={{0,4},{2,6},{4,0},{6,2},{8,12},{10,14},{12,8},{14,10},{16,20},{18,... | collective-permute-start | bytes 1105928 | tf_op jit(solution)/shard_map/ppermute | solution.py:402
  314.2 32.9 %collective-permute-start.11 = (bf16[24,1920]{1,0:T(8,128)(2,1)S(1)}, bf16[24,1920]{1,0:T(8,128)(2,1)S(1)}, u32[]{:S(2)}, u32[]{:S(2)}) collective-permute-start(bf16[24,1920]{1,0:T(8,128)(2,1)S(1)} %get-tuple-element.60), channel_id=1, source_target_pairs={{0,8},{2,10},{4,12},{6,14},{8,0},{10,2},{12,4},{14,6},{16,24},{18,... | collective-permute-start | bytes 276488 | tf_op jit(solution)/shard_map/ppermute | solution.py:402
  318.9 28.1 %collective-permute-start.12 = (bf16[24,1920]{1,0:T(8,128)(2,1)S(1)}, bf16[24,1920]{1,0:T(8,128)(2,1)S(1)}, u32[]{:S(2)}, u32[]{:S(2)}) collective-permute-start(bf16[24,1920]{1,0:T(8,128)(2,1)S(1)} %get-tuple-element.62), channel_id=1, source_target_pairs={{0,16},{2,18},{4,20},{6,22},{8,24},{10,26},{12,28},{14,30},{16,0},... | collective-permute-start | bytes 276488 | tf_op jit(solution)/shard_map/ppermute | solution.py:402
  319.7 27.4 %collective-permute-start.13 = (bf16[24,1920]{1,0:T(8,128)(2,1)S(1)}, bf16[24,1920]{1,0:T(8,128)(2,1)S(1)}, u32[]{:S(2)}, u32[]{:S(2)}) collective-permute-start(bf16[24,1920]{1,0:T(8,128)(2,1)S(1)} %get-tuple-element.61), channel_id=1, source_target_pairs={{0,24},{2,26},{4,28},{6,30},{8,16},{10,18},{12,20},{14,22},{16,8},... | collective-permute-start | bytes 276488 | tf_op jit(solution)/shard_map/ppermute | solution.py:402
  325.5 24.7 %copy-start.5 = (bf16[24,3352]{1,0:T(8,128)(2,1)S(1)}, bf16[24,3352]{1,0:T(8,128)(2,1)}, u32[]{:S(2)}) copy-start(bf16[24,3352]{1,0:T(8,128)(2,1)} %param.17) | copy-start | bytes 482692
  325.5 25.6 %copy-start.18 = (bf16[24]{0:T(256)(128)(2,1)S(1)}, bf16[24]{0:T(256)(128)(2,1)}, u32[]{:S(2)}) copy-start(bf16[24]{0:T(256)(128)(2,1)} %param.16) | copy-start | bytes 148
  347.1 5.6 %copy-start.7 = (bf16[48,768]{1,0:T(8,128)(2,1)S(1)}, bf16[48,768]{1,0:T(8,128)(2,1)}, u32[]{:S(2)}) copy-start(bf16[48,768]{1,0:T(8,128)(2,1)} %param.24) | copy-start | bytes 221188
  347.1 5.7 %copy-start.19 = (bf16[48]{0:T(256)(128)(2,1)S(1)}, bf16[48]{0:T(256)(128)(2,1)}, u32[]{:S(2)}) copy-start(bf16[48]{0:T(256)(128)(2,1)} %param.23) | copy-start | bytes 292
  352.6 0.7 copy-start.6
Sparse Core Ops, SparseCore 0:
  11.5 68.6 all-gather.2
  197.9 114.9 reduce-scatter.1

commit v2 on v1

--- a/solution.py
+++ b/solution.py
@@ -57,6 +57,13 @@
     return soft, log_soft
 
 
+def marks(mark):
+    mark = mark.astype(f32)
+    doc = jnp.floor(mark * 0.25)
+    age = mark - 4.0 * doc
+    return doc, [(age > s - 0.5).astype(f32) for s in (3, 2, 1)]
+
+
 def scan_factors(z, rate, doc, prev_doc):
     soft, log_soft = step_terms(z)
     a = cumsum_rows(soft * (rate * LOG2E))
@@ -75,7 +82,7 @@
     return jnp.where(low, left, right)
 
 
-def forward_scan_kernel(heads, per_seq, tok, wc, gain, cw, cb, sb, rate, skip, docc, docr, m1, m2, m3,
+def forward_scan_kernel(heads, per_seq, tok, wc, gain, cw, cb, sb, rate, skip, mark, docr,
                         cin_o, pre_o, nrm_o, scan_o, st_o, z_o, pbuf, vbuf, state, pdoc):
     i = pl.program_id(0)
 
@@ -93,7 +100,7 @@
     z = proj[:, CONV:] + sb[...]
     z_o[...] = z
     pbuf[8 : 8 + Q, :] = proj[:, :CONV]
-    masks = (m3[...].astype(f32), m2[...].astype(f32), m1[...].astype(f32))
+    doc, masks = marks(mark[...])
     for t in range(CONV // 128):
         cols = slice(128 * t, 128 * t + 128)
         now = pbuf[8 : 8 + Q, cols]
@@ -105,7 +112,6 @@
         vbuf[:, cols] = (pre * sigmoid(pre)).astype(bf16)
     pbuf[0:8, :] = pbuf[Q : Q + 8, :]
 
-    doc = docc[...]
     prev = pdoc[0:1, :]
     soft, a, b, reach, tail, keep = scan_factors(z, rate[...], doc, prev)
     pdoc[...] = jnp.broadcast_to(doc[Q - 1 : Q, :], pdoc.shape)
@@ -139,7 +145,7 @@
         state[:, cols] = state[:, cols] * pair_of(keep, p, low_row) + dot(bt_mat, xw)
 
 
-def forward_scan(tok, wc, gain, cw, cb, sb, rate, skip, docc, docr, m1, m2, m3, heads, seqs):
+def forward_scan(tok, wc, gain, cw, cb, sb, rate, skip, mark, docr, heads, seqs):
     rows = tok.shape[0]
     n = rows // Q
     one = pl.Buffered(buffer_count=1)
@@ -149,7 +155,7 @@
         functools.partial(forward_scan_kernel, heads, n // seqs),
         grid=(n,),
         in_specs=[blk(D), full(wc), full(gain), full(cw), full(cb), full(sb), full(rate), full(skip),
-                  blk(128), pl.BlockSpec((1, 8, 128), lambda i: (i, 0, 0)), blk(128), blk(128), blk(128)],
+                  blk(128), pl.BlockSpec((1, 8, 128), lambda i: (i, 0, 0))],
         out_specs=[blk(CONV), blk(CONV), blk(D), blk(DI), pl.BlockSpec((1, N, DI), lambda i: (i, 0, 0)), blk(128)],
         out_shape=[jax.ShapeDtypeStruct((rows, CONV), bf16), jax.ShapeDtypeStruct((rows, CONV), bf16),
                    jax.ShapeDtypeStruct((rows, D), bf16), jax.ShapeDtypeStruct((rows, DI), bf16),
@@ -158,17 +164,34 @@
                         pltpu.VMEM((N, DI), f32), pltpu.VMEM((8, 128), f32)],
         compiler_params=pltpu.CompilerParams(vmem_limit_bytes=VM),
         name="forward_scan",
-    )(tok, wc, gain, cw, cb, sb, rate, skip, docc, docr, m1, m2, m3)
-
-
-def gate_kernel(nrm, scan, cot, tok, wg_abs, wo, gg, order, out_o, dscan_o, gn_o, gwg_o, gwo_o, acc_g, acc_o, wg):
+    )(tok, wc, gain, cw, cb, sb, rate, skip, mark, docr)
+
+
+def block_order(ri):
+    row = lax.broadcasted_iota(jnp.int32, (192, 192), 0)
+    lane = lax.broadcasted_iota(jnp.int32, (192, 192), 1)
+    second = lane >= 96
+    at = jnp.where(second, lane - 96, lane)
+    owner = lax.div(at, ri)
+    target = owner * (2 * ri) + (at - owner * ri) + jnp.where(second, ri, 0)
+    return (row == target).astype(bf16)
+
+
+def gate_kernel(ri, nrm, scan, cot, later, gg, order, mixed_o, dscan_o, dgate_o, early_o, wo_o, wg_o, acc_g, acc_o, wg, wo):
     i = pl.program_id(0)
 
     @pl.when(i == 0)
     def _():
         acc_g[...] = jnp.zeros_like(acc_g)
         acc_o[...] = jnp.zeros_like(acc_o)
-        wg[...] = dot_tn(order[...], wg_abs[...]).astype(bf16)
+        wg[...] = dot_tn(order[...], later[:, :DI]).astype(bf16)
+        blocks = block_order(ri)
+        for g in range(D // 96):
+            at = slice(96 * g, 96 * g + 96)
+            halves = jnp.concatenate([later[at, DI : DI + D], later[at, DI + D :]], axis=0)
+            wo[192 * g : 192 * g + 192, :] = dot(blocks, halves).astype(bf16)
+        wo_o[...] = wo[...]
+        wg_o[...] = wg[...]
 
     nb = nrm[...]
     up = cot[...]
@@ -180,39 +203,61 @@
     rr = lax.rsqrt(jnp.mean(gated * gated, axis=-1, keepdims=True) + EPS)
     unit = gated * rr
     mixed = (unit * gg[...]).astype(bf16)
-    out_o[...] = (tok[...].astype(f32) + dot(mixed, wo[...])).astype(bf16)
+    mixed_o[...] = mixed
     acc_o[...] += dot_tn(mixed, up)
-    gm = dot_nt(up, wo[...])
-    e = gm * gg[...]
+    e = dot_nt(up, wo[...]) * gg[...]
     dgated = rr * (e - unit * jnp.mean(unit * e, axis=-1, keepdims=True))
     dscan_o[...] = (dgated * act).astype(bf16)
     dgate = (dgated * sc * (sig + act * (1.0 - sig))).astype(bf16)
+    dgate_o[...] = dgate
     acc_g[...] += dot_tn(nb, dgate)
-    gn_o[...] = dot_nt(dgate, wg[...])
 
     @pl.when(i == pl.num_programs(0) - 1)
     def _():
-        gwg_o[...] = dot(order[...], acc_g[...].astype(bf16)).astype(bf16)
-        gwo_o[...] = acc_o[...].astype(bf16)
-
-
-def gate_pass(nrm, scan, cot, tok, wg, wo, gg, order, bm=256):
+        early_o[:, :DI] = dot(order[...], acc_g[...].astype(bf16)).astype(bf16)
+        blocks = block_order(ri)
+        for g in range(D // 96):
+            at = slice(96 * g, 96 * g + 96)
+            halves = dot_tn(blocks, acc_o[192 * g : 192 * g + 192, :].astype(bf16)).astype(bf16)
+            early_o[at, DI : DI + D] = halves[:96]
+            early_o[at, DI + D :] = halves[96:]
+
+
+def gate_pass(nrm, scan, cot, later, gg, order, ri, bm=256):
     rows = nrm.shape[0]
     one = pl.Buffered(buffer_count=1)
     full = lambda shape: pl.BlockSpec(shape, lambda i: (0,) * len(shape), pipeline_mode=one)
     blk = lambda w: pl.BlockSpec((bm, w), lambda i: (i, 0))
+    low = lambda *shape: jax.ShapeDtypeStruct(shape, bf16)
     return pl.pallas_call(
-        gate_kernel,
+        functools.partial(gate_kernel, ri),
         grid=(rows // bm,),
-        in_specs=[blk(D), blk(DI), blk(D), blk(D), full(wg.shape), full(wo.shape), full(gg.shape), full(order.shape)],
-        out_specs=[blk(D), blk(DI), blk(D), full((D, DI)), full((DI, D))],
-        out_shape=[jax.ShapeDtypeStruct((rows, D), bf16), jax.ShapeDtypeStruct((rows, DI), bf16),
-                   jax.ShapeDtypeStruct((rows, D), f32), jax.ShapeDtypeStruct((D, DI), bf16),
-                   jax.ShapeDtypeStruct((DI, D), bf16)],
-        scratch_shapes=[pltpu.VMEM((D, DI), f32), pltpu.VMEM((DI, D), f32), pltpu.VMEM((D, DI), bf16)],
+        in_specs=[blk(D), blk(DI), blk(D), full(later.shape), full(gg.shape), full(order.shape)],
+        out_specs=[blk(DI), blk(DI), blk(DI), full((D, 2 * DI)), full((DI, D)), full((D, DI))],
+        out_shape=[low(rows, DI), low(rows, DI), low(rows, DI), low(D, 2 * DI), low(DI, D), low(D, DI)],
+        scratch_shapes=[pltpu.VMEM((D, DI), f32), pltpu.VMEM((DI, D), f32), pltpu.VMEM((D, DI), bf16),
+                        pltpu.VMEM((DI, D), bf16)],
         compiler_params=pltpu.CompilerParams(vmem_limit_bytes=VM),
         name="gate_pass",
-    )(nrm, scan, cot, tok, wg, wo, gg, order)
+    )(nrm, scan, cot, later, gg, order)
+
+
+def out_kernel(mixed, tok, wo, out_o):
+    out_o[...] = (tok[...].astype(f32) + dot(mixed[...], wo[...])).astype(bf16)
+
+
+def out_pass(mixed, tok, wo, bm=512):
+    rows = tok.shape[0]
+    blk = lambda w: pl.BlockSpec((bm, w), lambda i: (i, 0))
+    return pl.pallas_call(
+        out_kernel,
+        grid=(rows // bm,),
+        in_specs=[blk(DI), blk(D), pl.BlockSpec((DI, D), lambda i: (0, 0), pipeline_mode=pl.Buffered(buffer_count=1))],
+        out_specs=blk(D),
+        out_shape=jax.ShapeDtypeStruct((rows, D), bf16),
+        compiler_params=pltpu.CompilerParams(vmem_limit_bytes=VM),
+        name="out_pass",
+    )(mixed, tok, wo)
 
 
 def head_sums(v, onehot):
@@ -221,9 +266,9 @@
     return dot(hi, onehot) + dot(lo, onehot)
 
 
-def backward_scan_kernel(heads, per_seq, dscan, cin, pre_r, z_r, st, cw, rate, skip, docc, docr, pdocr, m1, m2, m3, onehot,
+def backward_scan_kernel(heads, per_seq, dscan, cin, pre_r, z_r, st, cw, rate, skip, mark, docr, pdocr,
                          dproj_o, gcw_o, gcb_o, gsk_o, ghd_o,
-                         vbuf, dbuf, dstate, p1buf, qbuf, xwbuf, rowbuf, lastbuf, mbuf):
+                         vbuf, dbuf, dstate, p1buf, qbuf, xwbuf, rowbuf, lastbuf, mbuf, onehot):
     i = pl.program_id(0)
 
     @pl.when(i == 0)
@@ -233,6 +278,8 @@
         gsk_o[...] = jnp.zeros_like(gsk_o)
         ghd_o[...] = jnp.zeros_like(ghd_o)
         rowbuf[...] = jnp.zeros_like(rowbuf)
+        head = lax.broadcasted_iota(jnp.int32, onehot.shape, 0) >> 6
+        onehot[...] = (head == lax.broadcasted_iota(jnp.int32, onehot.shape, 1)).astype(bf16)
 
     @pl.when(lax.rem(i, per_seq) == 0)
     def _():
@@ -245,7 +292,7 @@
         vbuf[:, cols] = (pre * sigmoid(pre)).astype(bf16)
 
     z = z_r[...]
-    doc = docc[...]
+    doc, masks = marks(mark[...])
     prev = pdocr[0, 0:1, :]
     soft, a, b, reach, tail, keep = scan_factors(z, rate[...], doc, prev)
     at = a.T
@@ -311,7 +358,6 @@
     ghd_o[0:8, :] += jnp.sum(dz.reshape(-1, 8, 128), axis=0)
     ghd_o[8:16, :] += jnp.sum((g * soft).reshape(-1, 8, 128), axis=0)
 
-    masks = (m3[...].astype(f32), m2[...].astype(f32), m1[...].astype(f32))
     for t in range(CONV // 128):
         cols = slice(128 * t, 128 * t + 128)
         pre = pre_r[:, cols].astype(f32)
@@ -331,7 +377,7 @@
     mbuf[:, Q : Q + 8, :] = mbuf[:, 0:8, :]
 
 
-def backward_scan(dscan, cin, pre, z, st, cw, rate, skip, docc, docr, pdocr, m1, m2, m3, onehot, heads, seqs):
+def backward_scan(dscan, cin, pre, z, st, cw, rate, skip, mark, docr, pdocr, heads, seqs):
     rows = dscan.shape[0]
     n = rows // Q
     one = pl.Buffered(buffer_count=1)
@@ -342,21 +388,22 @@
         functools.partial(backward_scan_kernel, heads, n // seqs),
         grid=(n,),
         in_specs=[blk(DI), blk(CONV), blk(CONV), blk(128), blk3(N, DI), full(cw.shape), full(rate.shape), full(skip.shape),
-                  blk(128), blk3(8, 128), blk3(8, 128), blk(128), blk(128), blk(128), full(onehot.shape)],
+                  blk(128), blk3(8, 128), blk3(8, 128)],
         out_specs=[blk(CONV + 128), full((32, CONV)), full((8, CONV)), full((8, DI)), full((16, 128))],
         out_shape=[jax.ShapeDtypeStruct((rows, CONV + 128), bf16), jax.ShapeDtypeStruct((32, CONV), f32),
                    jax.ShapeDtypeStruct((8, CONV), f32), jax.ShapeDtypeStruct((8, DI), f32),
                    jax.ShapeDtypeStruct((16, 128), f32)],
         scratch_shapes=[pltpu.VMEM((Q, CONV), bf16), pltpu.VMEM((Q, CONV), f32), pltpu.VMEM((N, DI), f32),
                         pltpu.VMEM((Q, DI), f32), pltpu.VMEM((Q, DI), f32), pltpu.VMEM((Q, 2 * DI), bf16),
-                        pltpu.VMEM((128, 128), f32), pltpu.VMEM((8, DI), f32), pltpu.VMEM((3, Q + 8, CONV), f32)],
+                        pltpu.VMEM((128, 128), f32), pltpu.VMEM((8, DI), f32), pltpu.VMEM((3, Q + 8, CONV), f32),
+                        pltpu.VMEM((DI, 128), bf16)],
         compiler_params=pltpu.CompilerParams(vmem_limit_bytes=VM),
         name="backward_scan",
-    )(dscan, cin, pre, z, st, cw, rate, skip, docc, docr, pdocr, m1, m2, m3, onehot)
-
-
-def norm_back_kernel(dproj, gn, tok, cot, wc, gain, order, out_o):
-    grad = gn[...] + dot_nt(dproj[...], wc[...])
+    )(dscan, cin, pre, z, st, cw, rate, skip, mark, docr, pdocr)
+
+
+def norm_back_kernel(dproj, dgate, tok, cot, wc, wg, gain, order, out_o):
+    grad = dot_nt(dgate[...], wg[...]) + dot_nt(dproj[...], wc[...])
     x = tok[...].astype(f32)
     r = lax.rsqrt(jnp.mean(x * x, axis=-1, keepdims=True) + EPS)
     unit = x * r
@@ -366,7 +413,7 @@
     out_o[...] = dot_nt(res, order[...]).astype(bf16)
 
 
-def norm_back(dproj, gn, tok, cot, wc, gain, order, bm=512):
+def norm_back(dproj, dgate, tok, cot, wc, wg, gain, order, bm=512):
     rows = dproj.shape[0]
     one = pl.Buffered(buffer_count=1)
     full = lambda shape: pl.BlockSpec(shape, lambda i: (0,) * len(shape), pipeline_mode=one)
@@ -374,12 +421,12 @@
     return pl.pallas_call(
         norm_back_kernel,
         grid=(rows // bm,),
-        in_specs=[blk(CONV + 128), blk(D), blk(D), blk(D), full(wc.shape), full(gain.shape), full(order.shape)],
+        in_specs=[blk(CONV + 128), blk(DI), blk(D), blk(D), full(wc.shape), full(wg.shape), full(gain.shape), full(order.shape)],
         out_specs=blk(D),
         out_shape=jax.ShapeDtypeStruct((rows, D), bf16),
         compiler_params=pltpu.CompilerParams(vmem_limit_bytes=VM),
         name="norm_back",
-    )(dproj, gn, tok, cot, wc, gain, order)
+    )(dproj, dgate, tok, cot, wc, wg, gain, order)
 
 
 def stages_of(mesh):
@@ -402,33 +449,33 @@
     return lax.ppermute(arr, axis, [(i, i ^ offset) for i in range(size)])
 
 
-def gather_slots(shard, stages, sizes):
-    block = shard
-    for axis, stride, group, _ in stages:
-        block = jnp.stack([block] + [swap(block, axis, sizes[axis], k * stride) for k in range(1, group)])
-    return block
-
-
-def scatter_slots(terms, stages, sizes):
-    low, kept = terms, terms
-    for axis, stride, group, _ in stages[::-1]:
-        got = [swap(low[k], axis, sizes[axis], k * stride) for k in range(1, group)]
-        kept = kept[0].astype(f32)
-        for part in got:
-            kept = kept + part.astype(f32)
-        low = kept.astype(bf16)
-    return kept
+def gather_stage(block, stage, sizes):
+    axis, stride, group, _ = stage
+    return jnp.stack([block] + [swap(block, axis, sizes[axis], k * stride) for k in range(1, group)])
+
+
+def scatter_stage(kept, stage, sizes):
+    axis, stride, group, _ = stage
+    low = kept.astype(bf16)
+    got = [swap(low[k], axis, sizes[axis], k * stride) for k in range(1, group)]
+    total = kept[0].astype(f32)
+    for part in got:
+        total = total + part.astype(f32)
+    return total
+
+
+def before(value, *others):
+    return lax.optimization_barrier((value,) + others)
 
 
 def three_parts(v):
     hi = lax.reduce_precision(v, 8, 7)
     mid = lax.reduce_precision(v - hi, 8, 7)
-    return jnp.concatenate([hi.astype(bf16), mid.astype(bf16), (v - hi - mid).astype(bf16)])
-
-
-def whole_parts(v):
-    hi, mid, lo = jnp.split(v.astype(f32), 3, axis=-1)
-    return (hi + mid + lo).reshape(-1)
+    return jnp.concatenate([hi, mid, v - hi - mid], axis=0).astype(bf16)
+
+
+def row(v):
+    return jnp.pad(v, ((0, 0), (0, 128 - v.shape[1])))
 
 
 def doc_terms(segments):
@@ -437,12 +484,14 @@
     n = rows // Q
     seg = segments.astype(f32)
     pad = jnp.pad(seg, ((0, 0), (3, 0)), constant_values=-1.0)
-    wide = lambda v: jnp.broadcast_to(v.reshape(rows, 1), (rows, 128))
-    same = [wide((pad[:, 3 - s : 3 - s + length] == seg).astype(f32)) for s in (1, 2, 3)]
+    mark = 4.0 * seg
+    for s in (1, 2, 3):
+        mark = mark + (pad[:, 3 - s : 3 - s + length] == seg).astype(f32)
+    mark = jnp.broadcast_to(mark.astype(bf16).reshape(rows, 1), (rows, 128))
     docr = jnp.broadcast_to(seg.reshape(n, 1, Q), (n, 8, Q))
     ends = seg.reshape(seqs, length // Q, Q)[:, :, -1]
     prev = jnp.concatenate([jnp.full((seqs, 1), -1.0, f32), ends[:, :-1]], axis=1).reshape(n, 1, 1)
-    return wide(seg), docr, jnp.broadcast_to(prev, (n, 8, 128)), same
+    return mark, docr, jnp.broadcast_to(prev, (n, 8, 128))
 
 
 def local(mesh, tokens, cotangent, segments, in_gain, weight_in, conv_weight, conv_bias, step_bias, decay_log, skip_gain,
@@ -467,50 +516,45 @@
     order = (jnp.arange(D)[:, None] == feature[None, :]).astype(bf16)
     slot_hot = (device[:, None] == jnp.arange(nd)[None, :]).astype(bf16)
 
-    small = jnp.concatenate([in_gain, conv_weight.reshape(-1), conv_bias, gate_gain, three_parts(step_bias),
-                             three_parts(decay_log), three_parts(skip_gain)])
-    small = jnp.pad(small, (0, ri * free - small.shape[0])).reshape(ri, free)
-    gathered = gather_slots(jnp.concatenate([weight_in[:, DI:], small], axis=1), stages, sizes)
-    wc = gathered.reshape(D, CONV + 128)
-    later = jnp.concatenate([weight_in[:, :DI], weight_out.reshape(2, ri, D).transpose(1, 0, 2).reshape(ri, DI)], axis=0)
-    later = lax.all_gather(later, axes, axis=0)
+    later = jnp.concatenate([weight_in[:, :DI], weight_out[:ri], weight_out[ri:]], axis=1)
+    later = lax.all_gather(later, axes, axis=0, tiled=True)
+    wc = jnp.pad(weight_in[:, DI:], ((0, 0), (0, 128 - heads)))
+    small = jnp.concatenate([row(in_gain[None]), row(conv_weight), row(conv_bias[None]), row(gate_gain[None]),
+                             row(three_parts(jnp.stack([step_bias, decay_log, skip_gain])))], axis=0)
     tok = tokens.reshape(rows, D)
     up = cotangent.reshape(rows, D)
+    mark, docr, pdocr = doc_terms(segments)
+    wc = gather_stage(wc, stages[0], sizes)
+    wc, order, mark, docr, pdocr, small = before(wc, order, mark, docr, pdocr, small)
+    for stage in stages:
+        small = gather_stage(small, stage, sizes)
+    for stage in stages[1:-1]:
+        wc = gather_stage(wc, stage, sizes)
     tok_s = jnp.dot(tok, order, preferred_element_type=bf16)
     up_s = jnp.dot(up, order, preferred_element_type=bf16)
-    docc, docr, pdocr, same = doc_terms(segments)
-
-    packed = gathered.reshape(nd, ri, CONV + 128)[:, :, CONV + heads :].reshape(nd, ri * free)
-    gain = packed[:, :ri].reshape(1, D).astype(f32)
-    packed = lax.dot_general(slot_hot, packed, (((0,), (0,)), ((), ())), preferred_element_type=f32)
-    at = ri
-    cw = packed[:, at : at + 4 * cc].reshape(nd, 4, cc).transpose(1, 0, 2).reshape(4, CONV)
-    at += 4 * cc
-    cb = packed[:, at : at + cc].reshape(1, CONV)
-    at += cc
-    gg = packed[:, at : at + ro].reshape(1, DI)
-    at += ro
-    per_head = []
-    for _ in range(3):
-        per_head.append(whole_parts(packed[:nf, at : at + 3 * share]))
-        at += 3 * share
+
+    small = small.reshape(nd, 16 * 128)
+    gain = small[:, :ri].reshape(1, D).astype(f32)
+    small = lax.dot_general(slot_hot, small, (((0,), (0,)), ((), ())), preferred_element_type=f32).reshape(nd, 16, 128)
+    cw = jnp.pad(small[:, 1:5, :cc].transpose(1, 0, 2).reshape(4, CONV), ((0, 4), (0, 0)))
+    cb = small[:, 5, :cc].reshape(1, CONV)
+    gg = small[:, 6, :ro].reshape(1, DI)
+    per_head = small[:nf, 7:16, :share]
+    per_head = (per_head[:, 0:3] + per_head[:, 3:6] + per_head[:, 6:9]).transpose(1, 0, 2).reshape(3, heads)
     lanes = lambda v: jnp.pad(v, (0, 128 - heads))[None]
+    sb = lanes(per_head[0])
     rate = lanes(-jnp.exp(per_head[1]))
     skip = jnp.repeat(per_head[2], HD)[None]
-    cw = jnp.pad(cw, ((0, 4), (0, 0)))
-    onehot = (jnp.arange(DI)[:, None] // HD == jnp.arange(128)[None, :]).astype(bf16)
+    wc, tok_s, up_s, gain, cw, cb, gg, sb, rate, skip = before(wc, tok_s, up_s, gain, cw, cb, gg, sb, rate, skip)
+    wc = gather_stage(wc, stages[-1], sizes).reshape(D, CONV + 128)
 
     cin, pre, nrm, scan, st, z = forward_scan(
-        tok_s, wc, gain, cw, cb, lanes(per_head[0]), rate, skip, docc, docr, *same, heads, seqs)
-
-    wg = later[:, :ri].reshape(D, DI)
-    wo = later[:, ri:].reshape(nd, ri, 2, D).transpose(0, 2, 1, 3).reshape(DI, D)
-    out, dscan, gn, gwg, gwo = gate_pass(nrm, scan, up, tok, wg, wo, gg, order)
-    early = jnp.concatenate([gwg.reshape(nd, ri, DI), gwo.reshape(nd, 2, ri, D).transpose(0, 2, 1, 3).reshape(nd, ri, DI)], axis=1)
-    early = lax.psum_scatter(early, axes, scatter_dimension=0)
+        tok_s, wc, gain, cw, cb, sb, rate, skip, mark, docr, heads, seqs)
+    mixed, dscan, dgate, early, wo, wg = gate_pass(nrm, scan, up, later, gg, order, ri)
+    early = lax.psum_scatter(early, axes, scatter_dimension=0, tiled=True)
 
     dproj, gcw, gcb, gsk, ghd = backward_scan(
-        dscan, cin, pre, z, st, cw, rate, skip, docc, docr, pdocr, *same, onehot, heads, seqs)
+        dscan, cin, pre, z, st, cw, rate, skip, mark, docr, pdocr, heads, seqs)
     gwc = lax.dot_general(nrm, dproj, (((0,), (0,)), ((), ())), preferred_element_type=f32).astype(bf16)
 
     taps = jnp.concatenate([gcw.reshape(4, 8, CONV).sum(1), gcb.sum(0)[None]], axis=0)
@@ -525,13 +569,19 @@
     width = 5 * cc + 3 * share
     both = jnp.pad(both, ((0, 0), (0, ri * free - 2 * width))).reshape(nd, ri, free)
     gwc = jnp.concatenate([gwc.reshape(nd, ri, CONV + 128)[:, :, : CONV + heads], both], axis=2)
-    total = scatter_slots(gwc.reshape([g for _, _, g, _ in stages[::-1]] + [ri, CONV + 128]), stages, sizes)
-
-    gtok = norm_back(dproj, gn, tok_s, up_s, wc, gain, order)
+    total = gwc.reshape([g for _, _, g, _ in stages[::-1]] + [ri, CONV + 128])
+    for at, stage in enumerate(stages[::-1]):
+        if at == len(stages) - 2:
+            total, gain = before(total, gain)
+            gtok = norm_back(dproj, dgate, tok_s, up_s, wc, wg, gain, order)
+        if at == len(stages) - 1:
+            total, gtok, wo = before(total, gtok, wo)
+        total = scatter_stage(total, stage, sizes)
+    out = out_pass(mixed, tok, wo)
 
     early = early.astype(f32)
-    g_in = jnp.concatenate([early[:ri], total[:, : CONV + heads]], axis=1)
-    g_out = early[ri:].reshape(ri, 2, D).transpose(1, 0, 2).reshape(ro, D)
+    g_in = jnp.concatenate([early[:, :DI], total[:, : CONV + heads]], axis=1)
+    g_out = jnp.concatenate([early[:, DI : DI + D], early[:, DI + D :]], axis=0)
     packed = total[:, CONV + heads :].reshape(-1)
     packed = packed[:width] + packed[width : 2 * width]
     g_in_gain = jnp.sum(weight_in.astype(f32) * g_in, axis=1) / in_gain.astype(f32)

time: 361 us -> 314 us (0.87)
  waiting for transfers between devices: 38.4 us -> 8.21 us
  local copies, waits for them, and re-layouts: 44.6 us -> 19.2 us
  starting transfers between devices: 21.2 us -> 28 us
  Pallas kernels: 204 us -> 209 us
    ppermute x14 -> x21, waiting for transfers between devices: 38.3 us -> 8.16 us  [swap(): return lax.ppermute(arr, axis, [(i, i ^ offset) for i in range(size)])]
    reshape x15 -> x1, local copies, waits for them, and re-layouts: 12.9 us -> 0.1 us  [local(): small[:, 1:5, :cc].transpose(1, 0, 2).reshape(4, CONV)]
    broadcast_in_dim x7 -> x3, local copies, waits for them, and re-layouts: 9.37 us -> 1.92 us  [the longest x1 1.12 us: doc_terms(): mark = jnp.broadcast_to(mark.astype(bf16).reshape(rows, 1), (rows, 128))]
    ppermute x14 -> x21, starting transfers between devices: 21.2 us -> 27.9 us  [swap(): return lax.ppermute(arr, axis, [(i, i ^ offset) for i in range(size)])]
    pallas_call x1, Pallas kernels: 21.6 us -> 26.9 us  [norm_back(): pl.pallas_call(norm_back_kernel, grid=(rows // bm,), in_specs=[blk(CONV +...]
    slice x8 -> x6, local copies, waits for them, and re-layouts: 7.86 us -> 3.4 us  [the longest x1 0.9 us: local(): wc = jnp.pad(weight_in[:, DI:], ((0, 0), (0, 128 - heads)))]
    pallas_call x1 -> x2, Pallas kernels: 54.8 us -> 55.3 us  [the longest x1 45.2 us: gate_pass(): pl.pallas_call(functools.partial(gate_kernel, ri), grid=(rows // bm,), in...]
  transfers between devices with their start and end apart: 16 -> 23, of which waited for: 7 -> 4; matrix products, arithmetic and copies ran while one was open for 16% -> 15% of each run, Pallas kernels for 41% -> 52%
where the time goes in v2:
time: 314 us; the launch traced here: 313 us
  Pallas kernels  209 us (67%)
  starting transfers between devices  28 us (9%)
  matrix products  20 us (6%)
  local copies, waits for them, and re-layouts  19.2 us (6%)
  between operations  14.5 us (5%)
  other arithmetic  14 us (4%)
  waiting for transfers between devices  8.21 us (3%)
    pallas_call x1, Pallas kernels, backward_scan(): pl.pallas_call(functools.partial(backward_scan_kernel, heads, n // seqs),...  73.8 us
    pallas_call x1, Pallas kernels, forward_scan(): pl.pallas_call(functools.partial(forward_scan_kernel, heads, n // seqs),...  53.3 us
    pallas_call x1, Pallas kernels, gate_pass(): pl.pallas_call(functools.partial(gate_kernel, ri), grid=(rows // bm,), in...  45.2 us
    ppermute x21, starting transfers between devices, swap(): return lax.ppermute(arr, axis, [(i, i ^ offset) for i in range(size)])  27.9 us
    pallas_call x1, Pallas kernels, norm_back(): pl.pallas_call(norm_back_kernel, grid=(rows // bm,), in_specs=[blk(CONV +...  26.9 us
    pallas_call x1, Pallas kernels, out_pass(): pl.pallas_call(out_kernel, grid=(rows // bm,), in_specs=[blk(DI), blk(D),...  10 us
    dot_general x1, matrix products, local(): lax.dot_general(nrm, dproj, (((0,), (0,)), ((), ())), preferred_element_t...  9.18 us
    ppermute x21, waiting for transfers between devices, swap(): return lax.ppermute(arr, axis, [(i, i ^ offset) for i in range(size)])  8.16 us
  transfers between devices with their start and end apart: 23, of which 4 were waited for; matrix products, arithmetic and copies ran while one was open for 15% of the time, Pallas kernels for 52%

profile of v2, /device:TPU:0, one launch (start us, length us, event | category | flops | bytes accessed | tf_op | source)
XLA Modules:
  0.0 313.2 jit_solution(15518909438312522944)
XLA Ops:
  7.2 0.8 fusion.35
  8.0 0.9 slice.175
  8.9 0.7 pad_maximum_fusion.5
  9.7 0.9 slice.159
  10.6 3.1 collective-permute-start
  13.7 2.6 collective-permute-start.1
  16.3 0.7 pad.47
  16.9 0.7 pad.46
  17.6 0.7 pad.48
  18.3 0.7 pad.49
  18.9 0.7 broadcast_xor_fusion
  19.7 0.7 convert_bitcast_fusion
  20.9 0.7 reduce-precision_convert_fusion.2
  22.2 1.4 collective-permute-done.1
  23.7 1.1 broadcast_in_dim.46.mark
  24.8 0.6 broadcast_in_dim.48.docr
  25.4 0.7 broadcast_in_dim.50.pdocr
  26.1 1.5 collective-permute-start.6
  27.7 1.5 collective-permute-start.7
  29.2 1.3 collective-permute-start.8
  30.5 1.5 collective-permute-start.3
  32.0 1.5 collective-permute-start.4
  33.6 1.0 collective-permute-done.8
  34.6 1.5 collective-permute-start.9
  36.1 1.5 collective-permute-start.10
  38.1 6.5 %convolution_bitcast_fusion.cot = bf16[2048,768]{1,0:T(8,128)(2,1)} fusion(bf16[2048,768]{1,0:T(8,128)(2,1)} %bitcast.132, bf16[768,768]{1,0:T(8,128)(2,1)S(1)} %fusion.order), kind=kOutput, calls=%fused_computation.1 | convolution fusion | flops 2415919104 | bytes 7471104 | tf_op jit(solution)/shard_map/dot_general | solution.py:534
  44.6 2.3 collective-permute-start.5
  47.0 4.0 %convolution_bitcast_fusion.1.tok = bf16[2048,768]{1,0:T(8,128)(2,1)} fusion(bf16[2048,768]{1,0:T(8,128)(2,1)S(1)} %bitcast.129, bf16[768,768]{1,0:T(8,128)(2,1)S(1)} %fusion.order), kind=kOutput, calls=%fused_computation.2 | convolution fusion | flops 2415919104 | bytes 7471104 | tf_op jit(solution)/shard_map/dot_general | solution.py:533
  51.7 0.7 broadcast_in_dim_reshape.4.skip
  52.4 0.7 reshape_squeeze.6.cb
  53.1 0.7 reshape_squeeze.7.gg
  53.7 0.7 reshape.172.gain
  54.4 0.6 pad.51.cw
  55.8 0.5 collective-permute-start.13
  56.4 2.8 collective-permute-done.13
  59.2 1.9 pad_maximum_fusion
  61.2 53.3 %forward_scan.1 = (bf16[2048,1792]{1,0:T(8,128)(2,1)}, bf16[2048,1792]{1,0:T(8,128)(2,1)}, bf16[2048,768]{1,0:T(8,128)(2,1)}, bf16[2048,1536]{1,0:T(8,128)(2,1)}...) custom-call(bf16[2048,768]{1,0:T(8,128)(2,1)} %convolution_bitcast_fusion.1.tok, bf16[768,1920]{1,0:T(8,128)(2,1)} %bitcast.124, ...), custom_call_target="tpu_custom_call" | custom-call | tf_op jit(solution)/shard_map/forward_scan/pallas_call | solution.py:154
  114.5 45.2 %gate_pass.1 = (bf16[2048,1536]{1,0:T(8,128)(2,1)}, bf16[2048,1536]{1,0:T(8,128)(2,1)}, bf16[2048,1536]{1,0:T(8,128)(2,1)}, bf16[768,3072]{1,0:T(8,128)(2,1)}, b...) custom-call(bf16[2048,768]{1,0:T(8,128)(2,1)} %get-tuple-element.62.nrm, bf16[2048,1536]{1,0:T(8,128)(2,1)} %get-tuple-element.63.scan, ...), custom_call_target="tpu_custom_call" | custom-call | tf_op jit(solution)/shard_map/gate_pass/pallas_call | solution.py:232
  159.8 73.8 %backward_scan.1 = (bf16[2048,1920]{1,0:T(8,128)(2,1)}, f32[32,1792]{1,0:T(8,128)}, f32[8,1792]{1,0:T(8,128)}, f32[8,1536]{1,0:T(8,128)}, f32[16,128]{1,0:T(8,128)}) custom-call(bf16[2048,1536]{1,0:T(8,128)(2,1)} %get-tuple-element.66.dscan, bf16[2048,1792]{1,0:T(8,128)(2,1)} %get-tuple-element.67.cin, bf16[2048,1792]{1,0:T(8,128)(2,1)} %get-tuple-element.68.pre_r, ...), custom_call_target="tpu_custom_call" | custom-call | tf_op jit(solution)/shard_map/backward_scan/pallas_call | solution.py:387
  233.6 1.0 bitcast_reduce_fusion
  234.7 0.8 reduce_sum.73
  235.8 0.7 slice_reduce_fusion.1
  236.6 0.8 reduce_sum.76
  238.5 9.2 %convolution_convert_fusion = bf16[768,1920]{1,0:T(8,128)(2,1)S(1)} fusion(bf16[2048,768]{1,0:T(8,128)(2,1)S(1)} %copy-done.2, bf16[2048,1920]{1,0:T(8,128)(2,1)} %get-tuple-element.72.dproj), kind=kOutput, calls=%fused_computation | convolution fusion | flops 6041272320 | bytes 13959168 | tf_op jit(solution)/shard_map/dot_general | solution.py:558
  248.4 2.9 collective-permute-done.14
  251.8 0.9 slice_bitcast_fusion.2
  252.7 0.6 collective-permute-start.15
  253.3 1.0 collective-permute-start.16
  254.3 1.9 collective-permute-start.17
  256.2 26.9 %norm_back.1 = bf16[2048,768]{1,0:T(8,128)(2,1)} custom-call(bf16[2048,1920]{1,0:T(8,128)(2,1)} %get-tuple-element.72.dproj, bf16[2048,1536]{1,0:T(8,128)(2,1)} %get-tuple-element.78.dgate, bf16[2048,768]{1,0:T(8,128)(2,1)} %convolution_bitcast_fusion.1.tok, bf16[2048,768]{1,0:T(8,128)(2,1)} %convolution_bitcast_fusion.cot, bf16[768,1920]{1,0:T(8,128)(2,1)} %bitcast.125, ...), custom_call_target="tpu_custom_call" | custom-call | tf_op jit(solution)/shard_map/norm_back/pallas_call | solution.py:421
  283.2 0.7 copy-done.4
  283.9 1.2 fusion.3
  285.2 0.6 collective-permute-start.18
  285.8 2.5 collective-permute-start.19
  288.3 1.4 collective-permute-start.20
  289.7 10.0 %out_pass.1 = bf16[2048,768]{1,0:T(8,128)(2,1)} custom-call(bf16[2048,1536]{1,0:T(8,128)(2,1)} %get-tuple-element.65.mixed, bf16[2048,768]{1,0:T(8,128)(2,1)} %bitcast.128, bf16[1536,768]{1,0:T(8,128)(2,1)} %get-tuple-element.83.wo), custom_call_target="tpu_custom_call" | custom-call | tf_op jit(solution)/shard_map/out_pass/pallas_call | solution.py:252
  300.1 0.6 slice.201
  300.6 0.7 reshape.171
  301.3 0.6 fusion.37
  301.9 0.8 fusion.34
  302.7 0.8 multiply_reduce_fusion.1
  303.5 0.5 convert_divide_fusion
  304.0 0.9 slice.224
  304.9 0.9 multiply_reduce_fusion
  (109 shorter events, 7.1 us)
Async XLA Ops:
  7.2 107.3 %all-gather.2.cloned.1.call-start = ((), (), s32[]{:S(2)}) async-start(), calls=%async_computation.1 | async-start | bytes 4866048 | tf_op jit(solution)/shard_map/all_gather | solution.py:520
  9.6 292.3 %reduce-scatter.2.cloned.1.call-start = ((), (), s32[]{:S(2)}) async-start(), calls=%async_computation.2 | async-start | bytes 4866048 | tf_op jit(solution)/shard_map/reduce_scatter | solution.py:554
  10.6 11.7 %collective-permute-start = (bf16[24,1920]{1,0:T(8,128)(2,1)S(1)}, bf16[24,1920]{1,0:T(8,128)(2,1)S(1)}, u32[]{:S(2)}, u32[]{:S(2)}) collective-permute-start(bf16[24,1920]{1,0:T(8,128)(2,1)S(1)} %get-tuple-element.106), channel_id=1, source_target_pairs={{0,8},{2,10},{4,12},{6,14},{8,0},{10,2},{12,4},{14,6},{16,24},{18,... | collective-permute-start | bytes 276488 | tf_op jit(solution)/shard_map/ppermute | solution.py:449
  13.7 10.0 %collective-permute-start.1 = (bf16[24,1920]{1,0:T(8,128)(2,1)S(1)}, bf16[24,1920]{1,0:T(8,128)(2,1)S(1)}, u32[]{:S(2)}, u32[]{:S(2)}) collective-permute-start(bf16[24,1920]{1,0:T(8,128)(2,1)S(1)} %get-tuple-element.106), channel_id=1, source_target_pairs={{0,16},{2,18},{4,20},{6,22},{8,24},{10,26},{12,28},{14,30},{16,0},... | collective-permute-start | bytes 276488 | tf_op jit(solution)/shard_map/ppermute | solution.py:449
  16.2 7.4 %collective-permute-start.2 = (bf16[24,1920]{1,0:T(8,128)(2,1)S(1)}, bf16[24,1920]{1,0:T(8,128)(2,1)S(1)}, u32[]{:S(2)}, u32[]{:S(2)}) collective-permute-start(bf16[24,1920]{1,0:T(8,128)(2,1)S(1)} %get-tuple-element.106), channel_id=1, source_target_pairs={{0,24},{2,26},{4,28},{6,30},{8,16},{10,18},{12,20},{14,22},{16,8},... | collective-permute-start | bytes 276488 | tf_op jit(solution)/shard_map/ppermute | solution.py:449
  22.0 24.9 %copy-start = (bf16[768,768]{1,0:T(8,128)(2,1)}, bf16[768,768]{1,0:T(8,128)(2,1)S(1)}, u32[]{:S(2)}) copy-start(bf16[768,768]{1,0:T(8,128)(2,1)S(1)} %fusion.order) | copy-start | bytes 3538948
  26.1 7.4 %collective-permute-start.6 = (bf16[16,128]{1,0:T(8,128)(2,1)S(1)}, bf16[16,128]{1,0:T(8,128)(2,1)S(1)}, u32[]{:S(2)}, u32[]{:S(2)}) collective-permute-start(bf16[16,128]{1,0:T(8,128)(2,1)S(1)} %concatenate.40), channel_id=1, source_target_pairs={{0,8},{2,10},{4,12},{6,14},{8,0},{10,2},{12,4},{14,6},{16,24},{18,... | collective-permute-start | bytes 12296 | tf_op jit(solution)/shard_map/ppermute | solution.py:449
  27.7 5.9 %collective-permute-start.7 = (bf16[16,128]{1,0:T(8,128)(2,1)S(1)}, bf16[16,128]{1,0:T(8,128)(2,1)S(1)}, u32[]{:S(2)}, u32[]{:S(2)}) collective-permute-start(bf16[16,128]{1,0:T(8,128)(2,1)S(1)} %concatenate.40), channel_id=1, source_target_pairs={{0,16},{2,18},{4,20},{6,22},{8,24},{10,26},{12,28},{14,30},{16,0},... | collective-permute-start | bytes 12296 | tf_op jit(solution)/shard_map/ppermute | solution.py:449
  29.2 5.4 %collective-permute-start.8 = (bf16[16,128]{1,0:T(8,128)(2,1)S(1)}, bf16[16,128]{1,0:T(8,128)(2,1)S(1)}, u32[]{:S(2)}, u32[]{:S(2)}) collective-permute-start(bf16[16,128]{1,0:T(8,128)(2,1)S(1)} %concatenate.40), channel_id=1, source_target_pairs={{0,24},{2,26},{4,28},{6,30},{8,16},{10,18},{12,20},{14,22},{16,8},... | collective-permute-start | bytes 12296 | tf_op jit(solution)/shard_map/ppermute | solution.py:449
  30.5 25.0 %collective-permute-start.3 = (bf16[4,24,1920]{2,1,0:T(8,128)(2,1)S(1)}, bf16[4,24,1920]{2,1,0:T(8,128)(2,1)S(1)}, u32[]{:S(2)}, u32[]{:S(2)}) collective-permute-start(bf16[4,24,1920]{2,1,0:T(8,128)(2,1)S(1)} %pad_maximum_fusion.3), channel_id=1, source_target_pairs={{0,2},{2,0},{4,6},{6,4},{8,10},{10,8},{12,14},{14,12},{16,18},{18,... | collective-permute-start | bytes 1105928 | tf_op jit(solution)/shard_map/ppermute | solution.py:449
  32.0 23.5 %collective-permute-start.4 = (bf16[4,24,1920]{2,1,0:T(8,128)(2,1)S(1)}, bf16[4,24,1920]{2,1,0:T(8,128)(2,1)S(1)}, u32[]{:S(2)}, u32[]{:S(2)}) collective-permute-start(bf16[4,24,1920]{2,1,0:T(8,128)(2,1)S(1)} %pad_maximum_fusion.3), channel_id=1, source_target_pairs={{0,4},{2,6},{4,0},{6,2},{8,12},{10,14},{12,8},{14,10},{16,20},{18,... | collective-permute-start | bytes 1105928 | tf_op jit(solution)/shard_map/ppermute | solution.py:449
  34.6 10.0 %collective-permute-start.9 = (bf16[4,16,128]{2,1,0:T(8,128)(2,1)S(1)}, bf16[4,16,128]{2,1,0:T(8,128)(2,1)S(1)}, u32[]{:S(2)}, u32[]{:S(2)}) collective-permute-start(bf16[4,16,128]{2,1,0:T(8,128)(2,1)S(1)} %get-tuple-element.114), channel_id=1, source_target_pairs={{0,2},{2,0},{4,6},{6,4},{8,10},{10,8},{12,14},{14,12},{16,18},{18,... | collective-permute-start | bytes 49160 | tf_op jit(solution)/shard_map/ppermute | solution.py:449
  36.1 10.8 %collective-permute-start.10 = (bf16[4,16,128]{2,1,0:T(8,128)(2,1)S(1)}, bf16[4,16,128]{2,1,0:T(8,128)(2,1)S(1)}, u32[]{:S(2)}, u32[]{:S(2)}) collective-permute-start(bf16[4,16,128]{2,1,0:T(8,128)(2,1)S(1)} %get-tuple-element.114), channel_id=1, source_target_pairs={{0,4},{2,6},{4,0},{6,2},{8,12},{10,14},{12,8},{14,10},{16,20},{18,... | collective-permute-start | bytes 49160 | tf_op jit(solution)/shard_map/ppermute | solution.py:449
  37.6 9.3 %collective-permute-start.11 = (bf16[4,16,128]{2,1,0:T(8,128)(2,1)S(1)}, bf16[4,16,128]{2,1,0:T(8,128)(2,1)S(1)}, u32[]{:S(2)}, u32[]{:S(2)}) collective-permute-start(bf16[4,16,128]{2,1,0:T(8,128)(2,1)S(1)} %get-tuple-element.114), channel_id=1, source_target_pairs={{0,6},{2,4},{4,2},{6,0},{8,14},{10,12},{12,10},{14,8},{16,22},{18,... | collective-permute-start | bytes 49160 | tf_op jit(solution)/shard_map/ppermute | solution.py:449
  38.1 8.9 %copy-start.1 = (bf16[2,1024,768]{2,1,0:T(8,128)(2,1)S(1)}, bf16[2,1024,768]{2,1,0:T(8,128)(2,1)}, u32[]{:S(2)}) copy-start(bf16[2,1024,768]{2,1,0:T(8,128)(2,1)} %param.13) | copy-start | bytes 9437188
  44.6 11.0 %collective-permute-start.5 = (bf16[4,24,1920]{2,1,0:T(8,128)(2,1)S(1)}, bf16[4,24,1920]{2,1,0:T(8,128)(2,1)S(1)}, u32[]{:S(2)}, u32[]{:S(2)}) collective-permute-start(bf16[4,24,1920]{2,1,0:T(8,128)(2,1)S(1)} %pad_maximum_fusion.3), channel_id=1, source_target_pairs={{0,6},{2,4},{4,2},{6,0},{8,14},{10,12},{12,10},{14,8},{16,22},{18,... | collective-permute-start | bytes 1105928 | tf_op jit(solution)/shard_map/ppermute | solution.py:449
  46.9 4.1 %collective-permute-start.12 = (bf16[4,4,16,128]{3,2,1,0:T(8,128)(2,1)S(1)}, bf16[4,4,16,128]{3,2,1,0:T(8,128)(2,1)S(1)}, u32[]{:S(2)}, u32[]{:S(2)}) collective-permute-start(bf16[4,4,16,128]{3,2,1,0:T(8,128)(2,1)S(1)} %get-tuple-element.112), channel_id=1, source_target_pairs={{0,1},{1,0},{2,3},{3,2},{4,5},{5,4},{6,7},{7,6},{8,9},{9,8},{10,11... | collective-permute-start | bytes 196616 | tf_op jit(solution)/shard_map/ppermute | solution.py:449
  55.6 5.6 %copy-start.6 = (f32[1,128]{1,0:T(1,128)}, f32[1,128]{1,0:T(1,128)S(1)}, u32[]{:S(2)}) copy-start(f32[1,128]{1,0:T(1,128)S(1)} %get-tuple-element.58.rate) | copy-start | bytes 1540
  55.8 3.4 %collective-permute-start.13 = (bf16[4,4,24,1920]{3,2,1,0:T(8,128)(2,1)S(1)}, bf16[4,4,24,1920]{3,2,1,0:T(8,128)(2,1)S(1)}, u32[]{:S(2)}, u32[]{:S(2)}) collective-permute-start(bf16[4,4,24,1920]{3,2,1,0:T(8,128)(2,1)S(1)} %pad_maximum_fusion.2), channel_id=1, source_target_pairs={{0,1},{1,0},{2,3},{3,2},{4,5},{5,4},{6,7},{7,6},{8,9},{9,8},{10,11... | collective-permute-start | bytes 4423688 | tf_op jit(solution)/shard_map/ppermute | solution.py:449
  159.8 78.7 %copy-start.2 = (bf16[2048,768]{1,0:T(8,128)(2,1)S(1)}, bf16[2048,768]{1,0:T(8,128)(2,1)}, u32[]{:S(2)}) copy-start(bf16[2048,768]{1,0:T(8,128)(2,1)} %get-tuple-element.62.nrm) | copy-start | bytes 9437188
  247.9 3.4 %collective-permute-start.14 = (bf16[4,4,24,1920]{3,2,1,0:T(8,128)(2,1)S(1)}, bf16[4,4,24,1920]{3,2,1,0:T(8,128)(2,1)S(1)}, u32[]{:S(2)}, u32[]{:S(2)}) collective-permute-start(bf16[4,4,24,1920]{3,2,1,0:T(8,128)(2,1)S(1)} %bitcast.136), channel_id=1, source_target_pairs={{0,1},{1,0},{2,3},{3,2},{4,5},{5,4},{6,7},{7,6},{8,9},{9,8},{10,11... | collective-permute-start | bytes 4423688 | tf_op jit(solution)/shard_map/ppermute | solution.py:449
  252.7 30.4 %collective-permute-start.15 = (bf16[4,24,1920]{2,1,0:T(8,128)(2,1)}, bf16[4,24,1920]{2,1,0:T(8,128)(2,1)S(1)}, u32[]{:S(2)}, u32[]{:S(2)}) collective-permute-start(bf16[4,24,1920]{2,1,0:T(8,128)(2,1)} %get-tuple-element.95), channel_id=1, source_target_pairs={{0,2},{2,0},{4,6},{6,4},{8,10},{10,8},{12,14},{14,12},{16,18},{18,... | collective-permute-start | bytes 1105928 | tf_op jit(solution)/shard_map/ppermute | solution.py:449
  253.3 29.9 %collective-permute-start.16 = (bf16[4,24,1920]{2,1,0:T(8,128)(2,1)}, bf16[4,24,1920]{2,1,0:T(8,128)(2,1)S(1)}, u32[]{:S(2)}, u32[]{:S(2)}) collective-permute-start(bf16[4,24,1920]{2,1,0:T(8,128)(2,1)} %get-tuple-element.97), channel_id=1, source_target_pairs={{0,4},{2,6},{4,0},{6,2},{8,12},{10,14},{12,8},{14,10},{16,20},{18,... | collective-permute-start | bytes 1105928 | tf_op jit(solution)/shard_map/ppermute | solution.py:449
  254.3 29.6 %collective-permute-start.17 = (bf16[4,24,1920]{2,1,0:T(8,128)(2,1)S(1)}, bf16[4,24,1920]{2,1,0:T(8,128)(2,1)}, u32[]{:S(2)}, u32[]{:S(2)}) collective-permute-start(bf16[4,24,1920]{2,1,0:T(8,128)(2,1)S(1)} %get-tuple-element.96), channel_id=1, source_target_pairs={{0,6},{2,4},{4,2},{6,0},{8,14},{10,12},{12,10},{14,8},{16,22},{18,... | collective-permute-start | bytes 1105928 | tf_op jit(solution)/shard_map/ppermute | solution.py:449
  283.2 0.7 copy-start.4
  285.2 14.5 %collective-permute-start.18 = (bf16[24,1920]{1,0:T(8,128)(2,1)S(1)}, bf16[24,1920]{1,0:T(8,128)(2,1)S(1)}, u32[]{:S(2)}, u32[]{:S(2)}) collective-permute-start(bf16[24,1920]{1,0:T(8,128)(2,1)S(1)} %get-tuple-element.98), channel_id=1, source_target_pairs={{0,8},{2,10},{4,12},{6,14},{8,0},{10,2},{12,4},{14,6},{16,24},{18,... | collective-permute-start | bytes 276488 | tf_op jit(solution)/shard_map/ppermute | solution.py:449
  285.8 13.9 %collective-permute-start.19 = (bf16[24,1920]{1,0:T(8,128)(2,1)S(1)}, bf16[24,1920]{1,0:T(8,128)(2,1)S(1)}, u32[]{:S(2)}, u32[]{:S(2)}) collective-permute-start(bf16[24,1920]{1,0:T(8,128)(2,1)S(1)} %get-tuple-element.100), channel_id=1, source_target_pairs={{0,16},{2,18},{4,20},{6,22},{8,24},{10,26},{12,28},{14,30},{16,0},... | collective-permute-start | bytes 276488 | tf_op jit(solution)/shard_map/ppermute | solution.py:449
  288.3 11.5 %collective-permute-start.20 = (bf16[24,1920]{1,0:T(8,128)(2,1)S(1)}, bf16[24,1920]{1,0:T(8,128)(2,1)S(1)}, u32[]{:S(2)}, u32[]{:S(2)}) collective-permute-start(bf16[24,1920]{1,0:T(8,128)(2,1)S(1)} %get-tuple-element.99), channel_id=1, source_target_pairs={{0,24},{2,26},{4,28},{6,30},{8,16},{10,18},{12,20},{14,22},{16,8},... | collective-permute-start | bytes 276488 | tf_op jit(solution)/shard_map/ppermute | solution.py:449
  289.7 13.0 %copy-start.5 = (bf16[48,768]{1,0:T(8,128)(2,1)S(1)}, bf16[48,768]{1,0:T(8,128)(2,1)}, u32[]{:S(2)}) copy-start(bf16[48,768]{1,0:T(8,128)(2,1)} %param.24) | copy-start | bytes 221188
  289.7 13.8 %copy-start.7 = (bf16[48]{0:T(256)(128)(2,1)S(1)}, bf16[48]{0:T(256)(128)(2,1)}, u32[]{:S(2)}) copy-start(bf16[48]{0:T(256)(128)(2,1)} %param.23) | copy-start | bytes 292
  289.7 15.2 %copy-start.3 = (bf16[24,3352]{1,0:T(8,128)(2,1)S(1)}, bf16[24,3352]{1,0:T(8,128)(2,1)}, u32[]{:S(2)}) copy-start(bf16[24,3352]{1,0:T(8,128)(2,1)} %param.17) | copy-start | bytes 482692
  289.7 16.1 %copy-start.8 = (bf16[24]{0:T(256)(128)(2,1)S(1)}, bf16[24]{0:T(256)(128)(2,1)}, u32[]{:S(2)}) copy-start(bf16[24]{0:T(256)(128)(2,1)} %param.16) | copy-start | bytes 148
Sparse Core Ops, SparseCore 0:
  11.5 67.6 all-gather.1
  159.9 105.8 reduce-scatter.1

commit v3 on v2

v3 whole, which is shorter than its diff:
```python
import functools

import jax
import jax.numpy as jnp
import numpy as np
from jax import lax
from jax.experimental import pallas as pl
from jax.experimental.pallas import tpu as pltpu
from jax.sharding import PartitionSpec as P

EPS = 1e-05
LOG2E = 1.4426950408889634
NEG = -1e30
f32, bf16 = jnp.float32, jnp.bfloat16
Q = 128
VM = 60 * 1024 * 1024

D, DI, CONV, N, HD = 768, 1536, 1792, 128, 64


def dot(a, b):
    return lax.dot_general(a, b, (((1,), (0,)), ((), ())), preferred_element_type=f32)


def dot_nt(a, b):
    return lax.dot_general(a, b, (((1,), (1,)), ((), ())), preferred_element_type=f32)


def dot_tn(a, b):
    return lax.dot_general(a, b, (((0,), (0,)), ((), ())), preferred_element_type=f32)


def sigmoid(v):
    return 1.0 / (1.0 + jnp.exp(-v))


def cumsum_rows(v, reverse=False):
    rows = lax.broadcasted_iota(jnp.int32, v.shape, 0)
    count = v.shape[0]
    shift = 1
    while shift < count:
        if reverse:
            moved = pltpu.roll(v, count - shift, 0)
            v = v + jnp.where(rows < count - shift, moved, 0.0)
        else:
            moved = pltpu.roll(v, shift, 0)
            v = v + jnp.where(rows >= shift, moved, 0.0)
        shift *= 2
    return v


def step_terms(z):
    e = jnp.exp(-jnp.abs(z))
    soft = jnp.maximum(z, 0.0) + jnp.log1p(e)
    tiny = z < -15.0
    log_soft = jnp.where(tiny, z, jnp.log(jnp.where(tiny, 1.0, soft)))
    return soft, log_soft


def columns(row):
    return jnp.broadcast_to(row, (Q, 128)).T


def documents(row, before_row, docs):
    doc = columns(row)
    docs[0:8, :] = columns(before_row)[Q - 8 : Q, :]
    docs[8 : 8 + Q, :] = doc
    return doc, [(docs[8 - s : 8 - s + Q, :] == doc).astype(f32) for s in (3, 2, 1)]


def scan_factors(z, rate, doc, prev_doc):
    soft, log_soft = step_terms(z)
    a = cumsum_rows(soft * (rate * LOG2E))
    b = a - log_soft * LOG2E
    last = a[Q - 1 : Q, :]
    last_doc = doc[Q - 1 : Q, :]
    reach = jnp.where(doc == prev_doc, jnp.exp2(a), 0.0)
    tail = jnp.where(doc == last_doc, jnp.exp2(last - b), 0.0)
    keep = jnp.where(last_doc == prev_doc, jnp.exp2(last), 0.0)
    return soft, a, b, reach, tail, keep


def pair_of(cols, p, low):
    left = jnp.broadcast_to(cols[:, 2 * p : 2 * p + 1], low.shape)
    right = jnp.broadcast_to(cols[:, 2 * p + 1 : 2 * p + 2], low.shape)
    return jnp.where(low, left, right)


def two_parts(cols):
    hi = cols.astype(bf16)
    return jnp.concatenate([hi, (cols - hi.astype(f32)).astype(bf16)], axis=1)


def head_onehot(shape):
    head = lax.broadcasted_iota(jnp.int32, shape, 1) >> 6
    return (lax.broadcasted_iota(jnp.int32, shape, 0) & 127 == head).astype(bf16)


def pack_kernel(ri, w_in, w_out, in_gain, cw, cb, gg, heads_in, wc_o, later_o, rows):
    wc_o[...] = jnp.zeros_like(wc_o)
    wc_o[0:ri, : w_in.shape[1] - DI] = w_in[:, DI:]
    rows[...] = jnp.zeros_like(rows)
    rows[0:1, : in_gain.shape[1]] = in_gain[...].astype(f32)
    rows[1:5, : cw.shape[1]] = cw[...].astype(f32)
    rows[5:6, : cb.shape[1]] = cb[...].astype(f32)
    rows[6:7, : gg.shape[1]] = gg[...].astype(f32)
    value = heads_in[...]
    for n in range(3):
        part = value.astype(bf16).astype(f32)
        rows[7 + 3 * n : 10 + 3 * n, : value.shape[1]] = part
        value = value - part
    wc_o[0:16, CONV + 128 :] = rows[...].astype(bf16)
    later_o[:, :DI] = w_in[:, :DI]
    later_o[:, DI : DI + D] = w_out[0:ri, :]
    later_o[:, DI + D :] = w_out[ri:, :]


def pack(w_in, w_out, in_gain, cw, cb, gg, heads_in, ri, tall):
    return pl.pallas_call(
        functools.partial(pack_kernel, ri),
        out_shape=[jax.ShapeDtypeStruct((tall, CONV + 256), bf16), jax.ShapeDtypeStruct((ri, 2 * DI), bf16)],
        scratch_shapes=[pltpu.VMEM((16, 128), f32)],
        name="pack",
    )(w_in, w_out, in_gain, cw, cb, gg, heads_in)


def unpack_small(ri, ro, share, small, device, onehot, gain, gain_abs, cw, cb, gg, heads_o, skip):
    nd = small.shape[1]
    slot = lax.broadcasted_iota(jnp.int32, (nd, 128), 0).astype(f32)[:, 0:1]
    owner = device[...][:, 0:1]

    def spread(rows, width, total, who):
        lane = lax.broadcasted_iota(jnp.int32, (128, total), 1).astype(f32)
        piece = jnp.floor((lane + 0.5) * (1.0 / width))
        inner = lane - piece * width
        pick = (lax.broadcasted_iota(jnp.int32, (128, total), 0).astype(f32) == inner).astype(bf16)
        mine = piece[0:1, :] == who
        return [jnp.sum(jnp.where(mine, dot(small[r].astype(bf16), pick), 0.0), axis=0, keepdims=True) for r in rows]

    gain[...] = spread([0], ri, D, slot)[0]
    gain_abs[...] = spread([0], ri, D, owner)[0]
    taps = spread(range(1, 6), CONV // nd, CONV, owner)
    for k in range(4):
        cw[k : k + 1, :] = 0.5 * taps[k]
    cw[4:8, :] = jnp.zeros((4, CONV), f32)
    cb[...] = 0.5 * taps[4]
    gg[...] = spread([6], ro, DI, owner)[0]
    parts = spread(range(7, 16), share, 128, owner)
    per_head = [parts[n] + parts[n + 3] + parts[n + 6] for n in range(3)]
    heads_o[0:1, :] = per_head[0]
    heads_o[1:2, :] = -jnp.exp(per_head[1])
    skip[...] = dot(two_parts(jnp.broadcast_to(per_head[2], (8, 128))), onehot[...])[0:1, :]


def forward_scan_kernel(heads, per_seq, ri, ro, share, first, tok, wc_a, wc_b, small, device, seg, seg_before,
                        cin_o, act_o, dact_o, nrm_o, scan_o, st_o, z_o, gain, gain_abs, cw, cb, gg, heads_o, skip,
                        pbuf, zbuf, nbuf, pnext, znext, nnext, state, docs, onehot, wc, sems):
    i = pl.program_id(0)
    tiles = CONV // 128

    def normed(block):
        x = block[...].astype(f32)
        r = lax.rsqrt(jnp.mean(x * x, axis=-1, keepdims=True) + EPS)
        nnext[...] = (x * r * gain[...]).astype(bf16)

    def project(t):
        part = dot(nnext[...], wc[:, 128 * t : 128 * t + 256])
        pnext[t] = part[:, :128]
        pnext[t + 1] = part[:, 128:]

    def project_step():
        znext[...] = dot(nnext[...], wc[:, CONV:]) + heads_o[0:1, :]

    def advance():
        pbuf[:, 8 : 8 + Q, :] = pnext[...]
        zbuf[...] = znext[...]
        nbuf[...] = nnext[...]

    @pl.when(i == 0)
    def _():
        rows = wc_a.shape[0]
        copies = [pltpu.make_async_copy(wc_a.at[:, : CONV + 128], wc.at[0:rows], sems.at[0]),
                  pltpu.make_async_copy(wc_b.at[:, : CONV + 128], wc.at[rows : 2 * rows], sems.at[1])]
        for copy in copies:
            copy.start()
        onehot[...] = head_onehot(onehot.shape)
        unpack_small(ri, ro, share, small, device, onehot, gain, gain_abs, cw, cb, gg, heads_o, skip)
        normed(first)
        for copy in copies:
            copy.wait()
        for t in range(0, tiles, 2):
            project(t)
        project_step()
        advance()

    @pl.when(lax.rem(i, per_seq) == 0)
    def _():
        pbuf[:, 0:8, :] = jnp.zeros((tiles, 8, 128), f32)
        state[...] = jnp.zeros_like(state)

    nrm_o[...] = nbuf[...]
    z = zbuf[...]
    z_o[...] = z
    doc_row = seg[0].astype(f32)
    before_row = jnp.where(lax.rem(i, per_seq) == 0, -1.0, seg_before[0].astype(f32))
    doc, masks = documents(doc_row, before_row, docs)
    prev = docs[7:8, :]
    soft, a, b, reach, tail, keep = scan_factors(z, heads_o[1:2, :], doc, prev)
    factors = two_parts(jnp.concatenate([reach, tail, jnp.broadcast_to(keep, (8, 128))], axis=0))
    bt = b.T
    row = lax.broadcasted_iota(jnp.int32, (Q, Q), 0)
    lane = lax.broadcasted_iota(jnp.int32, (Q, Q), 1)
    joined = (row >= lane) & (doc == doc_row)
    low = lane < HD
    zero = jnp.zeros((Q, Q), bf16)

    def conv(t):
        cols = slice(128 * t, 128 * t + 128)
        here = pbuf[t, 8 : 8 + Q, :]
        cin_o[:, cols] = here.astype(bf16)
        half = cb[:, cols] + cw[3:4, cols] * here
        for k in range(3):
            half = half + cw[k : k + 1, cols] * (pbuf[t, 5 + k : 5 + k + Q, :] * masks[k])
        pbuf[t, 0:8, :] = pbuf[t, Q : Q + 8, :]
        th = jnp.tanh(half)
        dact_o[:, cols] = ((1.0 + th) * (1.0 + half * (1.0 - th))).astype(bf16)
        act = (half + half * th).astype(bf16)
        act_o[:, cols] = act
        return act

    normed(tok)
    bmat = conv(tiles - 2)
    cmat = conv(tiles - 1)
    bt_mat = bmat.astype(f32).T.astype(bf16)
    s = dot_nt(cmat, bmat)
    for p in range(heads // 2):
        cols = slice(128 * p, 128 * p + 128)
        half = slice(128 * (p % 2), 128 * (p % 2) + 128)
        if p % 2 == 0:
            group = slice(128 * p, 128 * p + 256)
            wide = dot(factors, onehot[:, group])
            st_low = state[:, group].astype(bf16)
            st_o[0, :, group] = st_low
            cs = dot(cmat, st_low)
        xp = conv(p)
        if p < tiles // 2:
            project(2 * p)
        if p == tiles // 2:
            project_step()
        parts = []
        for h in (2 * p, 2 * p + 1):
            spread = jnp.broadcast_to(a[:, h : h + 1], (Q, Q)) - bt[h : h + 1, :]
            parts.append((jnp.exp2(jnp.where(joined, spread, NEG)) * s).astype(bf16))
        xbd = jnp.concatenate([jnp.where(low, xp, zero), jnp.where(low, zero, xp)], axis=0)
        y = dot(jnp.concatenate(parts, axis=1), xbd)
        xf = xp.astype(f32)
        y = y + cs[:, half] * wide[0:Q, half] + xf * skip[:, cols]
        scan_o[:, cols] = y.astype(bf16)
        xw = (xf * wide[Q : 2 * Q, half]).astype(bf16)
        state[:, cols] = state[:, cols] * wide[2 * Q : 2 * Q + 1, half] + dot(bt_mat, xw)
    advance()


def forward_scan(tok, wc_a, wc_b, small, device, seg, seqs, ri, ro, share, heads):
    rows = tok.shape[0]
    n = rows // Q
    one = pl.Buffered(buffer_count=1)
    full = lambda arr: pl.BlockSpec(arr.shape, lambda i: (0,) * arr.ndim, pipeline_mode=one)
    blk = lambda w: pl.BlockSpec((Q, w), lambda i: (i, 0))
    hbm = pl.BlockSpec(memory_space=pl.ANY)
    low = lambda *shape: jax.ShapeDtypeStruct(shape, bf16)
    sides = [(1, D), (1, D), (8, CONV), (1, CONV), (1, DI), (8, 128), (1, DI)]
    side = lambda shape: pl.BlockSpec(shape, lambda i: (0, 0))
    return pl.pallas_call(
        functools.partial(forward_scan_kernel, heads, n // seqs, ri, ro, share),
        grid=(n,),
        in_specs=[pl.BlockSpec((Q, D), lambda i: (0, 0), pipeline_mode=one),
                  pl.BlockSpec((Q, D), lambda i: (jnp.minimum(i + 1, n - 1), 0)), hbm, hbm, full(small), full(device),
                  pl.BlockSpec((1, 1, Q), lambda i: (i, 0, 0)), pl.BlockSpec((1, 1, Q), lambda i: (jnp.maximum(i - 1, 0), 0, 0))],
        out_specs=[blk(CONV), blk(CONV), blk(CONV), blk(D), blk(DI), pl.BlockSpec((1, N, DI), lambda i: (i, 0, 0)), blk(128)]
        + [side(shape) for shape in sides],
        out_shape=[low(rows, CONV), low(rows, CONV), low(rows, CONV), low(rows, D), low(rows, DI), low(n, N, DI),
                   jax.ShapeDtypeStruct((rows, 128), f32)] + [jax.ShapeDtypeStruct(shape, f32) for shape in sides],
        scratch_shapes=[pltpu.VMEM((CONV // 128, Q + 8, 128), f32), pltpu.VMEM((Q, 128), f32), pltpu.VMEM((Q, D), bf16),
                        pltpu.VMEM((CONV // 128, Q, 128), f32), pltpu.VMEM((Q, 128), f32), pltpu.VMEM((Q, D), bf16),
                        pltpu.VMEM((N, DI), f32), pltpu.VMEM((Q + 8, 128), f32), pltpu.VMEM((256, DI), bf16),
                        pltpu.VMEM((D, CONV + 128), bf16), pltpu.SemaphoreType.DMA((2,))],
        compiler_params=pltpu.CompilerParams(vmem_limit_bytes=VM),
        name="forward_scan",
    )(tok, tok, wc_a, wc_b, small, device, seg, seg)


def block_order(ri):
    row = lax.broadcasted_iota(jnp.int32, (192, 192), 0)
    lane = lax.broadcasted_iota(jnp.int32, (192, 192), 1)
    second = lane >= 96
    at = jnp.where(second, lane - 96, lane)
    owner = lax.div(at, ri)
    target = owner * (2 * ri) + (at - owner * ri) + jnp.where(second, ri, 0)
    return (row == target).astype(bf16)


def gate_kernel(ri, tok, scan, cot, later, gain, gg, mixed_o, dscan_o, dgate_o, early_o, wo, acc_g, acc_o,
                nb_s, nbt_s, mixt_s, h_s, e_s, gated_s, eg_s):
    i = pl.program_id(0)
    bm, high = 256, 32
    blocks = tok.shape[0] // bm

    @pl.when(i == 0)
    def _():
        acc_g[...] = jnp.zeros_like(acc_g)
        acc_o[...] = jnp.zeros_like(acc_o)
        put = block_order(ri)
        for g in range(D // 96):
            at = slice(96 * g, 96 * g + 96)
            halves = jnp.concatenate([later[at, DI : DI + D], later[at, DI + D :]], axis=0)
            wo[192 * g : 192 * g + 192, :] = dot(put, halves).astype(bf16)

    x = tok[...].astype(f32)
    r = lax.rsqrt(jnp.mean(x * x, axis=-1, keepdims=True) + EPS)
    nb = (x * r * gain[...]).astype(bf16)
    nb_s[...] = nb * 0.5
    nbt_s[...] = nb.T

    def products(n):
        rows = slice(bm * n, bm * n + bm)
        for c in range(DI // 256):
            cols = slice(256 * c, 256 * c + 256)
            h_s[rows, cols] = dot(nb_s[rows, :], later[:, cols])
            yield
            e_s[rows, cols] = dot_nt(cot[rows, :], wo[cols, :])
            yield

    def sums(n):
        rows = slice(bm * n, bm * n + bm)
        for c in range(DI // 256):
            cols = slice(256 * c, 256 * c + 256)
            mixt_s[cols, :] = mixed_o[rows, cols].T
        for c in range(D // 256):
            cols = slice(256 * c, 256 * c + 256)
            acc_o[:, cols] += dot(mixt_s[...], cot[rows, cols])
            yield
        for c in range(DI // 256):
            cols = slice(256 * c, 256 * c + 256)
            acc_g[:, cols] += dot(nbt_s[:, rows], dgate_o[rows, cols])
            yield

    def elementwise(n, part):
        rows = slice(bm * n + part * high, bm * n + part * high + high)
        squares = jnp.zeros((high, 128), f32)
        cross = jnp.zeros((high, 128), f32)
        for t in range(DI // 128):
            cols = slice(128 * t, 128 * t + 128)
            h = h_s[rows, cols]
            gated = scan[rows, cols].astype(f32) * (h + h * jnp.tanh(h))
            eg = e_s[rows, cols] * gg[:, cols]
            squares = squares + gated * gated
            cross = cross + gated * eg
            gated_s[part, :, cols] = gated
            eg_s[part, :, cols] = eg
        rr = lax.rsqrt(jnp.sum(squares, axis=-1, keepdims=True) * (1.0 / DI) + EPS)
        pull = rr * rr * rr * (jnp.sum(cross, axis=-1, keepdims=True) * (1.0 / DI))
        rr = jnp.broadcast_to(rr, (high, 128))
        pull = jnp.broadcast_to(pull, (high, 128))
        yield
        for t in range(DI // 128):
            cols = slice(128 * t, 128 * t + 128)
            h = h_s[rows, cols]
            th = jnp.tanh(h)
            gated = gated_s[part, :, cols]
            mixed_o[rows, cols] = (gated * rr * gg[:, cols]).astype(bf16)
            dg = eg_s[part, :, cols] * rr - gated * pull
            act = h + h * th
            dscan_o[rows, cols] = (dg * act).astype(bf16)
            dg = dg * scan[rows, cols].astype(f32)
            dgate_o[rows, cols] = (dg * ((1.0 + th) + act * (1.0 - th))).astype(bf16)
        yield

    def both(n, matrix):
        vector = [step for part in range(bm // high) for step in [elementwise(n, part)] * 2]
        for step in vector:
            next(step)
            next(matrix, None)
        for _ in matrix:
            pass

    for _ in products(0):
        pass
    for n in range(blocks):
        both(n, products(n + 1) if n + 1 < blocks else sums(n - 1))
    for _ in sums(blocks - 1):
        pass

    @pl.when(i == pl.num_programs(0) - 1)
    def _():
        early_o[:, :DI] = (0.5 * acc_g[...]).astype(bf16)
        put = block_order(ri)
        for g in range(D // 96):
            at = slice(96 * g, 96 * g + 96)
            halves = dot_tn(put, acc_o[192 * g : 192 * g + 192, :].astype(bf16)).astype(bf16)
            early_o[at, DI : DI + D] = halves[:96]
            early_o[at, DI + D :] = halves[96:]


def gate_pass(tok, scan, cot, later, gain, gg, ri, bm=512):
    rows = tok.shape[0]
    one = pl.Buffered(buffer_count=1)
    full = lambda shape: pl.BlockSpec(shape, lambda i: (0,) * len(shape), pipeline_mode=one)
    blk = lambda w: pl.BlockSpec((bm, w), lambda i: (i, 0))
    low = lambda *shape: jax.ShapeDtypeStruct(shape, bf16)
    return pl.pallas_call(
        functools.partial(gate_kernel, ri),
        grid=(rows // bm,),
        in_specs=[blk(D), blk(DI), blk(D), full(later.shape), full(gain.shape), full(gg.shape)],
        out_specs=[blk(DI), blk(DI), blk(DI), full((D, 2 * DI)), full((DI, D))],
        out_shape=[low(rows, DI), low(rows, DI), low(rows, DI), low(D, 2 * DI), low(DI, D)],
        scratch_shapes=[pltpu.VMEM((D, DI), f32), pltpu.VMEM((DI, D), f32), pltpu.VMEM((bm, D), bf16), pltpu.VMEM((D, bm), bf16),
                        pltpu.VMEM((DI, 256), bf16),
                        pltpu.VMEM((bm, DI), f32), pltpu.VMEM((bm, DI), f32), pltpu.VMEM((8, 32, DI), f32),
                        pltpu.VMEM((8, 32, DI), f32)],
        compiler_params=pltpu.CompilerParams(vmem_limit_bytes=VM),
        name="gate_pass",
    )(tok, scan, cot, later, gain, gg)


def out_kernel(mixed, tok, wo, out_o):
    out_o[...] = (tok[...].astype(f32) + dot(mixed[...], wo[...])).astype(bf16)


def out_pass(mixed, tok, wo, bm=512):
    rows = tok.shape[0]
    blk = lambda w: pl.BlockSpec((bm, w), lambda i: (i, 0))
    return pl.pallas_call(
        out_kernel,
        grid=(rows // bm,),
        in_specs=[blk(DI), blk(D), pl.BlockSpec((DI, D), lambda i: (0, 0), pipeline_mode=pl.Buffered(buffer_count=1))],
        out_specs=blk(D),
        out_shape=jax.ShapeDtypeStruct((rows, D), bf16),
        compiler_params=pltpu.CompilerParams(vmem_limit_bytes=VM),
        cost_estimate=pl.CostEstimate(flops=0, bytes_accessed=0, transcendentals=0),
        name="out_pass",
    )(mixed, tok, wo)


def backward_scan_kernel(heads, per_seq, dscan, cin, act, dact, z_r, st, cw, head_terms, skip, seg, seg_before,
                         dproj_o, gcw_o, gcb_o, gsk_o, ghd_o,
                         dstate, p1buf, qbuf, xwbuf, rowbuf, lastbuf, mbuf, onehot, sums, docs):
    i = pl.program_id(0)

    @pl.when(i == 0)
    def _():
        gcw_o[...] = jnp.zeros_like(gcw_o)
        gcb_o[...] = jnp.zeros_like(gcb_o)
        gsk_o[...] = jnp.zeros_like(gsk_o)
        ghd_o[...] = jnp.zeros_like(ghd_o)
        rowbuf[...] = jnp.zeros_like(rowbuf)
        lastbuf[...] = jnp.zeros_like(lastbuf)
        onehot[...] = head_onehot(onehot.shape)
        head = lax.broadcasted_iota(jnp.int32, sums.shape, 0) >> 6
        sums[...] = (head == lax.broadcasted_iota(jnp.int32, sums.shape, 1)).astype(bf16)

    @pl.when(lax.rem(i, per_seq) == 0)
    def _():
        mbuf[:, :, Q : Q + 8, :] = jnp.zeros((3, CONV // 128, 8, 128), f32)
        dstate[...] = jnp.zeros_like(dstate)

    z = z_r[...]
    rate = head_terms[1:2, :]
    doc_row = seg[0].astype(f32)
    before_row = jnp.where(lax.rem(i, per_seq) == per_seq - 1, -1.0, seg_before[0].astype(f32))
    doc, masks = documents(doc_row, before_row, docs)
    prev = docs[7:8, :]
    soft, a, b, reach, tail, keep = scan_factors(z, rate, doc, prev)
    factors = two_parts(jnp.concatenate([reach, tail, jnp.broadcast_to(keep, (8, 128))], axis=0))
    at = a.T
    row = lax.broadcasted_iota(jnp.int32, (Q, Q), 0)
    lane = lax.broadcasted_iota(jnp.int32, (Q, Q), 1)
    joined = (lane >= row) & (doc == doc_row)
    low = lane < HD
    bmat = act[:, DI : DI + N]
    cmat = act[:, DI + N :]
    ct_mat = cmat.astype(f32).T.astype(bf16)
    s = dot_nt(bmat, cmat)
    ds_low = dstate[...].astype(bf16)
    zero = jnp.zeros((Q, Q), bf16)
    dst = jnp.zeros((Q, Q), f32)

    def conv_back(t, grad):
        cols = slice(128 * t, 128 * t + 128)
        dpre = grad * dact[:, cols].astype(f32)
        for k in range(3):
            mbuf[k, t, 0:Q, :] = dpre * masks[k]
        cv = cin[:, cols].astype(f32)
        dcin = cw[3:4, cols] * dpre
        gcb_o[:, cols] += jnp.sum(dpre.reshape(-1, 8, 128), axis=0)
        gcw_o[24:32, cols] += jnp.sum((cv * dpre).reshape(-1, 8, 128), axis=0)
        for k in range(3):
            moved = mbuf[k, t, 3 - k : 3 - k + Q, :]
            dcin = dcin + cw[k : k + 1, cols] * moved
            gcw_o[8 * k : 8 * k + 8, cols] += jnp.sum((cv * moved).reshape(-1, 8, 128), axis=0)
        dproj_o[:, cols] = dcin.astype(bf16)
        mbuf[:, t, Q : Q + 8, :] = mbuf[:, t, 0:8, :]

    for p in range(heads // 2):
        cols = slice(128 * p, 128 * p + 128)
        half = slice(128 * (p % 2), 128 * (p % 2) + 128)
        if p % 2 == 0:
            group = slice(128 * p, 128 * p + 256)
            wide = dot(factors, onehot[:, group])
            cs = dot(cmat, st[0, :, group])
            bd = dot(bmat, ds_low[:, group])
        xp = act[:, cols]
        dy = dscan[:, cols]
        dybd = jnp.concatenate([jnp.where(low, dy, zero), jnp.where(low, zero, dy)], axis=0)
        dm = dot_nt(xp, dybd)
        parts = []
        for n, h in enumerate((2 * p, 2 * p + 1)):
            spread = at[h : h + 1, :] - jnp.broadcast_to(b[:, h : h + 1], (Q, Q))
            e = jnp.exp2(jnp.where(joined, spread, NEG))
            m = (e * s).astype(bf16)
            parts.append(m)
            dmh = dm[:, 128 * n : 128 * n + 128]
            dst = dst + dmh * e
            rowbuf[h : h + 1, :] = jnp.sum(dmh * m.astype(f32), axis=0, keepdims=True)
        xf = xp.astype(f32)
        dyf = dy.astype(f32)
        tail_p = wide[Q : 2 * Q, half]
        fresh = bd[:, half] * tail_p
        dx = dot(jnp.concatenate(parts, axis=1), dybd) + fresh
        p1 = xf * dx
        hi = p1.astype(bf16)
        p1buf[:, cols] = hi
        p1buf[:, DI + 128 * p : DI + 128 * p + 128] = (p1 - hi.astype(f32)).astype(bf16)
        dyr = dyf * wide[0:Q, half]
        qbuf[:, cols] = (dyr * cs[:, half]).astype(bf16)
        dyr = dyr.astype(bf16)
        ds = dstate[:, cols]
        lastbuf[0:1, cols] = jnp.sum(xf * fresh, axis=0, keepdims=True) + wide[2 * Q : 2 * Q + 1, half] * jnp.sum(
            ds * st[0, :, cols].astype(f32), axis=0, keepdims=True)
        gsk_o[:, cols] += jnp.sum((dyf * xf).reshape(-1, 8, 128), axis=0)
        xwbuf[:, cols] = (xf * tail_p).astype(bf16)
        xwbuf[:, DI + 128 * p : DI + 128 * p + 128] = dyr
        dstate[:, cols] = ds * wide[2 * Q : 2 * Q + 1, half] + dot(ct_mat, dyr)
        conv_back(p, dx + skip[:, cols] * dyf)
    dst_low = dst.astype(bf16)
    conv_back(DI // 128, dot(dst_low, cmat) + dot_nt(xwbuf[:, :DI], ds_low))
    conv_back(DI // 128 + 1, dot_tn(dst_low, bmat) + dot_nt(xwbuf[:, DI:], st[0]))
    hot = sums[...]
    p1 = dot(p1buf[:, :DI], hot) + dot(p1buf[:, DI:], hot)
    last = two_parts(lastbuf[...])
    last = (dot(last[:, :DI], hot) + dot(last[:, DI:], hot))[0:1, :]
    da = dot(qbuf[...], hot) - p1 + rowbuf[...].T
    g = cumsum_rows(da, reverse=True) + last
    sig = sigmoid(z)
    ratio = jnp.where(z < -15.0, 1.0, sig / jnp.where(z < -15.0, 1.0, soft))
    dz = g * rate * sig + p1 * ratio
    dproj_o[:, CONV:] = dz.astype(bf16)
    ghd_o[0:8, :] += jnp.sum(dz.reshape(-1, 8, 128), axis=0)
    ghd_o[8:16, :] += rate * jnp.sum((g * soft).reshape(-1, 8, 128), axis=0)


def backward_scan(dscan, cin, act, dact, z, st, cw, head_terms, skip, seg, heads, seqs):
    rows = dscan.shape[0]
    n = rows // Q
    one = pl.Buffered(buffer_count=1)
    full = lambda shape: pl.BlockSpec(shape, lambda i: (0,) * len(shape), pipeline_mode=one)
    blk = lambda w: pl.BlockSpec((Q, w), lambda i: (n - 1 - i, 0))
    blk3 = lambda s1, s2: pl.BlockSpec((1, s1, s2), lambda i: (n - 1 - i, 0, 0))
    return pl.pallas_call(
        functools.partial(backward_scan_kernel, heads, n // seqs),
        grid=(n,),
        in_specs=[blk(DI), blk(CONV), blk(CONV), blk(CONV), blk(128), blk3(N, DI), full(cw.shape), full(head_terms.shape),
                  full(skip.shape), blk3(1, Q), pl.BlockSpec((1, 1, Q), lambda i: (jnp.maximum(n - 2 - i, 0), 0, 0))],
        out_specs=[blk(CONV + 128), full((32, CONV)), full((8, CONV)), full((8, DI)), full((16, 128))],
        out_shape=[jax.ShapeDtypeStruct((rows, CONV + 128), bf16), jax.ShapeDtypeStruct((32, CONV), f32),
                   jax.ShapeDtypeStruct((8, CONV), f32), jax.ShapeDtypeStruct((8, DI), f32),
                   jax.ShapeDtypeStruct((16, 128), f32)],
        scratch_shapes=[pltpu.VMEM((N, DI), f32), pltpu.VMEM((Q, 2 * DI), bf16), pltpu.VMEM((Q, DI), bf16),
                        pltpu.VMEM((Q, 2 * DI), bf16), pltpu.VMEM((128, 128), f32), pltpu.VMEM((8, DI), f32),
                        pltpu.VMEM((3, CONV // 128, Q + 8, 128), f32), pltpu.VMEM((256, DI), bf16),
                        pltpu.VMEM((DI, 128), bf16), pltpu.VMEM((Q + 8, 128), f32)],
        compiler_params=pltpu.CompilerParams(vmem_limit_bytes=VM),
        cost_estimate=pl.CostEstimate(flops=0, bytes_accessed=0, transcendentals=0),
        name="backward_scan",
    )(dscan, cin, act, dact, z, st, cw, head_terms, skip, seg, seg)


def norm_back_kernel(dproj, dgate, tok, cot, wc_a, wc_b, wg_abs, gain, order, out_o, wc, wg, sems):
    @pl.when(pl.program_id(0) == 0)
    def _():
        rows = wc_a.shape[0]
        copies = [pltpu.make_async_copy(wc_a.at[:, : CONV + 128], wc.at[0:rows], sems.at[0]),
                  pltpu.make_async_copy(wc_b.at[:, : CONV + 128], wc.at[rows : 2 * rows], sems.at[1])]
        for copy in copies:
            copy.start()
        wg[...] = (0.5 * dot_tn(order[...], wg_abs[...])).astype(bf16)
        for copy in copies:
            copy.wait()

    grad = dot_nt(dgate[...], wg[...]) + dot_nt(dproj[...], wc[...])
    x = tok[...].astype(f32)
    r = lax.rsqrt(jnp.mean(x * x, axis=-1, keepdims=True) + EPS)
    unit = x * r
    e = gain[...] * grad
    back = r * (e - unit * jnp.mean(unit * e, axis=-1, keepdims=True))
    res = (cot[...].astype(f32) + back).astype(bf16)
    out_o[...] = dot_nt(res, order[...]).astype(bf16)


def norm_back(dproj, dgate, tok, cot, wc_a, wc_b, later, gain, order, start, count, into=None, bm=512):
    rows = dproj.shape[0]
    one = pl.Buffered(buffer_count=1)
    full = lambda shape: pl.BlockSpec(shape, lambda i: (0,) * len(shape), pipeline_mode=one)
    blk = lambda w: pl.BlockSpec((bm, w), lambda i: (start + i, 0))
    hbm = pl.BlockSpec(memory_space=pl.ANY)
    given = [] if into is None else [into]
    kernel = norm_back_kernel if into is None else lambda *refs: norm_back_kernel(*refs[:9], *refs[10:])
    return pl.pallas_call(
        kernel,
        grid=(count,),
        in_specs=[blk(CONV + 128), blk(DI), blk(D), blk(D), hbm, hbm, full((D, DI)), full(gain.shape), full(order.shape)]
        + [hbm] * len(given),
        out_specs=blk(D),
        out_shape=jax.ShapeDtypeStruct((rows, D), bf16),
        input_output_aliases={9: 0} if given else {},
        scratch_shapes=[pltpu.VMEM((D, CONV + 128), bf16), pltpu.VMEM((D, DI), bf16), pltpu.SemaphoreType.DMA((2,))],
        compiler_params=pltpu.CompilerParams(vmem_limit_bytes=VM),
        cost_estimate=pl.CostEstimate(flops=0, bytes_accessed=0, transcendentals=0),
        name="norm_back",
    )(dproj, dgate, tok, cot, wc_a, wc_b, later, gain, order, *given)


def conv_weight_kernel(nrm, dproj, small, out_o):
    grad = lax.dot_general(dproj[...], nrm[...], (((0,), (0,)), ((), ())), preferred_element_type=f32)
    out_o[...] = grad.astype(bf16).T

    @pl.when(pl.program_id(0) == pl.num_programs(0) - 1)
    def _():
        out_o[:, out_o.shape[1] - 128 :] = (grad[out_o.shape[1] - 128 :].T + small[...].astype(f32)).astype(bf16)


def conv_weight_grad(nrm, dproj, small, bn=640):
    rows = nrm.shape[0]
    one = pl.Buffered(buffer_count=1)
    return pl.pallas_call(
        conv_weight_kernel,
        grid=((CONV + 128) // bn,),
        in_specs=[pl.BlockSpec((rows, D), lambda i: (0, 0), pipeline_mode=one), pl.BlockSpec((rows, bn), lambda i: (0, i)),
                  pl.BlockSpec((D, 128), lambda i: (0, 0), pipeline_mode=one)],
        out_specs=pl.BlockSpec((D, bn), lambda i: (0, i)),
        out_shape=jax.ShapeDtypeStruct((D, CONV + 128), bf16),
        compiler_params=pltpu.CompilerParams(vmem_limit_bytes=VM),
        cost_estimate=pl.CostEstimate(flops=0, bytes_accessed=0, transcendentals=0),
        name="conv_weight_grad",
    )(nrm, dproj, small)


def stages_of(mesh):
    ndp, nf = mesh.shape["dp"], mesh.shape["fsdp"]
    out = []
    stride = 1
    while stride < nf:
        group = 2 if stride == 1 else min(4, nf // stride)
        out.append(("fsdp", stride, group, stride))
        stride *= group
    stride = 1
    while stride < ndp:
        group = min(4, ndp // stride)
        out.append(("dp", stride, group, stride * nf))
        stride *= group
    return out[::-1]


def pairs_of(stages):
    out = []
    for axis, stride, group, number in stages[::-1]:
        step = 1
        while step < group:
            out.append((axis, stride * step, 2, number * step))
            step *= 2
    return out


def slot_devices(stages):
    rel = np.zeros((1,), np.int32)
    for _, _, group, number in stages:
        rel = (np.arange(group, dtype=np.int32)[:, None] * number + rel[None, :]).reshape(-1)
    return jnp.asarray(rel)


def swap(arr, axis, size, offset):
    return lax.ppermute(arr, axis, [(i, i ^ offset) for i in range(size)])


def gather_stage(block, stage, sizes):
    axis, stride, group, _ = stage
    return jnp.stack([block] + [swap(block, axis, sizes[axis], k * stride) for k in range(1, group)])


def scatter_stage(kept, stage, sizes):
    axis, stride, group, _ = stage
    low = kept.astype(bf16)
    got = [swap(low[k], axis, sizes[axis], k * stride) for k in range(1, group)]
    total = kept[0].astype(f32)
    for part in got:
        total = total + part.astype(f32)
    return total


def before(value, *others):
    return lax.optimization_barrier((value,) + others)


def local(mesh, tokens, cotangent, segments, in_gain, weight_in, conv_weight, conv_bias, step_bias, decay_log, skip_gain,
          gate_gain, weight_out):
    sizes = {"dp": mesh.shape["dp"], "fsdp": mesh.shape["fsdp"]}
    nf = sizes["fsdp"]
    nd = sizes["dp"] * nf
    axes = ("dp", "fsdp")
    stages = stages_of(mesh)
    me = lax.axis_index("dp") * nf + lax.axis_index("fsdp")
    seqs, length, _ = tokens.shape
    rows = seqs * length
    ri, ro, cc, share = weight_in.shape[0], weight_out.shape[0], conv_bias.shape[0], step_bias.shape[0]
    heads = share * nf
    free = 128 - heads

    device = slot_devices(stages) ^ me
    feature = (device[:, None] * ri + jnp.arange(ri)[None, :]).reshape(-1)
    order = (jnp.arange(D)[:, None] == feature[None, :]).astype(bf16)
    slot_hot = (device[:, None] == jnp.arange(nd)[None, :]).astype(bf16)

    tall = max(ri, 16)
    wc, later = pack(weight_in, weight_out, in_gain[None], conv_weight, conv_bias[None], gate_gain[None],
                     jnp.stack([step_bias, decay_log, skip_gain]), ri, tall)
    later = lax.all_gather(later, axes, axis=0, tiled=True)
    tok = tokens.reshape(rows, D)
    up = cotangent.reshape(rows, D)
    seg = segments.reshape(rows // Q, 1, Q)
    wc = gather_stage(wc, stages[0], sizes)
    tok_s = jnp.dot(tok, order, preferred_element_type=bf16)
    wc, tok_s = before(wc, tok_s)
    for stage in stages[1:-1]:
        wc = gather_stage(wc, stage, sizes)
    up_s = jnp.dot(up, order, preferred_element_type=bf16)
    wc, up_s = before(wc, up_s)
    wc_b = swap(wc, stages[-1][0], sizes[stages[-1][0]], stages[-1][1])
    halves = [part.reshape(nd // 2, tall, CONV + 256) for part in (wc, wc_b)]
    small = jnp.concatenate([part[:, :16, CONV + 128 :] for part in halves], axis=0).transpose(1, 0, 2).astype(f32)
    wc_a, wc_b = [part[:, :ri].reshape(D // 2, CONV + 256) for part in halves]
    device_rows = jnp.broadcast_to(device.astype(f32)[:, None], (nd, 128))

    cin, act, dact, nrm, scan, st, z, gain, gain_abs, cw, cb, gg, head_terms, skip = forward_scan(
        tok_s, wc_a, wc_b, small, device_rows, seg, seqs, ri, ro, share, heads)
    mixed, dscan, dgate, early, wo = gate_pass(tok, scan, up, later, gain_abs, gg, ri)
    early = lax.psum_scatter(early, axes, scatter_dimension=0, tiled=True)

    dproj, gcw, gcb, gsk, ghd = backward_scan(
        dscan, cin, act, dact, z, st, cw, head_terms, skip, seg, heads, seqs)
    taps = 0.5 * jnp.concatenate([gcw.reshape(4, 8, CONV).sum(1), gcb.sum(0)[None]], axis=0)
    taps = taps.reshape(5, nd, cc).transpose(1, 0, 2).reshape(nd, 5 * cc)
    sums = jnp.stack([ghd[:8].sum(0)[:heads], ghd[8:16].sum(0)[:heads],
                            gsk.sum(0).reshape(heads, HD).sum(1)])
    sums = jnp.tile(sums.reshape(3, nf, share).transpose(1, 0, 2).reshape(nf, 3 * share), (nd // nf, 1))
    terms = jnp.concatenate([taps, sums], axis=1)
    hi = lax.reduce_precision(terms, 8, 7)
    both = jnp.concatenate([hi, terms - hi], axis=1).astype(bf16)
    both = jnp.dot(slot_hot, both, preferred_element_type=f32).astype(bf16)
    width = 5 * cc + 3 * share
    both = jnp.pad(both, ((0, 0), (0, ri * free - 2 * width))).reshape(D, free)
    gwc = conv_weight_grad(nrm, dproj, jnp.pad(both, ((0, 0), (heads, 0))))
    total = gwc.reshape([g for _, _, g, _ in stages[::-1]] + [ri, CONV + 128])
    for at, stage in enumerate(stages[::-1]):
        if at == len(stages) - 2:
            total, gain = before(total, gain)
            gtok = norm_back(dproj, dgate, tok_s, up_s, wc_a, wc_b, later, gain, order, 0, 4)
        if at == len(stages) - 1:
            total, gtok, wo, early = before(total, gtok, wo, early)
        total = scatter_stage(total, stage, sizes)
    out = out_pass(mixed, tok, wo)

    early = early.astype(f32)
    g_in = jnp.concatenate([early[:, :DI], total[:, : CONV + heads]], axis=1)
    g_out = jnp.concatenate([early[:, DI : DI + D], early[:, DI + D :]], axis=0)
    packed = total[:, CONV + heads :].reshape(-1)
    packed = packed[:width] + packed[width : 2 * width]
    g_in_gain = jnp.sum(weight_in.astype(f32) * g_in, axis=1) / in_gain.astype(f32)
    g_gate_gain = jnp.sum(weight_out.astype(f32) * g_out, axis=1) / gate_gain.astype(f32)
    by_head = packed[5 * cc :].reshape(3, share)
    return (out.reshape(tokens.shape), gtok.reshape(tokens.shape), g_in_gain, g_in, packed[: 4 * cc].reshape(4, cc),
            packed[4 * cc : 5 * cc], by_head[0], by_head[1], by_head[2], g_gate_gain, g_out)


def solution(mesh):
    every = ("dp", "fsdp")
    return jax.shard_map(
        functools.partial(local, mesh),
        mesh=mesh,
        in_specs=(P(every, None, None), P(every, None, None), P(every, None), P(every), P(every, None), P(None, every),
                  P(every), P("fsdp"), P("fsdp"), P("fsdp"), P(every), P(every, None)),
        out_specs=(P(every, None, None), P(every, None, None), P(every), P(every, None), P(None, every), P(every),
                   P("fsdp"), P("fsdp"), P("fsdp"), P(every), P(every, None)),
        check_vma=False,
    )
```

time: 314 us -> 280 us (0.89)
  Pallas kernels: 209 us -> 192 us
  waiting for transfers between devices: 8.21 us -> 21.6 us
  starting transfers between devices: 28 us -> 17.7 us
  matrix products: 20 us -> 10.7 us
  local copies, waits for them, and re-layouts: 19.2 us -> 10 us
    ppermute x21 -> x14, waiting for transfers between devices: 8.16 us -> 21.5 us  [swap(): return lax.ppermute(arr, axis, [(i, i ^ offset) for i in range(size)])]
    pallas_call x1, Pallas kernels: 73.8 us -> 60.6 us  [backward_scan(): pl.pallas_call(functools.partial(backward_scan_kernel, heads, n // seqs),...]
    ppermute x21 -> x14, starting transfers between devices: 27.9 us -> 17.6 us  [swap(): return lax.ppermute(arr, axis, [(i, i ^ offset) for i in range(size)])]
    dot_general x2 -> x0, matrix products: 9.34 us -> none  [the longest x1 9.18 us: local(): lax.dot_general(nrm, dproj, (((0,), (0,)), ((), ())), preferred_element_t...]
    pallas_call x1, Pallas kernels: 45.2 us -> 38.6 us  [gate_pass(): pl.pallas_call(functools.partial(gate_kernel, ri), grid=(rows // bm,), in...]
    pallas_call x2 -> x4, Pallas kernels: 80.2 us -> 82.6 us  [the longest x1 42.3 us: forward_scan(): pl.pallas_call(functools.partial(forward_scan_kernel, heads, n // seqs, r...]
  transfers between devices with their start and end apart: 23 -> 16, of which waited for: 4 -> 6; matrix products, arithmetic and copies ran while one was open for 15% -> 10% of each run, Pallas kernels for 52% -> 54%
where the time goes in v3:
time: 280 us; the launch traced here: 279 us
  Pallas kernels  192 us (69%)
  waiting for transfers between devices  21.6 us (8%)
  starting transfers between devices  17.7 us (6%)
  between operations  14.4 us (5%)
  other arithmetic  13.3 us (5%)
  matrix products  10.7 us (4%)
  local copies, waits for them, and re-layouts  10 us (4%)
    pallas_call x1, Pallas kernels, backward_scan(): pl.pallas_call(functools.partial(backward_scan_kernel, heads, n // seqs),...  60.6 us
    pallas_call x1, Pallas kernels, forward_scan(): pl.pallas_call(functools.partial(forward_scan_kernel, heads, n // seqs, r...  42.3 us
    pallas_call x1, Pallas kernels, gate_pass(): pl.pallas_call(functools.partial(gate_kernel, ri), grid=(rows // bm,), in...  38.6 us
    pallas_call x1, Pallas kernels, norm_back(): pl.pallas_call(kernel, grid=(count,), in_specs=[blk(CONV + 128), blk(DI),...  27.7 us
    ppermute x14, waiting for transfers between devices, swap(): return lax.ppermute(arr, axis, [(i, i ^ offset) for i in range(size)])  21.5 us
    ppermute x14, starting transfers between devices, swap(): return lax.ppermute(arr, axis, [(i, i ^ offset) for i in range(size)])  17.6 us
    pallas_call x1, Pallas kernels, conv_weight_grad(): pl.pallas_call(conv_weight_kernel, grid=((CONV + 128) // bn,), in_specs=[...  10.9 us
    pallas_call x1, Pallas kernels, out_pass(): pl.pallas_call(out_kernel, grid=(rows // bm,), in_specs=[blk(DI), blk(D),...  10 us
  transfers between devices with their start and end apart: 16, of which 6 were waited for; matrix products, arithmetic and copies ran while one was open for 10% of the time, Pallas kernels for 54%

profile of v3, /device:TPU:0, one launch (start us, length us, event | category | flops | bytes accessed | tf_op | source)
XLA Modules:
  0.0 279.4 jit_solution(15099978321676324094)
XLA Ops:
  7.2 1.3 pad_maximum_fusion.5.heads_in
  8.5 1.7 pack.1
  10.3 5.1 %collective-permute-start.2 = (bf16[24,2048]{1,0:T(8,128)(2,1)}, bf16[24,2048]{1,0:T(8,128)(2,1)S(1)}, u32[]{:S(2)}, u32[]{:S(2)}) collective-permute-start(bf16[24,2048]{1,0:T(8,128)(2,1)} %get-tuple-element.46), channel_id=1, source_target_pairs={{0,24},{2,26},{4,28},{6,30},{8,16},{10,18},{12,20},{14,22},{16,8},... | collective-permute-start | bytes 294920 | tf_op jit(solution)/shard_map/ppermute | solution.py:692
  15.4 0.6 collective-permute-start.1
  16.0 0.7 broadcast_xor_fusion
  16.8 0.1 add.57
  16.9 6.4 %convolution_bitcast_fusion.1.first.tok = bf16[2048,768]{1,0:T(8,128)(2,1)} fusion(bf16[2048,768]{1,0:T(8,128)(2,1)} %bitcast.70, s32[768]{0:T(1024)S(1)} %add.57), kind=kOutput, calls=%fused_computation.1 | convolution fusion | flops 2416508928 | bytes 6294528 | tf_op jit(solution)/shard_map/dot_general | solution.py:741
  23.3 0.6 collective-permute-done.1
  23.9 1.6 collective-permute-start.3
  25.5 1.5 collective-permute-start.4
  27.0 0.5 collective-permute-start.5
  27.5 4.1 %convolution_bitcast_fusion.cot = bf16[2048,768]{1,0:T(8,128)(2,1)} fusion(bf16[2048,768]{1,0:T(8,128)(2,1)S(1)} %bitcast.80, s32[768]{0:T(1024)S(1)} %add.57), kind=kOutput, calls=%fused_computation | convolution fusion | flops 2416508928 | bytes 6294528 | tf_op jit(solution)/shard_map/dot_general | solution.py:745
  31.6 4.4 %collective-permute-done.3 = bf16[4,24,2048]{2,1,0:T(8,128)(2,1)S(1)} collective-permute-done((bf16[4,24,2048]{2,1,0:T(8,128)(2,1)S(1)}, bf16[4,24,2048]{2,1,0:T(8,128)(2,1)S(1)}, u32[]{:S(2)}, u32[]{:S(2)}) %collective-permute-start.3) | collective-permute-done | bytes 393248 | tf_op jit(solution)/shard_map/ppermute | solution.py:692
  36.0 8.0 %collective-permute-done.4 = bf16[4,24,2048]{2,1,0:T(8,128)(2,1)S(1)} collective-permute-done((bf16[4,24,2048]{2,1,0:T(8,128)(2,1)S(1)}, bf16[4,24,2048]{2,1,0:T(8,128)(2,1)S(1)}, u32[]{:S(2)}, u32[]{:S(2)}) %collective-permute-start.4) | collective-permute-done | bytes 393248 | tf_op jit(solution)/shard_map/ppermute | solution.py:692
  44.0 2.7 collective-permute-done.5
  46.8 0.2 pad_maximum_fusion
  47.1 0.8 reshape.112.seg.seg_before
  47.9 2.6 collective-permute-done.6
  50.5 0.8 convert_bitcast_fusion.small
  51.3 0.7 broadcast_in_dim.11.device
  52.0 42.3 %forward_scan.1 = (bf16[2048,1792]{1,0:T(8,128)(2,1)}, bf16[2048,1792]{1,0:T(8,128)(2,1)}, bf16[2048,1792]{1,0:T(8,128)(2,1)}, bf16[2048,768]{1,0:T(8,128)(2,1)}...) custom-call(bf16[2048,768]{1,0:T(8,128)(2,1)} %convolution_bitcast_f, ...), custom_call_target="tpu_custom_call" | custom-call | tf_op jit(solution)/shard_map/forward_scan/pallas_call | solution.py:274
  94.4 38.6 %gate_pass.1 = (bf16[2048,1536]{1,0:T(8,128)(2,1)}, bf16[2048,1536]{1,0:T(8,128)(2,1)}, bf16[2048,1536]{1,0:T(8,128)(2,1)}, bf16[768,3072]{1,0:T(8,128)(2,1)}, bf16[1536,768]{1,0:T(8,128)(2,1)}) custom-call(bf16[2048,768]{1,0:T(8,128)(2,1)} %bitcast.71, bf16[2048,1536]{1,0:T(8,128)(2,1)} %get-tuple-element.50.scan, bf16[2048,768]{1,0:T(8,128)(2,1)} %bitcast.79, ...), custom_call_target="tpu_custom_call" | custom-call | tf_op jit(solution)/shard_map/gate_pass/pallas_call | solution.py:411
  133.0 60.6 %backward_scan.1 = (bf16[2048,1920]{1,0:T(8,128)(2,1)}, f32[32,1792]{1,0:T(8,128)}, f32[8,1792]{1,0:T(8,128)}, f32[8,1536]{1,0:T(8,128)}, f32[16,128]{1,0:T(8,128)}) custom-call(bf16[2048,1536]{1,0:T(8,128)(2,1)} %get-tuple-element.56.dscan, bf16[2048,1792]{1,0:T(8,128)(2,1)} %get-tuple-element.57.cin, bf16[2048,1792]{1,0:T(8,128)(2,1)} %get-tuple-element.58.act, ...), custom_call_target="tpu_custom_call" | custom-call | tf_op jit(solution)/shard_map/backward_scan/pallas_call | solution.py:569
  193.6 1.0 bitcast_reduce_fusion
  194.6 0.1 concatenate.26
  194.7 0.8 reduce_sum.73
  195.7 0.1 reshape.114
  195.8 0.8 reduce_sum.76
  196.7 0.1 reduce_sum.77
  196.8 0.1 stack.70
  196.9 0.7 slice_reduce_fusion.1
  197.6 0.1 stack.68
  197.7 0.1 stack.69
  197.8 0.1 tile.10
  197.8 0.1 reduce-precision_convert_fusion
  197.9 0.2 convolution_convert_fusion
  198.2 0.3 reshape.116
  198.5 0.8 pad.9.small
  199.3 10.9 %conv_weight_grad.1 = bf16[768,1920]{1,0:T(8,128)(2,1)} custom-call(bf16[2048,768]{1,0:T(8,128)(2,1)} %get-tuple-element.55.nrm, bf16[2048,1920]{1,0:T(8,128)(2,1)} %get-tuple-element.65.dproj, bf16[768,128]{1,0:T(8,128)(2,1)} %pad.9.small), custom_call_target="tpu_custom_call" | custom-call | tf_op jit(solution)/shard_map/conv_weight_grad/pallas_call | solution.py:645
  210.1 2.0 fusion.15
  212.1 0.2 collective-permute-start.7
  212.4 3.1 %collective-permute-done.7 = bf16[4,4,24,1920]{3,2,1,0:T(8,128)(2,1)S(1)} collective-permute-done((bf16[4,4,24,1920]{3,2,1,0:T(8,128)(2,1)S(1)}, bf16[4,4,24,1920]{3,2,1,0:T(8,128)(2,1)S(1)}, u32[]{:S(2)}, u32[]{:S(2)}) %collective-permute-start.7) | collective-permute-done | bytes 1474592 | tf_op jit(solution)/shard_map/ppermute | solution.py:692
  215.5 0.3 convert_add_fusion
  215.8 0.2 convert_element_type.75
  215.9 0.8 slice_bitcast_fusion.2
  216.8 2.3 collective-permute-start.10
  219.1 1.2 collective-permute-start.9
  220.3 1.5 fusion.order
  221.8 27.7 %norm_back.1 = bf16[2048,768]{1,0:T(8,128)(2,1)} custom-call(bf16[2048,1920]{1,0:T(8,128)(2,1)} %get-tuple-element.65.dproj, bf16[2048,1536]{1,0:T(8,128)(2,1)} %get-tuple-element.72.dgate, bf16[2048,768]{1,0:T(8,128)(2,1)} %convolution_bitcast_fusion.1.first.tok, bf16[2048,768]{1,0:T(8,128)(2,1)} %convolution_bitcast_fusion.cot, ...), custom_call_target="tpu_custom_call" | custom-call | tf_op jit(solution)/shard_map/norm_back/pallas_call | solution.py:618
  249.5 1.2 fusion.4
  250.8 0.8 fusion.16
  251.7 0.4 collective-permute-start.11
  252.0 3.3 %collective-permute-start.12 = (bf16[24,1920]{1,0:T(8,128)(2,1)S(1)}, bf16[24,1920]{1,0:T(8,128)(2,1)S(1)}, u32[]{:S(2)}, u32[]{:S(2)}) collective-permute-start(bf16[24,1920]{1,0:T(8,128)(2,1)S(1)} %get-tuple-element.94), channel_id=1, source_target_pairs={{0,16},{2,18},{4,20},{6,22},{8,24},{10,26},{12,28},{14,30},{16,0},... | collective-permute-start | bytes 276488 | tf_op jit(solution)/shard_map/ppermute | solution.py:692
  255.3 0.8 collective-permute-start.13
  256.1 0.8 multiply_reduce_fusion.1
  256.9 1.2 convert_divide_fusion
  258.1 0.9 slice.128
  259.0 10.0 %out_pass.1 = bf16[2048,768]{1,0:T(8,128)(2,1)} custom-call(bf16[2048,1536]{1,0:T(8,128)(2,1)} %get-tuple-element.54.mixed, bf16[2048,768]{1,0:T(8,128)(2,1)} %bitcast.72, bf16[1536,768]{1,0:T(8,128)(2,1)} %get-tuple-element.77.wo), custom_call_target="tpu_custom_call" | custom-call | tf_op jit(solution)/shard_map/out_pass/pallas_call | solution.py:433
  269.2 0.1 reshape.119
  269.4 0.6 fusion.17
  270.0 0.6 slice.115
  270.5 0.9 multiply_reduce_fusion
  271.4 0.5 convert_divide_fusion.1
  271.9 0.7 reshape.120
  (53 shorter events, 1.0 us)
Async XLA Ops:
  7.2 87.2 %all-gather.2.cloned.1.call-start = ((), (), s32[]{:S(2)}) async-start(), calls=%async_computation.1 | async-start | bytes 4866048 | tf_op jit(solution)/shard_map/all_gather | solution.py:736
  10.2 240.6 %reduce-scatter.2.cloned.1.call-start = ((), (), s32[]{:S(2)}) async-start(), calls=%async_computation.2 | async-start | bytes 4866048 | tf_op jit(solution)/shard_map/reduce_scatter | solution.py:756
  10.3 13.0 %collective-permute-start.2 = (bf16[24,2048]{1,0:T(8,128)(2,1)}, bf16[24,2048]{1,0:T(8,128)(2,1)S(1)}, u32[]{:S(2)}, u32[]{:S(2)}) collective-permute-start(bf16[24,2048]{1,0:T(8,128)(2,1)} %get-tuple-element.46), channel_id=1, source_target_pairs={{0,24},{2,26},{4,28},{6,30},{8,16},{10,18},{12,20},{14,22},{16,8},... | collective-permute-start | bytes 294920 | tf_op jit(solution)/shard_map/ppermute | solution.py:692
  15.4 7.9 %collective-permute-start = (bf16[24,2048]{1,0:T(8,128)(2,1)}, bf16[24,2048]{1,0:T(8,128)(2,1)S(1)}, u32[]{:S(2)}, u32[]{:S(2)}) collective-permute-start(bf16[24,2048]{1,0:T(8,128)(2,1)} %get-tuple-element.46), channel_id=1, source_target_pairs={{0,8},{2,10},{4,12},{6,14},{8,0},{10,2},{12,4},{14,6},{16,24},{18,... | collective-permute-start | bytes 294920 | tf_op jit(solution)/shard_map/ppermute | solution.py:692
  15.4 8.5 %collective-permute-start.1 = (bf16[24,2048]{1,0:T(8,128)(2,1)}, bf16[24,2048]{1,0:T(8,128)(2,1)S(1)}, u32[]{:S(2)}, u32[]{:S(2)}) collective-permute-start(bf16[24,2048]{1,0:T(8,128)(2,1)} %get-tuple-element.46), channel_id=1, source_target_pairs={{0,16},{2,18},{4,20},{6,22},{8,24},{10,26},{12,28},{14,30},{16,0},... | collective-permute-start | bytes 294920 | tf_op jit(solution)/shard_map/ppermute | solution.py:692
  16.9 7.0 %copy-start.5 = (bf16[24,2048]{1,0:T(8,128)(2,1)S(1)}, bf16[24,2048]{1,0:T(8,128)(2,1)}, u32[]{:S(2)}) copy-start(bf16[24,2048]{1,0:T(8,128)(2,1)} %get-tuple-element.46) | copy-start | bytes 294916
  16.9 10.6 %copy-start.2 = (bf16[2,1024,768]{2,1,0:T(8,128)(2,1)S(1)}, bf16[2,1024,768]{2,1,0:T(8,128)(2,1)}, u32[]{:S(2)}) copy-start(bf16[2,1024,768]{2,1,0:T(8,128)(2,1)} %param.14) | copy-start | bytes 9437188
  23.9 12.1 %collective-permute-start.3 = (bf16[4,24,2048]{2,1,0:T(8,128)(2,1)S(1)}, bf16[4,24,2048]{2,1,0:T(8,128)(2,1)S(1)}, u32[]{:S(2)}, u32[]{:S(2)}) collective-permute-start(bf16[4,24,2048]{2,1,0:T(8,128)(2,1)S(1)} %pad_maximum_fusion.1), channel_id=1, source_target_pairs={{0,2},{2,0},{4,6},{6,4},{8,10},{10,8},{12,14},{14,12},{16,18},{18,... | collective-permute-start | bytes 1179656 | tf_op jit(solution)/shard_map/ppermute | solution.py:692
  25.5 18.5 %collective-permute-start.4 = (bf16[4,24,2048]{2,1,0:T(8,128)(2,1)S(1)}, bf16[4,24,2048]{2,1,0:T(8,128)(2,1)S(1)}, u32[]{:S(2)}, u32[]{:S(2)}) collective-permute-start(bf16[4,24,2048]{2,1,0:T(8,128)(2,1)S(1)} %pad_maximum_fusion.1), channel_id=1, source_target_pairs={{0,4},{2,6},{4,0},{6,2},{8,12},{10,14},{12,8},{14,10},{16,20},{18,... | collective-permute-start | bytes 1179656 | tf_op jit(solution)/shard_map/ppermute | solution.py:692
  27.0 19.8 %collective-permute-start.5 = (bf16[4,24,2048]{2,1,0:T(8,128)(2,1)S(1)}, bf16[4,24,2048]{2,1,0:T(8,128)(2,1)S(1)}, u32[]{:S(2)}, u32[]{:S(2)}) collective-permute-start(bf16[4,24,2048]{2,1,0:T(8,128)(2,1)S(1)} %pad_maximum_fusion.1), channel_id=1, source_target_pairs={{0,6},{2,4},{4,2},{6,0},{8,14},{10,12},{12,10},{14,8},{16,22},{18,... | collective-permute-start | bytes 1179656 | tf_op jit(solution)/shard_map/ppermute | solution.py:692
  31.6 15.5 %copy-start.6 = (s32[2,1024]{1,0:T(2,128)S(1)}, s32[2,1024]{1,0:T(2,128)}, u32[]{:S(2)}) copy-start(s32[2,1024]{1,0:T(2,128)} %param.15) | copy-start | bytes 24580
  47.0 5.0 %copy-start = (bf16[4,4,24,2048]{3,2,1,0:T(8,128)(2,1)}, bf16[4,4,24,2048]{3,2,1,0:T(8,128)(2,1)S(1)}, u32[]{:S(2)}) copy-start(bf16[4,4,24,2048]{3,2,1,0:T(8,128)(2,1)S(1)} %pad_maximum_fusion) | copy-start | bytes 4718596
  47.0 3.5 %collective-permute-start.6 = (bf16[4,4,24,2048]{3,2,1,0:T(8,128)(2,1)S(1)}, bf16[4,4,24,2048]{3,2,1,0:T(8,128)(2,1)S(1)}, u32[]{:S(2)}, u32[]{:S(2)}) collective-permute-start(bf16[4,4,24,2048]{3,2,1,0:T(8,128)(2,1)S(1)} %pad_maximum_fusion), channel_id=1, source_target_pairs={{0,1},{1,0},{2,3},{3,2},{4,5},{5,4},{6,7},{7,6},{8,9},{9,8},{10,11... | collective-permute-start | bytes 4718600 | tf_op jit(solution)/shard_map/ppermute | solution.py:692
  50.4 1.5 copy-start.1
  212.1 3.3 %collective-permute-start.7 = (bf16[4,4,24,1920]{3,2,1,0:T(8,128)(2,1)S(1)}, bf16[4,4,24,1920]{3,2,1,0:T(8,128)(2,1)S(1)}, u32[]{:S(2)}, u32[]{:S(2)}) collective-permute-start(bf16[4,4,24,1920]{3,2,1,0:T(8,128)(2,1)S(1)} %bitcast.82), channel_id=1, source_target_pairs={{0,1},{1,0},{2,3},{3,2},{4,5},{5,4},{6,7},{7,6},{8,9},{9,8},{10,11... | collective-permute-start | bytes 4423688 | tf_op jit(solution)/shard_map/ppermute | solution.py:692
  216.8 32.7 %collective-permute-start.10 = (bf16[4,24,1920]{2,1,0:T(8,128)(2,1)}, bf16[4,24,1920]{2,1,0:T(8,128)(2,1)S(1)}, u32[]{:S(2)}, u32[]{:S(2)}) collective-permute-start(bf16[4,24,1920]{2,1,0:T(8,128)(2,1)} %get-tuple-element.90), channel_id=1, source_target_pairs={{0,6},{2,4},{4,2},{6,0},{8,14},{10,12},{12,10},{14,8},{16,22},{18,... | collective-permute-start | bytes 1105928 | tf_op jit(solution)/shard_map/ppermute | solution.py:692
  219.1 30.4 %collective-permute-start.8 = (bf16[4,24,1920]{2,1,0:T(8,128)(2,1)S(1)}, bf16[4,24,1920]{2,1,0:T(8,128)(2,1)}, u32[]{:S(2)}, u32[]{:S(2)}) collective-permute-start(bf16[4,24,1920]{2,1,0:T(8,128)(2,1)S(1)} %get-tuple-element.89), channel_id=1, source_target_pairs={{0,2},{2,0},{4,6},{6,4},{8,10},{10,8},{12,14},{14,12},{16,18},{18,... | collective-permute-start | bytes 1105928 | tf_op jit(solution)/shard_map/ppermute | solution.py:692
  219.1 30.4 %collective-permute-start.9 = (bf16[4,24,1920]{2,1,0:T(8,128)(2,1)S(1)}, bf16[4,24,1920]{2,1,0:T(8,128)(2,1)}, u32[]{:S(2)}, u32[]{:S(2)}) collective-permute-start(bf16[4,24,1920]{2,1,0:T(8,128)(2,1)S(1)} %get-tuple-element.91), channel_id=1, source_target_pairs={{0,4},{2,6},{4,0},{6,2},{8,12},{10,14},{12,8},{14,10},{16,20},{18,... | collective-permute-start | bytes 1105928 | tf_op jit(solution)/shard_map/ppermute | solution.py:692
  249.5 6.7 %copy-start.4 = (bf16[48,768]{1,0:T(8,128)(2,1)S(1)}, bf16[48,768]{1,0:T(8,128)(2,1)}, u32[]{:S(2)}) copy-start(bf16[48,768]{1,0:T(8,128)(2,1)} %w_out.1) | copy-start | bytes 221188
  251.7 17.4 %collective-permute-start.11 = (bf16[24,1920]{1,0:T(8,128)(2,1)S(1)}, bf16[24,1920]{1,0:T(8,128)(2,1)S(1)}, u32[]{:S(2)}, u32[]{:S(2)}) collective-permute-start(bf16[24,1920]{1,0:T(8,128)(2,1)S(1)} %get-tuple-element.92), channel_id=1, source_target_pairs={{0,8},{2,10},{4,12},{6,14},{8,0},{10,2},{12,4},{14,6},{16,24},{18,... | collective-permute-start | bytes 276488 | tf_op jit(solution)/shard_map/ppermute | solution.py:692
  252.0 17.0 %collective-permute-start.12 = (bf16[24,1920]{1,0:T(8,128)(2,1)S(1)}, bf16[24,1920]{1,0:T(8,128)(2,1)S(1)}, u32[]{:S(2)}, u32[]{:S(2)}) collective-permute-start(bf16[24,1920]{1,0:T(8,128)(2,1)S(1)} %get-tuple-element.94), channel_id=1, source_target_pairs={{0,16},{2,18},{4,20},{6,22},{8,24},{10,26},{12,28},{14,30},{16,0},... | collective-permute-start | bytes 276488 | tf_op jit(solution)/shard_map/ppermute | solution.py:692
  255.3 13.7 %collective-permute-start.13 = (bf16[24,1920]{1,0:T(8,128)(2,1)S(1)}, bf16[24,1920]{1,0:T(8,128)(2,1)S(1)}, u32[]{:S(2)}, u32[]{:S(2)}) collective-permute-start(bf16[24,1920]{1,0:T(8,128)(2,1)S(1)} %get-tuple-element.93), channel_id=1, source_target_pairs={{0,24},{2,26},{4,28},{6,30},{8,16},{10,18},{12,20},{14,22},{16,8},... | collective-permute-start | bytes 276488 | tf_op jit(solution)/shard_map/ppermute | solution.py:692
  259.0 11.5 %copy-start.3 = (bf16[24,3352]{1,0:T(8,128)(2,1)S(1)}, bf16[24,3352]{1,0:T(8,128)(2,1)}, u32[]{:S(2)}) copy-start(bf16[24,3352]{1,0:T(8,128)(2,1)} %w_in.1) | copy-start | bytes 482692
  259.0 12.4 %copy-start.7 = (bf16[24]{0:T(256)(128)(2,1)S(1)}, bf16[24]{0:T(256)(128)(2,1)}, u32[]{:S(2)}) copy-start(bf16[24]{0:T(256)(128)(2,1)} %param.16) | copy-start | bytes 148
Sparse Core Ops, SparseCore 0:
  11.5 67.7 all-gather.1
  133.1 107.2 reduce-scatter.1

commit v4 on v3

--- a/solution.py
+++ b/solution.py
@@ -96,7 +96,7 @@
     return (lax.broadcasted_iota(jnp.int32, shape, 0) & 127 == head).astype(bf16)
 
 
-def pack_kernel(ri, w_in, w_out, in_gain, cw, cb, gg, heads_in, wc_o, later_o, rows):
+def pack_kernel(ri, w_in, w_out, in_gain, cw, cb, gg, sb, dl, sg, wc_o, later_o, rows):
     wc_o[...] = jnp.zeros_like(wc_o)
     wc_o[0:ri, : w_in.shape[1] - DI] = w_in[:, DI:]
     rows[...] = jnp.zeros_like(rows)
@@ -104,24 +104,25 @@
     rows[1:5, : cw.shape[1]] = cw[...].astype(f32)
     rows[5:6, : cb.shape[1]] = cb[...].astype(f32)
     rows[6:7, : gg.shape[1]] = gg[...].astype(f32)
-    value = heads_in[...]
-    for n in range(3):
-        part = value.astype(bf16).astype(f32)
-        rows[7 + 3 * n : 10 + 3 * n, : value.shape[1]] = part
-        value = value - part
+    for k, term in enumerate((sb, dl, sg)):
+        value = term[...]
+        for n in range(3):
+            part = value.astype(bf16).astype(f32)
+            rows[7 + 3 * n + k : 8 + 3 * n + k, : value.shape[1]] = part
+            value = value - part
     wc_o[0:16, CONV + 128 :] = rows[...].astype(bf16)
     later_o[:, :DI] = w_in[:, :DI]
     later_o[:, DI : DI + D] = w_out[0:ri, :]
     later_o[:, DI + D :] = w_out[ri:, :]
 
 
-def pack(w_in, w_out, in_gain, cw, cb, gg, heads_in, ri, tall):
+def pack(w_in, w_out, in_gain, cw, cb, gg, sb, dl, sg, ri, tall):
     return pl.pallas_call(
         functools.partial(pack_kernel, ri),
         out_shape=[jax.ShapeDtypeStruct((tall, CONV + 256), bf16), jax.ShapeDtypeStruct((ri, 2 * DI), bf16)],
         scratch_shapes=[pltpu.VMEM((16, 128), f32)],
         name="pack",
-    )(w_in, w_out, in_gain, cw, cb, gg, heads_in)
+    )(w_in, w_out, in_gain, cw, cb, gg, sb, dl, sg)
 
 
 def unpack_small(ri, ro, share, small, device, onehot, gain, gain_abs, cw, cb, gg, heads_o, skip):
@@ -442,13 +443,57 @@
     )(mixed, tok, wo)
 
 
-def backward_scan_kernel(heads, per_seq, dscan, cin, act, dact, z_r, st, cw, head_terms, skip, seg, seg_before,
-                         dproj_o, gcw_o, gcb_o, gsk_o, ghd_o,
-                         dstate, p1buf, qbuf, xwbuf, rowbuf, lastbuf, mbuf, onehot, sums, docs):
+def pack_grads(nf, share, tall, gcw, gcb, gsk, ghd, device, sums, rows, out_o):
+    nd = device.shape[0]
+    owner = device[...][:, 0:1]
+    first_lane = nf * share
+
+    def spread(values, width, who):
+        total = values.shape[1]
+        lane = lax.broadcasted_iota(jnp.int32, (128, total), 1).astype(f32)
+        piece = jnp.floor((lane + 0.5) * (1.0 / width))
+        place = lax.broadcasted_iota(jnp.int32, (128, total), 0).astype(f32) - first_lane
+        pick = ((place == lane - piece * width) & (place < width)).astype(bf16)
+        mine = piece[0:1, :] == who
+        hi = values.astype(bf16).astype(f32)
+        return [dot_nt(jnp.where(mine, part, 0.0).astype(bf16), pick) for part in (hi, values - hi)]
+
+    rows[...] = jnp.zeros_like(rows)
+
+    def put(n, values):
+        rows[pl.ds(n, nd, stride=tall), :] = values
+
+    for k in range(5):
+        terms = gcw[8 * k : 8 * k + 8, :] if k < 4 else gcb[...]
+        hi, lo = spread(0.5 * jnp.sum(terms, axis=0, keepdims=True), CONV // nd, owner)
+        put(k, hi)
+        put(5 + k, lo)
+    group = owner - nf * jnp.floor((owner + 0.5) * (1.0 / nf))
+    skips = two_parts(jnp.broadcast_to(jnp.sum(gsk[...], axis=0, keepdims=True), (8, DI)))
+    skips = dot(skips[:, :DI], sums[...]) + dot(skips[:, DI:], sums[...])
+    per_head = [jnp.sum(ghd[0:8, :], axis=0, keepdims=True), jnp.sum(ghd[8:16, :], axis=0, keepdims=True), skips[0:1, :]]
+    for n in range(3):
+        hi, lo = spread(per_head[n], share, group)
+        put(10 + n, hi)
+        put(13 + n, lo)
+    out_o[...] = rows[...].astype(bf16)
+
+
+def backward_scan_kernel(heads, per_seq, nf, share, tall, dscan, cin, act, dact, z_r, st, cw, head_terms, skip, seg, seg_before,
+                         wc_a, wc_b, device, dproj_o, gproj_o, pack_o,
+                         dstate, p1buf, qbuf, xwbuf, rowbuf, lastbuf, mbuf, onehot, sums, docs,
+                         gcw_o, gcb_o, gsk_o, ghd_o, rows_s, wc, dlast, sems):
     i = pl.program_id(0)
+    steps = pl.num_programs(0)
 
     @pl.when(i == 0)
     def _():
+        half = wc_a.shape[0]
+        copies = [pltpu.make_async_copy(wc_a.at[:, : CONV + 128], wc.at[0:half], sems.at[0]),
+                  pltpu.make_async_copy(wc_b.at[:, : CONV + 128], wc.at[half : 2 * half], sems.at[1])]
+        for copy in copies:
+            copy.start()
+        dlast[...] = jnp.zeros_like(dlast)
         gcw_o[...] = jnp.zeros_like(gcw_o)
         gcb_o[...] = jnp.zeros_like(gcb_o)
         gsk_o[...] = jnp.zeros_like(gsk_o)
@@ -458,6 +503,8 @@
         onehot[...] = head_onehot(onehot.shape)
         head = lax.broadcasted_iota(jnp.int32, sums.shape, 0) >> 6
         sums[...] = (head == lax.broadcasted_iota(jnp.int32, sums.shape, 1)).astype(bf16)
+        for copy in copies:
+            copy.wait()
 
     @pl.when(lax.rem(i, per_seq) == 0)
     def _():
@@ -501,6 +548,11 @@
         dproj_o[:, cols] = dcin.astype(bf16)
         mbuf[:, t, Q : Q + 8, :] = mbuf[:, t, 0:8, :]
 
+    def project_back(given, block, part):
+        cols = slice(256 * part, 256 * part + 256)
+        gproj_o[pl.ds(block * Q, Q), cols] = dot_nt(given[...], wc[cols, :]).astype(bf16)
+
+    block_before = steps - jnp.maximum(i, 1)
     for p in range(heads // 2):
         cols = slice(128 * p, 128 * p + 128)
         half = slice(128 * (p % 2), 128 * (p % 2) + 128)
@@ -509,6 +561,8 @@
             wide = dot(factors, onehot[:, group])
             cs = dot(cmat, st[0, :, group])
             bd = dot(bmat, ds_low[:, group])
+        if p % 4 == 1:
+            project_back(dlast, block_before, p // 4)
         xp = act[:, cols]
         dy = dscan[:, cols]
         dybd = jnp.concatenate([jnp.where(low, dy, zero), jnp.where(low, zero, dy)], axis=0)
@@ -557,47 +611,58 @@
     dproj_o[:, CONV:] = dz.astype(bf16)
     ghd_o[0:8, :] += jnp.sum(dz.reshape(-1, 8, 128), axis=0)
     ghd_o[8:16, :] += rate * jnp.sum((g * soft).reshape(-1, 8, 128), axis=0)
-
-
-def backward_scan(dscan, cin, act, dact, z, st, cw, head_terms, skip, seg, heads, seqs):
+    dlast[...] = dproj_o[...]
+
+    @pl.when(i == steps - 1)
+    def _():
+        for part in range(D // 256):
+            project_back(dlast, 0, part)
+        pack_grads(nf, share, tall, gcw_o, gcb_o, gsk_o, ghd_o, device, sums, rows_s, pack_o)
+
+
+def backward_scan(dscan, cin, act, dact, z, st, cw, head_terms, skip, seg, wc_a, wc_b, device, heads, seqs, nf, share, tall):
     rows = dscan.shape[0]
     n = rows // Q
+    nd = device.shape[0]
     one = pl.Buffered(buffer_count=1)
     full = lambda shape: pl.BlockSpec(shape, lambda i: (0,) * len(shape), pipeline_mode=one)
     blk = lambda w: pl.BlockSpec((Q, w), lambda i: (n - 1 - i, 0))
     blk3 = lambda s1, s2: pl.BlockSpec((1, s1, s2), lambda i: (n - 1 - i, 0, 0))
+    hbm = pl.BlockSpec(memory_space=pl.ANY)
     return pl.pallas_call(
-        functools.partial(backward_scan_kernel, heads, n // seqs),
+        functools.partial(backward_scan_kernel, heads, n // seqs, nf, share, tall),
         grid=(n,),
         in_specs=[blk(DI), blk(CONV), blk(CONV), blk(CONV), blk(128), blk3(N, DI), full(cw.shape), full(head_terms.shape),
-                  full(skip.shape), blk3(1, Q), pl.BlockSpec((1, 1, Q), lambda i: (jnp.maximum(n - 2 - i, 0), 0, 0))],
-        out_specs=[blk(CONV + 128), full((32, CONV)), full((8, CONV)), full((8, DI)), full((16, 128))],
-        out_shape=[jax.ShapeDtypeStruct((rows, CONV + 128), bf16), jax.ShapeDtypeStruct((32, CONV), f32),
-                   jax.ShapeDtypeStruct((8, CONV), f32), jax.ShapeDtypeStruct((8, DI), f32),
-                   jax.ShapeDtypeStruct((16, 128), f32)],
+                  full(skip.shape), blk3(1, Q), pl.BlockSpec((1, 1, Q), lambda i: (jnp.maximum(n - 2 - i, 0), 0, 0)),
+                  hbm, hbm, full(device.shape)],
+        out_specs=[blk(CONV + 128), full((rows, D)), full((nd * tall, 128))],
+        out_shape=[jax.ShapeDtypeStruct((rows, CONV + 128), bf16), jax.ShapeDtypeStruct((rows, D), bf16),
+                   jax.ShapeDtypeStruct((nd * tall, 128), bf16)],
         scratch_shapes=[pltpu.VMEM((N, DI), f32), pltpu.VMEM((Q, 2 * DI), bf16), pltpu.VMEM((Q, DI), bf16),
                         pltpu.VMEM((Q, 2 * DI), bf16), pltpu.VMEM((128, 128), f32), pltpu.VMEM((8, DI), f32),
                         pltpu.VMEM((3, CONV // 128, Q + 8, 128), f32), pltpu.VMEM((256, DI), bf16),
-                        pltpu.VMEM((DI, 128), bf16), pltpu.VMEM((Q + 8, 128), f32)],
+                        pltpu.VMEM((DI, 128), bf16), pltpu.VMEM((Q + 8, 128), f32), pltpu.VMEM((32, CONV), f32),
+                        pltpu.VMEM((8, CONV), f32), pltpu.VMEM((8, DI), f32), pltpu.VMEM((16, 128), f32),
+                        pltpu.VMEM((nd * tall, 128), f32), pltpu.VMEM((D, CONV + 128), bf16), pltpu.VMEM((Q, CONV + 128), bf16),
+                        pltpu.SemaphoreType.DMA((2,))],
         compiler_params=pltpu.CompilerParams(vmem_limit_bytes=VM),
         cost_estimate=pl.CostEstimate(flops=0, bytes_accessed=0, transcendentals=0),
         name="backward_scan",
-    )(dscan, cin, act, dact, z, st, cw, head_terms, skip, seg, seg)
-
-
-def norm_back_kernel(dproj, dgate, tok, cot, wc_a, wc_b, wg_abs, gain, order, out_o, wc, wg, sems):
+    )(dscan, cin, act, dact, z, st, cw, head_terms, skip, seg, seg, wc_a, wc_b, device)
+
+
+def norm_back_kernel(ri, gproj, dgate, tok, cot, wg_abs, gain, device, out_o, wg, order):
     @pl.when(pl.program_id(0) == 0)
     def _():
-        rows = wc_a.shape[0]
-        copies = [pltpu.make_async_copy(wc_a.at[:, : CONV + 128], wc.at[0:rows], sems.at[0]),
-                  pltpu.make_async_copy(wc_b.at[:, : CONV + 128], wc.at[rows : 2 * rows], sems.at[1])]
-        for copy in copies:
-            copy.start()
+        column = lax.broadcasted_iota(jnp.int32, (8, D), 1).astype(f32)
+        slot = jnp.floor((column + 0.5) * (1.0 / ri))
+        nd = device.shape[0]
+        mine = lax.broadcasted_iota(jnp.int32, (nd, D), 0).astype(f32) == slot[0:1, :]
+        feature = jnp.sum(jnp.where(mine, device[...][:, 0:1], 0.0), axis=0, keepdims=True) * ri + (column - slot * ri)[0:1, :]
+        order[...] = (lax.broadcasted_iota(jnp.int32, (D, D), 0).astype(f32) == feature).astype(bf16)
         wg[...] = (0.5 * dot_tn(order[...], wg_abs[...])).astype(bf16)
-        for copy in copies:
-            copy.wait()
-
-    grad = dot_nt(dgate[...], wg[...]) + dot_nt(dproj[...], wc[...])
+
+    grad = dot_nt(dgate[...], wg[...]) + gproj[...].astype(f32)
     x = tok[...].astype(f32)
     r = lax.rsqrt(jnp.mean(x * x, axis=-1, keepdims=True) + EPS)
     unit = x * r
@@ -607,36 +672,37 @@
     out_o[...] = dot_nt(res, order[...]).astype(bf16)
 
 
-def norm_back(dproj, dgate, tok, cot, wc_a, wc_b, later, gain, order, start, count, into=None, bm=512):
-    rows = dproj.shape[0]
+def norm_back(gproj, dgate, tok, cot, later, gain, device, ri, bm=512):
+    rows = gproj.shape[0]
     one = pl.Buffered(buffer_count=1)
     full = lambda shape: pl.BlockSpec(shape, lambda i: (0,) * len(shape), pipeline_mode=one)
-    blk = lambda w: pl.BlockSpec((bm, w), lambda i: (start + i, 0))
-    hbm = pl.BlockSpec(memory_space=pl.ANY)
-    given = [] if into is None else [into]
-    kernel = norm_back_kernel if into is None else lambda *refs: norm_back_kernel(*refs[:9], *refs[10:])
+    blk = lambda w: pl.BlockSpec((bm, w), lambda i: (i, 0))
     return pl.pallas_call(
-        kernel,
-        grid=(count,),
-        in_specs=[blk(CONV + 128), blk(DI), blk(D), blk(D), hbm, hbm, full((D, DI)), full(gain.shape), full(order.shape)]
-        + [hbm] * len(given),
+        functools.partial(norm_back_kernel, ri),
+        grid=(rows // bm,),
+        in_specs=[blk(D), blk(DI), blk(D), blk(D), full((D, DI)), full(gain.shape), full(device.shape)],
         out_specs=blk(D),
         out_shape=jax.ShapeDtypeStruct((rows, D), bf16),
-        input_output_aliases={9: 0} if given else {},
-        scratch_shapes=[pltpu.VMEM((D, CONV + 128), bf16), pltpu.VMEM((D, DI), bf16), pltpu.SemaphoreType.DMA((2,))],
-        compiler_params=pltpu.CompilerParams(vmem_limit_bytes=VM),
+        scratch_shapes=[pltpu.VMEM((D, DI), bf16), pltpu.VMEM((D, D), bf16)],
+        compiler_params=pltpu.CompilerParams(vmem_limit_bytes=36 << 20),
         cost_estimate=pl.CostEstimate(flops=0, bytes_accessed=0, transcendentals=0),
         name="norm_back",
-    )(dproj, dgate, tok, cot, wc_a, wc_b, later, gain, order, *given)
-
-
-def conv_weight_kernel(nrm, dproj, small, out_o):
+    )(gproj, dgate, tok, cot, later, gain, device)
+
+
+def conv_weight_kernel(nrm, dproj, small, a_o, b_o):
     grad = lax.dot_general(dproj[...], nrm[...], (((0,), (0,)), ((), ())), preferred_element_type=f32)
-    out_o[...] = grad.astype(bf16).T
+    half = a_o.shape[0]
+    out = grad.astype(bf16).T
+    a_o[...] = out[:half]
+    b_o[...] = out[half:]
 
     @pl.when(pl.program_id(0) == pl.num_programs(0) - 1)
     def _():
-        out_o[:, out_o.shape[1] - 128 :] = (grad[out_o.shape[1] - 128 :].T + small[...].astype(f32)).astype(bf16)
+        last = slice(a_o.shape[1] - 128, a_o.shape[1])
+        out = (grad[a_o.shape[1] - 128 :].T + small[...].astype(f32)).astype(bf16)
+        a_o[:, last] = out[:half]
+        b_o[:, last] = out[half:]
 
 
 def conv_weight_grad(nrm, dproj, small, bn=640):
@@ -647,12 +713,49 @@
         grid=((CONV + 128) // bn,),
         in_specs=[pl.BlockSpec((rows, D), lambda i: (0, 0), pipeline_mode=one), pl.BlockSpec((rows, bn), lambda i: (0, i)),
                   pl.BlockSpec((D, 128), lambda i: (0, 0), pipeline_mode=one)],
-        out_specs=pl.BlockSpec((D, bn), lambda i: (0, i)),
-        out_shape=jax.ShapeDtypeStruct((D, CONV + 128), bf16),
+        out_specs=[pl.BlockSpec((D // 2, bn), lambda i: (0, i))] * 2,
+        out_shape=[jax.ShapeDtypeStruct((D // 2, CONV + 128), bf16)] * 2,
         compiler_params=pltpu.CompilerParams(vmem_limit_bytes=VM),
         cost_estimate=pl.CostEstimate(flops=0, bytes_accessed=0, transcendentals=0),
         name="conv_weight_grad",
     )(nrm, dproj, small)
+
+
+def finish_kernel(heads, share, parts, early, w_in, w_out, in_gain, gate_gain, *refs):
+    own, got = refs[0], refs[1:parts]
+    in_o, out_o, in_gain_o, gate_gain_o, cw_o, cb_o, sb_o, dl_o, sg_o, total = refs[parts:]
+    ri, ro, cc = w_in.shape[0], w_out.shape[0], cb_o.shape[1]
+    value = own[...]
+    for part in got:
+        value = value + part[...].astype(f32)
+    total[...] = value
+    in_o[:, :DI] = early[:, :DI].astype(f32)
+    in_o[:, DI:] = total[0:ri, : CONV + heads]
+    out_o[0:ri, :] = early[:, DI : DI + D].astype(f32)
+    out_o[ri:, :] = early[:, DI + D :].astype(f32)
+
+    def across(column, count):
+        spot = lax.broadcasted_iota(jnp.int32, (count, count), 0) == lax.broadcasted_iota(jnp.int32, (count, count), 1)
+        return jnp.sum(jnp.where(spot, column, 0.0), axis=0, keepdims=True)
+
+    in_gain_o[...] = across(jnp.sum(w_in[...].astype(f32) * in_o[...], axis=-1, keepdims=True), ri) / in_gain[...].astype(f32)
+    gate_gain_o[...] = across(jnp.sum(w_out[...].astype(f32) * out_o[...], axis=-1, keepdims=True), ro) / gate_gain[...].astype(f32)
+    at = CONV + heads
+    cw_o[...] = total[0:4, at : at + cc] + total[5:9, at : at + cc]
+    cb_o[...] = total[4:5, at : at + cc] + total[9:10, at : at + cc]
+    for k, term in enumerate((sb_o, dl_o, sg_o)):
+        term[...] = total[10 + k : 11 + k, at : at + share] + total[13 + k : 14 + k, at : at + share]
+
+
+def finish(early, w_in, w_out, in_gain, gate_gain, own, got, heads, share, cc):
+    ri, ro = w_in.shape[0], w_out.shape[0]
+    shapes = [(ri, w_in.shape[1]), (ro, D), (1, ri), (1, ro), (4, cc), (1, cc)] + [(1, share)] * 3
+    return pl.pallas_call(
+        functools.partial(finish_kernel, heads, share, 1 + len(got)),
+        out_shape=[jax.ShapeDtypeStruct(shape, f32) for shape in shapes],
+        scratch_shapes=[pltpu.VMEM(own.shape, f32)],
+        name="finish",
+    )(early, w_in, w_out, in_gain, gate_gain, own, *got)
 
 
 def stages_of(mesh):
@@ -697,12 +800,15 @@
     return jnp.stack([block] + [swap(block, axis, sizes[axis], k * stride) for k in range(1, group)])
 
 
-def scatter_stage(kept, stage, sizes):
+def scatter_parts(kept, stage, sizes):
     axis, stride, group, _ = stage
     low = kept.astype(bf16)
-    got = [swap(low[k], axis, sizes[axis], k * stride) for k in range(1, group)]
-    total = kept[0].astype(f32)
-    for part in got:
+    return [swap(low[k], axis, sizes[axis], k * stride) for k in range(1, group)]
+
+
+def scatter_stage(kept, stage, sizes):
+    total = kept[0]
+    for part in scatter_parts(kept, stage, sizes):
         total = total + part.astype(f32)
     return total
 
@@ -723,23 +829,22 @@
     rows = seqs * length
     ri, ro, cc, share = weight_in.shape[0], weight_out.shape[0], conv_bias.shape[0], step_bias.shape[0]
     heads = share * nf
-    free = 128 - heads
 
     device = slot_devices(stages) ^ me
     feature = (device[:, None] * ri + jnp.arange(ri)[None, :]).reshape(-1)
     order = (jnp.arange(D)[:, None] == feature[None, :]).astype(bf16)
-    slot_hot = (device[:, None] == jnp.arange(nd)[None, :]).astype(bf16)
 
     tall = max(ri, 16)
     wc, later = pack(weight_in, weight_out, in_gain[None], conv_weight, conv_bias[None], gate_gain[None],
-                     jnp.stack([step_bias, decay_log, skip_gain]), ri, tall)
+                     step_bias[None], decay_log[None], skip_gain[None], ri, tall)
     later = lax.all_gather(later, axes, axis=0, tiled=True)
     tok = tokens.reshape(rows, D)
     up = cotangent.reshape(rows, D)
-    seg = segments.reshape(rows // Q, 1, Q)
     wc = gather_stage(wc, stages[0], sizes)
     tok_s = jnp.dot(tok, order, preferred_element_type=bf16)
-    wc, tok_s = before(wc, tok_s)
+    device_rows = jnp.broadcast_to(device.astype(f32)[:, None], (nd, 128))
+    seg = segments.reshape(rows // Q, 1, Q)
+    wc, tok_s, device_rows, seg = before(wc, tok_s, device_rows, seg)
     for stage in stages[1:-1]:
         wc = gather_stage(wc, stage, sizes)
     up_s = jnp.dot(up, order, preferred_element_type=bf16)
@@ -748,47 +853,38 @@
     halves = [part.reshape(nd // 2, tall, CONV + 256) for part in (wc, wc_b)]
     small = jnp.concatenate([part[:, :16, CONV + 128 :] for part in halves], axis=0).transpose(1, 0, 2).astype(f32)
     wc_a, wc_b = [part[:, :ri].reshape(D // 2, CONV + 256) for part in halves]
-    device_rows = jnp.broadcast_to(device.astype(f32)[:, None], (nd, 128))
 
     cin, act, dact, nrm, scan, st, z, gain, gain_abs, cw, cb, gg, head_terms, skip = forward_scan(
         tok_s, wc_a, wc_b, small, device_rows, seg, seqs, ri, ro, share, heads)
     mixed, dscan, dgate, early, wo = gate_pass(tok, scan, up, later, gain_abs, gg, ri)
     early = lax.psum_scatter(early, axes, scatter_dimension=0, tiled=True)
 
-    dproj, gcw, gcb, gsk, ghd = backward_scan(
-        dscan, cin, act, dact, z, st, cw, head_terms, skip, seg, heads, seqs)
-    taps = 0.5 * jnp.concatenate([gcw.reshape(4, 8, CONV).sum(1), gcb.sum(0)[None]], axis=0)
-    taps = taps.reshape(5, nd, cc).transpose(1, 0, 2).reshape(nd, 5 * cc)
-    sums = jnp.stack([ghd[:8].sum(0)[:heads], ghd[8:16].sum(0)[:heads],
-                            gsk.sum(0).reshape(heads, HD).sum(1)])
-    sums = jnp.tile(sums.reshape(3, nf, share).transpose(1, 0, 2).reshape(nf, 3 * share), (nd // nf, 1))
-    terms = jnp.concatenate([taps, sums], axis=1)
-    hi = lax.reduce_precision(terms, 8, 7)
-    both = jnp.concatenate([hi, terms - hi], axis=1).astype(bf16)
-    both = jnp.dot(slot_hot, both, preferred_element_type=f32).astype(bf16)
-    width = 5 * cc + 3 * share
-    both = jnp.pad(both, ((0, 0), (0, ri * free - 2 * width))).reshape(D, free)
-    gwc = conv_weight_grad(nrm, dproj, jnp.pad(both, ((0, 0), (heads, 0))))
-    total = gwc.reshape([g for _, _, g, _ in stages[::-1]] + [ri, CONV + 128])
-    for at, stage in enumerate(stages[::-1]):
-        if at == len(stages) - 2:
-            total, gain = before(total, gain)
-            gtok = norm_back(dproj, dgate, tok_s, up_s, wc_a, wc_b, later, gain, order, 0, 4)
-        if at == len(stages) - 1:
-            total, gtok, wo, early = before(total, gtok, wo, early)
+    dproj, gproj, small = backward_scan(
+        dscan, cin, act, dact, z, st, cw, head_terms, skip, seg, wc_a, wc_b, device_rows, heads, seqs, nf, share, tall)
+    if ri == tall:
+        halves = conv_weight_grad(nrm, dproj, small)
+        halves = [half.reshape(nd // 2, tall, CONV + 128) for half in halves]
+    else:
+        halves = conv_weight_grad(nrm, dproj, jnp.zeros((D, 128), bf16))
+        halves = [jnp.pad(half.reshape(nd // 2, ri, CONV + 128), ((0, 0), (0, tall - ri), (0, 0))) for half in halves]
+        small = jnp.pad(small.reshape(nd, tall, 128), ((0, 0), (0, 0), (CONV, 0)))
+        halves = [half + part for half, part in zip(halves, (small[: nd // 2], small[nd // 2 :]))]
+
+    axis, stride, group, _ = stages[-1]
+    total = halves[0].astype(f32) + swap(halves[1], axis, sizes[axis], stride).astype(f32)
+    total = total.reshape([g for _, _, g, _ in stages[-2::-1]] + [tall, CONV + 128])
+    total, gain = before(total, gain)
+    gtok = norm_back(gproj, dgate, tok_s, up_s, later, gain, device_rows, ri)
+    for stage in stages[-2:0:-1]:
         total = scatter_stage(total, stage, sizes)
+    total, gtok, wo = before(total, gtok, wo)
+    got = scatter_parts(total, stages[0], sizes)
     out = out_pass(mixed, tok, wo)
-
-    early = early.astype(f32)
-    g_in = jnp.concatenate([early[:, :DI], total[:, : CONV + heads]], axis=1)
-    g_out = jnp.concatenate([early[:, DI : DI + D], early[:, DI + D :]], axis=0)
-    packed = total[:, CONV + heads :].reshape(-1)
-    packed = packed[:width] + packed[width : 2 * width]
-    g_in_gain = jnp.sum(weight_in.astype(f32) * g_in, axis=1) / in_gain.astype(f32)
-    g_gate_gain = jnp.sum(weight_out.astype(f32) * g_out, axis=1) / gate_gain.astype(f32)
-    by_head = packed[5 * cc :].reshape(3, share)
-    return (out.reshape(tokens.shape), gtok.reshape(tokens.shape), g_in_gain, g_in, packed[: 4 * cc].reshape(4, cc),
-            packed[4 * cc : 5 * cc], by_head[0], by_head[1], by_head[2], g_gate_gain, g_out)
+    early, out = before(early, out)
+    g_in, g_out, g_in_gain, g_gate_gain, g_cw, g_cb, g_sb, g_dl, g_sg = finish(
+        early, weight_in, weight_out, in_gain[None], gate_gain[None], total[0], got, heads, share, cc)
+    return (out.reshape(tokens.shape), gtok.reshape(tokens.shape), g_in_gain[0], g_in, g_cw, g_cb[0],
+            g_sb[0], g_dl[0], g_sg[0], g_gate_gain[0], g_out)
 
 
 def solution(mesh):

time: 280 us -> 262 us (0.936)
  other arithmetic: 13.3 us -> 3.91 us
  local copies, waits for them, and re-layouts: 10 us -> 5.82 us
    reduce_sum x7 -> x0, other arithmetic: 5.14 us -> none  [the longest x1 1.01 us: local(): gcw.reshape(4, 8, CONV).sum(1)]
    slice x7 -> x0, local copies, waits for them, and re-layouts: 4.97 us -> none  [the longest x1 2.03 us: scatter_stage(): got = [swap(low[k], axis, sizes[axis], k * stride) for k in range(1, group)]]
    unnamed x18 -> x28, local copies, waits for them, and re-layouts: 0.08 us -> 3.61 us
    pallas_call x2 -> x3, Pallas kernels: 88.3 us -> 86.6 us  [the longest x1 68.5 us: backward_scan(): pl.pallas_call(functools.partial(backward_scan_kernel, heads, n // seqs,...]
  transfers between devices with their start and end apart: 16 -> 16, of which waited for: 6 -> 6; matrix products, arithmetic and copies ran while one was open for 10% -> 6% of each run, Pallas kernels for 54% -> 56%
where the time goes in v4:
time: 262 us
  Pallas kernels  190 us (73%)
  waiting for transfers between devices  19 us (7%)
  starting transfers between devices  17.5 us (7%)
  between operations  14.3 us (5%)
  matrix products  10.8 us (4%)
  local copies, waits for them, and re-layouts  5.82 us (2%)
  other arithmetic  3.91 us (1%)
    pallas_call x1, Pallas kernels, backward_scan(): pl.pallas_call(functools.partial(backward_scan_kernel, heads, n // seqs,...  68.5 us
    pallas_call x1, Pallas kernels, forward_scan(): pl.pallas_call(functools.partial(forward_scan_kernel, heads, n // seqs, r...  42.4 us
    pallas_call x1, Pallas kernels, gate_pass(): pl.pallas_call(functools.partial(gate_kernel, ri), grid=(rows // bm,), in...  38.6 us
    ppermute x14, waiting for transfers between devices, swap(): return lax.ppermute(arr, axis, [(i, i ^ offset) for i in range(size)])  18.9 us
    ppermute x14, starting transfers between devices, swap(): return lax.ppermute(arr, axis, [(i, i ^ offset) for i in range(size)])  17.4 us
    pallas_call x1, Pallas kernels, norm_back(): pl.pallas_call(functools.partial(norm_back_kernel, ri), grid=(rows // bm,...  16 us
    pallas_call x1, Pallas kernels, conv_weight_grad(): pl.pallas_call(conv_weight_kernel, grid=((CONV + 128) // bn,), in_specs=[...  11 us
    pallas_call x1, Pallas kernels, out_pass(): pl.pallas_call(out_kernel, grid=(rows // bm,), in_specs=[blk(DI), blk(D),...  9.96 us
  transfers between devices with their start and end apart: 16, of which 6 were waited for; matrix products, arithmetic and copies ran while one was open for 6% of the time, Pallas kernels for 56%

profile of v4, /device:TPU:0, one launch (start us, length us, event | category | flops | bytes accessed | tf_op | source)
XLA Modules:
  0.0 261.6 jit_solution(4621046241216275000)
XLA Ops:
  7.2 0.0 all-gather.2.cloned.1.call-start
  7.2 1.7 pack.1
  8.9 0.0 all-gather.2.cloned.1.call-update
  9.0 0.0 reduce-scatter.2.cloned.1.call-start
  9.0 5.1 %collective-permute-start.2 = (bf16[24,2048]{1,0:T(8,128)(2,1)}, bf16[24,2048]{1,0:T(8,128)(2,1)S(1)}, u32[]{:S(2)}, u32[]{:S(2)}) collective-permute-start(bf16[24,2048]{1,0:T(8,128)(2,1)} %get-tuple-element.58), channel_id=1, source_target_pairs={{0,24},{2,26},{4,28},{6,30},{8,16},{10,18},{12,20},{14,22},{16,8},... | collective-permute-start | bytes 294920 | tf_op jit(solution)/shard_map/ppermute | solution.py:795
  14.1 0.0 collective-permute-start.1
  14.1 0.6 collective-permute-start
  14.8 0.7 xor_convert_fusion
  15.4 0.1 iota_add_fusion
  15.5 0.1 add.41
  15.6 0.0 copy-start.10
  15.6 0.0 copy-start.6
  15.6 6.3 %convolution_bitcast_fusion.1.first.tok = bf16[2048,768]{1,0:T(8,128)(2,1)} fusion(bf16[2048,768]{1,0:T(8,128)(2,1)} %bitcast.67, s32[768]{0:T(1024)S(1)} %add.41), kind=kOutput, calls=%fused_computation.1 | convolution fusion | flops 2416508928 | bytes 6294528 | tf_op jit(solution)/shard_map/dot_general | solution.py:844
  21.9 0.6 reshape.70.seg.seg_before
  22.5 0.0 collective-permute-done.2
  22.5 0.1 collective-permute-done.1
  22.6 0.0 collective-permute-done
  22.6 0.1 pad_maximum_fusion.1
  22.7 0.7 broadcast_in_dim.35.device
  23.3 2.5 collective-permute-start.5
  25.8 0.5 collective-permute-start.4
  26.4 0.5 collective-permute-start.3
  26.8 4.6 %convolution_bitcast_fusion.cot = bf16[2048,768]{1,0:T(8,128)(2,1)S(1)} fusion(bf16[2048,768]{1,0:T(8,128)(2,1)} %bitcast.74, s32[768]{0:T(1024)S(1)} %add.41), kind=kOutput, calls=%fused_computation | convolution fusion | flops 2416508928 | bytes 6294528 | tf_op jit(solution)/shard_map/dot_general | solution.py:850
  31.4 4.9 %collective-permute-done.5 = bf16[4,24,2048]{2,1,0:T(8,128)(2,1)S(1)} collective-permute-done((bf16[4,24,2048]{2,1,0:T(8,128)(2,1)S(1)}, bf16[4,24,2048]{2,1,0:T(8,128)(2,1)S(1)}, u32[]{:S(2)}, u32[]{:S(2)}) %collective-permute-start.5) | collective-permute-done | bytes 393248 | tf_op jit(solution)/shard_map/ppermute | solution.py:795
  36.3 7.3 %collective-permute-done.4 = bf16[4,24,2048]{2,1,0:T(8,128)(2,1)S(1)} collective-permute-done((bf16[4,24,2048]{2,1,0:T(8,128)(2,1)S(1)}, bf16[4,24,2048]{2,1,0:T(8,128)(2,1)S(1)}, u32[]{:S(2)}, u32[]{:S(2)}) %collective-permute-start.4) | collective-permute-done | bytes 393248 | tf_op jit(solution)/shard_map/ppermute | solution.py:795
  43.6 0.0 collective-permute-done.3
  43.6 0.2 pad_maximum_fusion
  43.8 0.1 collective-permute-start.6
  43.9 1.1 copy-done.4
  45.1 2.3 collective-permute-done.6
  47.3 1.2 copy-done.5
  48.5 0.7 convert_bitcast_fusion.small
  49.3 42.4 %forward_scan.1 = (bf16[2048,1792]{1,0:T(8,128)(2,1)}, bf16[2048,1792]{1,0:T(8,128)(2,1)}, bf16[2048,1792]{1,0:T(8,128)(2,1)}, bf16[2048,768]{1,0:T(8,128)(2,1)}...) custom-call(bf16[2048,768]{1,0:T(8,128)(2,1)} %convolution_bitcast_f, ...), custom_call_target="tpu_custom_call" | custom-call | tf_op jit(solution)/shard_map/forward_scan/pallas_call | solution.py:275
  91.6 0.0 all-gather.2.cloned.1.call-done.later.wg_abs
  91.7 38.6 %gate_pass.1 = (bf16[2048,1536]{1,0:T(8,128)(2,1)}, bf16[2048,1536]{1,0:T(8,128)(2,1)}, bf16[2048,1536]{1,0:T(8,128)(2,1)}, bf16[768,3072]{1,0:T(8,128)(2,1)}, bf16[1536,768]{1,0:T(8,128)(2,1)}) custom-call(bf16[2048,768]{1,0:T(8,128)(2,1)} %bitcast.68, bf16[2048,1536]{1,0:T(8,128)(2,1)} %get-tuple-element.64.scan, bf16[2048,768]{1,0:T(8,128)(2,1)} %bitcast.75, ...), custom_call_target="tpu_custom_call" | custom-call | tf_op jit(solution)/shard_map/gate_pass/pallas_call | solution.py:412
  130.3 0.0 reduce-scatter.2.cloned.1.call-update
  130.3 68.5 %backward_scan.1 = (bf16[2048,1920]{1,0:T(8,128)(2,1)}, bf16[2048,768]{1,0:T(8,128)(2,1)}, bf16[768,128]{1,0:T(8,128)(2,1)}) custom-call(bf16[2048,1536]{1,0:T(8,128)(2,1)} %get-tuple-element.71.dscan, bf16[2048,1792]{1,0:T(8,128)(2,1)} %get-tuple-element.72.cin, bf16[2048,1792]{1,0:T(8,128)(2,1)} %get-tuple-element.73.act, ...), custom_call_target="tpu_custom_call" | custom-call | tf_op jit(solution)/shard_map/backward_scan/pallas_call | solution.py:632
  198.8 0.0 slice-start
  198.8 11.0 %conv_weight_grad.1 = (bf16[384,1920]{1,0:T(8,128)(2,1)}, bf16[384,1920]{1,0:T(8,128)(2,1)}) custom-call(bf16[2048,768]{1,0:T(8,128)(2,1)} %get-tuple-element.70.nrm, bf16[2048,1920]{1,0:T(8,128)(2,1)} %get-tuple-element.80.dproj, bf16[768,128]{1,0:T(8,128)(2,1)} %get-tuple-element.81.small), custom_call_target="tpu_custom_call" | custom-call | tf_op jit(solution)/shard_map/conv_weight_grad/pallas_call | solution.py:711
  209.8 0.1 collective-permute-start.7
  209.9 3.4 %collective-permute-done.7 = bf16[16,24,1920]{2,1,0:T(8,128)(2,1)S(1)} collective-permute-done((bf16[16,24,1920]{2,1,0:T(8,128)(2,1)}, bf16[16,24,1920]{2,1,0:T(8,128)(2,1)S(1)}, u32[]{:S(2)}, u32[]{:S(2)}) %collective-permute-start.7) | collective-permute-done | bytes 1474592 | tf_op jit(solution)/shard_map/ppermute | solution.py:795
  213.3 1.8 convert_add_fusion
  215.1 0.0 copy-start
  215.2 0.2 convert_element_type.39
  215.3 0.1 slice_bitcast_fusion.2
  215.4 1.4 collective-permute-start.10
  216.8 1.5 collective-permute-start.9
  218.3 0.7 collective-permute-start.8
  219.0 16.0 %norm_back.1 = bf16[2048,768]{1,0:T(8,128)(2,1)} custom-call(bf16[2048,768]{1,0:T(8,128)(2,1)S(1)} %copy-done.1, bf16[2048,1536]{1,0:T(8,128)(2,1)} %get-tuple-element.87.dgate, bf16[2048,768]{1,0:T(8,128)(2,1)S(1)} %copy-done, bf16[2048,768]{1,0:T(8,128)(2,1)S(1)} %convolution_bitcast_fusion.cot, bf16[768,3072]{1,0:T(8,128)(2,1)S(1)} %bitcast.61, ...), custom_call_target="tpu_custom_call" | custom-call | tf_op jit(solution)/shard_map/norm_back/pallas_call | solution.py:680
  235.0 0.0 collective-permute-done.10
  235.0 1.0 collective-permute-done.9
  236.0 0.0 collective-permute-done.8
  236.0 0.2 fusion.3
  236.2 1.4 collective-permute-start.11
  237.7 2.7 %collective-permute-start.12 = (bf16[24,1920]{1,0:T(8,128)(2,1)S(1)}, bf16[24,1920]{1,0:T(8,128)(2,1)S(1)}, u32[]{:S(2)}, u32[]{:S(2)}) collective-permute-start(bf16[24,1920]{1,0:T(8,128)(2,1)S(1)} %get-tuple-element.109), channel_id=1, source_target_pairs={{0,16},{2,18},{4,20},{6,22},{8,24},{10,26},{12,28},{14,30},{16,0},... | collective-permute-start | bytes 276488 | tf_op jit(solution)/shard_map/ppermute | solution.py:795
  240.3 0.4 collective-permute-start.13
  240.7 0.7 slice_bitcast_fusion.3.refs_0_
  241.4 10.0 %out_pass.1 = bf16[2048,768]{1,0:T(8,128)(2,1)} custom-call(bf16[2048,1536]{1,0:T(8,128)(2,1)} %get-tuple-element.69.mixed, bf16[2048,768]{1,0:T(8,128)(2,1)} %bitcast.69, bf16[1536,768]{1,0:T(8,128)(2,1)} %get-tuple-element.91.wo), custom_call_target="tpu_custom_call" | custom-call | tf_op jit(solution)/shard_map/out_pass/pallas_call | solution.py:434
  251.4 0.0 collective-permute-done.12.refs_2_
  251.4 0.0 collective-permute-done.13.refs_3_
  251.4 0.6 copy-done.7
  252.0 0.0 copy-done.8
  252.0 0.6 copy-done.9
  252.7 2.1 finish.1
  (26 shorter events, 0.2 us)
Async XLA Ops:
  7.2 84.5 %all-gather.2.cloned.1.call-start = ((), (), s32[]{:S(2)}) async-start(), calls=%async_computation.1 | async-start | bytes 4866048 | tf_op jit(solution)/shard_map/all_gather | solution.py:840
  9.0 242.4 %reduce-scatter.2.cloned.1.call-start = ((), (), s32[]{:S(2)}) async-start(), calls=%async_computation.2 | async-start | bytes 4866048 | tf_op jit(solution)/shard_map/reduce_scatter | solution.py:860
  9.0 13.5 %collective-permute-start.2 = (bf16[24,2048]{1,0:T(8,128)(2,1)}, bf16[24,2048]{1,0:T(8,128)(2,1)S(1)}, u32[]{:S(2)}, u32[]{:S(2)}) collective-permute-start(bf16[24,2048]{1,0:T(8,128)(2,1)} %get-tuple-element.58), channel_id=1, source_target_pairs={{0,24},{2,26},{4,28},{6,30},{8,16},{10,18},{12,20},{14,22},{16,8},... | collective-permute-start | bytes 294920 | tf_op jit(solution)/shard_map/ppermute | solution.py:795
  14.1 8.5 %collective-permute-start.1 = (bf16[24,2048]{1,0:T(8,128)(2,1)}, bf16[24,2048]{1,0:T(8,128)(2,1)S(1)}, u32[]{:S(2)}, u32[]{:S(2)}) collective-permute-start(bf16[24,2048]{1,0:T(8,128)(2,1)} %get-tuple-element.58), channel_id=1, source_target_pairs={{0,16},{2,18},{4,20},{6,22},{8,24},{10,26},{12,28},{14,30},{16,0},... | collective-permute-start | bytes 294920 | tf_op jit(solution)/shard_map/ppermute | solution.py:795
  14.1 8.5 %collective-permute-start = (bf16[24,2048]{1,0:T(8,128)(2,1)}, bf16[24,2048]{1,0:T(8,128)(2,1)S(1)}, u32[]{:S(2)}, u32[]{:S(2)}) collective-permute-start(bf16[24,2048]{1,0:T(8,128)(2,1)} %get-tuple-element.58), channel_id=1, source_target_pairs={{0,8},{2,10},{4,12},{6,14},{8,0},{10,2},{12,4},{14,6},{16,24},{18,... | collective-permute-start | bytes 294920 | tf_op jit(solution)/shard_map/ppermute | solution.py:795
  15.6 6.3 %copy-start.10 = (s32[2,1024]{1,0:T(2,128)S(1)}, s32[2,1024]{1,0:T(2,128)}, u32[]{:S(2)}) copy-start(s32[2,1024]{1,0:T(2,128)} %param.15) | copy-start | bytes 24580
  15.6 7.0 %copy-start.6 = (bf16[24,2048]{1,0:T(8,128)(2,1)S(1)}, bf16[24,2048]{1,0:T(8,128)(2,1)}, u32[]{:S(2)}) copy-start(bf16[24,2048]{1,0:T(8,128)(2,1)} %get-tuple-element.58) | copy-start | bytes 294916
  23.3 13.0 %collective-permute-start.5 = (bf16[4,24,2048]{2,1,0:T(8,128)(2,1)S(1)}, bf16[4,24,2048]{2,1,0:T(8,128)(2,1)S(1)}, u32[]{:S(2)}, u32[]{:S(2)}) collective-permute-start(bf16[4,24,2048]{2,1,0:T(8,128)(2,1)S(1)} %pad_maximum_fusion.1), channel_id=1, source_target_pairs={{0,6},{2,4},{4,2},{6,0},{8,14},{10,12},{12,10},{14,8},{16,22},{18,... | collective-permute-start | bytes 1179656 | tf_op jit(solution)/shard_map/ppermute | solution.py:795
  25.8 17.8 %collective-permute-start.4 = (bf16[4,24,2048]{2,1,0:T(8,128)(2,1)S(1)}, bf16[4,24,2048]{2,1,0:T(8,128)(2,1)S(1)}, u32[]{:S(2)}, u32[]{:S(2)}) collective-permute-start(bf16[4,24,2048]{2,1,0:T(8,128)(2,1)S(1)} %pad_maximum_fusion.1), channel_id=1, source_target_pairs={{0,4},{2,6},{4,0},{6,2},{8,12},{10,14},{12,8},{14,10},{16,20},{18,... | collective-permute-start | bytes 1179656 | tf_op jit(solution)/shard_map/ppermute | solution.py:795
  26.4 17.3 %collective-permute-start.3 = (bf16[4,24,2048]{2,1,0:T(8,128)(2,1)S(1)}, bf16[4,24,2048]{2,1,0:T(8,128)(2,1)S(1)}, u32[]{:S(2)}, u32[]{:S(2)}) collective-permute-start(bf16[4,24,2048]{2,1,0:T(8,128)(2,1)S(1)} %pad_maximum_fusion.1), channel_id=1, source_target_pairs={{0,2},{2,0},{4,6},{6,4},{8,10},{10,8},{12,14},{14,12},{16,18},{18,... | collective-permute-start | bytes 1179656 | tf_op jit(solution)/shard_map/ppermute | solution.py:795
  43.8 1.2 copy-start.4
  43.8 3.5 %collective-permute-start.6 = (bf16[4,4,24,2048]{3,2,1,0:T(8,128)(2,1)S(1)}, bf16[4,4,24,2048]{3,2,1,0:T(8,128)(2,1)S(1)}, u32[]{:S(2)}, u32[]{:S(2)}) collective-permute-start(bf16[4,4,24,2048]{3,2,1,0:T(8,128)(2,1)S(1)} %pad_maximum_fusion), channel_id=1, source_target_pairs={{0,1},{1,0},{2,3},{3,2},{4,5},{5,4},{6,7},{7,6},{8,9},{9,8},{10,11... | collective-permute-start | bytes 4718600 | tf_op jit(solution)/shard_map/ppermute | solution.py:795
  47.3 1.2 copy-start.5
  198.8 20.1 %slice-start = ((s8[4718592]{0:T(1024)(128)(4,1)}), s8[524288]{0:T(1024)(128)(4,1)S(1)}, s32[]{:S(2)}) async-start(s8[4718592]{0:T(1024)(128)(4,1)} %bitcast.60), calls=%async_computation.3 | async-start | bytes 1048576
  209.8 3.5 %collective-permute-start.7 = (bf16[16,24,1920]{2,1,0:T(8,128)(2,1)}, bf16[16,24,1920]{2,1,0:T(8,128)(2,1)S(1)}, u32[]{:S(2)}, u32[]{:S(2)}) collective-permute-start(bf16[16,24,1920]{2,1,0:T(8,128)(2,1)} %bitcast.94), channel_id=1, source_target_pairs={{0,1},{1,0},{2,3},{3,2},{4,5},{5,4},{6,7},{7,6},{8,9},{9,8},{10,11... | collective-permute-start | bytes 4423688 | tf_op jit(solution)/shard_map/ppermute | solution.py:795
  213.3 5.7 %slice-start.1 = ((s8[4718592]{0:T(1024)(128)(4,1)}), s8[4194304]{0:T(1024)(128)(4,1)S(1)}, s32[]{:S(2)}) async-start(s8[4718592]{0:T(1024)(128)(4,1)} %bitcast.60), calls=%async_computation.4 | async-start | bytes 8388608
  215.1 3.9 %copy-start = (bf16[2048,768]{1,0:T(8,128)(2,1)S(1)}, bf16[2048,768]{1,0:T(8,128)(2,1)}, u32[]{:S(2)}) copy-start(bf16[2048,768]{1,0:T(8,128)(2,1)} %convolution_bitcast_fusion.1.first.tok) | copy-start | bytes 9437188
  215.1 3.8 %copy-start.1 = (bf16[2048,768]{1,0:T(8,128)(2,1)S(1)}, bf16[2048,768]{1,0:T(8,128)(2,1)}, u32[]{:S(2)}) copy-start(bf16[2048,768]{1,0:T(8,128)(2,1)} %get-tuple-element.86.gproj) | copy-start | bytes 9437188
  215.1 3.8 %copy-start.2 = (f32[32,128]{1,0:T(8,128)S(1)}, f32[32,128]{1,0:T(8,128)}, u32[]{:S(2)}) copy-start(f32[32,128]{1,0:T(8,128)} %broadcast_in_dim.35.device) | copy-start | bytes 49156
  215.2 3.8 %copy-start.3 = (f32[1,768]{1,0:T(1,128)S(1)}, f32[1,768]{1,0:T(1,128)}, u32[]{:S(2)}) copy-start(f32[1,768]{1,0:T(1,128)} %get-tuple-element.89.gain) | copy-start | bytes 9220
  215.4 19.6 %collective-permute-start.10 = (bf16[4,24,1920]{2,1,0:T(8,128)(2,1)S(1)}, bf16[4,24,1920]{2,1,0:T(8,128)(2,1)S(1)}, u32[]{:S(2)}, u32[]{:S(2)}) collective-permute-start(bf16[4,24,1920]{2,1,0:T(8,128)(2,1)S(1)} %get-tuple-element.106), channel_id=1, source_target_pairs={{0,6},{2,4},{4,2},{6,0},{8,14},{10,12},{12,10},{14,8},{16,22},{18,... | collective-permute-start | bytes 1105928 | tf_op jit(solution)/shard_map/ppermute | solution.py:795
  216.8 19.1 %collective-permute-start.9 = (bf16[4,24,1920]{2,1,0:T(8,128)(2,1)S(1)}, bf16[4,24,1920]{2,1,0:T(8,128)(2,1)S(1)}, u32[]{:S(2)}, u32[]{:S(2)}) collective-permute-start(bf16[4,24,1920]{2,1,0:T(8,128)(2,1)S(1)} %get-tuple-element.107), channel_id=1, source_target_pairs={{0,4},{2,6},{4,0},{6,2},{8,12},{10,14},{12,8},{14,10},{16,20},{18,... | collective-permute-start | bytes 1105928 | tf_op jit(solution)/shard_map/ppermute | solution.py:795
  218.3 17.7 %collective-permute-start.8 = (bf16[4,24,1920]{2,1,0:T(8,128)(2,1)S(1)}, bf16[4,24,1920]{2,1,0:T(8,128)(2,1)S(1)}, u32[]{:S(2)}, u32[]{:S(2)}) collective-permute-start(bf16[4,24,1920]{2,1,0:T(8,128)(2,1)S(1)} %get-tuple-element.105), channel_id=1, source_target_pairs={{0,2},{2,0},{4,6},{6,4},{8,10},{10,8},{12,14},{14,12},{16,18},{18,... | collective-permute-start | bytes 1105928 | tf_op jit(solution)/shard_map/ppermute | solution.py:795
  236.2 15.1 %collective-permute-start.11 = (bf16[24,1920]{1,0:T(8,128)(2,1)S(1)}, bf16[24,1920]{1,0:T(8,128)(2,1)S(1)}, u32[]{:S(2)}, u32[]{:S(2)}) collective-permute-start(bf16[24,1920]{1,0:T(8,128)(2,1)S(1)} %get-tuple-element.110), channel_id=1, source_target_pairs={{0,8},{2,10},{4,12},{6,14},{8,0},{10,2},{12,4},{14,6},{16,24},{18,... | collective-permute-start | bytes 276488 | tf_op jit(solution)/shard_map/ppermute | solution.py:795
  237.7 13.7 %collective-permute-start.12 = (bf16[24,1920]{1,0:T(8,128)(2,1)S(1)}, bf16[24,1920]{1,0:T(8,128)(2,1)S(1)}, u32[]{:S(2)}, u32[]{:S(2)}) collective-permute-start(bf16[24,1920]{1,0:T(8,128)(2,1)S(1)} %get-tuple-element.109), channel_id=1, source_target_pairs={{0,16},{2,18},{4,20},{6,22},{8,24},{10,26},{12,28},{14,30},{16,0},... | collective-permute-start | bytes 276488 | tf_op jit(solution)/shard_map/ppermute | solution.py:795
  240.3 11.1 %collective-permute-start.13 = (bf16[24,1920]{1,0:T(8,128)(2,1)S(1)}, bf16[24,1920]{1,0:T(8,128)(2,1)S(1)}, u32[]{:S(2)}, u32[]{:S(2)}) collective-permute-start(bf16[24,1920]{1,0:T(8,128)(2,1)S(1)} %get-tuple-element.108), channel_id=1, source_target_pairs={{0,24},{2,26},{4,28},{6,30},{8,16},{10,18},{12,20},{14,22},{16,8},... | collective-permute-start | bytes 276488 | tf_op jit(solution)/shard_map/ppermute | solution.py:795
  251.4 0.6 copy-start.7
  251.4 0.6 copy-start.8
  252.0 0.6 copy-start.9
Sparse Core Ops, SparseCore 0:
  11.5 74.1 all-gather.1
  130.4 107.8 reduce-scatter.1

commit v5 on v4

--- a/solution.py
+++ b/solution.py
@@ -100,17 +100,22 @@
     wc_o[...] = jnp.zeros_like(wc_o)
     wc_o[0:ri, : w_in.shape[1] - DI] = w_in[:, DI:]
     rows[...] = jnp.zeros_like(rows)
-    rows[0:1, : in_gain.shape[1]] = in_gain[...].astype(f32)
-    rows[1:5, : cw.shape[1]] = cw[...].astype(f32)
-    rows[5:6, : cb.shape[1]] = cb[...].astype(f32)
-    rows[6:7, : gg.shape[1]] = gg[...].astype(f32)
+    at = w_in.shape[1] - DI - CONV
+
+    def put(n, value):
+        rows[n : n + value.shape[0], at : at + value.shape[1]] = value.astype(f32)
+
+    put(0, in_gain[...])
+    put(1, cw[...])
+    put(5, cb[...])
+    put(6, gg[...])
     for k, term in enumerate((sb, dl, sg)):
         value = term[...]
         for n in range(3):
             part = value.astype(bf16).astype(f32)
-            rows[7 + 3 * n + k : 8 + 3 * n + k, : value.shape[1]] = part
+            put(7 + 3 * n + k, part)
             value = value - part
-    wc_o[0:16, CONV + 128 :] = rows[...].astype(bf16)
+    wc_o[0:16, CONV:] = (wc_o[0:16, CONV:].astype(f32) + rows[...]).astype(bf16)
     later_o[:, :DI] = w_in[:, :DI]
     later_o[:, DI : DI + D] = w_out[0:ri, :]
     later_o[:, DI + D :] = w_out[ri:, :]
@@ -119,13 +124,13 @@
 def pack(w_in, w_out, in_gain, cw, cb, gg, sb, dl, sg, ri, tall):
     return pl.pallas_call(
         functools.partial(pack_kernel, ri),
-        out_shape=[jax.ShapeDtypeStruct((tall, CONV + 256), bf16), jax.ShapeDtypeStruct((ri, 2 * DI), bf16)],
+        out_shape=[jax.ShapeDtypeStruct((tall, CONV + 128), bf16), jax.ShapeDtypeStruct((ri, 2 * DI), bf16)],
         scratch_shapes=[pltpu.VMEM((16, 128), f32)],
         name="pack",
     )(w_in, w_out, in_gain, cw, cb, gg, sb, dl, sg)
 
 
-def unpack_small(ri, ro, share, small, device, onehot, gain, gain_abs, cw, cb, gg, heads_o, skip):
+def unpack_small(ri, ro, share, first_lane, small, device, onehot, gain, gain_abs, cw, cb, gg, heads_o, skip):
     nd = small.shape[1]
     slot = lax.broadcasted_iota(jnp.int32, (nd, 128), 0).astype(f32)[:, 0:1]
     owner = device[...][:, 0:1]
@@ -134,9 +139,10 @@
         lane = lax.broadcasted_iota(jnp.int32, (128, total), 1).astype(f32)
         piece = jnp.floor((lane + 0.5) * (1.0 / width))
         inner = lane - piece * width
-        pick = (lax.broadcasted_iota(jnp.int32, (128, total), 0).astype(f32) == inner).astype(bf16)
+        pick = (lax.broadcasted_iota(jnp.int32, (128, total), 0).astype(f32) - first_lane == inner).astype(bf16)
         mine = piece[0:1, :] == who
-        return [jnp.sum(jnp.where(mine, dot(small[r].astype(bf16), pick), 0.0), axis=0, keepdims=True) for r in rows]
+        out = dot(jnp.concatenate([small[r].astype(bf16) for r in rows], axis=0), pick)
+        return [jnp.sum(jnp.where(mine, out[nd * n : nd * n + nd], 0.0), axis=0, keepdims=True) for n in range(len(rows))]
 
     gain[...] = spread([0], ri, D, slot)[0]
     gain_abs[...] = spread([0], ri, D, owner)[0]
@@ -153,6 +159,11 @@
     skip[...] = dot(two_parts(jnp.broadcast_to(per_head[2], (8, 128))), onehot[...])[0:1, :]
 
 
+def clear_free(wc, heads):
+    last = wc[:, CONV:]
+    wc[:, CONV:] = jnp.where(lax.broadcasted_iota(jnp.int32, last.shape, 1) < heads, last, jnp.zeros_like(last))
+
+
 def forward_scan_kernel(heads, per_seq, ri, ro, share, first, tok, wc_a, wc_b, small, device, seg, seg_before,
                         cin_o, act_o, dact_o, nrm_o, scan_o, st_o, z_o, gain, gain_abs, cw, cb, gg, heads_o, skip,
                         pbuf, zbuf, nbuf, pnext, znext, nnext, state, docs, onehot, wc, sems):
@@ -180,15 +191,16 @@
     @pl.when(i == 0)
     def _():
         rows = wc_a.shape[0]
-        copies = [pltpu.make_async_copy(wc_a.at[:, : CONV + 128], wc.at[0:rows], sems.at[0]),
-                  pltpu.make_async_copy(wc_b.at[:, : CONV + 128], wc.at[rows : 2 * rows], sems.at[1])]
+        copies = [pltpu.make_async_copy(wc_a, wc.at[0:rows], sems.at[0]),
+                  pltpu.make_async_copy(wc_b, wc.at[rows : 2 * rows], sems.at[1])]
         for copy in copies:
             copy.start()
         onehot[...] = head_onehot(onehot.shape)
-        unpack_small(ri, ro, share, small, device, onehot, gain, gain_abs, cw, cb, gg, heads_o, skip)
+        unpack_small(ri, ro, share, heads, small, device, onehot, gain, gain_abs, cw, cb, gg, heads_o, skip)
         normed(first)
         for copy in copies:
             copy.wait()
+        clear_free(wc, heads)
         for t in range(0, tiles, 2):
             project(t)
         project_step()
@@ -223,9 +235,10 @@
         for k in range(3):
             half = half + cw[k : k + 1, cols] * (pbuf[t, 5 + k : 5 + k + Q, :] * masks[k])
         pbuf[t, 0:8, :] = pbuf[t, Q : Q + 8, :]
-        th = jnp.tanh(half)
-        dact_o[:, cols] = ((1.0 + th) * (1.0 + half * (1.0 - th))).astype(bf16)
-        act = (half + half * th).astype(bf16)
+        up = 1.0 + jnp.tanh(half)
+        act = half * up
+        dact_o[:, cols] = (up + act * (2.0 - up)).astype(bf16)
+        act = act.astype(bf16)
         act_o[:, cols] = act
         return act
 
@@ -286,7 +299,7 @@
                         pltpu.VMEM((CONV // 128, Q, 128), f32), pltpu.VMEM((Q, 128), f32), pltpu.VMEM((Q, D), bf16),
                         pltpu.VMEM((N, DI), f32), pltpu.VMEM((Q + 8, 128), f32), pltpu.VMEM((256, DI), bf16),
                         pltpu.VMEM((D, CONV + 128), bf16), pltpu.SemaphoreType.DMA((2,))],
-        compiler_params=pltpu.CompilerParams(vmem_limit_bytes=VM),
+        compiler_params=pltpu.CompilerParams(vmem_limit_bytes=56 << 20),
         name="forward_scan",
     )(tok, tok, wc_a, wc_b, small, device, seg, seg)
 
@@ -301,21 +314,30 @@
     return (row == target).astype(bf16)
 
 
-def gate_kernel(ri, tok, scan, cot, later, gain, gg, mixed_o, dscan_o, dgate_o, early_o, wo, acc_g, acc_o,
-                nb_s, nbt_s, mixt_s, h_s, e_s, gated_s, eg_s):
+def gate_kernel(ri, tok, scan, cot, later_in, gain, gg, mixed_o, dscan_o, dgate_o, early_o, wo_o, later, wo, early, sems,
+                acc_g, acc_o, nb_s, nbt_s, mixt_s, h_s, e_s, gated_s, eg_s):
     i = pl.program_id(0)
     bm, high = 256, 32
     blocks = tok.shape[0] // bm
 
+    wo_copy = pltpu.make_async_copy(wo, wo_o, sems.at[2])
+
     @pl.when(i == 0)
     def _():
+        copies = [pltpu.make_async_copy(later_in.at[:, cols], later.at[:, cols], sems.at[n])
+                  for n, cols in enumerate((slice(DI, 2 * DI), slice(0, DI)))]
+        for copy in copies:
+            copy.start()
         acc_g[...] = jnp.zeros_like(acc_g)
         acc_o[...] = jnp.zeros_like(acc_o)
+        copies[0].wait()
         put = block_order(ri)
         for g in range(D // 96):
             at = slice(96 * g, 96 * g + 96)
             halves = jnp.concatenate([later[at, DI : DI + D], later[at, DI + D :]], axis=0)
             wo[192 * g : 192 * g + 192, :] = dot(put, halves).astype(bf16)
+        wo_copy.start()
+        copies[1].wait()
 
     x = tok[...].astype(f32)
     r = lax.rsqrt(jnp.mean(x * x, axis=-1, keepdims=True) + EPS)
@@ -394,13 +416,18 @@
 
     @pl.when(i == pl.num_programs(0) - 1)
     def _():
-        early_o[:, :DI] = (0.5 * acc_g[...]).astype(bf16)
         put = block_order(ri)
         for g in range(D // 96):
             at = slice(96 * g, 96 * g + 96)
+            early[at, :DI] = (0.5 * acc_g[at, :]).astype(bf16)
             halves = dot_tn(put, acc_o[192 * g : 192 * g + 192, :].astype(bf16)).astype(bf16)
-            early_o[at, DI : DI + D] = halves[:96]
-            early_o[at, DI + D :] = halves[96:]
+            early[at, DI : DI + D] = halves[:96]
+            early[at, DI + D :] = halves[96:]
+            pltpu.make_async_copy(early.at[at], early_o.at[at], sems.at[3 + g]).start()
+        for g in range(D // 96):
+            at = slice(96 * g, 96 * g + 96)
+            pltpu.make_async_copy(early.at[at], early_o.at[at], sems.at[3 + g]).wait()
+        wo_copy.wait()
 
 
 def gate_pass(tok, scan, cot, later, gain, gg, ri, bm=512):
@@ -408,14 +435,16 @@
     one = pl.Buffered(buffer_count=1)
     full = lambda shape: pl.BlockSpec(shape, lambda i: (0,) * len(shape), pipeline_mode=one)
     blk = lambda w: pl.BlockSpec((bm, w), lambda i: (i, 0))
+    hbm = pl.BlockSpec(memory_space=pl.ANY)
     low = lambda *shape: jax.ShapeDtypeStruct(shape, bf16)
     return pl.pallas_call(
         functools.partial(gate_kernel, ri),
         grid=(rows // bm,),
-        in_specs=[blk(D), blk(DI), blk(D), full(later.shape), full(gain.shape), full(gg.shape)],
-        out_specs=[blk(DI), blk(DI), blk(DI), full((D, 2 * DI)), full((DI, D))],
+        in_specs=[blk(D), blk(DI), blk(D), hbm, full(gain.shape), full(gg.shape)],
+        out_specs=[blk(DI), blk(DI), blk(DI), hbm, hbm],
         out_shape=[low(rows, DI), low(rows, DI), low(rows, DI), low(D, 2 * DI), low(DI, D)],
-        scratch_shapes=[pltpu.VMEM((D, DI), f32), pltpu.VMEM((DI, D), f32), pltpu.VMEM((bm, D), bf16), pltpu.VMEM((D, bm), bf16),
+        scratch_shapes=[pltpu.VMEM((D, 2 * DI), bf16), pltpu.VMEM((DI, D), bf16), pltpu.VMEM((D, 2 * DI), bf16),
+                        pltpu.SemaphoreType.DMA((3 + D // 96,)), pltpu.VMEM((D, DI), f32), pltpu.VMEM((DI, D), f32), pltpu.VMEM((bm, D), bf16), pltpu.VMEM((D, bm), bf16),
                         pltpu.VMEM((DI, 256), bf16),
                         pltpu.VMEM((bm, DI), f32), pltpu.VMEM((bm, DI), f32), pltpu.VMEM((8, 32, DI), f32),
                         pltpu.VMEM((8, 32, DI), f32)],
@@ -437,7 +466,7 @@
         in_specs=[blk(DI), blk(D), pl.BlockSpec((DI, D), lambda i: (0, 0), pipeline_mode=pl.Buffered(buffer_count=1))],
         out_specs=blk(D),
         out_shape=jax.ShapeDtypeStruct((rows, D), bf16),
-        compiler_params=pltpu.CompilerParams(vmem_limit_bytes=VM),
+        compiler_params=pltpu.CompilerParams(vmem_limit_bytes=50 << 20),
         cost_estimate=pl.CostEstimate(flops=0, bytes_accessed=0, transcendentals=0),
         name="out_pass",
     )(mixed, tok, wo)
@@ -449,38 +478,39 @@
     first_lane = nf * share
 
     def spread(values, width, who):
-        total = values.shape[1]
+        total = values[0].shape[1]
         lane = lax.broadcasted_iota(jnp.int32, (128, total), 1).astype(f32)
         piece = jnp.floor((lane + 0.5) * (1.0 / width))
         place = lax.broadcasted_iota(jnp.int32, (128, total), 0).astype(f32) - first_lane
         pick = ((place == lane - piece * width) & (place < width)).astype(bf16)
         mine = piece[0:1, :] == who
-        hi = values.astype(bf16).astype(f32)
-        return [dot_nt(jnp.where(mine, part, 0.0).astype(bf16), pick) for part in (hi, values - hi)]
+        terms = []
+        for value in values:
+            hi = value.astype(bf16).astype(f32)
+            terms += [jnp.where(mine, part, 0.0).astype(bf16) for part in (hi, value - hi)]
+        out = dot_nt(jnp.concatenate(terms, axis=0), pick)
+        return [out[nd * k : nd * k + nd] for k in range(len(terms))]
 
     rows[...] = jnp.zeros_like(rows)
 
     def put(n, values):
         rows[pl.ds(n, nd, stride=tall), :] = values
 
-    for k in range(5):
-        terms = gcw[8 * k : 8 * k + 8, :] if k < 4 else gcb[...]
-        hi, lo = spread(0.5 * jnp.sum(terms, axis=0, keepdims=True), CONV // nd, owner)
-        put(k, hi)
-        put(5 + k, lo)
+    taps = [0.5 * jnp.sum(gcw[8 * k : 8 * k + 8, :], axis=0, keepdims=True) for k in range(4)]
+    taps.append(0.5 * jnp.sum(gcb[...], axis=0, keepdims=True))
+    for k, part in enumerate(spread(taps, CONV // nd, owner)):
+        put(k // 2 + 5 * (k % 2), part)
     group = owner - nf * jnp.floor((owner + 0.5) * (1.0 / nf))
     skips = two_parts(jnp.broadcast_to(jnp.sum(gsk[...], axis=0, keepdims=True), (8, DI)))
     skips = dot(skips[:, :DI], sums[...]) + dot(skips[:, DI:], sums[...])
     per_head = [jnp.sum(ghd[0:8, :], axis=0, keepdims=True), jnp.sum(ghd[8:16, :], axis=0, keepdims=True), skips[0:1, :]]
-    for n in range(3):
-        hi, lo = spread(per_head[n], share, group)
-        put(10 + n, hi)
-        put(13 + n, lo)
+    for k, part in enumerate(spread(per_head, share, group)):
+        put(10 + k // 2 + 3 * (k % 2), part)
     out_o[...] = rows[...].astype(bf16)
 
 
 def backward_scan_kernel(heads, per_seq, nf, share, tall, dscan, cin, act, dact, z_r, st, cw, head_terms, skip, seg, seg_before,
-                         wc_a, wc_b, device, dproj_o, gproj_o, pack_o,
+                         wc_a, wc_b, device, dproj_o, gproj_o, pack_o, gproj,
                          dstate, p1buf, qbuf, xwbuf, rowbuf, lastbuf, mbuf, onehot, sums, docs,
                          gcw_o, gcb_o, gsk_o, ghd_o, rows_s, wc, dlast, sems):
     i = pl.program_id(0)
@@ -489,8 +519,8 @@
     @pl.when(i == 0)
     def _():
         half = wc_a.shape[0]
-        copies = [pltpu.make_async_copy(wc_a.at[:, : CONV + 128], wc.at[0:half], sems.at[0]),
-                  pltpu.make_async_copy(wc_b.at[:, : CONV + 128], wc.at[half : 2 * half], sems.at[1])]
+        copies = [pltpu.make_async_copy(wc_a, wc.at[0:half], sems.at[0]),
+                  pltpu.make_async_copy(wc_b, wc.at[half : 2 * half], sems.at[1])]
         for copy in copies:
             copy.start()
         dlast[...] = jnp.zeros_like(dlast)
@@ -505,6 +535,7 @@
         sums[...] = (head == lax.broadcasted_iota(jnp.int32, sums.shape, 1)).astype(bf16)
         for copy in copies:
             copy.wait()
+        clear_free(wc, heads)
 
     @pl.when(lax.rem(i, per_seq) == 0)
     def _():
@@ -550,7 +581,7 @@
 
     def project_back(given, block, part):
         cols = slice(256 * part, 256 * part + 256)
-        gproj_o[pl.ds(block * Q, Q), cols] = dot_nt(given[...], wc[cols, :]).astype(bf16)
+        gproj[pl.ds(block * Q, Q), cols] = dot_nt(given[...], wc[cols, :]).astype(bf16)
 
     block_before = steps - jnp.maximum(i, 1)
     for p in range(heads // 2):
@@ -613,11 +644,21 @@
     ghd_o[8:16, :] += rate * jnp.sum((g * soft).reshape(-1, 8, 128), axis=0)
     dlast[...] = dproj_o[...]
 
+    def copy_out(block):
+        at = pl.ds(block * Q, Q)
+        return pltpu.make_async_copy(gproj.at[at], gproj_o.at[at], sems.at[2])
+
+    @pl.when(i > 0)
+    def _():
+        copy_out(block_before).start()
+
     @pl.when(i == steps - 1)
     def _():
         for part in range(D // 256):
             project_back(dlast, 0, part)
+        copy_out(0).start()
         pack_grads(nf, share, tall, gcw_o, gcb_o, gsk_o, ghd_o, device, sums, rows_s, pack_o)
+        pltpu.make_async_copy(gproj, gproj_o, sems.at[2]).wait()
 
 
 def backward_scan(dscan, cin, act, dact, z, st, cw, head_terms, skip, seg, wc_a, wc_b, device, heads, seqs, nf, share, tall):
@@ -635,16 +676,16 @@
         in_specs=[blk(DI), blk(CONV), blk(CONV), blk(CONV), blk(128), blk3(N, DI), full(cw.shape), full(head_terms.shape),
                   full(skip.shape), blk3(1, Q), pl.BlockSpec((1, 1, Q), lambda i: (jnp.maximum(n - 2 - i, 0), 0, 0)),
                   hbm, hbm, full(device.shape)],
-        out_specs=[blk(CONV + 128), full((rows, D)), full((nd * tall, 128))],
+        out_specs=[blk(CONV + 128), hbm, full((nd * tall, 128))],
         out_shape=[jax.ShapeDtypeStruct((rows, CONV + 128), bf16), jax.ShapeDtypeStruct((rows, D), bf16),
                    jax.ShapeDtypeStruct((nd * tall, 128), bf16)],
-        scratch_shapes=[pltpu.VMEM((N, DI), f32), pltpu.VMEM((Q, 2 * DI), bf16), pltpu.VMEM((Q, DI), bf16),
+        scratch_shapes=[pltpu.VMEM((rows, D), bf16), pltpu.VMEM((N, DI), f32), pltpu.VMEM((Q, 2 * DI), bf16), pltpu.VMEM((Q, DI), bf16),
                         pltpu.VMEM((Q, 2 * DI), bf16), pltpu.VMEM((128, 128), f32), pltpu.VMEM((8, DI), f32),
                         pltpu.VMEM((3, CONV // 128, Q + 8, 128), f32), pltpu.VMEM((256, DI), bf16),
                         pltpu.VMEM((DI, 128), bf16), pltpu.VMEM((Q + 8, 128), f32), pltpu.VMEM((32, CONV), f32),
                         pltpu.VMEM((8, CONV), f32), pltpu.VMEM((8, DI), f32), pltpu.VMEM((16, 128), f32),
                         pltpu.VMEM((nd * tall, 128), f32), pltpu.VMEM((D, CONV + 128), bf16), pltpu.VMEM((Q, CONV + 128), bf16),
-                        pltpu.SemaphoreType.DMA((2,))],
+                        pltpu.SemaphoreType.DMA((3,))],
         compiler_params=pltpu.CompilerParams(vmem_limit_bytes=VM),
         cost_estimate=pl.CostEstimate(flops=0, bytes_accessed=0, transcendentals=0),
         name="backward_scan",
@@ -684,7 +725,7 @@
         out_specs=blk(D),
         out_shape=jax.ShapeDtypeStruct((rows, D), bf16),
         scratch_shapes=[pltpu.VMEM((D, DI), bf16), pltpu.VMEM((D, D), bf16)],
-        compiler_params=pltpu.CompilerParams(vmem_limit_bytes=36 << 20),
+        compiler_params=pltpu.CompilerParams(vmem_limit_bytes=46 << 20),
         cost_estimate=pl.CostEstimate(flops=0, bytes_accessed=0, transcendentals=0),
         name="norm_back",
     )(gproj, dgate, tok, cot, later, gain, device)
@@ -802,8 +843,7 @@
 
 def scatter_parts(kept, stage, sizes):
     axis, stride, group, _ = stage
-    low = kept.astype(bf16)
-    return [swap(low[k], axis, sizes[axis], k * stride) for k in range(1, group)]
+    return [swap(kept[k].astype(bf16), axis, sizes[axis], k * stride) for k in range(1, group)]
 
 
 def scatter_stage(kept, stage, sizes):
@@ -850,9 +890,9 @@
     up_s = jnp.dot(up, order, preferred_element_type=bf16)
     wc, up_s = before(wc, up_s)
     wc_b = swap(wc, stages[-1][0], sizes[stages[-1][0]], stages[-1][1])
-    halves = [part.reshape(nd // 2, tall, CONV + 256) for part in (wc, wc_b)]
-    small = jnp.concatenate([part[:, :16, CONV + 128 :] for part in halves], axis=0).transpose(1, 0, 2).astype(f32)
-    wc_a, wc_b = [part[:, :ri].reshape(D // 2, CONV + 256) for part in halves]
+    halves = [part.reshape(nd // 2, tall, CONV + 128) for part in (wc, wc_b)]
+    small = jnp.concatenate([part[:, :16, CONV:] for part in halves], axis=0).transpose(1, 0, 2).astype(f32)
+    wc_a, wc_b = [part[:, :ri].reshape(D // 2, CONV + 128) for part in halves]
 
     cin, act, dact, nrm, scan, st, z, gain, gain_abs, cw, cb, gg, head_terms, skip = forward_scan(
         tok_s, wc_a, wc_b, small, device_rows, seg, seqs, ri, ro, share, heads)
@@ -871,9 +911,11 @@
         halves = [half + part for half, part in zip(halves, (small[: nd // 2], small[nd // 2 :]))]
 
     axis, stride, group, _ = stages[-1]
-    total = halves[0].astype(f32) + swap(halves[1], axis, sizes[axis], stride).astype(f32)
-    total = total.reshape([g for _, _, g, _ in stages[-2::-1]] + [tall, CONV + 128])
-    total, gain = before(total, gain)
+    got = swap(halves[1], axis, sizes[axis], stride)
+    shape = [g for _, _, g, _ in stages[-2::-1]] + [tall, CONV + 128]
+    pieces = zip(halves[0].reshape(shape), got.reshape(shape))
+    total = [mine.astype(f32) + part.astype(f32) for mine, part in pieces]
+    total[0], gain = before(total[0], gain)
     gtok = norm_back(gproj, dgate, tok_s, up_s, later, gain, device_rows, ri)
     for stage in stages[-2:0:-1]:
         total = scatter_stage(total, stage, sizes)

time: 262 us -> 253 us (0.966)
  Pallas kernels: 190 us -> 186 us
  transfers between devices with their start and end apart: 16 -> 16, of which waited for: 6 -> 5; matrix products, arithmetic and copies ran while one was open for 6% -> 7% of each run, Pallas kernels for 56% -> 57%
where the time goes in v5:
time: 253 us
  Pallas kernels  186 us (74%)
  starting transfers between devices  17.5 us (7%)
  waiting for transfers between devices  17 us (7%)
  between operations  14.3 us (6%)
  matrix products  10.4 us (4%)
  local copies, waits for them, and re-layouts  5.47 us (2%)
    pallas_call x1, Pallas kernels, backward_scan(): pl.pallas_call(functools.partial(backward_scan_kernel, heads, n // seqs,...  66.7 us
    pallas_call x1, Pallas kernels, forward_scan(): pl.pallas_call(functools.partial(forward_scan_kernel, heads, n // seqs, r...  41.8 us
    pallas_call x1, Pallas kernels, gate_pass(): pl.pallas_call(functools.partial(gate_kernel, ri), grid=(rows // bm,), in...  37.2 us
    ppermute x14, starting transfers between devices, swap(): return lax.ppermute(arr, axis, [(i, i ^ offset) for i in range(size)])  17.5 us
    ppermute x14, waiting for transfers between devices, swap(): return lax.ppermute(arr, axis, [(i, i ^ offset) for i in range(size)])  17 us
    pallas_call x1, Pallas kernels, norm_back(): pl.pallas_call(functools.partial(norm_back_kernel, ri), grid=(rows // bm,...  16.7 us
    pallas_call x1, Pallas kernels, conv_weight_grad(): pl.pallas_call(conv_weight_kernel, grid=((CONV + 128) // bn,), in_specs=[...  10.9 us
    pallas_call x1, Pallas kernels, out_pass(): pl.pallas_call(out_kernel, grid=(rows // bm,), in_specs=[blk(DI), blk(D),...  8.7 us
  transfers between devices with their start and end apart: 16, of which 5 were waited for; matrix products, arithmetic and copies ran while one was open for 7% of the time, Pallas kernels for 57%

profile of v5, /device:TPU:0, one launch (start us, length us, event | category | flops | bytes accessed | tf_op | source)
XLA Modules:
  0.0 253.0 jit_solution(7857155344486636025)
XLA Ops:
  7.2 0.0 all-gather.2.cloned.1.call-start
  7.2 1.7 pack.1
  9.0 0.0 all-gather.2.cloned.1.call-update
  9.0 0.0 reduce-scatter.2.cloned.1.call-start
  9.0 5.1 %collective-permute-start.2 = (bf16[24,1920]{1,0:T(8,128)(2,1)}, bf16[24,1920]{1,0:T(8,128)(2,1)S(1)}, u32[]{:S(2)}, u32[]{:S(2)}) collective-permute-start(bf16[24,1920]{1,0:T(8,128)(2,1)} %get-tuple-element.58), channel_id=1, source_target_pairs={{0,24},{2,26},{4,28},{6,30},{8,16},{10,18},{12,20},{14,22},{16,8},... | collective-permute-start | bytes 276488 | tf_op jit(solution)/shard_map/ppermute | solution.py:836
  14.2 0.0 collective-permute-start.1
  14.2 0.6 collective-permute-start
  14.8 0.7 xor_convert_fusion
  15.5 0.1 iota_add_fusion
  15.5 0.1 add.50
  15.6 0.0 copy-start.12
  15.6 0.0 copy-start.11
  15.6 0.0 copy-start.7
  15.7 6.4 %convolution_bitcast_fusion.1.first.tok = bf16[2048,768]{1,0:T(8,128)(2,1)} fusion(bf16[2048,768]{1,0:T(8,128)(2,1)} %bitcast.56, s32[768]{0:T(1024)S(1)} %add.50), kind=kOutput, calls=%fused_computation.1 | convolution fusion | flops 2416508928 | bytes 6294528 | tf_op jit(solution)/shard_map/dot_general | solution.py:884
  22.0 0.6 reshape.92.seg.seg_before
  22.7 0.0 collective-permute-done.2
  22.7 0.0 collective-permute-done.1
  22.7 0.0 collective-permute-done
  22.7 0.1 pad_maximum_fusion.1
  22.7 0.7 broadcast_in_dim.35.device
  23.4 2.6 %collective-permute-start.5 = (bf16[4,24,1920]{2,1,0:T(8,128)(2,1)S(1)}, bf16[4,24,1920]{2,1,0:T(8,128)(2,1)S(1)}, u32[]{:S(2)}, u32[]{:S(2)}) collective-permute-start(bf16[4,24,1920]{2,1,0:T(8,128)(2,1)S(1)} %pad_maximum_fusion.1), channel_id=1, source_target_pairs={{0,6},{2,4},{4,2},{6,0},{8,14},{10,12},{12,10},{14,8},{16,22},{18,... | collective-permute-start | bytes 1105928 | tf_op jit(solution)/shard_map/ppermute | solution.py:836
  26.0 0.5 collective-permute-start.4
  26.5 0.4 collective-permute-start.3
  26.9 4.0 %convolution_bitcast_fusion.cot = bf16[2048,768]{1,0:T(8,128)(2,1)} fusion(bf16[2048,768]{1,0:T(8,128)(2,1)S(1)} %bitcast.64, s32[768]{0:T(1024)S(1)} %add.50), kind=kOutput, calls=%fused_computation | convolution fusion | flops 2416508928 | bytes 6294528 | tf_op jit(solution)/shard_map/dot_general | solution.py:890
  30.9 4.9 %collective-permute-done.5 = bf16[4,24,1920]{2,1,0:T(8,128)(2,1)S(1)} collective-permute-done((bf16[4,24,1920]{2,1,0:T(8,128)(2,1)S(1)}, bf16[4,24,1920]{2,1,0:T(8,128)(2,1)S(1)}, u32[]{:S(2)}, u32[]{:S(2)}) %collective-permute-start.5) | collective-permute-done | bytes 368672 | tf_op jit(solution)/shard_map/ppermute | solution.py:836
  35.9 7.0 %collective-permute-done.4 = bf16[4,24,1920]{2,1,0:T(8,128)(2,1)S(1)} collective-permute-done((bf16[4,24,1920]{2,1,0:T(8,128)(2,1)S(1)}, bf16[4,24,1920]{2,1,0:T(8,128)(2,1)S(1)}, u32[]{:S(2)}, u32[]{:S(2)}) %collective-permute-start.4) | collective-permute-done | bytes 368672 | tf_op jit(solution)/shard_map/ppermute | solution.py:836
  42.8 0.0 collective-permute-done.3
  42.8 0.2 pad_maximum_fusion
  43.1 0.1 collective-permute-start.6
  43.2 3.2 %collective-permute-done.6 = bf16[4,4,24,1920]{3,2,1,0:T(8,128)(2,1)S(1)} collective-permute-done((bf16[4,4,24,1920]{3,2,1,0:T(8,128)(2,1)S(1)}, bf16[4,4,24,1920]{3,2,1,0:T(8,128)(2,1)S(1)}, u32[]{:S(2)}, u32[]{:S(2)}) %collective-permute-start.6) | collective-permute-done | bytes 1474592 | tf_op jit(solution)/shard_map/ppermute | solution.py:836
  46.5 0.8 convert_bitcast_fusion.small
  47.3 0.4 copy-done.6
  47.7 41.8 %forward_scan.1 = (bf16[2048,1792]{1,0:T(8,128)(2,1)}, bf16[2048,1792]{1,0:T(8,128)(2,1)}, bf16[2048,1792]{1,0:T(8,128)(2,1)}, bf16[2048,768]{1,0:T(8,128)(2,1)}...) custom-call(bf16[2048,768]{1,0:T(8,128)(2,1)} %convolution_bitcast_f, ...), custom_call_target="tpu_custom_call" | custom-call | tf_op jit(solution)/shard_map/forward_scan/pallas_call | solution.py:288
  89.5 0.0 all-gather.2.cloned.1.call-done.later_in.wg_abs
  89.5 37.2 %gate_pass.1 = (bf16[2048,1536]{1,0:T(8,128)(2,1)}, bf16[2048,1536]{1,0:T(8,128)(2,1)}, bf16[2048,1536]{1,0:T(8,128)(2,1)}, bf16[768,3072]{1,0:T(8,128)(2,1)}, bf16[1536,768]{1,0:T(8,128)(2,1)}) custom-call(bf16[2048,768]{1,0:T(8,128)(2,1)} %bitcast.57, bf16[2048,1536]{1,0:T(8,128)(2,1)} %get-tuple-element.64.scan, bf16[2048,768]{1,0:T(8,128)(2,1)} %bitcast.63, ...), custom_call_target="tpu_custom_call" | custom-call | tf_op jit(solution)/shard_map/gate_pass/pallas_call | solution.py:440
  126.7 0.0 reduce-scatter.2.cloned.1.call-update
  126.8 66.7 %backward_scan.1 = (bf16[2048,1920]{1,0:T(8,128)(2,1)}, bf16[2048,768]{1,0:T(8,128)(2,1)}, bf16[768,128]{1,0:T(8,128)(2,1)}) custom-call(bf16[2048,1536]{1,0:T(8,128)(2,1)} %get-tuple-element.71.dscan, bf16[2048,1792]{1,0:T(8,128)(2,1)} %get-tuple-element.72.cin, bf16[2048,1792]{1,0:T(8,128)(2,1)} %get-tuple-element.73.act, ...), custom_call_target="tpu_custom_call" | custom-call | tf_op jit(solution)/shard_map/backward_scan/pallas_call | solution.py:673
  193.4 10.9 %conv_weight_grad.1 = (bf16[384,1920]{1,0:T(8,128)(2,1)}, bf16[384,1920]{1,0:T(8,128)(2,1)}) custom-call(bf16[2048,768]{1,0:T(8,128)(2,1)} %get-tuple-element.70.nrm, bf16[2048,1920]{1,0:T(8,128)(2,1)} %get-tuple-element.80.dproj, bf16[768,128]{1,0:T(8,128)(2,1)} %get-tuple-element.81.small), custom_call_target="tpu_custom_call" | custom-call | tf_op jit(solution)/shard_map/conv_weight_grad/pallas_call | solution.py:752
  204.3 0.1 collective-permute-start.7
  204.5 1.6 fusion.5
  206.1 0.0 copy-start
  206.1 1.7 collective-permute-done.7
  207.8 0.3 fusion.4
  208.1 1.1 collective-permute-start.10
  209.3 1.5 collective-permute-start.9
  210.8 0.9 collective-permute-start.8
  211.7 0.0 copy-done.4
  211.7 16.7 %norm_back.1 = bf16[2048,768]{1,0:T(8,128)(2,1)} custom-call(bf16[2048,768]{1,0:T(8,128)(2,1)S(1)} %copy-done.1, bf16[2048,1536]{1,0:T(8,128)(2,1)} %get-tuple-element.87.dgate, bf16[2048,768]{1,0:T(8,128)(2,1)S(1)} %copy-done, bf16[2048,768]{1,0:T(8,128)(2,1)} %convolution_bitcast_fusion.cot, ...), custom_call_target="tpu_custom_call" | custom-call | tf_op jit(solution)/shard_map/norm_back/pallas_call | solution.py:721
  228.4 0.0 collective-permute-done.10
  228.4 0.1 collective-permute-done.9
  228.6 0.0 collective-permute-done.8
  228.6 0.2 convert_add_fusion.4
  228.8 1.5 collective-permute-start.11
  230.3 2.5 collective-permute-start.12
  232.8 0.5 collective-permute-start.13
  233.3 0.7 slice_bitcast_fusion.refs_0_
  234.0 8.7 %out_pass.1 = bf16[2048,768]{1,0:T(8,128)(2,1)} custom-call(bf16[2048,1536]{1,0:T(8,128)(2,1)} %get-tuple-element.69.mixed, bf16[2048,768]{1,0:T(8,128)(2,1)} %bitcast.58, bf16[1536,768]{1,0:T(8,128)(2,1)S(1)} %copy-done.2), custom_call_target="tpu_custom_call" | custom-call | tf_op jit(solution)/shard_map/out_pass/pallas_call | solution.py:463
  242.7 0.0 collective-permute-done.11.refs_1_
  242.7 0.0 collective-permute-done.12.refs_2_
  242.7 0.0 collective-permute-done.13.refs_3_
  242.7 0.6 copy-done.8
  243.3 0.0 copy-done.9
  243.4 0.6 copy-done.10
  244.0 2.1 finish.1
  (24 shorter events, 0.2 us)
Async XLA Ops:
  7.2 82.3 %all-gather.2.cloned.1.call-start = ((), (), s32[]{:S(2)}) async-start(), calls=%async_computation.1 | async-start | bytes 4866048 | tf_op jit(solution)/shard_map/all_gather | solution.py:880
  9.0 233.7 %reduce-scatter.2.cloned.1.call-start = ((), (), s32[]{:S(2)}) async-start(), calls=%async_computation.2 | async-start | bytes 4866048 | tf_op jit(solution)/shard_map/reduce_scatter | solution.py:900
  9.0 13.6 %collective-permute-start.2 = (bf16[24,1920]{1,0:T(8,128)(2,1)}, bf16[24,1920]{1,0:T(8,128)(2,1)S(1)}, u32[]{:S(2)}, u32[]{:S(2)}) collective-permute-start(bf16[24,1920]{1,0:T(8,128)(2,1)} %get-tuple-element.58), channel_id=1, source_target_pairs={{0,24},{2,26},{4,28},{6,30},{8,16},{10,18},{12,20},{14,22},{16,8},... | collective-permute-start | bytes 276488 | tf_op jit(solution)/shard_map/ppermute | solution.py:836
  14.2 8.5 %collective-permute-start.1 = (bf16[24,1920]{1,0:T(8,128)(2,1)}, bf16[24,1920]{1,0:T(8,128)(2,1)S(1)}, u32[]{:S(2)}, u32[]{:S(2)}) collective-permute-start(bf16[24,1920]{1,0:T(8,128)(2,1)} %get-tuple-element.58), channel_id=1, source_target_pairs={{0,16},{2,18},{4,20},{6,22},{8,24},{10,26},{12,28},{14,30},{16,0},... | collective-permute-start | bytes 276488 | tf_op jit(solution)/shard_map/ppermute | solution.py:836
  14.2 8.5 %collective-permute-start = (bf16[24,1920]{1,0:T(8,128)(2,1)}, bf16[24,1920]{1,0:T(8,128)(2,1)S(1)}, u32[]{:S(2)}, u32[]{:S(2)}) collective-permute-start(bf16[24,1920]{1,0:T(8,128)(2,1)} %get-tuple-element.58), channel_id=1, source_target_pairs={{0,8},{2,10},{4,12},{6,14},{8,0},{10,2},{12,4},{14,6},{16,24},{18,... | collective-permute-start | bytes 276488 | tf_op jit(solution)/shard_map/ppermute | solution.py:836
  15.6 6.4 %copy-start.12 = (s32[2,1024]{1,0:T(2,128)S(1)}, s32[2,1024]{1,0:T(2,128)}, u32[]{:S(2)}) copy-start(s32[2,1024]{1,0:T(2,128)} %param.15) | copy-start | bytes 24580
  15.6 7.0 %copy-start.11 = (bf16[24,1920]{1,0:T(8,128)(2,1)S(1)}, bf16[24,1920]{1,0:T(8,128)(2,1)}, u32[]{:S(2)}) copy-start(bf16[24,1920]{1,0:T(8,128)(2,1)} %get-tuple-element.58) | copy-start | bytes 276484
  15.6 11.3 %copy-start.7 = (bf16[2,1024,768]{2,1,0:T(8,128)(2,1)S(1)}, bf16[2,1024,768]{2,1,0:T(8,128)(2,1)}, u32[]{:S(2)}) copy-start(bf16[2,1024,768]{2,1,0:T(8,128)(2,1)} %param.14) | copy-start | bytes 9437188
  23.4 12.4 %collective-permute-start.5 = (bf16[4,24,1920]{2,1,0:T(8,128)(2,1)S(1)}, bf16[4,24,1920]{2,1,0:T(8,128)(2,1)S(1)}, u32[]{:S(2)}, u32[]{:S(2)}) collective-permute-start(bf16[4,24,1920]{2,1,0:T(8,128)(2,1)S(1)} %pad_maximum_fusion.1), channel_id=1, source_target_pairs={{0,6},{2,4},{4,2},{6,0},{8,14},{10,12},{12,10},{14,8},{16,22},{18,... | collective-permute-start | bytes 1105928 | tf_op jit(solution)/shard_map/ppermute | solution.py:836
  26.0 16.8 %collective-permute-start.4 = (bf16[4,24,1920]{2,1,0:T(8,128)(2,1)S(1)}, bf16[4,24,1920]{2,1,0:T(8,128)(2,1)S(1)}, u32[]{:S(2)}, u32[]{:S(2)}) collective-permute-start(bf16[4,24,1920]{2,1,0:T(8,128)(2,1)S(1)} %pad_maximum_fusion.1), channel_id=1, source_target_pairs={{0,4},{2,6},{4,0},{6,2},{8,12},{10,14},{12,8},{14,10},{16,20},{18,... | collective-permute-start | bytes 1105928 | tf_op jit(solution)/shard_map/ppermute | solution.py:836
  26.5 16.3 %collective-permute-start.3 = (bf16[4,24,1920]{2,1,0:T(8,128)(2,1)S(1)}, bf16[4,24,1920]{2,1,0:T(8,128)(2,1)S(1)}, u32[]{:S(2)}, u32[]{:S(2)}) collective-permute-start(bf16[4,24,1920]{2,1,0:T(8,128)(2,1)S(1)} %pad_maximum_fusion.1), channel_id=1, source_target_pairs={{0,2},{2,0},{4,6},{6,4},{8,10},{10,8},{12,14},{14,12},{16,18},{18,... | collective-permute-start | bytes 1105928 | tf_op jit(solution)/shard_map/ppermute | solution.py:836
  43.1 4.2 %copy-start.5 = (bf16[4,4,24,1920]{3,2,1,0:T(8,128)(2,1)}, bf16[4,4,24,1920]{3,2,1,0:T(8,128)(2,1)S(1)}, u32[]{:S(2)}) copy-start(bf16[4,4,24,1920]{3,2,1,0:T(8,128)(2,1)S(1)} %pad_maximum_fusion) | copy-start | bytes 4423684
  43.1 3.3 %collective-permute-start.6 = (bf16[4,4,24,1920]{3,2,1,0:T(8,128)(2,1)S(1)}, bf16[4,4,24,1920]{3,2,1,0:T(8,128)(2,1)S(1)}, u32[]{:S(2)}, u32[]{:S(2)}) collective-permute-start(bf16[4,4,24,1920]{3,2,1,0:T(8,128)(2,1)S(1)} %pad_maximum_fusion), channel_id=1, source_target_pairs={{0,1},{1,0},{2,3},{3,2},{4,5},{5,4},{6,7},{7,6},{8,9},{9,8},{10,11... | collective-permute-start | bytes 4423688 | tf_op jit(solution)/shard_map/ppermute | solution.py:836
  46.4 1.3 copy-start.6
  204.3 3.5 %collective-permute-start.7 = (bf16[16,24,1920]{2,1,0:T(8,128)(2,1)}, bf16[16,24,1920]{2,1,0:T(8,128)(2,1)S(1)}, u32[]{:S(2)}, u32[]{:S(2)}) collective-permute-start(bf16[16,24,1920]{2,1,0:T(8,128)(2,1)} %bitcast.86), channel_id=1, source_target_pairs={{0,1},{1,0},{2,3},{3,2},{4,5},{5,4},{6,7},{7,6},{8,9},{9,8},{10,11... | collective-permute-start | bytes 4423688 | tf_op jit(solution)/shard_map/ppermute | solution.py:836
  204.5 7.2 %copy-start.1 = (bf16[2048,768]{1,0:T(8,128)(2,1)S(1)}, bf16[2048,768]{1,0:T(8,128)(2,1)}, u32[]{:S(2)}) copy-start(bf16[2048,768]{1,0:T(8,128)(2,1)} %get-tuple-element.86.gproj) | copy-start | bytes 9437188
  206.1 5.7 %copy-start = (bf16[2048,768]{1,0:T(8,128)(2,1)S(1)}, bf16[2048,768]{1,0:T(8,128)(2,1)}, u32[]{:S(2)}) copy-start(bf16[2048,768]{1,0:T(8,128)(2,1)} %convolution_bitcast_fusion.1.first.tok) | copy-start | bytes 9437188
  206.1 5.6 %copy-start.3 = (f32[32,128]{1,0:T(8,128)S(1)}, f32[32,128]{1,0:T(8,128)}, u32[]{:S(2)}) copy-start(f32[32,128]{1,0:T(8,128)} %broadcast_in_dim.35.device) | copy-start | bytes 49156
  206.1 5.6 %copy-start.4 = (f32[1,768]{1,0:T(1,128)S(1)}, f32[1,768]{1,0:T(1,128)}, u32[]{:S(2)}) copy-start(f32[1,768]{1,0:T(1,128)} %get-tuple-element.89.gain) | copy-start | bytes 9220
  208.1 20.3 %collective-permute-start.10 = (bf16[4,24,1920]{2,1,0:T(8,128)(2,1)S(1)}, bf16[4,24,1920]{2,1,0:T(8,128)(2,1)S(1)}, u32[]{:S(2)}, u32[]{:S(2)}) collective-permute-start(bf16[4,24,1920]{2,1,0:T(8,128)(2,1)S(1)} %get-tuple-element.106), channel_id=1, source_target_pairs={{0,6},{2,4},{4,2},{6,0},{8,14},{10,12},{12,10},{14,8},{16,22},{18,... | collective-permute-start | bytes 1105928 | tf_op jit(solution)/shard_map/ppermute | solution.py:836
  209.3 19.3 %collective-permute-start.9 = (bf16[4,24,1920]{2,1,0:T(8,128)(2,1)S(1)}, bf16[4,24,1920]{2,1,0:T(8,128)(2,1)S(1)}, u32[]{:S(2)}, u32[]{:S(2)}) collective-permute-start(bf16[4,24,1920]{2,1,0:T(8,128)(2,1)S(1)} %get-tuple-element.107), channel_id=1, source_target_pairs={{0,4},{2,6},{4,0},{6,2},{8,12},{10,14},{12,8},{14,10},{16,20},{18,... | collective-permute-start | bytes 1105928 | tf_op jit(solution)/shard_map/ppermute | solution.py:836
  210.8 17.8 %collective-permute-start.8 = (bf16[4,24,1920]{2,1,0:T(8,128)(2,1)S(1)}, bf16[4,24,1920]{2,1,0:T(8,128)(2,1)S(1)}, u32[]{:S(2)}, u32[]{:S(2)}) collective-permute-start(bf16[4,24,1920]{2,1,0:T(8,128)(2,1)S(1)} %get-tuple-element.105), channel_id=1, source_target_pairs={{0,2},{2,0},{4,6},{6,4},{8,10},{10,8},{12,14},{14,12},{16,18},{18,... | collective-permute-start | bytes 1105928 | tf_op jit(solution)/shard_map/ppermute | solution.py:836
  228.4 5.6 %copy-start.2 = (bf16[1536,768]{1,0:T(8,128)(2,1)S(1)}, bf16[1536,768]{1,0:T(8,128)(2,1)}, u32[]{:S(2)}) copy-start(bf16[1536,768]{1,0:T(8,128)(2,1)} %get-tuple-element.91.wo) | copy-start | bytes 7077892
  228.8 13.9 %collective-permute-start.11 = (bf16[24,1920]{1,0:T(8,128)(2,1)S(1)}, bf16[24,1920]{1,0:T(8,128)(2,1)S(1)}, u32[]{:S(2)}, u32[]{:S(2)}) collective-permute-start(bf16[24,1920]{1,0:T(8,128)(2,1)S(1)} %get-tuple-element.115), channel_id=1, source_target_pairs={{0,8},{2,10},{4,12},{6,14},{8,0},{10,2},{12,4},{14,6},{16,24},{18,... | collective-permute-start | bytes 276488 | tf_op jit(solution)/shard_map/ppermute | solution.py:836
  230.3 12.4 %collective-permute-start.12 = (bf16[24,1920]{1,0:T(8,128)(2,1)S(1)}, bf16[24,1920]{1,0:T(8,128)(2,1)S(1)}, u32[]{:S(2)}, u32[]{:S(2)}) collective-permute-start(bf16[24,1920]{1,0:T(8,128)(2,1)S(1)} %get-tuple-element.114), channel_id=1, source_target_pairs={{0,16},{2,18},{4,20},{6,22},{8,24},{10,26},{12,28},{14,30},{16,0},... | collective-permute-start | bytes 276488 | tf_op jit(solution)/shard_map/ppermute | solution.py:836
  232.8 9.9 %collective-permute-start.13 = (bf16[24,1920]{1,0:T(8,128)(2,1)S(1)}, bf16[24,1920]{1,0:T(8,128)(2,1)S(1)}, u32[]{:S(2)}, u32[]{:S(2)}) collective-permute-start(bf16[24,1920]{1,0:T(8,128)(2,1)S(1)} %get-tuple-element.113), channel_id=1, source_target_pairs={{0,24},{2,26},{4,28},{6,30},{8,16},{10,18},{12,20},{14,22},{16,8},... | collective-permute-start | bytes 276488 | tf_op jit(solution)/shard_map/ppermute | solution.py:836
  242.7 0.6 copy-start.8
  242.7 0.7 copy-start.9
  243.4 0.6 copy-start.10
Sparse Core Ops, SparseCore 0:
  11.5 72.9 all-gather.1
  126.9 106.9 reduce-scatter.1

commit v6 on v5

--- a/solution.py
+++ b/solution.py
@@ -16,6 +16,7 @@
 VM = 60 * 1024 * 1024
 
 D, DI, CONV, N, HD = 768, 1536, 1792, 128, 64
+SPLIT = 1024
 
 
 def dot(a, b):
@@ -159,12 +160,19 @@
     skip[...] = dot(two_parts(jnp.broadcast_to(per_head[2], (8, 128))), onehot[...])[0:1, :]
 
 
+def copies_of(pieces, wc, sems):
+    rows = pieces[0].shape[0]
+    spots = [(n // 2, slice(0, SPLIT) if n % 2 == 0 else slice(SPLIT, CONV + 128)) for n in range(4)]
+    return [pltpu.make_async_copy(piece, wc.at[rows * r : rows * r + rows, cols], sems.at[n])
+            for n, (piece, (r, cols)) in enumerate(zip(pieces, spots))]
+
+
 def clear_free(wc, heads):
     last = wc[:, CONV:]
     wc[:, CONV:] = jnp.where(lax.broadcasted_iota(jnp.int32, last.shape, 1) < heads, last, jnp.zeros_like(last))
 
 
-def forward_scan_kernel(heads, per_seq, ri, ro, share, first, tok, wc_a, wc_b, small, device, seg, seg_before,
+def forward_scan_kernel(heads, per_seq, ri, ro, share, first, tok, wc_0, wc_1, wc_2, wc_3, small, device, seg, seg_before,
                         cin_o, act_o, dact_o, nrm_o, scan_o, st_o, z_o, gain, gain_abs, cw, cb, gg, heads_o, skip,
                         pbuf, zbuf, nbuf, pnext, znext, nnext, state, docs, onehot, wc, sems):
     i = pl.program_id(0)
@@ -190,9 +198,7 @@
 
     @pl.when(i == 0)
     def _():
-        rows = wc_a.shape[0]
-        copies = [pltpu.make_async_copy(wc_a, wc.at[0:rows], sems.at[0]),
-                  pltpu.make_async_copy(wc_b, wc.at[rows : 2 * rows], sems.at[1])]
+        copies = copies_of((wc_0, wc_1, wc_2, wc_3), wc, sems)
         for copy in copies:
             copy.start()
         onehot[...] = head_onehot(onehot.shape)
@@ -275,7 +281,7 @@
     advance()
 
 
-def forward_scan(tok, wc_a, wc_b, small, device, seg, seqs, ri, ro, share, heads):
+def forward_scan(tok, wc, small, device, seg, seqs, ri, ro, share, heads):
     rows = tok.shape[0]
     n = rows // Q
     one = pl.Buffered(buffer_count=1)
@@ -289,7 +295,7 @@
         functools.partial(forward_scan_kernel, heads, n // seqs, ri, ro, share),
         grid=(n,),
         in_specs=[pl.BlockSpec((Q, D), lambda i: (0, 0), pipeline_mode=one),
-                  pl.BlockSpec((Q, D), lambda i: (jnp.minimum(i + 1, n - 1), 0)), hbm, hbm, full(small), full(device),
+                  pl.BlockSpec((Q, D), lambda i: (jnp.minimum(i + 1, n - 1), 0)), hbm, hbm, hbm, hbm, full(small), full(device),
                   pl.BlockSpec((1, 1, Q), lambda i: (i, 0, 0)), pl.BlockSpec((1, 1, Q), lambda i: (jnp.maximum(i - 1, 0), 0, 0))],
         out_specs=[blk(CONV), blk(CONV), blk(CONV), blk(D), blk(DI), pl.BlockSpec((1, N, DI), lambda i: (i, 0, 0)), blk(128)]
         + [side(shape) for shape in sides],
@@ -298,10 +304,10 @@
         scratch_shapes=[pltpu.VMEM((CONV // 128, Q + 8, 128), f32), pltpu.VMEM((Q, 128), f32), pltpu.VMEM((Q, D), bf16),
                         pltpu.VMEM((CONV // 128, Q, 128), f32), pltpu.VMEM((Q, 128), f32), pltpu.VMEM((Q, D), bf16),
                         pltpu.VMEM((N, DI), f32), pltpu.VMEM((Q + 8, 128), f32), pltpu.VMEM((256, DI), bf16),
-                        pltpu.VMEM((D, CONV + 128), bf16), pltpu.SemaphoreType.DMA((2,))],
+                        pltpu.VMEM((D, CONV + 128), bf16), pltpu.SemaphoreType.DMA((4,))],
         compiler_params=pltpu.CompilerParams(vmem_limit_bytes=56 << 20),
         name="forward_scan",
-    )(tok, tok, wc_a, wc_b, small, device, seg, seg)
+    )(tok, tok, *wc, small, device, seg, seg)
 
 
 def block_order(ri):
@@ -510,7 +516,7 @@
 
 
 def backward_scan_kernel(heads, per_seq, nf, share, tall, dscan, cin, act, dact, z_r, st, cw, head_terms, skip, seg, seg_before,
-                         wc_a, wc_b, device, dproj_o, gproj_o, pack_o, gproj,
+                         wc_0, wc_1, wc_2, wc_3, device, dproj_o, gproj_o, pack_o, gproj,
                          dstate, p1buf, qbuf, xwbuf, rowbuf, lastbuf, mbuf, onehot, sums, docs,
                          gcw_o, gcb_o, gsk_o, ghd_o, rows_s, wc, dlast, sems):
     i = pl.program_id(0)
@@ -518,9 +524,7 @@
 
     @pl.when(i == 0)
     def _():
-        half = wc_a.shape[0]
-        copies = [pltpu.make_async_copy(wc_a, wc.at[0:half], sems.at[0]),
-                  pltpu.make_async_copy(wc_b, wc.at[half : 2 * half], sems.at[1])]
+        copies = copies_of((wc_0, wc_1, wc_2, wc_3), wc, sems)
         for copy in copies:
             copy.start()
         dlast[...] = jnp.zeros_like(dlast)
@@ -646,7 +650,7 @@
 
     def copy_out(block):
         at = pl.ds(block * Q, Q)
-        return pltpu.make_async_copy(gproj.at[at], gproj_o.at[at], sems.at[2])
+        return pltpu.make_async_copy(gproj.at[at], gproj_o.at[at], sems.at[4])
 
     @pl.when(i > 0)
     def _():
@@ -658,10 +662,10 @@
             project_back(dlast, 0, part)
         copy_out(0).start()
         pack_grads(nf, share, tall, gcw_o, gcb_o, gsk_o, ghd_o, device, sums, rows_s, pack_o)
-        pltpu.make_async_copy(gproj, gproj_o, sems.at[2]).wait()
-
-
-def backward_scan(dscan, cin, act, dact, z, st, cw, head_terms, skip, seg, wc_a, wc_b, device, heads, seqs, nf, share, tall):
+        pltpu.make_async_copy(gproj, gproj_o, sems.at[4]).wait()
+
+
+def backward_scan(dscan, cin, act, dact, z, st, cw, head_terms, skip, seg, wc, device, heads, seqs, nf, share, tall):
     rows = dscan.shape[0]
     n = rows // Q
     nd = device.shape[0]
@@ -675,7 +679,7 @@
         grid=(n,),
         in_specs=[blk(DI), blk(CONV), blk(CONV), blk(CONV), blk(128), blk3(N, DI), full(cw.shape), full(head_terms.shape),
                   full(skip.shape), blk3(1, Q), pl.BlockSpec((1, 1, Q), lambda i: (jnp.maximum(n - 2 - i, 0), 0, 0)),
-                  hbm, hbm, full(device.shape)],
+                  hbm, hbm, hbm, hbm, full(device.shape)],
         out_specs=[blk(CONV + 128), hbm, full((nd * tall, 128))],
         out_shape=[jax.ShapeDtypeStruct((rows, CONV + 128), bf16), jax.ShapeDtypeStruct((rows, D), bf16),
                    jax.ShapeDtypeStruct((nd * tall, 128), bf16)],
@@ -685,11 +689,11 @@
                         pltpu.VMEM((DI, 128), bf16), pltpu.VMEM((Q + 8, 128), f32), pltpu.VMEM((32, CONV), f32),
                         pltpu.VMEM((8, CONV), f32), pltpu.VMEM((8, DI), f32), pltpu.VMEM((16, 128), f32),
                         pltpu.VMEM((nd * tall, 128), f32), pltpu.VMEM((D, CONV + 128), bf16), pltpu.VMEM((Q, CONV + 128), bf16),
-                        pltpu.SemaphoreType.DMA((3,))],
-        compiler_params=pltpu.CompilerParams(vmem_limit_bytes=VM),
+                        pltpu.SemaphoreType.DMA((5,))],
+        compiler_params=pltpu.CompilerParams(vmem_limit_bytes=52 << 20),
         cost_estimate=pl.CostEstimate(flops=0, bytes_accessed=0, transcendentals=0),
         name="backward_scan",
-    )(dscan, cin, act, dact, z, st, cw, head_terms, skip, seg, seg, wc_a, wc_b, device)
+    )(dscan, cin, act, dact, z, st, cw, head_terms, skip, seg, seg, *wc, device)
 
 
 def norm_back_kernel(ri, gproj, dgate, tok, cot, wg_abs, gain, device, out_o, wg, order):
@@ -756,7 +760,7 @@
                   pl.BlockSpec((D, 128), lambda i: (0, 0), pipeline_mode=one)],
         out_specs=[pl.BlockSpec((D // 2, bn), lambda i: (0, i))] * 2,
         out_shape=[jax.ShapeDtypeStruct((D // 2, CONV + 128), bf16)] * 2,
-        compiler_params=pltpu.CompilerParams(vmem_limit_bytes=VM),
+        compiler_params=pltpu.CompilerParams(vmem_limit_bytes=50 << 20),
         cost_estimate=pl.CostEstimate(flops=0, bytes_accessed=0, transcendentals=0),
         name="conv_weight_grad",
     )(nrm, dproj, small)
@@ -795,6 +799,7 @@
         functools.partial(finish_kernel, heads, share, 1 + len(got)),
         out_shape=[jax.ShapeDtypeStruct(shape, f32) for shape in shapes],
         scratch_shapes=[pltpu.VMEM(own.shape, f32)],
+        compiler_params=pltpu.CompilerParams(vmem_limit_bytes=12 << 20),
         name="finish",
     )(early, w_in, w_out, in_gain, gate_gain, own, *got)
 
@@ -836,9 +841,16 @@
     return lax.ppermute(arr, axis, [(i, i ^ offset) for i in range(size)])
 
 
-def gather_stage(block, stage, sizes):
+def gather_stage(block, stage, sizes, first=0):
     axis, stride, group, _ = stage
-    return jnp.stack([block] + [swap(block, axis, sizes[axis], k * stride) for k in range(1, group)])
+    if first == 0 or group != 4:
+        return jnp.stack([block] + [swap(block, axis, sizes[axis], k * stride) for k in range(1, group)])
+    if first == 1:
+        block = jnp.stack([block, swap(block, axis, sizes[axis], stride)])
+        return jnp.concatenate([block, swap(block, axis, sizes[axis], 2 * stride)])
+    block = jnp.stack([block, swap(block, axis, sizes[axis], 2 * stride)])
+    block = jnp.stack([block, swap(block, axis, sizes[axis], stride)], axis=1)
+    return block.reshape((4,) + block.shape[2:])
 
 
 def scatter_parts(kept, stage, sizes):
@@ -885,22 +897,26 @@
     device_rows = jnp.broadcast_to(device.astype(f32)[:, None], (nd, 128))
     seg = segments.reshape(rows // Q, 1, Q)
     wc, tok_s, device_rows, seg = before(wc, tok_s, device_rows, seg)
+    one, two = wc[..., :SPLIT], wc[..., SPLIT:]
     for stage in stages[1:-1]:
-        wc = gather_stage(wc, stage, sizes)
+        one = gather_stage(one, stage, sizes, 1)
+        two = gather_stage(two, stage, sizes, 2)
     up_s = jnp.dot(up, order, preferred_element_type=bf16)
-    wc, up_s = before(wc, up_s)
-    wc_b = swap(wc, stages[-1][0], sizes[stages[-1][0]], stages[-1][1])
-    halves = [part.reshape(nd // 2, tall, CONV + 128) for part in (wc, wc_b)]
-    small = jnp.concatenate([part[:, :16, CONV:] for part in halves], axis=0).transpose(1, 0, 2).astype(f32)
-    wc_a, wc_b = [part[:, :ri].reshape(D // 2, CONV + 128) for part in halves]
+    two, up_s = before(two, up_s)
+    axis, stride = stages[-1][:2]
+    quarters = [part.reshape(nd // 2, tall, part.shape[-1])
+                for part in (one, two, swap(one, axis, sizes[axis], stride), swap(two, axis, sizes[axis], stride))]
+    last = [part[:, :16, CONV - SPLIT :] for part in (quarters[1], quarters[3])]
+    small = jnp.concatenate(last, axis=0).transpose(1, 0, 2).astype(f32)
+    wc = [part[:, :ri].reshape(D // 2, part.shape[-1]) for part in quarters]
 
     cin, act, dact, nrm, scan, st, z, gain, gain_abs, cw, cb, gg, head_terms, skip = forward_scan(
-        tok_s, wc_a, wc_b, small, device_rows, seg, seqs, ri, ro, share, heads)
+        tok_s, wc, small, device_rows, seg, seqs, ri, ro, share, heads)
     mixed, dscan, dgate, early, wo = gate_pass(tok, scan, up, later, gain_abs, gg, ri)
     early = lax.psum_scatter(early, axes, scatter_dimension=0, tiled=True)
 
     dproj, gproj, small = backward_scan(
-        dscan, cin, act, dact, z, st, cw, head_terms, skip, seg, wc_a, wc_b, device_rows, heads, seqs, nf, share, tall)
+        dscan, cin, act, dact, z, st, cw, head_terms, skip, seg, wc, device_rows, heads, seqs, nf, share, tall)
     if ri == tall:
         halves = conv_weight_grad(nrm, dproj, small)
         halves = [half.reshape(nd // 2, tall, CONV + 128) for half in halves]

time: 253 us -> 248 us (0.980)
  waiting for transfers between devices: 17 us -> 12.5 us
  Pallas kernels: 186 us -> 183 us
    ppermute x14 -> x16, waiting for transfers between devices: 17 us -> 12.4 us  [swap(): return lax.ppermute(arr, axis, [(i, i ^ offset) for i in range(size)])]
    ppermute x14 -> x16, starting transfers between devices: 17.5 us -> 19.9 us  [swap(): return lax.ppermute(arr, axis, [(i, i ^ offset) for i in range(size)])]
  transfers between devices with their start and end apart: 16 -> 18, of which waited for: 5 -> 5; matrix products, arithmetic and copies ran while one was open for 7% -> 6% of each run, Pallas kernels for 57% -> 58%
where the time goes in v6:
time: 248 us
  Pallas kernels  183 us (74%)
  starting transfers between devices  20 us (8%)
  between operations  14.5 us (6%)
  waiting for transfers between devices  12.5 us (5%)
  matrix products  10.3 us (4%)
  local copies, waits for them, and re-layouts  4.82 us (2%)
  other arithmetic  2.53 us (1%)
    pallas_call x1, Pallas kernels, backward_scan(): pl.pallas_call(functools.partial(backward_scan_kernel, heads, n // seqs,...  65.9 us
    pallas_call x1, Pallas kernels, forward_scan(): pl.pallas_call(functools.partial(forward_scan_kernel, heads, n // seqs, r...  41.7 us
    pallas_call x1, Pallas kernels, gate_pass(): pl.pallas_call(functools.partial(gate_kernel, ri), grid=(rows // bm,), in...  37.2 us
    ppermute x16, starting transfers between devices, swap(): return lax.ppermute(arr, axis, [(i, i ^ offset) for i in range(size)])  19.9 us
    pallas_call x1, Pallas kernels, norm_back(): pl.pallas_call(functools.partial(norm_back_kernel, ri), grid=(rows // bm,...  16.7 us
    ppermute x16, waiting for transfers between devices, swap(): return lax.ppermute(arr, axis, [(i, i ^ offset) for i in range(size)])  12.4 us
    pallas_call x1, Pallas kernels, conv_weight_grad(): pl.pallas_call(conv_weight_kernel, grid=((CONV + 128) // bn,), in_specs=[...  10.2 us
    pallas_call x1, Pallas kernels, out_pass(): pl.pallas_call(out_kernel, grid=(rows // bm,), in_specs=[blk(DI), blk(D),...  8.8 us
  transfers between devices with their start and end apart: 18, of which 5 were waited for; matrix products, arithmetic and copies ran while one was open for 6% of the time, Pallas kernels for 58%

profile of v6, /device:TPU:0, one launch (start us, length us, event | category | flops | bytes accessed | tf_op | source)
XLA Modules:
  0.0 247.8 jit_solution(17968593956844887005)
XLA Ops:
  7.2 0.0 all-gather.2.cloned.1.call-start
  7.2 1.7 pack.1
  9.0 0.0 all-gather.2.cloned.1.call-update
  9.0 0.0 reduce-scatter.2.cloned.1.call-start
  9.0 5.1 %collective-permute-start.2 = (bf16[24,1920]{1,0:T(8,128)(2,1)}, bf16[24,1920]{1,0:T(8,128)(2,1)S(1)}, u32[]{:S(2)}, u32[]{:S(2)}) collective-permute-start(bf16[24,1920]{1,0:T(8,128)(2,1)} %get-tuple-element.58), channel_id=1, source_target_pairs={{0,24},{2,26},{4,28},{6,30},{8,16},{10,18},{12,20},{14,22},{16,8},... | collective-permute-start | bytes 276488 | tf_op jit(solution)/shard_map/ppermute | solution.py:841
  14.2 0.0 collective-permute-start.1
  14.2 0.6 collective-permute-start
  14.8 0.7 xor_convert_fusion
  15.5 0.1 iota_add_fusion
  15.5 0.1 add.50
  15.6 0.0 copy-start.22
  15.6 0.0 copy-start.21
  15.6 6.3 %convolution_bitcast_fusion.1.first.tok = bf16[2048,768]{1,0:T(8,128)(2,1)} fusion(bf16[2048,768]{1,0:T(8,128)(2,1)} %bitcast.73, s32[768]{0:T(1024)S(1)} %add.50), kind=kOutput, calls=%fused_computation.1 | convolution fusion | flops 2416508928 | bytes 6294528 | tf_op jit(solution)/shard_map/dot_general | solution.py:896
  21.9 0.6 reshape.95.seg.seg_before
  22.5 0.0 collective-permute-done.2
  22.5 0.0 collective-permute-done.1
  22.5 0.0 collective-permute-done
  22.5 0.1 pad_maximum_fusion.3
  22.6 0.7 broadcast_in_dim.35.device
  23.3 1.7 collective-permute-start.5
  25.1 1.6 collective-permute-start.3
  26.6 3.3 %collective-permute-done.5 = bf16[4,24,896]{2,1,0:T(8,128)(2,1)S(1)} collective-permute-done((bf16[4,24,896]{2,1,0:T(8,128)(2,1)S(1)}, bf16[4,24,896]{2,1,0:T(8,128)(2,1)S(1)}, u32[]{:S(2)}, u32[]{:S(2)}) %collective-permute-start.5) | collective-permute-done | bytes 172064 | tf_op jit(solution)/shard_map/ppermute | solution.py:841
  30.0 0.1 fusion.5
  30.0 1.6 collective-permute-start.6
  31.6 0.9 collective-permute-start.4
  32.6 4.1 %convolution_bitcast_fusion.cot = bf16[2048,768]{1,0:T(8,128)(2,1)} fusion(bf16[2048,768]{1,0:T(8,128)(2,1)S(1)} %bitcast.80, s32[768]{0:T(1024)S(1)} %add.50), kind=kOutput, calls=%fused_computation | convolution fusion | flops 2416508928 | bytes 6294528 | tf_op jit(solution)/shard_map/dot_general | solution.py:904
  36.6 2.9 %collective-permute-done.6 = bf16[2,4,24,896]{3,2,1,0:T(8,128)(2,1)S(1)} collective-permute-done((bf16[2,4,24,896]{3,2,1,0:T(8,128)(2,1)S(1)}, bf16[2,4,24,896]{3,2,1,0:T(8,128)(2,1)S(1)}, u32[]{:S(2)}, u32[]{:S(2)}) %collective-permute-start.6) | collective-permute-done | bytes 344096 | tf_op jit(solution)/shard_map/ppermute | solution.py:841
  39.5 0.1 pad_maximum_fusion.1
  39.6 0.1 copy.29
  39.7 0.1 collective-permute-start.8
  39.7 2.0 collective-permute-done.4
  41.7 0.1 pad_maximum_fusion
  41.8 0.1 collective-permute-start.7
  42.0 0.9 convert_bitcast_fusion.small
  42.9 1.2 collective-permute-done.7
  44.2 0.9 copy-done.20
  45.1 41.7 %forward_scan.1 = (bf16[2048,1792]{1,0:T(8,128)(2,1)}, bf16[2048,1792]{1,0:T(8,128)(2,1)}, bf16[2048,1792]{1,0:T(8,128)(2,1)}, bf16[2048,768]{1,0:T(8,128)(2,1)}...) custom-call(bf16[2048,768]{1,0:T(8,128)(2,1)} %convolution_bitcast_f, ...), custom_call_target="tpu_custom_call" | custom-call | tf_op jit(solution)/shard_map/forward_scan/pallas_call | solution.py:294
  86.8 0.0 all-gather.2.cloned.1.call-done.later_in.wg_abs
  86.8 37.2 %gate_pass.1 = (bf16[2048,1536]{1,0:T(8,128)(2,1)}, bf16[2048,1536]{1,0:T(8,128)(2,1)}, bf16[2048,1536]{1,0:T(8,128)(2,1)}, bf16[768,3072]{1,0:T(8,128)(2,1)}, bf16[1536,768]{1,0:T(8,128)(2,1)}) custom-call(bf16[2048,768]{1,0:T(8,128)(2,1)} %bitcast.74, bf16[2048,1536]{1,0:T(8,128)(2,1)} %get-tuple-element.64.scan, bf16[2048,768]{1,0:T(8,128)(2,1)} %bitcast.79, ...), custom_call_target="tpu_custom_call" | custom-call | tf_op jit(solution)/shard_map/gate_pass/pallas_call | solution.py:446
  124.1 0.0 reduce-scatter.2.cloned.1.call-update
  124.2 1.0 copy-done.2
  125.2 0.2 copy-done.5
  125.4 65.9 %backward_scan.1 = (bf16[2048,1920]{1,0:T(8,128)(2,1)}, bf16[2048,768]{1,0:T(8,128)(2,1)}, bf16[768,128]{1,0:T(8,128)(2,1)S(1)}) custom-call(bf16[2048,1536]{1,0:T(8,128)(2,1)} %get-tuple-element.71.dscan, bf16[2048,1792]{1,0:T(8,128)(2,1)} %get-tuple-element.72.cin, bf16[2048,1792]{1,0:T(8,128)(2,1)} %get-tuple-element.73.act, ...), custom_call_target="tpu_custom_call" | custom-call | tf_op jit(solution)/shard_map/backward_scan/pallas_call | solution.py:677
  191.3 10.2 %conv_weight_grad.1 = (bf16[384,1920]{1,0:T(8,128)(2,1)S(1)}, bf16[384,1920]{1,0:T(8,128)(2,1)S(1)}) custom-call(bf16[2048,768]{1,0:T(8,128)(2,1)} %get-tuple-element.70.nrm, bf16[2048,1920]{1,0:T(8,128)(2,1)} %get-tuple-element.80.dproj, bf16[768,128]{1,0:T(8,128)(2,1)S(1)} %get-tuple-element.81.small), custom_call_target="tpu_custom_call" | custom-call | tf_op jit(solution)/shard_map/conv_weight_grad/pallas_call | solution.py:756
  201.5 0.2 collective-permute-start.9
  201.7 0.1 fusion.6
  201.8 0.0 copy-start
  201.9 3.0 %collective-permute-done.9 = bf16[16,24,1920]{2,1,0:T(8,128)(2,1)S(1)} collective-permute-done((bf16[16,24,1920]{2,1,0:T(8,128)(2,1)S(1)}, bf16[16,24,1920]{2,1,0:T(8,128)(2,1)S(1)}, u32[]{:S(2)}, u32[]{:S(2)}) %collective-permute-start.9) | collective-permute-done | bytes 1474592 | tf_op jit(solution)/shard_map/ppermute | solution.py:841
  204.8 0.3 fusion.4
  205.2 0.5 collective-permute-start.12
  205.7 1.7 collective-permute-start.11
  207.4 1.3 collective-permute-start.10
  208.7 16.7 %norm_back.1 = bf16[2048,768]{1,0:T(8,128)(2,1)} custom-call(bf16[2048,768]{1,0:T(8,128)(2,1)S(1)} %copy-done.3, bf16[2048,1536]{1,0:T(8,128)(2,1)} %get-tuple-element.87.dgate, bf16[2048,768]{1,0:T(8,128)(2,1)S(1)} %copy-done, bf16[2048,768]{1,0:T(8,128)(2,1)} %convolution_bitcast_fusion.cot, ...), custom_call_target="tpu_custom_call" | custom-call | tf_op jit(solution)/shard_map/norm_back/pallas_call | solution.py:725
  225.5 0.2 convert_add_fusion.4
  225.7 1.6 collective-permute-start.13
  227.4 2.4 collective-permute-start.14
  229.8 0.4 collective-permute-start.15
  230.2 0.0 copy-start.7
  230.2 0.0 copy-start.8
  230.3 0.0 copy-start.16
  230.3 0.0 copy-start.17
  230.3 8.8 %out_pass.1 = bf16[2048,768]{1,0:T(8,128)(2,1)} custom-call(bf16[2048,1536]{1,0:T(8,128)(2,1)} %get-tuple-element.69.mixed, bf16[2048,768]{1,0:T(8,128)(2,1)} %bitcast.75, bf16[1536,768]{1,0:T(8,128)(2,1)S(1)} %copy-done.6), custom_call_target="tpu_custom_call" | custom-call | tf_op jit(solution)/shard_map/out_pass/pallas_call | solution.py:469
  239.2 0.9 copy-done.11
  240.1 0.9 finish.1
  (54 shorter events, 0.3 us)
Async XLA Ops:
  7.2 79.6 %all-gather.2.cloned.1.call-start = ((), (), s32[]{:S(2)}) async-start(), calls=%async_computation.1 | async-start | bytes 4866048 | tf_op jit(solution)/shard_map/all_gather | solution.py:892
  9.0 230.1 %reduce-scatter.2.cloned.1.call-start = ((), (), s32[]{:S(2)}) async-start(), calls=%async_computation.2 | async-start | bytes 4866048 | tf_op jit(solution)/shard_map/reduce_scatter | solution.py:916
  9.0 13.5 %collective-permute-start.2 = (bf16[24,1920]{1,0:T(8,128)(2,1)}, bf16[24,1920]{1,0:T(8,128)(2,1)S(1)}, u32[]{:S(2)}, u32[]{:S(2)}) collective-permute-start(bf16[24,1920]{1,0:T(8,128)(2,1)} %get-tuple-element.58), channel_id=1, source_target_pairs={{0,24},{2,26},{4,28},{6,30},{8,16},{10,18},{12,20},{14,22},{16,8},... | collective-permute-start | bytes 276488 | tf_op jit(solution)/shard_map/ppermute | solution.py:841
  14.2 8.4 %collective-permute-start.1 = (bf16[24,1920]{1,0:T(8,128)(2,1)}, bf16[24,1920]{1,0:T(8,128)(2,1)S(1)}, u32[]{:S(2)}, u32[]{:S(2)}) collective-permute-start(bf16[24,1920]{1,0:T(8,128)(2,1)} %get-tuple-element.58), channel_id=1, source_target_pairs={{0,16},{2,18},{4,20},{6,22},{8,24},{10,26},{12,28},{14,30},{16,0},... | collective-permute-start | bytes 276488 | tf_op jit(solution)/shard_map/ppermute | solution.py:841
  14.2 8.4 %collective-permute-start = (bf16[24,1920]{1,0:T(8,128)(2,1)}, bf16[24,1920]{1,0:T(8,128)(2,1)S(1)}, u32[]{:S(2)}, u32[]{:S(2)}) collective-permute-start(bf16[24,1920]{1,0:T(8,128)(2,1)} %get-tuple-element.58), channel_id=1, source_target_pairs={{0,8},{2,10},{4,12},{6,14},{8,0},{10,2},{12,4},{14,6},{16,24},{18,... | collective-permute-start | bytes 276488 | tf_op jit(solution)/shard_map/ppermute | solution.py:841
  15.6 6.3 %copy-start.22 = (s32[2,1024]{1,0:T(2,128)S(1)}, s32[2,1024]{1,0:T(2,128)}, u32[]{:S(2)}) copy-start(s32[2,1024]{1,0:T(2,128)} %param.15) | copy-start | bytes 24580
  15.6 6.9 %copy-start.21 = (bf16[24,1920]{1,0:T(8,128)(2,1)S(1)}, bf16[24,1920]{1,0:T(8,128)(2,1)}, u32[]{:S(2)}) copy-start(bf16[24,1920]{1,0:T(8,128)(2,1)} %get-tuple-element.58) | copy-start | bytes 276484
  21.9 10.7 %copy-start.19 = (bf16[2,1024,768]{2,1,0:T(8,128)(2,1)S(1)}, bf16[2,1024,768]{2,1,0:T(8,128)(2,1)}, u32[]{:S(2)}) copy-start(bf16[2,1024,768]{2,1,0:T(8,128)(2,1)} %param.14) | copy-start | bytes 9437188
  23.3 6.7 %collective-permute-start.5 = (bf16[4,24,896]{2,1,0:T(8,128)(2,1)S(1)}, bf16[4,24,896]{2,1,0:T(8,128)(2,1)S(1)}, u32[]{:S(2)}, u32[]{:S(2)}) collective-permute-start(bf16[4,24,896]{2,1,0:T(8,128)(2,1)S(1)} %get-tuple-element.117), channel_id=1, source_target_pairs={{0,4},{2,6},{4,0},{6,2},{8,12},{10,14},{12,8},{14,10},{16,20},{18,... | collective-permute-start | bytes 516104 | tf_op jit(solution)/shard_map/ppermute | solution.py:841
  25.1 6.5 %collective-permute-start.3 = (bf16[4,24,1024]{2,1,0:T(8,128)(2,1)S(1)}, bf16[4,24,1024]{2,1,0:T(8,128)(2,1)S(1)}, u32[]{:S(2)}, u32[]{:S(2)}) collective-permute-start(bf16[4,24,1024]{2,1,0:T(8,128)(2,1)S(1)} %get-tuple-element.119), channel_id=1, source_target_pairs={{0,2},{2,0},{4,6},{6,4},{8,10},{10,8},{12,14},{14,12},{16,18},{18,... | collective-permute-start | bytes 589832 | tf_op jit(solution)/shard_map/ppermute | solution.py:841
  30.0 9.5 %collective-permute-start.6 = (bf16[2,4,24,896]{3,2,1,0:T(8,128)(2,1)S(1)}, bf16[2,4,24,896]{3,2,1,0:T(8,128)(2,1)S(1)}, u32[]{:S(2)}, u32[]{:S(2)}) collective-permute-start(bf16[2,4,24,896]{3,2,1,0:T(8,128)(2,1)S(1)} %get-tuple-element.121), channel_id=1, source_target_pairs={{0,2},{2,0},{4,6},{6,4},{8,10},{10,8},{12,14},{14,12},{16,18},{18,... | collective-permute-start | bytes 1032200 | tf_op jit(solution)/shard_map/ppermute | solution.py:841
  31.6 10.1 %collective-permute-start.4 = (bf16[2,4,24,1024]{3,2,1,0:T(8,128)(2,1)S(1)}, bf16[2,4,24,1024]{3,2,1,0:T(8,128)(2,1)S(1)}, u32[]{:S(2)}, u32[]{:S(2)}) collective-permute-start(bf16[2,4,24,1024]{3,2,1,0:T(8,128)(2,1)S(1)} %pad_maximum_fusion.2), channel_id=1, source_target_pairs={{0,4},{2,6},{4,0},{6,2},{8,12},{10,14},{12,8},{14,10},{16,20},{18,... | collective-permute-start | bytes 1179656 | tf_op jit(solution)/shard_map/ppermute | solution.py:841
  39.7 4.5 %copy-start.1 = (bf16[2,2,4,24,896]{4,3,2,1,0:T(8,128)(2,1)}, bf16[2,2,4,24,896]{4,3,2,1,0:T(8,128)(2,1)S(1)}, u32[]{:S(2)}) copy-start(bf16[2,2,4,24,896]{4,3,2,1,0:T(8,128)(2,1)S(1)} %copy.29) | copy-start | bytes 2064388
  39.7 2.3 collective-permute-start.8
  41.8 2.4 copy-start.18
  41.8 2.4 collective-permute-start.7
  41.9 2.2 copy-start.4
  44.1 0.9 copy-start.20
  124.1 1.1 copy-start.2
  124.1 1.3 copy-start.5
  124.1 1.3 copy-start.9
  124.1 1.3 copy-start.10
  124.1 1.3 copy-start.12
  124.1 1.3 copy-start.13
  124.1 1.3 copy-start.14
  201.5 3.3 %collective-permute-start.9 = (bf16[16,24,1920]{2,1,0:T(8,128)(2,1)S(1)}, bf16[16,24,1920]{2,1,0:T(8,128)(2,1)S(1)}, u32[]{:S(2)}, u32[]{:S(2)}) collective-permute-start(bf16[16,24,1920]{2,1,0:T(8,128)(2,1)S(1)} %bitcast.72), channel_id=1, source_target_pairs={{0,1},{1,0},{2,3},{3,2},{4,5},{5,4},{6,7},{7,6},{8,9},{9,8},{10,11... | collective-permute-start | bytes 4423688 | tf_op jit(solution)/shard_map/ppermute | solution.py:841
  201.7 7.0 %copy-start.3 = (bf16[2048,768]{1,0:T(8,128)(2,1)S(1)}, bf16[2048,768]{1,0:T(8,128)(2,1)}, u32[]{:S(2)}) copy-start(bf16[2048,768]{1,0:T(8,128)(2,1)} %get-tuple-element.86.gproj) | copy-start | bytes 9437188
  201.8 6.9 %copy-start = (bf16[2048,768]{1,0:T(8,128)(2,1)S(1)}, bf16[2048,768]{1,0:T(8,128)(2,1)}, u32[]{:S(2)}) copy-start(bf16[2048,768]{1,0:T(8,128)(2,1)} %convolution_bitcast_fusion.1.first.tok) | copy-start | bytes 9437188
  201.8 6.9 %copy-start.15 = (f32[1,768]{1,0:T(1,128)S(1)}, f32[1,768]{1,0:T(1,128)}, u32[]{:S(2)}) copy-start(f32[1,768]{1,0:T(1,128)} %get-tuple-element.89.gain) | copy-start | bytes 9220
  205.2 20.3 %collective-permute-start.12 = (bf16[4,24,1920]{2,1,0:T(8,128)(2,1)S(1)}, bf16[4,24,1920]{2,1,0:T(8,128)(2,1)S(1)}, u32[]{:S(2)}, u32[]{:S(2)}) collective-permute-start(bf16[4,24,1920]{2,1,0:T(8,128)(2,1)S(1)} %get-tuple-element.106), channel_id=1, source_target_pairs={{0,6},{2,4},{4,2},{6,0},{8,14},{10,12},{12,10},{14,8},{16,22},{18,... | collective-permute-start | bytes 1105928 | tf_op jit(solution)/shard_map/ppermute | solution.py:841
  205.7 19.8 %collective-permute-start.11 = (bf16[4,24,1920]{2,1,0:T(8,128)(2,1)S(1)}, bf16[4,24,1920]{2,1,0:T(8,128)(2,1)S(1)}, u32[]{:S(2)}, u32[]{:S(2)}) collective-permute-start(bf16[4,24,1920]{2,1,0:T(8,128)(2,1)S(1)} %get-tuple-element.107), channel_id=1, source_target_pairs={{0,4},{2,6},{4,0},{6,2},{8,12},{10,14},{12,8},{14,10},{16,20},{18,... | collective-permute-start | bytes 1105928 | tf_op jit(solution)/shard_map/ppermute | solution.py:841
  207.4 18.0 %collective-permute-start.10 = (bf16[4,24,1920]{2,1,0:T(8,128)(2,1)S(1)}, bf16[4,24,1920]{2,1,0:T(8,128)(2,1)S(1)}, u32[]{:S(2)}, u32[]{:S(2)}) collective-permute-start(bf16[4,24,1920]{2,1,0:T(8,128)(2,1)S(1)} %get-tuple-element.105), channel_id=1, source_target_pairs={{0,2},{2,0},{4,6},{6,4},{8,10},{10,8},{12,14},{14,12},{16,18},{18,... | collective-permute-start | bytes 1105928 | tf_op jit(solution)/shard_map/ppermute | solution.py:841
  225.5 4.8 %copy-start.6 = (bf16[1536,768]{1,0:T(8,128)(2,1)S(1)}, bf16[1536,768]{1,0:T(8,128)(2,1)}, u32[]{:S(2)}) copy-start(bf16[1536,768]{1,0:T(8,128)(2,1)} %get-tuple-element.91.wo) | copy-start | bytes 7077892
  225.7 13.3 %collective-permute-start.13 = (bf16[24,1920]{1,0:T(8,128)(2,1)S(1)}, bf16[24,1920]{1,0:T(8,128)(2,1)S(1)}, u32[]{:S(2)}, u32[]{:S(2)}) collective-permute-start(bf16[24,1920]{1,0:T(8,128)(2,1)S(1)} %get-tuple-element.115), channel_id=1, source_target_pairs={{0,8},{2,10},{4,12},{6,14},{8,0},{10,2},{12,4},{14,6},{16,24},{18,... | collective-permute-start | bytes 276488 | tf_op jit(solution)/shard_map/ppermute | solution.py:841
  227.4 11.7 %collective-permute-start.14 = (bf16[24,1920]{1,0:T(8,128)(2,1)S(1)}, bf16[24,1920]{1,0:T(8,128)(2,1)S(1)}, u32[]{:S(2)}, u32[]{:S(2)}) collective-permute-start(bf16[24,1920]{1,0:T(8,128)(2,1)S(1)} %get-tuple-element.114), channel_id=1, source_target_pairs={{0,16},{2,18},{4,20},{6,22},{8,24},{10,26},{12,28},{14,30},{16,0},... | collective-permute-start | bytes 276488 | tf_op jit(solution)/shard_map/ppermute | solution.py:841
  229.8 9.3 %collective-permute-start.15 = (bf16[24,1920]{1,0:T(8,128)(2,1)S(1)}, bf16[24,1920]{1,0:T(8,128)(2,1)S(1)}, u32[]{:S(2)}, u32[]{:S(2)}) collective-permute-start(bf16[24,1920]{1,0:T(8,128)(2,1)S(1)} %get-tuple-element.113), channel_id=1, source_target_pairs={{0,24},{2,26},{4,28},{6,30},{8,16},{10,18},{12,20},{14,22},{16,8},... | collective-permute-start | bytes 276488 | tf_op jit(solution)/shard_map/ppermute | solution.py:841
  230.2 8.9 %copy-start.7 = (bf16[24,3352]{1,0:T(8,128)(2,1)S(1)}, bf16[24,3352]{1,0:T(8,128)(2,1)}, u32[]{:S(2)}) copy-start(bf16[24,3352]{1,0:T(8,128)(2,1)} %w_in.3) | copy-start | bytes 482692
  230.2 8.9 %copy-start.8 = (bf16[48,768]{1,0:T(8,128)(2,1)S(1)}, bf16[48,768]{1,0:T(8,128)(2,1)}, u32[]{:S(2)}) copy-start(bf16[48,768]{1,0:T(8,128)(2,1)} %w_out.3) | copy-start | bytes 221188
  230.3 8.9 %copy-start.16 = (bf16[24]{0:T(256)(128)(2,1)S(1)}, bf16[24]{0:T(256)(128)(2,1)}, u32[]{:S(2)}) copy-start(bf16[24]{0:T(256)(128)(2,1)} %param.16) | copy-start | bytes 148
  230.3 8.9 %copy-start.17 = (bf16[48]{0:T(256)(128)(2,1)S(1)}, bf16[48]{0:T(256)(128)(2,1)}, u32[]{:S(2)}) copy-start(bf16[48]{0:T(256)(128)(2,1)} %param.23) | copy-start | bytes 292
  239.1 0.9 copy-start.11
Sparse Core Ops, SparseCore 0:
  11.5 66.4 all-gather.1
  124.3 106.5 reduce-scatter.1

commit v7 on v6

--- a/solution.py
+++ b/solution.py
@@ -766,16 +766,19 @@
     )(nrm, dproj, small)
 
 
-def finish_kernel(heads, share, parts, early, w_in, w_out, in_gain, gate_gain, *refs):
+def finish_kernel(heads, share, parts, early_in, w_in, w_out, in_gain, gate_gain, *refs):
     own, got = refs[0], refs[1:parts]
-    in_o, out_o, in_gain_o, gate_gain_o, cw_o, cb_o, sb_o, dl_o, sg_o, total = refs[parts:]
+    in_o, out_o, in_gain_o, gate_gain_o, cw_o, cb_o, sb_o, dl_o, sg_o, total, early, sem = refs[parts:]
+    copy = pltpu.make_async_copy(early_in, early, sem)
+    copy.start()
     ri, ro, cc = w_in.shape[0], w_out.shape[0], cb_o.shape[1]
     value = own[...]
     for part in got:
         value = value + part[...].astype(f32)
     total[...] = value
+    in_o[:, DI:] = total[0:ri, : CONV + heads]
+    copy.wait()
     in_o[:, :DI] = early[:, :DI].astype(f32)
-    in_o[:, DI:] = total[0:ri, : CONV + heads]
     out_o[0:ri, :] = early[:, DI : DI + D].astype(f32)
     out_o[ri:, :] = early[:, DI + D :].astype(f32)
 
@@ -798,7 +801,8 @@
     return pl.pallas_call(
         functools.partial(finish_kernel, heads, share, 1 + len(got)),
         out_shape=[jax.ShapeDtypeStruct(shape, f32) for shape in shapes],
-        scratch_shapes=[pltpu.VMEM(own.shape, f32)],
+        in_specs=[pl.BlockSpec(memory_space=pl.ANY)] + [pl.BlockSpec(memory_space=pltpu.VMEM)] * (5 + len(got)),
+        scratch_shapes=[pltpu.VMEM(own.shape, f32), pltpu.VMEM(early.shape, bf16), pltpu.SemaphoreType.DMA],
         compiler_params=pltpu.CompilerParams(vmem_limit_bytes=12 << 20),
         name="finish",
     )(early, w_in, w_out, in_gain, gate_gain, own, *got)
@@ -896,13 +900,13 @@
     tok_s = jnp.dot(tok, order, preferred_element_type=bf16)
     device_rows = jnp.broadcast_to(device.astype(f32)[:, None], (nd, 128))
     seg = segments.reshape(rows // Q, 1, Q)
-    wc, tok_s, device_rows, seg = before(wc, tok_s, device_rows, seg)
+    wc, tok_s = before(wc, tok_s)
     one, two = wc[..., :SPLIT], wc[..., SPLIT:]
     for stage in stages[1:-1]:
         one = gather_stage(one, stage, sizes, 1)
         two = gather_stage(two, stage, sizes, 2)
     up_s = jnp.dot(up, order, preferred_element_type=bf16)
-    two, up_s = before(two, up_s)
+    two, up_s, device_rows, seg = before(two, up_s, device_rows, seg)
     axis, stride = stages[-1][:2]
     quarters = [part.reshape(nd // 2, tall, part.shape[-1])
                 for part in (one, two, swap(one, axis, sizes[axis], stride), swap(two, axis, sizes[axis], stride))]

time: 248 us -> 248 us (level)
  transfers between devices with their start and end apart: 18 -> 18, of which waited for: 5 -> 9; matrix products, arithmetic and copies ran while one was open for 6% -> 6% of each run, Pallas kernels for 58% -> 58%
where the time goes in v7:
time: 248 us; the launch traced here: 247 us
  Pallas kernels  183 us (74%)
  starting transfers between devices  19.5 us (8%)
  between operations  14.5 us (6%)
  waiting for transfers between devices  12.2 us (5%)
  matrix products  10.4 us (4%)
  local copies, waits for them, and re-layouts  4.95 us (2%)
    pallas_call x1, Pallas kernels, backward_scan(): pl.pallas_call(functools.partial(backward_scan_kernel, heads, n // seqs,...  65.9 us
    pallas_call x1, Pallas kernels, forward_scan(): pl.pallas_call(functools.partial(forward_scan_kernel, heads, n // seqs, r...  41.7 us
    pallas_call x1, Pallas kernels, gate_pass(): pl.pallas_call(functools.partial(gate_kernel, ri), grid=(rows // bm,), in...  37.2 us
    ppermute x16, starting transfers between devices, swap(): return lax.ppermute(arr, axis, [(i, i ^ offset) for i in range(size)])  19.4 us
    pallas_call x1, Pallas kernels, norm_back(): pl.pallas_call(functools.partial(norm_back_kernel, ri), grid=(rows // bm,...  16.7 us
    ppermute x16, waiting for transfers between devices, swap(): return lax.ppermute(arr, axis, [(i, i ^ offset) for i in range(size)])  12.1 us
    pallas_call x1, Pallas kernels, conv_weight_grad(): pl.pallas_call(conv_weight_kernel, grid=((CONV + 128) // bn,), in_specs=[...  10.2 us
    pallas_call x1, Pallas kernels, out_pass(): pl.pallas_call(out_kernel, grid=(rows // bm,), in_specs=[blk(DI), blk(D),...  8.81 us
  transfers between devices with their start and end apart: 18, of which 9 were waited for; matrix products, arithmetic and copies ran while one was open for 6% of the time, Pallas kernels for 58%

profile of v7, /device:TPU:0, one launch (start us, length us, event | category | flops | bytes accessed | tf_op | source)
XLA Modules:
  0.0 247.3 jit_solution(18230815205282137540)
XLA Ops:
  7.2 0.0 all-gather.2.cloned.1.call-start
  7.2 1.7 pack.1
  9.0 0.0 all-gather.2.cloned.1.call-update
  9.0 0.0 reduce-scatter.2.cloned.1.call-start
  9.0 5.1 %collective-permute-start.2 = (bf16[24,1920]{1,0:T(8,128)(2,1)}, bf16[24,1920]{1,0:T(8,128)(2,1)S(1)}, u32[]{:S(2)}, u32[]{:S(2)}) collective-permute-start(bf16[24,1920]{1,0:T(8,128)(2,1)} %get-tuple-element.58), channel_id=1, source_target_pairs={{0,24},{2,26},{4,28},{6,30},{8,16},{10,18},{12,20},{14,22},{16,8},... | collective-permute-start | bytes 276488 | tf_op jit(solution)/shard_map/ppermute | solution.py:845
  14.2 0.6 collective-permute-start
  14.8 0.7 xor_convert_fusion
  15.5 0.1 iota_add_fusion
  15.5 0.1 add.50
  15.6 0.0 copy-start.21
  15.6 6.3 %convolution_bitcast_fusion.1.first.tok = bf16[2048,768]{1,0:T(8,128)(2,1)} fusion(bf16[2048,768]{1,0:T(8,128)(2,1)} %bitcast.73, s32[768]{0:T(1024)S(1)} %add.50), kind=kOutput, calls=%fused_computation.1 | convolution fusion | flops 2416508928 | bytes 6294528 | tf_op jit(solution)/shard_map/dot_general | solution.py:900
  21.9 0.0 collective-permute-done.2
  21.9 0.2 collective-permute-done.1
  22.1 0.0 collective-permute-done
  22.1 0.1 pad_maximum_fusion.3
  22.2 1.6 collective-permute-start.5
  23.8 1.6 collective-permute-start.3
  25.4 3.4 %collective-permute-done.5 = bf16[4,24,896]{2,1,0:T(8,128)(2,1)S(1)} collective-permute-done((bf16[4,24,896]{2,1,0:T(8,128)(2,1)S(1)}, bf16[4,24,896]{2,1,0:T(8,128)(2,1)S(1)}, u32[]{:S(2)}, u32[]{:S(2)}) %collective-permute-start.5) | collective-permute-done | bytes 172064 | tf_op jit(solution)/shard_map/ppermute | solution.py:845
  28.8 0.1 fusion.5
  28.8 1.6 collective-permute-start.6
  30.4 0.9 collective-permute-done.3
  31.3 0.7 collective-permute-start.4
  32.0 4.1 %convolution_bitcast_fusion.cot = bf16[2048,768]{1,0:T(8,128)(2,1)} fusion(bf16[2048,768]{1,0:T(8,128)(2,1)S(1)} %bitcast.80, s32[768]{0:T(1024)S(1)} %add.50), kind=kOutput, calls=%fused_computation | convolution fusion | flops 2416508928 | bytes 6294528 | tf_op jit(solution)/shard_map/dot_general | solution.py:908
  36.1 0.6 reshape.97.seg.seg_before
  36.7 1.3 collective-permute-done.6
  38.0 0.1 pad_maximum_fusion.1
  38.1 0.1 copy.29
  38.1 0.8 broadcast_in_dim.35.device
  38.9 1.8 collective-permute-done.4
  40.7 0.1 pad_maximum_fusion
  40.8 0.1 collective-permute-start.7
  40.9 0.1 collective-permute-done.8
  41.1 0.8 convert_bitcast_fusion.small
  41.9 1.2 collective-permute-done.7
  43.2 0.9 copy-done.20
  44.1 41.7 %forward_scan.1 = (bf16[2048,1792]{1,0:T(8,128)(2,1)}, bf16[2048,1792]{1,0:T(8,128)(2,1)}, bf16[2048,1792]{1,0:T(8,128)(2,1)}, bf16[2048,768]{1,0:T(8,128)(2,1)}...) custom-call(bf16[2048,768]{1,0:T(8,128)(2,1)} %convolution_bitcast_f, ...), custom_call_target="tpu_custom_call" | custom-call | tf_op jit(solution)/shard_map/forward_scan/pallas_call | solution.py:294
  85.8 0.0 all-gather.2.cloned.1.call-done.later_in.wg_abs
  85.9 37.2 %gate_pass.1 = (bf16[2048,1536]{1,0:T(8,128)(2,1)}, bf16[2048,1536]{1,0:T(8,128)(2,1)}, bf16[2048,1536]{1,0:T(8,128)(2,1)}, bf16[768,3072]{1,0:T(8,128)(2,1)}, bf16[1536,768]{1,0:T(8,128)(2,1)}) custom-call(bf16[2048,768]{1,0:T(8,128)(2,1)} %bitcast.74, bf16[2048,1536]{1,0:T(8,128)(2,1)} %get-tuple-element.64.scan, bf16[2048,768]{1,0:T(8,128)(2,1)} %bitcast.79, ...), custom_call_target="tpu_custom_call" | custom-call | tf_op jit(solution)/shard_map/gate_pass/pallas_call | solution.py:446
  123.2 0.0 reduce-scatter.2.cloned.1.call-update
  123.2 1.0 copy-done.2
  124.2 0.2 copy-done.5
  124.4 65.9 %backward_scan.1 = (bf16[2048,1920]{1,0:T(8,128)(2,1)}, bf16[2048,768]{1,0:T(8,128)(2,1)}, bf16[768,128]{1,0:T(8,128)(2,1)S(1)}) custom-call(bf16[2048,1536]{1,0:T(8,128)(2,1)} %get-tuple-element.71.dscan, bf16[2048,1792]{1,0:T(8,128)(2,1)} %get-tuple-element.72.cin, bf16[2048,1792]{1,0:T(8,128)(2,1)} %get-tuple-element.73.act, ...), custom_call_target="tpu_custom_call" | custom-call | tf_op jit(solution)/shard_map/backward_scan/pallas_call | solution.py:677
  190.4 10.2 %conv_weight_grad.1 = (bf16[384,1920]{1,0:T(8,128)(2,1)S(1)}, bf16[384,1920]{1,0:T(8,128)(2,1)S(1)}) custom-call(bf16[2048,768]{1,0:T(8,128)(2,1)} %get-tuple-element.70.nrm, bf16[2048,1920]{1,0:T(8,128)(2,1)} %get-tuple-element.80.dproj, bf16[768,128]{1,0:T(8,128)(2,1)S(1)} %get-tuple-element.81.small), custom_call_target="tpu_custom_call" | custom-call | tf_op jit(solution)/shard_map/conv_weight_grad/pallas_call | solution.py:756
  200.5 0.2 collective-permute-start.9
  200.7 0.1 fusion.6
  200.8 0.0 copy-start
  200.9 3.0 %collective-permute-done.9 = bf16[16,24,1920]{2,1,0:T(8,128)(2,1)S(1)} collective-permute-done((bf16[16,24,1920]{2,1,0:T(8,128)(2,1)S(1)}, bf16[16,24,1920]{2,1,0:T(8,128)(2,1)S(1)}, u32[]{:S(2)}, u32[]{:S(2)}) %collective-permute-start.9) | collective-permute-done | bytes 1474592 | tf_op jit(solution)/shard_map/ppermute | solution.py:845
  203.9 0.3 fusion.4
  204.2 1.8 collective-permute-start.12
  206.0 0.0 collective-permute-start.11
  206.0 1.7 collective-permute-start.10
  207.8 16.7 %norm_back.1 = bf16[2048,768]{1,0:T(8,128)(2,1)} custom-call(bf16[2048,768]{1,0:T(8,128)(2,1)S(1)} %copy-done.3, bf16[2048,1536]{1,0:T(8,128)(2,1)} %get-tuple-element.87.dgate, bf16[2048,768]{1,0:T(8,128)(2,1)S(1)} %copy-done, bf16[2048,768]{1,0:T(8,128)(2,1)} %convolution_bitcast_fusion.cot, ...), custom_call_target="tpu_custom_call" | custom-call | tf_op jit(solution)/shard_map/norm_back/pallas_call | solution.py:725
  224.5 0.2 collective-permute-done.11
  224.8 0.2 convert_add_fusion.4
  225.0 1.7 collective-permute-start.13
  226.7 2.2 collective-permute-start.14
  228.9 0.6 collective-permute-start.15
  229.5 0.0 copy-start.7
  229.5 0.0 copy-start.8
  229.5 0.0 copy-start.16
  229.5 0.0 copy-start.17
  229.6 8.8 %out_pass.1 = bf16[2048,768]{1,0:T(8,128)(2,1)} custom-call(bf16[2048,1536]{1,0:T(8,128)(2,1)} %get-tuple-element.69.mixed, bf16[2048,768]{1,0:T(8,128)(2,1)} %bitcast.75, bf16[1536,768]{1,0:T(8,128)(2,1)S(1)} %copy-done.6), custom_call_target="tpu_custom_call" | custom-call | tf_op jit(solution)/shard_map/out_pass/pallas_call | solution.py:469
  238.4 0.9 copy-done.11
  239.3 1.1 finish.1
  (54 shorter events, 0.3 us)
Async XLA Ops:
  7.2 78.7 %all-gather.2.cloned.1.call-start = ((), (), s32[]{:S(2)}) async-start(), calls=%async_computation.1 | async-start | bytes 4866048 | tf_op jit(solution)/shard_map/all_gather | solution.py:896
  9.0 229.4 %reduce-scatter.2.cloned.1.call-start = ((), (), s32[]{:S(2)}) async-start(), calls=%async_computation.2 | async-start | bytes 4866048 | tf_op jit(solution)/shard_map/reduce_scatter | solution.py:920
  9.0 12.9 %collective-permute-start.2 = (bf16[24,1920]{1,0:T(8,128)(2,1)}, bf16[24,1920]{1,0:T(8,128)(2,1)S(1)}, u32[]{:S(2)}, u32[]{:S(2)}) collective-permute-start(bf16[24,1920]{1,0:T(8,128)(2,1)} %get-tuple-element.58), channel_id=1, source_target_pairs={{0,24},{2,26},{4,28},{6,30},{8,16},{10,18},{12,20},{14,22},{16,8},... | collective-permute-start | bytes 276488 | tf_op jit(solution)/shard_map/ppermute | solution.py:845
  14.2 7.9 %collective-permute-start.1 = (bf16[24,1920]{1,0:T(8,128)(2,1)}, bf16[24,1920]{1,0:T(8,128)(2,1)S(1)}, u32[]{:S(2)}, u32[]{:S(2)}) collective-permute-start(bf16[24,1920]{1,0:T(8,128)(2,1)} %get-tuple-element.58), channel_id=1, source_target_pairs={{0,16},{2,18},{4,20},{6,22},{8,24},{10,26},{12,28},{14,30},{16,0},... | collective-permute-start | bytes 276488 | tf_op jit(solution)/shard_map/ppermute | solution.py:845
  14.2 7.9 %collective-permute-start = (bf16[24,1920]{1,0:T(8,128)(2,1)}, bf16[24,1920]{1,0:T(8,128)(2,1)S(1)}, u32[]{:S(2)}, u32[]{:S(2)}) collective-permute-start(bf16[24,1920]{1,0:T(8,128)(2,1)} %get-tuple-element.58), channel_id=1, source_target_pairs={{0,8},{2,10},{4,12},{6,14},{8,0},{10,2},{12,4},{14,6},{16,24},{18,... | collective-permute-start | bytes 276488 | tf_op jit(solution)/shard_map/ppermute | solution.py:845
  15.6 6.5 %copy-start.21 = (bf16[24,1920]{1,0:T(8,128)(2,1)S(1)}, bf16[24,1920]{1,0:T(8,128)(2,1)}, u32[]{:S(2)}) copy-start(bf16[24,1920]{1,0:T(8,128)(2,1)} %get-tuple-element.58) | copy-start | bytes 276484
  21.9 10.1 %copy-start.19 = (bf16[2,1024,768]{2,1,0:T(8,128)(2,1)S(1)}, bf16[2,1024,768]{2,1,0:T(8,128)(2,1)}, u32[]{:S(2)}) copy-start(bf16[2,1024,768]{2,1,0:T(8,128)(2,1)} %param.14) | copy-start | bytes 9437188
  22.2 6.5 %collective-permute-start.5 = (bf16[4,24,896]{2,1,0:T(8,128)(2,1)S(1)}, bf16[4,24,896]{2,1,0:T(8,128)(2,1)S(1)}, u32[]{:S(2)}, u32[]{:S(2)}) collective-permute-start(bf16[4,24,896]{2,1,0:T(8,128)(2,1)S(1)} %get-tuple-element.117), channel_id=1, source_target_pairs={{0,4},{2,6},{4,0},{6,2},{8,12},{10,14},{12,8},{14,10},{16,20},{18,... | collective-permute-start | bytes 516104 | tf_op jit(solution)/shard_map/ppermute | solution.py:845
  23.8 7.4 %collective-permute-start.3 = (bf16[4,24,1024]{2,1,0:T(8,128)(2,1)S(1)}, bf16[4,24,1024]{2,1,0:T(8,128)(2,1)S(1)}, u32[]{:S(2)}, u32[]{:S(2)}) collective-permute-start(bf16[4,24,1024]{2,1,0:T(8,128)(2,1)S(1)} %get-tuple-element.119), channel_id=1, source_target_pairs={{0,2},{2,0},{4,6},{6,4},{8,10},{10,8},{12,14},{14,12},{16,18},{18,... | collective-permute-start | bytes 589832 | tf_op jit(solution)/shard_map/ppermute | solution.py:845
  28.8 9.2 %collective-permute-start.6 = (bf16[2,4,24,896]{3,2,1,0:T(8,128)(2,1)S(1)}, bf16[2,4,24,896]{3,2,1,0:T(8,128)(2,1)S(1)}, u32[]{:S(2)}, u32[]{:S(2)}) collective-permute-start(bf16[2,4,24,896]{3,2,1,0:T(8,128)(2,1)S(1)} %get-tuple-element.121), channel_id=1, source_target_pairs={{0,2},{2,0},{4,6},{6,4},{8,10},{10,8},{12,14},{14,12},{16,18},{18,... | collective-permute-start | bytes 1032200 | tf_op jit(solution)/shard_map/ppermute | solution.py:845
  31.3 9.4 %collective-permute-start.4 = (bf16[2,4,24,1024]{3,2,1,0:T(8,128)(2,1)S(1)}, bf16[2,4,24,1024]{3,2,1,0:T(8,128)(2,1)S(1)}, u32[]{:S(2)}, u32[]{:S(2)}) collective-permute-start(bf16[2,4,24,1024]{3,2,1,0:T(8,128)(2,1)S(1)} %pad_maximum_fusion.2), channel_id=1, source_target_pairs={{0,4},{2,6},{4,0},{6,2},{8,12},{10,14},{12,8},{14,10},{16,20},{18,... | collective-permute-start | bytes 1179656 | tf_op jit(solution)/shard_map/ppermute | solution.py:845
  32.0 4.1 %copy-start.22 = (s32[2,1024]{1,0:T(2,128)S(1)}, s32[2,1024]{1,0:T(2,128)}, u32[]{:S(2)}) copy-start(s32[2,1024]{1,0:T(2,128)} %param.15) | copy-start | bytes 24580
  38.1 5.0 %copy-start.1 = (bf16[2,2,4,24,896]{4,3,2,1,0:T(8,128)(2,1)}, bf16[2,2,4,24,896]{4,3,2,1,0:T(8,128)(2,1)S(1)}, u32[]{:S(2)}) copy-start(bf16[2,2,4,24,896]{4,3,2,1,0:T(8,128)(2,1)S(1)} %copy.29) | copy-start | bytes 2064388
  38.9 2.1 collective-permute-start.8
  40.8 2.4 copy-start.18
  40.8 2.4 collective-permute-start.7
  41.1 2.1 copy-start.4
  43.2 0.9 copy-start.20
  123.1 1.1 copy-start.2
  123.1 1.3 copy-start.5
  123.1 1.3 copy-start.9
  123.1 1.3 copy-start.10
  123.1 1.3 copy-start.12
  123.1 1.3 copy-start.13
  123.1 1.3 copy-start.14
  200.5 3.3 %collective-permute-start.9 = (bf16[16,24,1920]{2,1,0:T(8,128)(2,1)S(1)}, bf16[16,24,1920]{2,1,0:T(8,128)(2,1)S(1)}, u32[]{:S(2)}, u32[]{:S(2)}) collective-permute-start(bf16[16,24,1920]{2,1,0:T(8,128)(2,1)S(1)} %bitcast.72), channel_id=1, source_target_pairs={{0,1},{1,0},{2,3},{3,2},{4,5},{5,4},{6,7},{7,6},{8,9},{9,8},{10,11... | collective-permute-start | bytes 4423688 | tf_op jit(solution)/shard_map/ppermute | solution.py:845
  200.7 7.0 %copy-start.3 = (bf16[2048,768]{1,0:T(8,128)(2,1)S(1)}, bf16[2048,768]{1,0:T(8,128)(2,1)}, u32[]{:S(2)}) copy-start(bf16[2048,768]{1,0:T(8,128)(2,1)} %get-tuple-element.86.gproj) | copy-start | bytes 9437188
  200.8 6.9 %copy-start = (bf16[2048,768]{1,0:T(8,128)(2,1)S(1)}, bf16[2048,768]{1,0:T(8,128)(2,1)}, u32[]{:S(2)}) copy-start(bf16[2048,768]{1,0:T(8,128)(2,1)} %convolution_bitcast_fusion.1.first.tok) | copy-start | bytes 9437188
  200.9 6.9 %copy-start.15 = (f32[1,768]{1,0:T(1,128)S(1)}, f32[1,768]{1,0:T(1,128)}, u32[]{:S(2)}) copy-start(f32[1,768]{1,0:T(1,128)} %get-tuple-element.89.gain) | copy-start | bytes 9220
  204.2 20.3 %collective-permute-start.12 = (bf16[4,24,1920]{2,1,0:T(8,128)(2,1)S(1)}, bf16[4,24,1920]{2,1,0:T(8,128)(2,1)S(1)}, u32[]{:S(2)}, u32[]{:S(2)}) collective-permute-start(bf16[4,24,1920]{2,1,0:T(8,128)(2,1)S(1)} %get-tuple-element.106), channel_id=1, source_target_pairs={{0,6},{2,4},{4,2},{6,0},{8,14},{10,12},{12,10},{14,8},{16,22},{18,... | collective-permute-start | bytes 1105928 | tf_op jit(solution)/shard_map/ppermute | solution.py:845
  206.0 18.8 %collective-permute-start.11 = (bf16[4,24,1920]{2,1,0:T(8,128)(2,1)S(1)}, bf16[4,24,1920]{2,1,0:T(8,128)(2,1)S(1)}, u32[]{:S(2)}, u32[]{:S(2)}) collective-permute-start(bf16[4,24,1920]{2,1,0:T(8,128)(2,1)S(1)} %get-tuple-element.107), channel_id=1, source_target_pairs={{0,4},{2,6},{4,0},{6,2},{8,12},{10,14},{12,8},{14,10},{16,20},{18,... | collective-permute-start | bytes 1105928 | tf_op jit(solution)/shard_map/ppermute | solution.py:845
  206.0 18.7 %collective-permute-start.10 = (bf16[4,24,1920]{2,1,0:T(8,128)(2,1)S(1)}, bf16[4,24,1920]{2,1,0:T(8,128)(2,1)S(1)}, u32[]{:S(2)}, u32[]{:S(2)}) collective-permute-start(bf16[4,24,1920]{2,1,0:T(8,128)(2,1)S(1)} %get-tuple-element.105), channel_id=1, source_target_pairs={{0,2},{2,0},{4,6},{6,4},{8,10},{10,8},{12,14},{14,12},{16,18},{18,... | collective-permute-start | bytes 1105928 | tf_op jit(solution)/shard_map/ppermute | solution.py:845
  224.5 5.0 %copy-start.6 = (bf16[1536,768]{1,0:T(8,128)(2,1)S(1)}, bf16[1536,768]{1,0:T(8,128)(2,1)}, u32[]{:S(2)}) copy-start(bf16[1536,768]{1,0:T(8,128)(2,1)} %get-tuple-element.91.wo) | copy-start | bytes 7077892
  225.0 13.3 %collective-permute-start.13 = (bf16[24,1920]{1,0:T(8,128)(2,1)S(1)}, bf16[24,1920]{1,0:T(8,128)(2,1)S(1)}, u32[]{:S(2)}, u32[]{:S(2)}) collective-permute-start(bf16[24,1920]{1,0:T(8,128)(2,1)S(1)} %get-tuple-element.115), channel_id=1, source_target_pairs={{0,8},{2,10},{4,12},{6,14},{8,0},{10,2},{12,4},{14,6},{16,24},{18,... | collective-permute-start | bytes 276488 | tf_op jit(solution)/shard_map/ppermute | solution.py:845
  226.7 11.7 %collective-permute-start.14 = (bf16[24,1920]{1,0:T(8,128)(2,1)S(1)}, bf16[24,1920]{1,0:T(8,128)(2,1)S(1)}, u32[]{:S(2)}, u32[]{:S(2)}) collective-permute-start(bf16[24,1920]{1,0:T(8,128)(2,1)S(1)} %get-tuple-element.114), channel_id=1, source_target_pairs={{0,16},{2,18},{4,20},{6,22},{8,24},{10,26},{12,28},{14,30},{16,0},... | collective-permute-start | bytes 276488 | tf_op jit(solution)/shard_map/ppermute | solution.py:845
  228.9 9.5 %collective-permute-start.15 = (bf16[24,1920]{1,0:T(8,128)(2,1)S(1)}, bf16[24,1920]{1,0:T(8,128)(2,1)S(1)}, u32[]{:S(2)}, u32[]{:S(2)}) collective-permute-start(bf16[24,1920]{1,0:T(8,128)(2,1)S(1)} %get-tuple-element.113), channel_id=1, source_target_pairs={{0,24},{2,26},{4,28},{6,30},{8,16},{10,18},{12,20},{14,22},{16,8},... | collective-permute-start | bytes 276488 | tf_op jit(solution)/shard_map/ppermute | solution.py:845
  229.5 8.9 %copy-start.7 = (bf16[24,3352]{1,0:T(8,128)(2,1)S(1)}, bf16[24,3352]{1,0:T(8,128)(2,1)}, u32[]{:S(2)}) copy-start(bf16[24,3352]{1,0:T(8,128)(2,1)} %w_in.3) | copy-start | bytes 482692
  229.5 8.9 %copy-start.8 = (bf16[48,768]{1,0:T(8,128)(2,1)S(1)}, bf16[48,768]{1,0:T(8,128)(2,1)}, u32[]{:S(2)}) copy-start(bf16[48,768]{1,0:T(8,128)(2,1)} %w_out.3) | copy-start | bytes 221188
  229.5 8.9 %copy-start.16 = (bf16[24]{0:T(256)(128)(2,1)S(1)}, bf16[24]{0:T(256)(128)(2,1)}, u32[]{:S(2)}) copy-start(bf16[24]{0:T(256)(128)(2,1)} %param.16) | copy-start | bytes 148
  229.5 8.9 %copy-start.17 = (bf16[48]{0:T(256)(128)(2,1)S(1)}, bf16[48]{0:T(256)(128)(2,1)}, u32[]{:S(2)}) copy-start(bf16[48]{0:T(256)(128)(2,1)} %param.23) | copy-start | bytes 292
  238.4 0.9 copy-start.11
Sparse Core Ops, SparseCore 0:
  11.5 66.8 all-gather.1
  123.3 107.4 reduce-scatter.1

commit v8 on v6

--- a/solution.py
+++ b/solution.py
@@ -118,8 +118,8 @@
             value = value - part
     wc_o[0:16, CONV:] = (wc_o[0:16, CONV:].astype(f32) + rows[...]).astype(bf16)
     later_o[:, :DI] = w_in[:, :DI]
-    later_o[:, DI : DI + D] = w_out[0:ri, :]
-    later_o[:, DI + D :] = w_out[ri:, :]
+    later_o[:, DI : DI + D] = w_out[0]
+    later_o[:, DI + D :] = w_out[1]
 
 
 def pack(w_in, w_out, in_gain, cw, cb, gg, sb, dl, sg, ri, tall):
@@ -128,7 +128,7 @@
         out_shape=[jax.ShapeDtypeStruct((tall, CONV + 128), bf16), jax.ShapeDtypeStruct((ri, 2 * DI), bf16)],
         scratch_shapes=[pltpu.VMEM((16, 128), f32)],
         name="pack",
-    )(w_in, w_out, in_gain, cw, cb, gg, sb, dl, sg)
+    )(w_in, w_out.reshape(2, ri, D), in_gain, cw, cb, gg, sb, dl, sg)
 
 
 def unpack_small(ri, ro, share, first_lane, small, device, onehot, gain, gain_abs, cw, cb, gg, heads_o, skip):
@@ -896,13 +896,13 @@
     tok_s = jnp.dot(tok, order, preferred_element_type=bf16)
     device_rows = jnp.broadcast_to(device.astype(f32)[:, None], (nd, 128))
     seg = segments.reshape(rows // Q, 1, Q)
-    wc, tok_s, device_rows, seg = before(wc, tok_s, device_rows, seg)
+    wc, tok_s = before(wc, tok_s)
     one, two = wc[..., :SPLIT], wc[..., SPLIT:]
     for stage in stages[1:-1]:
         one = gather_stage(one, stage, sizes, 1)
         two = gather_stage(two, stage, sizes, 2)
     up_s = jnp.dot(up, order, preferred_element_type=bf16)
-    two, up_s = before(two, up_s)
+    two, up_s, device_rows, seg = before(two, up_s, device_rows, seg)
     axis, stride = stages[-1][:2]
     quarters = [part.reshape(nd // 2, tall, part.shape[-1])
                 for part in (one, two, swap(one, axis, sizes[axis], stride), swap(two, axis, sizes[axis], stride))]

time: 248 us -> 247 us (level)
  transfers between devices with their start and end apart: 18 -> 18, of which waited for: 5 -> 9; matrix products, arithmetic and copies ran while one was open for 6% -> 6% of each run, Pallas kernels for 58% -> 58%
where the time goes in v8:
time: 247 us
  Pallas kernels  183 us (74%)
  starting transfers between devices  19.5 us (8%)
  between operations  14.4 us (6%)
  waiting for transfers between devices  12.2 us (5%)
  matrix products  10.4 us (4%)
  local copies, waits for them, and re-layouts  4.95 us (2%)
    pallas_call x1, Pallas kernels, backward_scan(): pl.pallas_call(functools.partial(backward_scan_kernel, heads, n // seqs,...  65.9 us
    pallas_call x1, Pallas kernels, forward_scan(): pl.pallas_call(functools.partial(forward_scan_kernel, heads, n // seqs, r...  41.7 us
    pallas_call x1, Pallas kernels, gate_pass(): pl.pallas_call(functools.partial(gate_kernel, ri), grid=(rows // bm,), in...  37.2 us
    ppermute x16, starting transfers between devices, swap(): return lax.ppermute(arr, axis, [(i, i ^ offset) for i in range(size)])  19.4 us
    pallas_call x1, Pallas kernels, norm_back(): pl.pallas_call(functools.partial(norm_back_kernel, ri), grid=(rows // bm,...  16.7 us
    ppermute x16, waiting for transfers between devices, swap(): return lax.ppermute(arr, axis, [(i, i ^ offset) for i in range(size)])  12.1 us
    pallas_call x1, Pallas kernels, conv_weight_grad(): pl.pallas_call(conv_weight_kernel, grid=((CONV + 128) // bn,), in_specs=[...  10.2 us
    pallas_call x1, Pallas kernels, out_pass(): pl.pallas_call(out_kernel, grid=(rows // bm,), in_specs=[blk(DI), blk(D),...  8.81 us
  transfers between devices with their start and end apart: 18, of which 9 were waited for; matrix products, arithmetic and copies ran while one was open for 6% of the time, Pallas kernels for 58%

profile of v8, /device:TPU:0, one launch (start us, length us, event | category | flops | bytes accessed | tf_op | source)
XLA Modules:
  0.0 247.0 jit_solution(18394683249386817921)
XLA Ops:
  7.2 0.0 all-gather.2.cloned.1.call-start
  7.2 1.7 pack.1
  9.0 0.0 all-gather.2.cloned.1.call-update
  9.0 0.0 reduce-scatter.2.cloned.1.call-start
  9.0 5.1 %collective-permute-start.2 = (bf16[24,1920]{1,0:T(8,128)(2,1)}, bf16[24,1920]{1,0:T(8,128)(2,1)S(1)}, u32[]{:S(2)}, u32[]{:S(2)}) collective-permute-start(bf16[24,1920]{1,0:T(8,128)(2,1)} %get-tuple-element.58), channel_id=1, source_target_pairs={{0,24},{2,26},{4,28},{6,30},{8,16},{10,18},{12,20},{14,22},{16,8},... | collective-permute-start | bytes 276488 | tf_op jit(solution)/shard_map/ppermute | solution.py:841
  14.2 0.6 collective-permute-start
  14.8 0.7 xor_convert_fusion
  15.5 0.1 iota_add_fusion
  15.5 0.1 add.50
  15.6 0.0 copy-start.21
  15.6 6.3 %convolution_bitcast_fusion.1.first.tok = bf16[2048,768]{1,0:T(8,128)(2,1)} fusion(bf16[2048,768]{1,0:T(8,128)(2,1)} %bitcast.75, s32[768]{0:T(1024)S(1)} %add.50), kind=kOutput, calls=%fused_computation.1 | convolution fusion | flops 2416508928 | bytes 6294528 | tf_op jit(solution)/shard_map/dot_general | solution.py:896
  21.9 0.0 collective-permute-done.2
  21.9 0.2 collective-permute-done.1
  22.1 0.0 collective-permute-done
  22.1 0.1 pad_maximum_fusion.3
  22.2 1.6 collective-permute-start.5
  23.8 1.6 collective-permute-start.3
  25.4 3.4 %collective-permute-done.5 = bf16[4,24,896]{2,1,0:T(8,128)(2,1)S(1)} collective-permute-done((bf16[4,24,896]{2,1,0:T(8,128)(2,1)S(1)}, bf16[4,24,896]{2,1,0:T(8,128)(2,1)S(1)}, u32[]{:S(2)}, u32[]{:S(2)}) %collective-permute-start.5) | collective-permute-done | bytes 172064 | tf_op jit(solution)/shard_map/ppermute | solution.py:841
  28.8 0.1 fusion.5
  28.8 1.6 collective-permute-start.6
  30.4 0.9 collective-permute-done.3
  31.3 0.7 collective-permute-start.4
  32.0 4.1 %convolution_bitcast_fusion.cot = bf16[2048,768]{1,0:T(8,128)(2,1)} fusion(bf16[2048,768]{1,0:T(8,128)(2,1)S(1)} %bitcast.82, s32[768]{0:T(1024)S(1)} %add.50), kind=kOutput, calls=%fused_computation | convolution fusion | flops 2416508928 | bytes 6294528 | tf_op jit(solution)/shard_map/dot_general | solution.py:904
  36.1 0.6 reshape.101.seg.seg_before
  36.7 1.3 collective-permute-done.6
  38.0 0.1 pad_maximum_fusion.1
  38.1 0.1 copy.29
  38.1 0.8 broadcast_in_dim.35.device
  38.9 1.8 collective-permute-done.4
  40.7 0.1 pad_maximum_fusion
  40.8 0.1 collective-permute-start.7
  40.9 0.1 collective-permute-done.8
  41.1 0.8 convert_bitcast_fusion.small
  41.9 1.2 collective-permute-done.7
  43.2 0.9 copy-done.20
  44.1 41.7 %forward_scan.1 = (bf16[2048,1792]{1,0:T(8,128)(2,1)}, bf16[2048,1792]{1,0:T(8,128)(2,1)}, bf16[2048,1792]{1,0:T(8,128)(2,1)}, bf16[2048,768]{1,0:T(8,128)(2,1)}...) custom-call(bf16[2048,768]{1,0:T(8,128)(2,1)} %convolution_bitcast_f, ...), custom_call_target="tpu_custom_call" | custom-call | tf_op jit(solution)/shard_map/forward_scan/pallas_call | solution.py:294
  85.8 0.0 all-gather.2.cloned.1.call-done.later_in.wg_abs
  85.9 37.2 %gate_pass.1 = (bf16[2048,1536]{1,0:T(8,128)(2,1)}, bf16[2048,1536]{1,0:T(8,128)(2,1)}, bf16[2048,1536]{1,0:T(8,128)(2,1)}, bf16[768,3072]{1,0:T(8,128)(2,1)}, bf16[1536,768]{1,0:T(8,128)(2,1)}) custom-call(bf16[2048,768]{1,0:T(8,128)(2,1)} %bitcast.76, bf16[2048,1536]{1,0:T(8,128)(2,1)} %get-tuple-element.64.scan, bf16[2048,768]{1,0:T(8,128)(2,1)} %bitcast.81, ...), custom_call_target="tpu_custom_call" | custom-call | tf_op jit(solution)/shard_map/gate_pass/pallas_call | solution.py:446
  123.2 0.0 reduce-scatter.2.cloned.1.call-update
  123.2 1.0 copy-done.2
  124.2 0.2 copy-done.5
  124.4 65.9 %backward_scan.1 = (bf16[2048,1920]{1,0:T(8,128)(2,1)}, bf16[2048,768]{1,0:T(8,128)(2,1)}, bf16[768,128]{1,0:T(8,128)(2,1)S(1)}) custom-call(bf16[2048,1536]{1,0:T(8,128)(2,1)} %get-tuple-element.71.dscan, bf16[2048,1792]{1,0:T(8,128)(2,1)} %get-tuple-element.72.cin, bf16[2048,1792]{1,0:T(8,128)(2,1)} %get-tuple-element.73.act, ...), custom_call_target="tpu_custom_call" | custom-call | tf_op jit(solution)/shard_map/backward_scan/pallas_call | solution.py:677
  190.4 10.2 %conv_weight_grad.1 = (bf16[384,1920]{1,0:T(8,128)(2,1)S(1)}, bf16[384,1920]{1,0:T(8,128)(2,1)S(1)}) custom-call(bf16[2048,768]{1,0:T(8,128)(2,1)} %get-tuple-element.70.nrm, bf16[2048,1920]{1,0:T(8,128)(2,1)} %get-tuple-element.80.dproj, bf16[768,128]{1,0:T(8,128)(2,1)S(1)} %get-tuple-element.81.small), custom_call_target="tpu_custom_call" | custom-call | tf_op jit(solution)/shard_map/conv_weight_grad/pallas_call | solution.py:756
  200.5 0.2 collective-permute-start.9
  200.7 0.1 fusion.6
  200.8 0.0 copy-start
  200.9 3.0 %collective-permute-done.9 = bf16[16,24,1920]{2,1,0:T(8,128)(2,1)S(1)} collective-permute-done((bf16[16,24,1920]{2,1,0:T(8,128)(2,1)S(1)}, bf16[16,24,1920]{2,1,0:T(8,128)(2,1)S(1)}, u32[]{:S(2)}, u32[]{:S(2)}) %collective-permute-start.9) | collective-permute-done | bytes 1474592 | tf_op jit(solution)/shard_map/ppermute | solution.py:841
  203.9 0.3 fusion.4
  204.2 1.8 collective-permute-start.12
  206.0 0.0 collective-permute-start.11
  206.0 1.7 collective-permute-start.10
  207.8 16.7 %norm_back.1 = bf16[2048,768]{1,0:T(8,128)(2,1)} custom-call(bf16[2048,768]{1,0:T(8,128)(2,1)S(1)} %copy-done.3, bf16[2048,1536]{1,0:T(8,128)(2,1)} %get-tuple-element.87.dgate, bf16[2048,768]{1,0:T(8,128)(2,1)S(1)} %copy-done, bf16[2048,768]{1,0:T(8,128)(2,1)} %convolution_bitcast_fusion.cot, ...), custom_call_target="tpu_custom_call" | custom-call | tf_op jit(solution)/shard_map/norm_back/pallas_call | solution.py:725
  224.5 0.2 collective-permute-done.11
  224.8 0.2 convert_add_fusion.4
  225.0 1.7 collective-permute-start.13
  226.7 2.2 collective-permute-start.14
  228.9 0.6 collective-permute-start.15
  229.5 0.0 copy-start.7
  229.5 0.0 copy-start.8
  229.5 0.0 copy-start.16
  229.5 0.0 copy-start.17
  229.6 8.8 %out_pass.1 = bf16[2048,768]{1,0:T(8,128)(2,1)} custom-call(bf16[2048,1536]{1,0:T(8,128)(2,1)} %get-tuple-element.69.mixed, bf16[2048,768]{1,0:T(8,128)(2,1)} %bitcast.77, bf16[1536,768]{1,0:T(8,128)(2,1)S(1)} %copy-done.6), custom_call_target="tpu_custom_call" | custom-call | tf_op jit(solution)/shard_map/out_pass/pallas_call | solution.py:469
  238.4 0.9 copy-done.11
  239.3 0.9 finish.1
  (54 shorter events, 0.3 us)
Async XLA Ops:
  7.2 78.7 %all-gather.2.cloned.1.call-start = ((), (), s32[]{:S(2)}) async-start(), calls=%async_computation.1 | async-start | bytes 4866048 | tf_op jit(solution)/shard_map/all_gather | solution.py:892
  9.0 229.4 %reduce-scatter.2.cloned.1.call-start = ((), (), s32[]{:S(2)}) async-start(), calls=%async_computation.2 | async-start | bytes 4866048 | tf_op jit(solution)/shard_map/reduce_scatter | solution.py:916
  9.0 12.9 %collective-permute-start.2 = (bf16[24,1920]{1,0:T(8,128)(2,1)}, bf16[24,1920]{1,0:T(8,128)(2,1)S(1)}, u32[]{:S(2)}, u32[]{:S(2)}) collective-permute-start(bf16[24,1920]{1,0:T(8,128)(2,1)} %get-tuple-element.58), channel_id=1, source_target_pairs={{0,24},{2,26},{4,28},{6,30},{8,16},{10,18},{12,20},{14,22},{16,8},... | collective-permute-start | bytes 276488 | tf_op jit(solution)/shard_map/ppermute | solution.py:841
  14.2 7.9 %collective-permute-start.1 = (bf16[24,1920]{1,0:T(8,128)(2,1)}, bf16[24,1920]{1,0:T(8,128)(2,1)S(1)}, u32[]{:S(2)}, u32[]{:S(2)}) collective-permute-start(bf16[24,1920]{1,0:T(8,128)(2,1)} %get-tuple-element.58), channel_id=1, source_target_pairs={{0,16},{2,18},{4,20},{6,22},{8,24},{10,26},{12,28},{14,30},{16,0},... | collective-permute-start | bytes 276488 | tf_op jit(solution)/shard_map/ppermute | solution.py:841
  14.2 7.9 %collective-permute-start = (bf16[24,1920]{1,0:T(8,128)(2,1)}, bf16[24,1920]{1,0:T(8,128)(2,1)S(1)}, u32[]{:S(2)}, u32[]{:S(2)}) collective-permute-start(bf16[24,1920]{1,0:T(8,128)(2,1)} %get-tuple-element.58), channel_id=1, source_target_pairs={{0,8},{2,10},{4,12},{6,14},{8,0},{10,2},{12,4},{14,6},{16,24},{18,... | collective-permute-start | bytes 276488 | tf_op jit(solution)/shard_map/ppermute | solution.py:841
  15.6 6.5 %copy-start.21 = (bf16[24,1920]{1,0:T(8,128)(2,1)S(1)}, bf16[24,1920]{1,0:T(8,128)(2,1)}, u32[]{:S(2)}) copy-start(bf16[24,1920]{1,0:T(8,128)(2,1)} %get-tuple-element.58) | copy-start | bytes 276484
  21.9 10.1 %copy-start.19 = (bf16[2,1024,768]{2,1,0:T(8,128)(2,1)S(1)}, bf16[2,1024,768]{2,1,0:T(8,128)(2,1)}, u32[]{:S(2)}) copy-start(bf16[2,1024,768]{2,1,0:T(8,128)(2,1)} %param.14) | copy-start | bytes 9437188
  22.2 6.5 %collective-permute-start.5 = (bf16[4,24,896]{2,1,0:T(8,128)(2,1)S(1)}, bf16[4,24,896]{2,1,0:T(8,128)(2,1)S(1)}, u32[]{:S(2)}, u32[]{:S(2)}) collective-permute-start(bf16[4,24,896]{2,1,0:T(8,128)(2,1)S(1)} %get-tuple-element.117), channel_id=1, source_target_pairs={{0,4},{2,6},{4,0},{6,2},{8,12},{10,14},{12,8},{14,10},{16,20},{18,... | collective-permute-start | bytes 516104 | tf_op jit(solution)/shard_map/ppermute | solution.py:841
  23.8 7.4 %collective-permute-start.3 = (bf16[4,24,1024]{2,1,0:T(8,128)(2,1)S(1)}, bf16[4,24,1024]{2,1,0:T(8,128)(2,1)S(1)}, u32[]{:S(2)}, u32[]{:S(2)}) collective-permute-start(bf16[4,24,1024]{2,1,0:T(8,128)(2,1)S(1)} %get-tuple-element.119), channel_id=1, source_target_pairs={{0,2},{2,0},{4,6},{6,4},{8,10},{10,8},{12,14},{14,12},{16,18},{18,... | collective-permute-start | bytes 589832 | tf_op jit(solution)/shard_map/ppermute | solution.py:841
  28.8 9.2 %collective-permute-start.6 = (bf16[2,4,24,896]{3,2,1,0:T(8,128)(2,1)S(1)}, bf16[2,4,24,896]{3,2,1,0:T(8,128)(2,1)S(1)}, u32[]{:S(2)}, u32[]{:S(2)}) collective-permute-start(bf16[2,4,24,896]{3,2,1,0:T(8,128)(2,1)S(1)} %get-tuple-element.121), channel_id=1, source_target_pairs={{0,2},{2,0},{4,6},{6,4},{8,10},{10,8},{12,14},{14,12},{16,18},{18,... | collective-permute-start | bytes 1032200 | tf_op jit(solution)/shard_map/ppermute | solution.py:841
  31.3 9.4 %collective-permute-start.4 = (bf16[2,4,24,1024]{3,2,1,0:T(8,128)(2,1)S(1)}, bf16[2,4,24,1024]{3,2,1,0:T(8,128)(2,1)S(1)}, u32[]{:S(2)}, u32[]{:S(2)}) collective-permute-start(bf16[2,4,24,1024]{3,2,1,0:T(8,128)(2,1)S(1)} %pad_maximum_fusion.2), channel_id=1, source_target_pairs={{0,4},{2,6},{4,0},{6,2},{8,12},{10,14},{12,8},{14,10},{16,20},{18,... | collective-permute-start | bytes 1179656 | tf_op jit(solution)/shard_map/ppermute | solution.py:841
  32.0 4.1 %copy-start.22 = (s32[2,1024]{1,0:T(2,128)S(1)}, s32[2,1024]{1,0:T(2,128)}, u32[]{:S(2)}) copy-start(s32[2,1024]{1,0:T(2,128)} %param.15) | copy-start | bytes 24580
  38.1 5.0 %copy-start.1 = (bf16[2,2,4,24,896]{4,3,2,1,0:T(8,128)(2,1)}, bf16[2,2,4,24,896]{4,3,2,1,0:T(8,128)(2,1)S(1)}, u32[]{:S(2)}) copy-start(bf16[2,2,4,24,896]{4,3,2,1,0:T(8,128)(2,1)S(1)} %copy.29) | copy-start | bytes 2064388
  38.9 2.1 collective-permute-start.8
  40.8 2.4 copy-start.18
  40.8 2.4 collective-permute-start.7
  41.1 2.1 copy-start.4
  43.2 0.9 copy-start.20
  123.1 1.1 copy-start.2
  123.1 1.3 copy-start.5
  123.1 1.3 copy-start.9
  123.1 1.3 copy-start.10
  123.1 1.3 copy-start.12
  123.1 1.3 copy-start.13
  123.1 1.3 copy-start.14
  200.5 3.3 %collective-permute-start.9 = (bf16[16,24,1920]{2,1,0:T(8,128)(2,1)S(1)}, bf16[16,24,1920]{2,1,0:T(8,128)(2,1)S(1)}, u32[]{:S(2)}, u32[]{:S(2)}) collective-permute-start(bf16[16,24,1920]{2,1,0:T(8,128)(2,1)S(1)} %bitcast.74), channel_id=1, source_target_pairs={{0,1},{1,0},{2,3},{3,2},{4,5},{5,4},{6,7},{7,6},{8,9},{9,8},{10,11... | collective-permute-start | bytes 4423688 | tf_op jit(solution)/shard_map/ppermute | solution.py:841
  200.7 7.0 %copy-start.3 = (bf16[2048,768]{1,0:T(8,128)(2,1)S(1)}, bf16[2048,768]{1,0:T(8,128)(2,1)}, u32[]{:S(2)}) copy-start(bf16[2048,768]{1,0:T(8,128)(2,1)} %get-tuple-element.86.gproj) | copy-start | bytes 9437188
  200.8 6.9 %copy-start = (bf16[2048,768]{1,0:T(8,128)(2,1)S(1)}, bf16[2048,768]{1,0:T(8,128)(2,1)}, u32[]{:S(2)}) copy-start(bf16[2048,768]{1,0:T(8,128)(2,1)} %convolution_bitcast_fusion.1.first.tok) | copy-start | bytes 9437188
  200.9 6.9 %copy-start.15 = (f32[1,768]{1,0:T(1,128)S(1)}, f32[1,768]{1,0:T(1,128)}, u32[]{:S(2)}) copy-start(f32[1,768]{1,0:T(1,128)} %get-tuple-element.89.gain) | copy-start | bytes 9220
  204.2 20.3 %collective-permute-start.12 = (bf16[4,24,1920]{2,1,0:T(8,128)(2,1)S(1)}, bf16[4,24,1920]{2,1,0:T(8,128)(2,1)S(1)}, u32[]{:S(2)}, u32[]{:S(2)}) collective-permute-start(bf16[4,24,1920]{2,1,0:T(8,128)(2,1)S(1)} %get-tuple-element.106), channel_id=1, source_target_pairs={{0,6},{2,4},{4,2},{6,0},{8,14},{10,12},{12,10},{14,8},{16,22},{18,... | collective-permute-start | bytes 1105928 | tf_op jit(solution)/shard_map/ppermute | solution.py:841
  206.0 18.8 %collective-permute-start.11 = (bf16[4,24,1920]{2,1,0:T(8,128)(2,1)S(1)}, bf16[4,24,1920]{2,1,0:T(8,128)(2,1)S(1)}, u32[]{:S(2)}, u32[]{:S(2)}) collective-permute-start(bf16[4,24,1920]{2,1,0:T(8,128)(2,1)S(1)} %get-tuple-element.107), channel_id=1, source_target_pairs={{0,4},{2,6},{4,0},{6,2},{8,12},{10,14},{12,8},{14,10},{16,20},{18,... | collective-permute-start | bytes 1105928 | tf_op jit(solution)/shard_map/ppermute | solution.py:841
  206.0 18.7 %collective-permute-start.10 = (bf16[4,24,1920]{2,1,0:T(8,128)(2,1)S(1)}, bf16[4,24,1920]{2,1,0:T(8,128)(2,1)S(1)}, u32[]{:S(2)}, u32[]{:S(2)}) collective-permute-start(bf16[4,24,1920]{2,1,0:T(8,128)(2,1)S(1)} %get-tuple-element.105), channel_id=1, source_target_pairs={{0,2},{2,0},{4,6},{6,4},{8,10},{10,8},{12,14},{14,12},{16,18},{18,... | collective-permute-start | bytes 1105928 | tf_op jit(solution)/shard_map/ppermute | solution.py:841
  224.5 5.0 %copy-start.6 = (bf16[1536,768]{1,0:T(8,128)(2,1)S(1)}, bf16[1536,768]{1,0:T(8,128)(2,1)}, u32[]{:S(2)}) copy-start(bf16[1536,768]{1,0:T(8,128)(2,1)} %get-tuple-element.91.wo) | copy-start | bytes 7077892
  225.0 13.3 %collective-permute-start.13 = (bf16[24,1920]{1,0:T(8,128)(2,1)S(1)}, bf16[24,1920]{1,0:T(8,128)(2,1)S(1)}, u32[]{:S(2)}, u32[]{:S(2)}) collective-permute-start(bf16[24,1920]{1,0:T(8,128)(2,1)S(1)} %get-tuple-element.115), channel_id=1, source_target_pairs={{0,8},{2,10},{4,12},{6,14},{8,0},{10,2},{12,4},{14,6},{16,24},{18,... | collective-permute-start | bytes 276488 | tf_op jit(solution)/shard_map/ppermute | solution.py:841
  226.7 11.7 %collective-permute-start.14 = (bf16[24,1920]{1,0:T(8,128)(2,1)S(1)}, bf16[24,1920]{1,0:T(8,128)(2,1)S(1)}, u32[]{:S(2)}, u32[]{:S(2)}) collective-permute-start(bf16[24,1920]{1,0:T(8,128)(2,1)S(1)} %get-tuple-element.114), channel_id=1, source_target_pairs={{0,16},{2,18},{4,20},{6,22},{8,24},{10,26},{12,28},{14,30},{16,0},... | collective-permute-start | bytes 276488 | tf_op jit(solution)/shard_map/ppermute | solution.py:841
  228.9 9.5 %collective-permute-start.15 = (bf16[24,1920]{1,0:T(8,128)(2,1)S(1)}, bf16[24,1920]{1,0:T(8,128)(2,1)S(1)}, u32[]{:S(2)}, u32[]{:S(2)}) collective-permute-start(bf16[24,1920]{1,0:T(8,128)(2,1)S(1)} %get-tuple-element.113), channel_id=1, source_target_pairs={{0,24},{2,26},{4,28},{6,30},{8,16},{10,18},{12,20},{14,22},{16,8},... | collective-permute-start | bytes 276488 | tf_op jit(solution)/shard_map/ppermute | solution.py:841
  229.5 8.9 %copy-start.7 = (bf16[24,3352]{1,0:T(8,128)(2,1)S(1)}, bf16[24,3352]{1,0:T(8,128)(2,1)}, u32[]{:S(2)}) copy-start(bf16[24,3352]{1,0:T(8,128)(2,1)} %w_in.3) | copy-start | bytes 482692
  229.5 8.9 %copy-start.8 = (bf16[48,768]{1,0:T(8,128)(2,1)S(1)}, bf16[48,768]{1,0:T(8,128)(2,1)}, u32[]{:S(2)}) copy-start(bf16[48,768]{1,0:T(8,128)(2,1)} %w_out.1) | copy-start | bytes 221188
  229.5 8.9 %copy-start.16 = (bf16[24]{0:T(256)(128)(2,1)S(1)}, bf16[24]{0:T(256)(128)(2,1)}, u32[]{:S(2)}) copy-start(bf16[24]{0:T(256)(128)(2,1)} %param.16) | copy-start | bytes 148
  229.5 8.9 %copy-start.17 = (bf16[48]{0:T(256)(128)(2,1)S(1)}, bf16[48]{0:T(256)(128)(2,1)}, u32[]{:S(2)}) copy-start(bf16[48]{0:T(256)(128)(2,1)} %param.23) | copy-start | bytes 292
  238.4 0.9 copy-start.11
Sparse Core Ops, SparseCore 0:
  11.5 66.8 all-gather.1
  123.3 107.4 reduce-scatter.1
